TPU v7x, 32 devices: a whole 2x2x4 slice. The times are simulated.
32 devices in a mesh: groups: 2 (over y), dp: 8 (over z, x), tensor: 2 (over core).
Axes of the slice: x: 2, y: 2, z: 4, core: 2. Of those that a mesh axis runs over, the one named last changes fastest.
Arguments:
- hidden_in: bfloat16 [4096, 12288], P(('groups', 'dp'), 'tensor'), parts along dimension 0
- norm_gain: bfloat16 [12288], P('tensor')
- projection: bfloat16 [2, 6144, 1024], P('tensor', 'dp')
- lengths: int32 [16, 2], P(('groups', 'dp')), parts along dimension 0, may hold values from 16 to 240, as said below
Outputs:
- context: bfloat16 [4096, 768], P(('groups', 'dp'), 'tensor'), parts along dimension 0
There are 2 independent parts, one for each index of `groups`. A program takes and returns all parts, laid end to end along the dimension named above; an argument that names none is the same for every part. Nothing has to cross between parts.
Inputs may be any that keep to these rules, and one draw needn't show every extreme that they name: `lengths`: column 0 is the prompt length, at least 16 and at most 128; column 1 the response length; their sum is at most 256, and equals 256 in every rollout of even index.
All inputs are finite; a program needn't handle non-finite values.
Results may differ from a plain program's by a relative error of at most 0.017.
Values may be sent and summed in bfloat16 or wider, within the bound.
No kernel may reach another device: no remote copies, remote signals or barrier semaphores. Data moves between devices by JAX's collectives and lax.ppermute only.
A program may use at most 64 MiB of HBM per device.

v0:
```python
import jax
import jax.numpy as jnp
from jax import lax
from jax.sharding import PartitionSpec as P

D = 12288
HEAD = 128
QHEADS = 6


ROPE_BASE = 1000000.0
EPSILON = 1e-05


def rotate(block, positions):
    half = block.shape[-1] // 2
    freq = ROPE_BASE ** (-(jnp.arange(half, dtype=jnp.float32) * 2.0 / block.shape[-1]))
    angle = positions.astype(jnp.float32)[:, None] * freq[None, :]
    cosine = jnp.cos(angle)[:, None, :]
    sine = jnp.sin(angle)[:, None, :]
    first = block[..., :half]
    second = block[..., half:]
    return jnp.concatenate(
        [first * cosine - second * sine, second * cosine + first * sine], axis=-1
    )


def attend(query_cols, key_value, length_pair, head_count):
    seq_len = query_cols.shape[0]
    positions = jnp.arange(seq_len, dtype=jnp.int32)
    queries = rotate(query_cols.reshape(seq_len, head_count, HEAD), positions).astype(jnp.bfloat16)
    keys = rotate(key_value[:, None, :HEAD], positions)[:, 0, :].astype(jnp.bfloat16)
    values = key_value[:, HEAD:].astype(jnp.bfloat16)
    scores = jnp.einsum(
        "qhd,kd->hqk", queries, keys, preferred_element_type=jnp.float32
    ) * HEAD ** (-0.5)
    total_len = length_pair[0] + length_pair[1]
    allowed = (positions[None, :] <= positions[:, None]) & (positions[None, :] < total_len)
    scores = jnp.where(allowed[None, :, :], scores, -1e30)
    largest = jnp.max(scores, axis=-1, keepdims=True)
    expo = jnp.exp(scores - largest)
    attn = (expo / jnp.sum(expo, axis=-1, keepdims=True)).astype(jnp.bfloat16)
    mixed = jnp.einsum("hqk,kd->qhd", attn, values, preferred_element_type=jnp.float32)
    keep = ((positions >= length_pair[0] - 1) & (positions < total_len - 1)).astype(jnp.float32)
    mixed = mixed * keep[:, None, None]
    return mixed.reshape(seq_len, head_count * HEAD).astype(jnp.bfloat16)


def local(hidden_in, norm_gain, projection, lengths):
    pair_size = lax.axis_size("tensor")
    pair_index = lax.axis_index("tensor")
    heads_local = QHEADS // pair_size
    query_width = QHEADS * HEAD
    wide32 = hidden_in.astype(jnp.float32)
    gated = (wide32 * norm_gain.astype(jnp.float32)[None, :]).astype(jnp.bfloat16)
    local_sq = jnp.sum(wide32 * wide32, axis=1)
    partial_cols = jnp.dot(
        gated,
        lax.all_gather(projection, "dp", axis=1, tiled=True)[0],
        preferred_element_type=jnp.float32,
    )
    projected, total_sq = lax.psum((partial_cols, local_sq), "tensor")
    query_own = lax.dynamic_slice_in_dim(
        projected, pair_index * heads_local * HEAD, heads_local * HEAD, 1
    )
    key_value = projected[:, query_width:]
    inv_rms = lax.rsqrt(total_sq / D + EPSILON)
    query_scaled = query_own * inv_rms[:, None]
    key_scaled = key_value * inv_rms[:, None]
    return attend(query_scaled, key_scaled, lengths[0], heads_local)


def solution(mesh):
    in_specs = (
        P(("groups", "dp"), "tensor"),
        P("tensor"),
        P("tensor", "dp", None),
        P(("groups", "dp"), None),
    )
    out_specs = P(("groups", "dp"), "tensor")
    return jax.shard_map(local, mesh=mesh, in_specs=in_specs, out_specs=out_specs, check_vma=False)
```

profile of v0, /device:TPU:0, one launch (start us, length us, event | category | flops | bytes accessed | tf_op | source)
XLA Modules:
  0.0 230.0 jit_solution(5908757926944933362)
XLA Ops:
  6.5 0.0 all-gather.2.cloned.1.call-start
  6.5 0.7 all-gather.2.cloned.1.call-update
  7.3 0.0 all-reduce.2.cloned.1.call-start
  7.3 0.7 convert_element_type.57
  8.0 1.3 fusion.35
  9.3 2.6 %fusion.4 = f32[256]{0:T(256)S(1)} fusion(bf16[256,6144]{1,0:T(8,128)(2,1)} %param.4), kind=kLoop, calls=%fused_computation.6 | loop fusion | flops 4718336 | bytes 3146752 | tf_op jit(solution)/shard_map/reduce_sum | solution.py:56
  11.9 176.8 %all-gather.2.cloned.1.call-done = bf16[1,6144,1024]{2,1,0:T(8,128)(2,1)} async-done(((bf16[1,768,1024]{2,1,0:T(8,128)(2,1)}), bf16[1,6144,1024]{2,1,0:T(8,128)(2,1)}) %all-gather.2.cloned.1.call-update) | async-done | bytes 12582928 | tf_op jit(solution)/shard_map/all_gather | solution.py:59
  188.7 11.6 %fusion.1 = f32[256,1024]{0,1:T(8,128)} fusion(bf16[1,6144,1024]{2,1,0:T(8,128)(2,1)} %all-gather.2.cloned.1.call-done, bf16[256,6144]{1,0:T(8,128)(2,1)} %param.4, f32[6144]{0:T(1024)S(1)} %convert_element_type.57), kind=kOutput, calls=%fused_computation.1 | convolution fusion | flops 3225944064 | bytes 16801792 | tf_op jit(solution)/shard_map/dot_general | solution.py:57
  200.3 0.0 all-reduce.2.cloned.1.call-update
  202.1 2.5 %psum.15 = f32[256]{0:T(256)S(1)} all-reduce(f32[256]{0:T(256)S(1)} %fusion.4), channel_id=1, replica_groups=mesh['groups'=2,'dp'=8,'tensor'=2] {'tensor'}, use_global_device_ids=true, to_apply=%region_2.0 | all-reduce | flops 256 | bytes 2048 | tf_op jit(solution)/shard_map/psum | solution.py:62
  204.6 0.1 fusion.12
  204.7 0.5 multiply_cosine_fusion
  205.3 13.0 %all-reduce.2.cloned.1.call-done = f32[256,1024]{0,1:T(8,128)} async-done(((f32[256,1024]{0,1:T(8,128)}), f32[256,1024]{0,1:T(8,128)}) %all-reduce.2.cloned.1.call-update) | async-done | bytes 1048592 | tf_op jit(solution)/shard_map/psum | solution.py:62
  218.3 1.0 dynamic-slice_multiply_fusion
  219.3 0.2 copy.26
  219.5 0.2 copy.27
  219.7 1.0 slice_multiply_fusion
  220.7 0.3 fusion.23
  221.0 0.1 subtract_convert_fusion
  221.1 0.4 fusion.10
  221.5 0.5 fusion.36
  222.0 0.4 fusion.11
  222.4 0.8 copy.21
  (7 shorter events, 0.1 us)
Async XLA Ops:
  6.5 182.2 %all-gather.2.cloned.1.call-start = ((), (), s32[]{:S(2)}) async-start(), calls=%async_computation | async-start | bytes 14155776 | tf_op jit(solution)/shard_map/all_gather | solution.py:59
  7.3 211.0 %all-reduce.2.cloned.1.call-start = ((), (), s32[]{:S(2)}) async-start(), calls=%async_computation.1 | async-start | bytes 2097152 | tf_op jit(solution)/shard_map/psum | solution.py:62
Sparse Core Ops, SparseCore 0:
  9.5 179.1 all-gather.1
  200.4 17.7 all-reduce.1
where the time goes:
time: 230 us
  waiting for transfers between devices  190 us (83%)
  between operations  15.3 us (7%)
  matrix products  12.8 us (6%)
  other arithmetic  6.39 us (3%)
  local copies, waits for them, and re-layouts  2.5 us (1%)
  blocking collectives  2.47 us (1%)
    all_gather x1, waiting for transfers between devices, local(): lax.all_gather(projection, 'dp', axis=1, tiled=True)[0]  177 us
    psum x1, waiting for transfers between devices, local(): projected, total_sq = lax.psum((partial_cols, local_sq), 'tensor')  13 us
    dot_general x1, matrix products, local(): jnp.dot(gated, lax.all_gather(projection, 'dp', axis=1, tiled=True)[0], p...  11.6 us
  transfers between devices with their start and end apart: 2, of which 2 were waited for; matrix products, arithmetic and copies ran while one was open for 2% of the time, Pallas kernels for 0%

commit v1 on v0

v1 whole, which is shorter than its diff:
```python
import jax
import jax.numpy as jnp
from jax import lax
from jax.sharding import PartitionSpec as P

D = 12288
HEAD = 128
QHEADS = 6
ROPE_BASE = 1000000.0
EPSILON = 1e-05


def tables(seq_len):
    half = HEAD // 2
    positions = jnp.arange(seq_len, dtype=jnp.int32)
    freq = ROPE_BASE ** (-(jnp.arange(half, dtype=jnp.float32) * 2.0 / HEAD))
    angle = positions.astype(jnp.float32)[:, None] * freq[None, :]
    return jnp.cos(angle), jnp.sin(angle)


def rotate(block, cosine, sine):
    half = HEAD // 2
    first = block[:, :half]
    second = block[:, half:]
    return jnp.concatenate([first * cosine - second * sine, second * cosine + first * sine], axis=-1)


def attend_head(query, keys, values, allowed, keep):
    scores = lax.dot_general(
        query, keys, (((1,), (1,)), ((), ())), preferred_element_type=jnp.float32
    ) * HEAD ** (-0.5)
    scores = jnp.where(allowed, scores, -1e30)
    largest = jnp.max(scores, axis=-1, keepdims=True)
    expo = jnp.exp(scores - largest)
    attn = (expo / jnp.sum(expo, axis=-1, keepdims=True)).astype(jnp.bfloat16)
    mixed = jnp.dot(attn, values, preferred_element_type=jnp.float32)
    return (mixed * keep).astype(jnp.bfloat16)


def swap(size):
    return [(i, i ^ 1) for i in range(size)]


def local(hidden_in, norm_gain, projection, lengths):
    groups = lax.axis_size("groups")
    dp = lax.axis_size("dp")
    tensor = lax.axis_size("tensor")
    y = lax.axis_index("groups")
    place = lax.axis_index("dp")
    core = lax.axis_index("tensor")
    x = place % 2
    z = place // 2
    depth = dp // 2
    tokens = hidden_in.shape[0]
    rows = projection.shape[1]
    part = rows // groups
    heads_local = QHEADS // tensor

    ring = [(i, (i + 2) % dp) for i in range(dp)]
    over_x = swap(dp)
    over_y = swap(groups)
    over_core = swap(tensor)
    across = [(g * dp + i, (g ^ 1) * dp + (i ^ 1)) for g in range(groups) for i in range(dp)]

    mine = lax.dynamic_slice_in_dim(projection[0], y * part, part, 0)

    def column(owner, index):
        start = (QHEADS + owner) * HEAD if index == 0 else (owner * heads_local + index - 1) * HEAD
        return lax.dynamic_slice_in_dim(mine, start, HEAD, 1)

    n_cols = heads_local + 1
    theirs = jnp.concatenate([column(1 - core, i) for i in range(n_cols)], axis=1)
    other = lax.ppermute(theirs, "tensor", over_core)
    weights = []
    for i in range(n_cols):
        slot = jnp.concatenate([column(core, i), other[:, i * HEAD:(i + 1) * HEAD]], axis=0)
        weights.append([slot])
    for _ in range(depth - 1):
        for i in range(n_cols):
            weights[i].append(lax.ppermute(weights[i][-1], "dp", ring))

    wide32 = hidden_in.astype(jnp.float32)
    gated = (wide32 * norm_gain.astype(jnp.float32)[None, :]).astype(jnp.bfloat16)
    local_sq = jnp.sum(wide32 * wide32, axis=1)
    total_sq = local_sq + lax.ppermute(local_sq, "tensor", over_core)
    inv_rms = lax.rsqrt(total_sq / D + EPSILON)[:, None]

    def piece(dx, dy):
        slabs = []
        for k in range(depth):
            shard = ((z - k + depth) % depth) * 2 + (x ^ dx)
            slabs.append(lax.dynamic_slice_in_dim(gated, shard * rows + (y ^ dy) * part, part, 1))
        return jnp.stack(slabs)

    sent = [piece(1, 1), piece(1, 0), piece(0, 1)]
    held = [
        lax.ppermute(sent[0], ("groups", "dp"), across),
        lax.ppermute(sent[1], "dp", over_x),
        lax.ppermute(sent[2], "groups", over_y),
        piece(0, 0),
    ]
    acts = []
    for h in held:
        acts.append(jnp.concatenate([h, lax.ppermute(h, "tensor", over_core)], axis=2))
    acts = jnp.concatenate(acts, axis=1)

    cosine, sine = tables(tokens)
    positions = jnp.arange(tokens, dtype=jnp.int32)
    prompt = lengths[0, 0]
    total_len = prompt + lengths[0, 1]
    allowed = (positions[None, :] <= positions[:, None]) & (positions[None, :] < total_len)
    keep = ((positions >= prompt - 1) & (positions < total_len - 1)).astype(jnp.float32)[:, None]

    outs = []
    keys = values = None
    for i in range(n_cols):
        partial = sum(
            jnp.dot(acts[k], weights[i][k], preferred_element_type=jnp.float32) for k in range(depth)
        )
        blocks = partial.reshape(4, tokens, HEAD)
        low = blocks[:3].astype(jnp.bfloat16)
        summed = blocks[3]
        summed = summed + lax.ppermute(low[0], ("groups", "dp"), across).astype(jnp.float32)
        summed = summed + lax.ppermute(low[1], "dp", over_x).astype(jnp.float32)
        summed = summed + lax.ppermute(low[2], "groups", over_y).astype(jnp.float32)
        scaled = summed * inv_rms
        if i == 0:
            turned = rotate(scaled, cosine, sine)
            kv = jnp.where(core == 0, turned, scaled).astype(jnp.bfloat16)
            vk = lax.ppermute(kv, "tensor", over_core)
            keys = jnp.where(core == 0, kv, vk)
            values = jnp.where(core == 0, vk, kv)
        else:
            query = rotate(scaled, cosine, sine).astype(jnp.bfloat16)
            outs.append(attend_head(query, keys, values, allowed, keep))
    return jnp.concatenate(outs, axis=1)


def solution(mesh):
    in_specs = (
        P(("groups", "dp"), "tensor"),
        P("tensor"),
        P("tensor", "dp", None),
        P(("groups", "dp"), None),
    )
    out_specs = P(("groups", "dp"), "tensor")
    return jax.shard_map(local, mesh=mesh, in_specs=in_specs, out_specs=out_specs, check_vma=False)
```

time: 230 us -> 124 us (0.54)
  waiting for transfers between devices: 190 us -> 60.7 us
  starting transfers between devices: 0.04 us -> 29.8 us
  between operations: 15.3 us -> 2.23 us
  other arithmetic: 6.39 us -> 14.3 us
  blocking collectives: 2.47 us -> 0 us
    all_gather x1 -> x0, waiting for transfers between devices: 177 us -> none  [local(): lax.all_gather(projection, 'dp', axis=1, tiled=True)[0]]
    ppermute x0 -> x34, waiting for transfers between devices: none -> 60.7 us  [the longest x12 38.1 us: local(): weights[i].append(lax.ppermute(weights[i][-1], 'dp', ring))]
    ppermute x0 -> x34, starting transfers between devices: none -> 29.8 us  [the longest x12 9.91 us: local(): weights[i].append(lax.ppermute(weights[i][-1], 'dp', ring))]
    psum x1 -> x0, waiting for transfers between devices: 13 us -> none  [local(): projected, total_sq = lax.psum((partial_cols, local_sq), 'tensor')]
    concatenate x0 -> x7, other arithmetic: none -> 8.08 us  [the longest x1 7.28 us: local(): acts = jnp.concatenate(acts, axis=1)]
    psum x1 -> x0, blocking collectives: 2.47 us -> none  [local(): projected, total_sq = lax.psum((partial_cols, local_sq), 'tensor')]
    dot_general x3 -> x22, matrix products: 12.3 us -> 12.7 us  [the longest x16 11.4 us: local(): jnp.dot(acts[k], weights[i][k], preferred_element_type=jnp.float32)]
  transfers between devices with their start and end apart: 2 -> 34, of which waited for: 2 -> 14; matrix products, arithmetic and copies ran while one was open for 2% -> 21% of each run, Pallas kernels for 0% -> 0%
where the time goes in v1:
time: 124 us
  waiting for transfers between devices  60.7 us (49%)
  starting transfers between devices  29.8 us (24%)
  other arithmetic  14.3 us (12%)
  matrix products  12.7 us (10%)
  local copies, waits for them, and re-layouts  4.18 us (3%)
  between operations  2.23 us (2%)
    ppermute x12, waiting for transfers between devices, local(): weights[i].append(lax.ppermute(weights[i][-1], 'dp', ring))  38.1 us
    ppermute x1, waiting for transfers between devices, local(): lax.ppermute(sent[1], 'dp', over_x)  16.8 us
    dot_general x16, matrix products, local(): jnp.dot(acts[k], weights[i][k], preferred_element_type=jnp.float32)  11.4 us
    ppermute x12, starting transfers between devices, local(): weights[i].append(lax.ppermute(weights[i][-1], 'dp', ring))  9.91 us
    ppermute x4, starting transfers between devices, local(): lax.ppermute(low[0], ('groups', 'dp'), across).astype(jnp.float32)  9.88 us
    concatenate x1, other arithmetic, local(): acts = jnp.concatenate(acts, axis=1)  7.28 us
    ppermute x1, starting transfers between devices, local(): lax.ppermute(sent[0], ('groups', 'dp'), across)  3.66 us
    reduce_sum x1, other arithmetic, local(): local_sq = jnp.sum(wide32 * wide32, axis=1)  3.07 us
  transfers between devices with their start and end apart: 34, of which 14 were waited for; matrix products, arithmetic and copies ran while one was open for 21% of the time, Pallas kernels for 0%

profile of v1, /device:TPU:0, one launch (start us, length us, event | category | flops | bytes accessed | tf_op | source)
XLA Modules:
  0.0 123.9 jit_solution(9437255922751564602)
XLA Ops:
  0.0 2.0 %dynamic-slice_bitcast_fusion.23 = (bf16[384,128]{1,0:T(8,128)(2,1)S(1)}, bf16[384,128]{1,0:T(8,128)(2,1)S(1)}, bf16[384,128]{1,0:T(8,128)(2,1)S(1)}, bf16[384,1...) fusion(bf16[1,768,1024]{2,1,0:T(8,128)(2,1)} %param.6, ...), kind=kLoop, calls=%fused_computation.103 | loop fusion | bytes 1572900 | tf_op jit(solution)/shard_map/dynamic_slice | solution.py:69
  2.6 0.7 convert_element_type.122
  3.3 3.1 %fusion.1 = (f32[256]{0:T(256)S(1)}, bf16[256,6144]{1,0:T(8,128)(2,1)S(1)}) fusion(bf16[256,6144]{1,0:T(8,128)(2,1)} %param.4, f32[6144]{0:T(1024)S(1)} %convert_element_type.122), kind=kLoop, calls=%fused_computation.3 | loop fusion | flops 7864064 | bytes 6317056 | tf_op jit(solution)/shard_map/reduce_sum | solution.py:84
  7.1 3.7 %collective-permute-start = (bf16[4,256,384]{2,1,0:T(8,128)(2,1)S(1)}, bf16[4,256,384]{2,1,0:T(8,128)(2,1)S(1)}, u32[]{:S(2)}, u32[]{:S(2)}) collective-permute-start(bf16[4,256,384]{2,1,0:T(8,128)(2,1)S(1)} %pad_maximum_fusion), channel_id=1, source_target_pairs={{0,18},{2,16},{4,22},{6,20},{8,26},{10,24},{12,30},{14,28},{16,2},... | collective-permute-start | bytes 2359304 | tf_op jit(solution)/shard_map/ppermute | solution.py:97
  11.9 2.1 %collective-permute-start.28 = (bf16[768,128]{1,0:T(8,128)(2,1)S(1)}, bf16[768,128]{1,0:T(8,128)(2,1)S(1)}, u32[]{:S(2)}, u32[]{:S(2)}) collective-permute-start(bf16[768,128]{1,0:T(8,128)(2,1)S(1)} %pad_maximum_fusion.8), channel_id=1, source_target_pairs={{0,4},{2,6},{4,8},{6,10},{8,12},{10,14},{12,0},{14,2},{1,5},{3,7},... | collective-permute-start | bytes 589832 | tf_op jit(solution)/shard_map/ppermute | solution.py:80
  14.0 1.0 pad_maximum_fusion.3
  15.0 5.5 %collective-permute-done.28 = bf16[768,128]{1,0:T(8,128)(2,1)S(1)} collective-permute-done((bf16[768,128]{1,0:T(8,128)(2,1)S(1)}, bf16[768,128]{1,0:T(8,128)(2,1)S(1)}, u32[]{:S(2)}, u32[]{:S(2)}) %collective-permute-start.28) | collective-permute-done | bytes 196640 | tf_op jit(solution)/shard_map/ppermute | solution.py:80
  20.6 7.5 %collective-permute-done.22 = bf16[768,128]{1,0:T(8,128)(2,1)S(1)} collective-permute-done((bf16[768,128]{1,0:T(8,128)(2,1)S(1)}, bf16[768,128]{1,0:T(8,128)(2,1)S(1)}, u32[]{:S(2)}, u32[]{:S(2)}) %collective-permute-start.22) | collective-permute-done | bytes 196640 | tf_op jit(solution)/shard_map/ppermute | solution.py:80
  28.0 1.1 collective-permute-done
  29.1 16.8 %collective-permute-done.2 = bf16[4,256,384]{2,1,0:T(8,128)(2,1)S(1)} collective-permute-done((bf16[4,256,384]{2,1,0:T(8,128)(2,1)S(1)}, bf16[4,256,384]{2,1,0:T(8,128)(2,1)S(1)}, u32[]{:S(2)}, u32[]{:S(2)}) %collective-permute-start.2) | collective-permute-done | bytes 786464 | tf_op jit(solution)/shard_map/ppermute | solution.py:98
  46.5 0.7 pad_maximum_fusion.6
  47.2 1.6 %collective-permute-start.8 = (bf16[768,128]{1,0:T(8,128)(2,1)}, bf16[768,128]{1,0:T(8,128)(2,1)}, u32[]{:S(2)}, u32[]{:S(2)}) collective-permute-start(bf16[768,128]{1,0:T(8,128)(2,1)} %pad_maximum_fusion.6), channel_id=1, source_target_pairs={{0,4},{2,6},{4,8},{6,10},{8,12},{10,14},{12,0},{14,2},{1,5},{3,7},... | collective-permute-start | bytes 589832 | tf_op jit(solution)/shard_map/ppermute | solution.py:80
  51.2 5.0 %collective-permute-done.8 = bf16[768,128]{1,0:T(8,128)(2,1)} collective-permute-done((bf16[768,128]{1,0:T(8,128)(2,1)}, bf16[768,128]{1,0:T(8,128)(2,1)}, u32[]{:S(2)}, u32[]{:S(2)}) %collective-permute-start.8) | collective-permute-done | bytes 196640 | tf_op jit(solution)/shard_map/ppermute | solution.py:80
  56.2 1.3 %collective-permute-start.23 = (bf16[768,128]{1,0:T(8,128)(2,1)S(1)}, bf16[768,128]{1,0:T(8,128)(2,1)S(1)}, u32[]{:S(2)}, u32[]{:S(2)}) collective-permute-start(bf16[768,128]{1,0:T(8,128)(2,1)S(1)} %collective-permute-done.22), channel_id=1, source_target_pairs={{0,4},{2,6},{4,8},{6,10},{8,12},{10,14},{12,0},{14,2},{1,5},{3,7},... | collective-permute-start | bytes 589832 | tf_op jit(solution)/shard_map/ppermute | solution.py:80
  57.5 8.5 %collective-permute-done.29 = bf16[768,128]{1,0:T(8,128)(2,1)S(1)} collective-permute-done((bf16[768,128]{1,0:T(8,128)(2,1)}, bf16[768,128]{1,0:T(8,128)(2,1)S(1)}, u32[]{:S(2)}, u32[]{:S(2)}) %collective-permute-start.29) | collective-permute-done | bytes 196640 | tf_op jit(solution)/shard_map/ppermute | solution.py:80
  66.0 3.9 %collective-permute-done.23 = bf16[768,128]{1,0:T(8,128)(2,1)S(1)} collective-permute-done((bf16[768,128]{1,0:T(8,128)(2,1)S(1)}, bf16[768,128]{1,0:T(8,128)(2,1)S(1)}, u32[]{:S(2)}, u32[]{:S(2)}) %collective-permute-start.23) | collective-permute-done | bytes 196640 | tf_op jit(solution)/shard_map/ppermute | solution.py:80
  69.9 5.6 %collective-permute-done.16 = bf16[768,128]{1,0:T(8,128)(2,1)S(1)} collective-permute-done((bf16[768,128]{1,0:T(8,128)(2,1)S(1)}, bf16[768,128]{1,0:T(8,128)(2,1)S(1)}, u32[]{:S(2)}, u32[]{:S(2)}) %collective-permute-start.16) | collective-permute-done | bytes 196640 | tf_op jit(solution)/shard_map/ppermute | solution.py:80
  75.6 2.1 %collective-permute-done.9 = bf16[768,128]{1,0:T(8,128)(2,1)S(1)} collective-permute-done((bf16[768,128]{1,0:T(8,128)(2,1)}, bf16[768,128]{1,0:T(8,128)(2,1)S(1)}, u32[]{:S(2)}, u32[]{:S(2)}) %collective-permute-start.9) | collective-permute-done | bytes 196640 | tf_op jit(solution)/shard_map/ppermute | solution.py:80
  77.7 0.8 collective-permute-start.17
  78.5 4.2 %collective-permute-start.10 = (bf16[768,128]{1,0:T(8,128)(2,1)S(1)}, bf16[768,128]{1,0:T(8,128)(2,1)S(1)}, u32[]{:S(2)}, u32[]{:S(2)}) collective-permute-start(bf16[768,128]{1,0:T(8,128)(2,1)S(1)} %collective-permute-done.9), channel_id=1, source_target_pairs={{0,4},{2,6},{4,8},{6,10},{8,12},{10,14},{12,0},{14,2},{1,5},{3,7},... | collective-permute-start | bytes 589832 | tf_op jit(solution)/shard_map/ppermute | solution.py:80
  82.6 7.3 %maximum_maximum_fusion = bf16[4,1024,768]{2,1,0:T(8,128)(2,1)S(1)} fusion(bf16[4,256,384]{2,1,0:T(8,128)(2,1)} %collective-permute-done.6, bf16[1,256,384]{2,1,0:T(8,128)(2,1)S(1)} %get-tuple-element.8, bf16[1,256,384]{2,1,0:T(8,128)(2,1)S(1)} %get-tuple-element.9, bf16[1,256,384]{2,1,0:T(8,128)(2,1)S(1)} %get-tuple-element.10, ...), kind=kLoop, calls=%fused_computation.4 | loop fusion | flops 69206016 | bytes 12582912 | tf_op jit(solution)/shard_map/concatenate | solution.py:105
  91.2 0.7 fusion.2
  91.9 0.7 fusion.88
  92.6 2.5 %collective-permute-start.31 = (bf16[256,128]{0,1:T(8,128)(2,1)S(1)}, bf16[256,128]{0,1:T(8,128)(2,1)S(1)}, u32[]{:S(2)}, u32[]{:S(2)}) collective-permute-start(bf16[256,128]{0,1:T(8,128)(2,1)S(1)} %get-tuple-element.41), channel_id=1, source_target_pairs={{0,18},{2,16},{4,22},{6,20},{8,26},{10,24},{12,30},{14,28},{16,2},... | collective-permute-start | bytes 196616 | tf_op jit(solution)/shard_map/ppermute | solution.py:123
  99.1 1.6 %fusion.15 = f32[1024,128]{0,1:T(8,128)S(1)} fusion(bf16[768,128]{1,0:T(8,128)(2,1)} %collective-permute-done.8, bf16[4,1024,768]{2,1,0:T(8,128)(2,1)S(1)} %maximum_maximum_fusion), kind=kOutput, calls=%fused_computation.36 | convolution fusion | flops 201326592 | bytes 2293760 | tf_op jit(solution)/shard_map/dot_general | solution.py:118
  104.5 2.5 %collective-permute-start.25 = (bf16[256,128]{0,1:T(8,128)(2,1)S(1)}, bf16[256,128]{0,1:T(8,128)(2,1)S(1)}, u32[]{:S(2)}, u32[]{:S(2)}) collective-permute-start(bf16[256,128]{0,1:T(8,128)(2,1)S(1)} %get-tuple-element.38), channel_id=1, source_target_pairs={{0,18},{2,16},{4,22},{6,20},{8,26},{10,24},{12,30},{14,28},{16,2},... | collective-permute-start | bytes 196616 | tf_op jit(solution)/shard_map/ppermute | solution.py:123
  108.8 2.5 %collective-permute-start.18 = (bf16[256,128]{0,1:T(8,128)(2,1)S(1)}, bf16[256,128]{0,1:T(8,128)(2,1)S(1)}, u32[]{:S(2)}, u32[]{:S(2)}) collective-permute-start(bf16[256,128]{0,1:T(8,128)(2,1)S(1)} %get-tuple-element.44), channel_id=1, source_target_pairs={{0,18},{2,16},{4,22},{6,20},{8,26},{10,24},{12,30},{14,28},{16,2},... | collective-permute-start | bytes 196616 | tf_op jit(solution)/shard_map/ppermute | solution.py:123
  112.5 2.4 %collective-permute-start.11 = (bf16[256,128]{0,1:T(8,128)(2,1)S(1)}, bf16[256,128]{0,1:T(8,128)(2,1)S(1)}, u32[]{:S(2)}, u32[]{:S(2)}) collective-permute-start(bf16[256,128]{0,1:T(8,128)(2,1)S(1)} %get-tuple-element.35), channel_id=1, source_target_pairs={{0,18},{2,16},{4,22},{6,20},{8,26},{10,24},{12,30},{14,28},{16,2},... | collective-permute-start | bytes 196616 | tf_op jit(solution)/shard_map/ppermute | solution.py:123
  116.2 1.4 %collective-permute-done.11 = bf16[256,128]{0,1:T(8,128)(2,1)S(1)} collective-permute-done((bf16[256,128]{0,1:T(8,128)(2,1)S(1)}, bf16[256,128]{0,1:T(8,128)(2,1)S(1)}, u32[]{:S(2)}, u32[]{:S(2)}) %collective-permute-start.11) | collective-permute-done | bytes 65568 | tf_op jit(solution)/shard_map/ppermute | solution.py:123
  117.6 1.5 %collective-permute-done.12 = bf16[256,128]{0,1:T(8,128)(2,1)S(1)} collective-permute-done((bf16[256,128]{0,1:T(8,128)(2,1)S(1)}, bf16[256,128]{0,1:T(8,128)(2,1)S(1)}, u32[]{:S(2)}, u32[]{:S(2)}) %collective-permute-start.12) | collective-permute-done | bytes 65568 | tf_op jit(solution)/shard_map/ppermute | solution.py:124
  120.6 0.9 collective-permute-done.21
  123.1 0.8 copy.5
  (99 shorter events, 19.9 us)
Async XLA Ops:
  2.1 9.7 %collective-permute-start.7 = (bf16[384,512]{1,0:T(8,128)(2,1)S(1)}, bf16[384,512]{1,0:T(8,128)(2,1)S(1)}, u32[]{:S(2)}, u32[]{:S(2)}) collective-permute-start(bf16[384,512]{1,0:T(8,128)(2,1)S(1)} %pad_maximum_fusion.4), channel_id=1, source_target_pairs={{0,1},{1,0},{2,3},{3,2},{4,5},{5,4},{6,7},{7,6},{8,9},{9,8},{10,11... | collective-permute-start | bytes 1179656 | tf_op jit(solution)/shard_map/ppermute | solution.py:73
  7.1 22.0 %collective-permute-start = (bf16[4,256,384]{2,1,0:T(8,128)(2,1)S(1)}, bf16[4,256,384]{2,1,0:T(8,128)(2,1)S(1)}, u32[]{:S(2)}, u32[]{:S(2)}) collective-permute-start(bf16[4,256,384]{2,1,0:T(8,128)(2,1)S(1)} %pad_maximum_fusion), channel_id=1, source_target_pairs={{0,18},{2,16},{4,22},{6,20},{8,26},{10,24},{12,30},{14,28},{16,2},... | collective-permute-start | bytes 2359304 | tf_op jit(solution)/shard_map/ppermute | solution.py:97
  10.9 35.1 %collective-permute-start.2 = (bf16[4,256,384]{2,1,0:T(8,128)(2,1)S(1)}, bf16[4,256,384]{2,1,0:T(8,128)(2,1)S(1)}, u32[]{:S(2)}, u32[]{:S(2)}) collective-permute-start(bf16[4,256,384]{2,1,0:T(8,128)(2,1)S(1)} %pad_maximum_fusion.1), channel_id=1, source_target_pairs={{0,2},{2,0},{4,6},{6,4},{8,10},{10,8},{12,14},{14,12},{1,3},{3,1},... | collective-permute-start | bytes 2359304 | tf_op jit(solution)/shard_map/ppermute | solution.py:98
  11.7 34.3 %collective-permute-start.4 = (bf16[4,256,384]{2,1,0:T(8,128)(2,1)S(1)}, bf16[4,256,384]{2,1,0:T(8,128)(2,1)}, u32[]{:S(2)}, u32[]{:S(2)}) collective-permute-start(bf16[4,256,384]{2,1,0:T(8,128)(2,1)S(1)} %pad_maximum_fusion.2), channel_id=1, source_target_pairs={{0,16},{16,0},{1,17},{17,1},{2,18},{18,2},{3,19},{19,3},{4,20},{20... | collective-permute-start | bytes 2359304 | tf_op jit(solution)/shard_map/ppermute | solution.py:99
  11.9 8.7 %collective-permute-start.28 = (bf16[768,128]{1,0:T(8,128)(2,1)S(1)}, bf16[768,128]{1,0:T(8,128)(2,1)S(1)}, u32[]{:S(2)}, u32[]{:S(2)}) collective-permute-start(bf16[768,128]{1,0:T(8,128)(2,1)S(1)} %pad_maximum_fusion.8), channel_id=1, source_target_pairs={{0,4},{2,6},{4,8},{6,10},{8,12},{10,14},{12,0},{14,2},{1,5},{3,7},... | collective-permute-start | bytes 589832 | tf_op jit(solution)/shard_map/ppermute | solution.py:80
  15.0 41.2 %collective-permute-start.6 = (bf16[4,256,384]{2,1,0:T(8,128)(2,1)}, bf16[4,256,384]{2,1,0:T(8,128)(2,1)}, u32[]{:S(2)}, u32[]{:S(2)}) collective-permute-start(bf16[4,256,384]{2,1,0:T(8,128)(2,1)} %pad_maximum_fusion.3), channel_id=1, source_target_pairs={{0,1},{1,0},{2,3},{3,2},{4,5},{5,4},{6,7},{7,6},{8,9},{9,8},{10,11... | collective-permute-start | bytes 2359304 | tf_op jit(solution)/shard_map/ppermute | solution.py:104
  20.5 7.5 %collective-permute-start.22 = (bf16[768,128]{1,0:T(8,128)(2,1)S(1)}, bf16[768,128]{1,0:T(8,128)(2,1)S(1)}, u32[]{:S(2)}, u32[]{:S(2)}) collective-permute-start(bf16[768,128]{1,0:T(8,128)(2,1)S(1)} %pad_maximum_fusion.7), channel_id=1, source_target_pairs={{0,4},{2,6},{4,8},{6,10},{8,12},{10,14},{12,0},{14,2},{1,5},{3,7},... | collective-permute-start | bytes 589832 | tf_op jit(solution)/shard_map/ppermute | solution.py:80
  28.0 19.2 %collective-permute-start.15 = (bf16[768,128]{1,0:T(8,128)(2,1)S(1)}, bf16[768,128]{1,0:T(8,128)(2,1)S(1)}, u32[]{:S(2)}, u32[]{:S(2)}) collective-permute-start(bf16[768,128]{1,0:T(8,128)(2,1)S(1)} %pad_maximum_fusion.5), channel_id=1, source_target_pairs={{0,4},{2,6},{4,8},{6,10},{8,12},{10,14},{12,0},{14,2},{1,5},{3,7},... | collective-permute-start | bytes 589832 | tf_op jit(solution)/shard_map/ppermute | solution.py:80
  29.1 48.5 %collective-permute-start.1 = (bf16[4,256,384]{2,1,0:T(8,128)(2,1)S(1)}, bf16[4,256,384]{2,1,0:T(8,128)(2,1)}, u32[]{:S(2)}, u32[]{:S(2)}) collective-permute-start(bf16[4,256,384]{2,1,0:T(8,128)(2,1)S(1)} %collective-permute-done), channel_id=1, source_target_pairs={{0,1},{1,0},{2,3},{3,2},{4,5},{5,4},{6,7},{7,6},{8,9},{9,8},{10,11... | collective-permute-start | bytes 2359304 | tf_op jit(solution)/shard_map/ppermute | solution.py:104
  46.0 31.7 %collective-permute-start.3 = (bf16[4,256,384]{2,1,0:T(8,128)(2,1)S(1)}, bf16[4,256,384]{2,1,0:T(8,128)(2,1)}, u32[]{:S(2)}, u32[]{:S(2)}) collective-permute-start(bf16[4,256,384]{2,1,0:T(8,128)(2,1)S(1)} %collective-permute-done.2), channel_id=1, source_target_pairs={{0,1},{1,0},{2,3},{3,2},{4,5},{5,4},{6,7},{7,6},{8,9},{9,8},{10,11... | collective-permute-start | bytes 2359304 | tf_op jit(solution)/shard_map/ppermute | solution.py:104
  46.0 32.5 %collective-permute-start.5 = (bf16[4,256,384]{2,1,0:T(8,128)(2,1)}, bf16[4,256,384]{2,1,0:T(8,128)(2,1)}, u32[]{:S(2)}, u32[]{:S(2)}) collective-permute-start(bf16[4,256,384]{2,1,0:T(8,128)(2,1)} %collective-permute-done.4), channel_id=1, source_target_pairs={{0,1},{1,0},{2,3},{3,2},{4,5},{5,4},{6,7},{7,6},{8,9},{9,8},{10,11... | collective-permute-start | bytes 2359304 | tf_op jit(solution)/shard_map/ppermute | solution.py:104
  47.2 9.0 %collective-permute-start.8 = (bf16[768,128]{1,0:T(8,128)(2,1)}, bf16[768,128]{1,0:T(8,128)(2,1)}, u32[]{:S(2)}, u32[]{:S(2)}) collective-permute-start(bf16[768,128]{1,0:T(8,128)(2,1)} %pad_maximum_fusion.6), channel_id=1, source_target_pairs={{0,4},{2,6},{4,8},{6,10},{8,12},{10,14},{12,0},{14,2},{1,5},{3,7},... | collective-permute-start | bytes 589832 | tf_op jit(solution)/shard_map/ppermute | solution.py:80
  56.2 9.8 %collective-permute-start.29 = (bf16[768,128]{1,0:T(8,128)(2,1)}, bf16[768,128]{1,0:T(8,128)(2,1)S(1)}, u32[]{:S(2)}, u32[]{:S(2)}) collective-permute-start(bf16[768,128]{1,0:T(8,128)(2,1)} %copy-done), channel_id=1, source_target_pairs={{0,4},{2,6},{4,8},{6,10},{8,12},{10,14},{12,0},{14,2},{1,5},{3,7},... | collective-permute-start | bytes 589832 | tf_op jit(solution)/shard_map/ppermute | solution.py:80
  56.2 13.7 %collective-permute-start.23 = (bf16[768,128]{1,0:T(8,128)(2,1)S(1)}, bf16[768,128]{1,0:T(8,128)(2,1)S(1)}, u32[]{:S(2)}, u32[]{:S(2)}) collective-permute-start(bf16[768,128]{1,0:T(8,128)(2,1)S(1)} %collective-permute-done.22), channel_id=1, source_target_pairs={{0,4},{2,6},{4,8},{6,10},{8,12},{10,14},{12,0},{14,2},{1,5},{3,7},... | collective-permute-start | bytes 589832 | tf_op jit(solution)/shard_map/ppermute | solution.py:80
  66.0 9.5 %collective-permute-start.16 = (bf16[768,128]{1,0:T(8,128)(2,1)S(1)}, bf16[768,128]{1,0:T(8,128)(2,1)S(1)}, u32[]{:S(2)}, u32[]{:S(2)}) collective-permute-start(bf16[768,128]{1,0:T(8,128)(2,1)S(1)} %collective-permute-done.15), channel_id=1, source_target_pairs={{0,4},{2,6},{4,8},{6,10},{8,12},{10,14},{12,0},{14,2},{1,5},{3,7},... | collective-permute-start | bytes 589832 | tf_op jit(solution)/shard_map/ppermute | solution.py:80
  69.9 7.8 %collective-permute-start.9 = (bf16[768,128]{1,0:T(8,128)(2,1)}, bf16[768,128]{1,0:T(8,128)(2,1)S(1)}, u32[]{:S(2)}, u32[]{:S(2)}) collective-permute-start(bf16[768,128]{1,0:T(8,128)(2,1)} %collective-permute-done.8), channel_id=1, source_target_pairs={{0,4},{2,6},{4,8},{6,10},{8,12},{10,14},{12,0},{14,2},{1,5},{3,7},... | collective-permute-start | bytes 589832 | tf_op jit(solution)/shard_map/ppermute | solution.py:80
  75.6 32.1 %collective-permute-start.14 = (f32[256]{0:T(256)S(1)}, f32[256]{0:T(256)S(1)}, u32[]{:S(2)}, u32[]{:S(2)}) collective-permute-start(f32[256]{0:T(256)S(1)} %get-tuple-element.5), channel_id=1, source_target_pairs={{0,1},{1,0},{2,3},{3,2},{4,5},{5,4},{6,7},{7,6},{8,9},{9,8},{10,11... | collective-permute-start | bytes 3080 | tf_op jit(solution)/shard_map/ppermute | solution.py:85
  77.7 14.2 %collective-permute-start.30 = (bf16[768,128]{1,0:T(8,128)(2,1)S(1)}, bf16[768,128]{1,0:T(8,128)(2,1)S(1)}, u32[]{:S(2)}, u32[]{:S(2)}) collective-permute-start(bf16[768,128]{1,0:T(8,128)(2,1)S(1)} %collective-permute-done.29), channel_id=1, source_target_pairs={{0,4},{2,6},{4,8},{6,10},{8,12},{10,14},{12,0},{14,2},{1,5},{3,7},... | collective-permute-start | bytes 589832 | tf_op jit(solution)/shard_map/ppermute | solution.py:80
  77.7 24.3 %collective-permute-start.24 = (bf16[768,128]{1,0:T(8,128)(2,1)S(1)}, bf16[768,128]{1,0:T(8,128)(2,1)S(1)}, u32[]{:S(2)}, u32[]{:S(2)}) collective-permute-start(bf16[768,128]{1,0:T(8,128)(2,1)S(1)} %collective-permute-done.23), channel_id=1, source_target_pairs={{0,4},{2,6},{4,8},{6,10},{8,12},{10,14},{12,0},{14,2},{1,5},{3,7},... | collective-permute-start | bytes 589832 | tf_op jit(solution)/shard_map/ppermute | solution.py:80
  77.7 25.6 %collective-permute-start.17 = (bf16[768,128]{1,0:T(8,128)(2,1)S(1)}, bf16[768,128]{1,0:T(8,128)(2,1)S(1)}, u32[]{:S(2)}, u32[]{:S(2)}) collective-permute-start(bf16[768,128]{1,0:T(8,128)(2,1)S(1)} %collective-permute-done.16), channel_id=1, source_target_pairs={{0,4},{2,6},{4,8},{6,10},{8,12},{10,14},{12,0},{14,2},{1,5},{3,7},... | collective-permute-start | bytes 589832 | tf_op jit(solution)/shard_map/ppermute | solution.py:80
  78.5 26.0 %collective-permute-start.10 = (bf16[768,128]{1,0:T(8,128)(2,1)S(1)}, bf16[768,128]{1,0:T(8,128)(2,1)S(1)}, u32[]{:S(2)}, u32[]{:S(2)}) collective-permute-start(bf16[768,128]{1,0:T(8,128)(2,1)S(1)} %collective-permute-done.9), channel_id=1, source_target_pairs={{0,4},{2,6},{4,8},{6,10},{8,12},{10,14},{12,0},{14,2},{1,5},{3,7},... | collective-permute-start | bytes 589832 | tf_op jit(solution)/shard_map/ppermute | solution.py:80
  92.6 15.7 %collective-permute-start.31 = (bf16[256,128]{0,1:T(8,128)(2,1)S(1)}, bf16[256,128]{0,1:T(8,128)(2,1)S(1)}, u32[]{:S(2)}, u32[]{:S(2)}) collective-permute-start(bf16[256,128]{0,1:T(8,128)(2,1)S(1)} %get-tuple-element.41), channel_id=1, source_target_pairs={{0,18},{2,16},{4,22},{6,20},{8,26},{10,24},{12,30},{14,28},{16,2},... | collective-permute-start | bytes 196616 | tf_op jit(solution)/shard_map/ppermute | solution.py:123
  102.0 6.9 %collective-permute-start.32 = (bf16[256,128]{0,1:T(8,128)(2,1)S(1)}, bf16[256,128]{0,1:T(8,128)(2,1)S(1)}, u32[]{:S(2)}, u32[]{:S(2)}) collective-permute-start(bf16[256,128]{0,1:T(8,128)(2,1)S(1)} %get-tuple-element.43), channel_id=1, source_target_pairs={{0,2},{2,0},{4,6},{6,4},{8,10},{10,8},{12,14},{14,12},{1,3},{3,1},... | collective-permute-start | bytes 196616 | tf_op jit(solution)/shard_map/ppermute | solution.py:124
  103.2 8.0 %collective-permute-start.33 = (bf16[256,128]{0,1:T(8,128)(2,1)S(1)}, bf16[256,128]{0,1:T(8,128)(2,1)S(1)}, u32[]{:S(2)}, u32[]{:S(2)}) collective-permute-start(bf16[256,128]{0,1:T(8,128)(2,1)S(1)} %get-tuple-element.42), channel_id=1, source_target_pairs={{0,16},{16,0},{1,17},{17,1},{2,18},{18,2},{3,19},{19,3},{4,20},{20... | collective-permute-start | bytes 196616 | tf_op jit(solution)/shard_map/ppermute | solution.py:125
  104.5 7.4 %collective-permute-start.25 = (bf16[256,128]{0,1:T(8,128)(2,1)S(1)}, bf16[256,128]{0,1:T(8,128)(2,1)S(1)}, u32[]{:S(2)}, u32[]{:S(2)}) collective-permute-start(bf16[256,128]{0,1:T(8,128)(2,1)S(1)} %get-tuple-element.38), channel_id=1, source_target_pairs={{0,18},{2,16},{4,22},{6,20},{8,26},{10,24},{12,30},{14,28},{16,2},... | collective-permute-start | bytes 196616 | tf_op jit(solution)/shard_map/ppermute | solution.py:123
  107.7 4.7 %collective-permute-start.26 = (bf16[256,128]{0,1:T(8,128)(2,1)S(1)}, bf16[256,128]{0,1:T(8,128)(2,1)S(1)}, u32[]{:S(2)}, u32[]{:S(2)}) collective-permute-start(bf16[256,128]{0,1:T(8,128)(2,1)S(1)} %get-tuple-element.40), channel_id=1, source_target_pairs={{0,2},{2,0},{4,6},{6,4},{8,10},{10,8},{12,14},{14,12},{1,3},{3,1},... | collective-permute-start | bytes 196616 | tf_op jit(solution)/shard_map/ppermute | solution.py:124
  108.3 6.5 %collective-permute-start.27 = (bf16[256,128]{0,1:T(8,128)(2,1)S(1)}, bf16[256,128]{0,1:T(8,128)(2,1)S(1)}, u32[]{:S(2)}, u32[]{:S(2)}) collective-permute-start(bf16[256,128]{0,1:T(8,128)(2,1)S(1)} %get-tuple-element.39), channel_id=1, source_target_pairs={{0,16},{16,0},{1,17},{17,1},{2,18},{18,2},{3,19},{19,3},{4,20},{20... | collective-permute-start | bytes 196616 | tf_op jit(solution)/shard_map/ppermute | solution.py:125
  108.8 6.6 %collective-permute-start.18 = (bf16[256,128]{0,1:T(8,128)(2,1)S(1)}, bf16[256,128]{0,1:T(8,128)(2,1)S(1)}, u32[]{:S(2)}, u32[]{:S(2)}) collective-permute-start(bf16[256,128]{0,1:T(8,128)(2,1)S(1)} %get-tuple-element.44), channel_id=1, source_target_pairs={{0,18},{2,16},{4,22},{6,20},{8,26},{10,24},{12,30},{14,28},{16,2},... | collective-permute-start | bytes 196616 | tf_op jit(solution)/shard_map/ppermute | solution.py:123
  111.3 4.7 %collective-permute-start.19 = (bf16[256,128]{0,1:T(8,128)(2,1)S(1)}, bf16[256,128]{0,1:T(8,128)(2,1)S(1)}, u32[]{:S(2)}, u32[]{:S(2)}) collective-permute-start(bf16[256,128]{0,1:T(8,128)(2,1)S(1)} %get-tuple-element.46), channel_id=1, source_target_pairs={{0,2},{2,0},{4,6},{6,4},{8,10},{10,8},{12,14},{14,12},{1,3},{3,1},... | collective-permute-start | bytes 196616 | tf_op jit(solution)/shard_map/ppermute | solution.py:124
  111.9 4.3 %collective-permute-start.20 = (bf16[256,128]{0,1:T(8,128)(2,1)S(1)}, bf16[256,128]{0,1:T(8,128)(2,1)S(1)}, u32[]{:S(2)}, u32[]{:S(2)}) collective-permute-start(bf16[256,128]{0,1:T(8,128)(2,1)S(1)} %get-tuple-element.45), channel_id=1, source_target_pairs={{0,16},{16,0},{1,17},{17,1},{2,18},{18,2},{3,19},{19,3},{4,20},{20... | collective-permute-start | bytes 196616 | tf_op jit(solution)/shard_map/ppermute | solution.py:125
  112.5 5.2 %collective-permute-start.11 = (bf16[256,128]{0,1:T(8,128)(2,1)S(1)}, bf16[256,128]{0,1:T(8,128)(2,1)S(1)}, u32[]{:S(2)}, u32[]{:S(2)}) collective-permute-start(bf16[256,128]{0,1:T(8,128)(2,1)S(1)} %get-tuple-element.35), channel_id=1, source_target_pairs={{0,18},{2,16},{4,22},{6,20},{8,26},{10,24},{12,30},{14,28},{16,2},... | collective-permute-start | bytes 196616 | tf_op jit(solution)/shard_map/ppermute | solution.py:123
  115.4 4.3 %collective-permute-start.13 = (bf16[256,128]{0,1:T(8,128)(2,1)S(1)}, bf16[256,128]{0,1:T(8,128)(2,1)S(1)}, u32[]{:S(2)}, u32[]{:S(2)}) collective-permute-start(bf16[256,128]{0,1:T(8,128)(2,1)S(1)} %get-tuple-element.36), channel_id=1, source_target_pairs={{0,16},{16,0},{1,17},{17,1},{2,18},{18,2},{3,19},{19,3},{4,20},{20... | collective-permute-start | bytes 196616 | tf_op jit(solution)/shard_map/ppermute | solution.py:125
  (5 other events, 89.6 us)

commit v2 on v1

--- a/solution.py
+++ b/solution.py
@@ -1,6 +1,10 @@
+import functools
+
 import jax
 import jax.numpy as jnp
 from jax import lax
+from jax.experimental import pallas as pl
+from jax.experimental.pallas import tpu as pltpu
 from jax.sharding import PartitionSpec as P
 
 D = 12288
@@ -41,7 +45,7 @@
     return [(i, i ^ 1) for i in range(size)]
 
 
-def local(hidden_in, norm_gain, projection, lengths):
+def general(hidden_in, norm_gain, projection, lengths):
     groups = lax.axis_size("groups")
     dp = lax.axis_size("dp")
     tensor = lax.axis_size("tensor")
@@ -136,6 +140,331 @@
     return jnp.concatenate(outs, axis=1)
 
 
+VMEM = pltpu.VMEM
+PLANE = ((1, 1), (1, 0), (0, 1), (0, 0))
+WHOLE = pl.BlockSpec(memory_space=VMEM)
+SCALARS = pl.BlockSpec(memory_space=pltpu.SMEM)
+
+
+def call(kernel, out_shape, limit=12, **kwargs):
+    return pl.pallas_call(
+        kernel,
+        out_shape=out_shape,
+        compiler_params=pltpu.CompilerParams(vmem_limit_bytes=limit * 2**20),
+        cost_estimate=pl.CostEstimate(flops=1, bytes_accessed=1, transcendentals=0),
+        **kwargs,
+    )
+
+
+def select_kernel(columns, part, place_ref, rows_ref, *refs):
+    out_refs, sems = refs[:len(columns)], refs[len(columns)]
+    rows = pl.ds(pl.multiple_of(place_ref[2] * part, HEAD), part)
+    copies = []
+    for starts, out_ref in zip(columns, out_refs):
+        for i, start in enumerate(starts):
+            copies.append(pltpu.make_async_copy(
+                rows_ref.at[0, rows, pl.ds(start, HEAD)],
+                out_ref.at[:, pl.ds(i * HEAD, HEAD)],
+                sems.at[len(copies)],
+            ))
+    for copy in copies:
+        copy.start()
+    for copy in copies:
+        copy.wait()
+
+
+def select(place, projection, part, columns):
+    chunk = jax.ShapeDtypeStruct((part, len(columns[0]) * HEAD), projection.dtype)
+    return call(
+        functools.partial(select_kernel, columns, part),
+        (chunk,) * len(columns),
+        in_specs=[SCALARS, pl.BlockSpec(memory_space=pltpu.HBM)],
+        out_specs=[pl.BlockSpec(memory_space=pl.ANY)] * len(columns),
+        scratch_shapes=[pltpu.SemaphoreType.DMA((len(columns) * len(columns[0]),))],
+    )(place, pltpu.with_memory_space_constraint(projection, pltpu.HBM))
+
+
+def gate_kernel(part, depth, place_ref, hidden_ref, gain_ref, *out_refs):
+    piece_refs, sq_ref, row_ref = out_refs[:4], out_refs[4], out_refs[5]
+    x, y = place_ref[1], place_ref[2]
+    base = lax.rem(place_ref[0] - pl.program_id(0) + depth, depth) * 4 * part
+
+    @pl.when(pl.program_id(0) == 0)
+    def _():
+        row_ref[0, :] = gain_ref[...].astype(jnp.float32)
+
+    total = jnp.zeros(sq_ref.shape, jnp.float32)
+    for piece_ref, (dx, dy) in zip(piece_refs, PLANE):
+        start = pl.multiple_of(((x ^ dx) * 2 + (y ^ dy)) * part, HEAD)
+        wide = hidden_ref[:, pl.ds(start, part)].astype(jnp.float32)
+        gain = row_ref[:, pl.ds(pl.multiple_of(base + start, HEAD), part)]
+        piece_ref[0] = (wide * gain).astype(jnp.bfloat16)
+        square = wide * wide
+        for j in range(0, part, HEAD):
+            total += square[:, j:j + HEAD]
+
+    @pl.when(pl.program_id(0) == 0)
+    def _():
+        sq_ref[...] = total
+
+    @pl.when(pl.program_id(0) > 0)
+    def _():
+        sq_ref[...] += total
+
+
+def gate(place, hidden_in, norm_gain, part, depth):
+    tokens = hidden_in.shape[0]
+    wide = 4 * part
+    piece = jax.ShapeDtypeStruct((depth, tokens, part), jnp.bfloat16)
+
+    def shard(k, place):
+        return (0, lax.rem(place[0] - k + depth, depth))
+
+    outs = call(
+        functools.partial(gate_kernel, part, depth),
+        (piece,) * 4 + (jax.ShapeDtypeStruct((tokens, HEAD), jnp.float32),),
+        grid_spec=pltpu.PrefetchScalarGridSpec(
+            num_scalar_prefetch=1,
+            grid=(depth,),
+            in_specs=[pl.BlockSpec((tokens, wide), shard), pl.BlockSpec(norm_gain.shape, lambda k, place: (0,))],
+            out_specs=[pl.BlockSpec((1, tokens, part), lambda k, place: (k, 0, 0))] * 4
+            + [pl.BlockSpec((tokens, HEAD), lambda k, place: (0, 0))],
+            scratch_shapes=[pltpu.VMEM((1, norm_gain.shape[0]), jnp.float32)],
+        ),
+    )(place, hidden_in, norm_gain)
+    return outs[:4], outs[4]
+
+
+def matmul_kernel(firsts, n_blocks, more, sent, place_ref, *refs):
+    n_slots = len(firsts)
+    acts, refs = refs[:4], refs[4:]
+    slots, refs = refs[:n_slots], refs[n_slots:]
+    right = [slot[...] for slot in slots]
+    wide = 2 * HEAD
+    for p in range(4):
+        total = jnp.dot(acts[p][firsts[0]], right[0], preferred_element_type=jnp.float32)
+        for k in range(1, n_slots):
+            total += jnp.dot(acts[p][firsts[k]], right[k], preferred_element_type=jnp.float32)
+        if more:
+            total += refs[0][p]
+        if not sent:
+            refs[-1][p] = total
+            continue
+        mine_ref = refs[-1]
+        theirs_refs = refs[-1 - sent:-1]
+        per = 4 * n_blocks // sent
+        for g in range(n_blocks):
+            low = total[:, g * wide:g * wide + HEAD]
+            high = total[:, g * wide + HEAD:(g + 1) * wide]
+            spot = g * 4 + p
+            theirs_refs[spot // per][spot % per] = jnp.where(place_ref[3] == 0, high, low).astype(jnp.bfloat16)
+            mine_ref[p, g] = jnp.where(place_ref[3] == 0, low, high)
+
+
+def matmul(place, acts, slots, firsts, so_far=None, sent=0):
+    n_slots, n_blocks = len(slots), slots[0].shape[1] // (2 * HEAD)
+    tokens = acts[0].shape[1]
+    args = [place, *acts, *slots]
+    if so_far is not None:
+        args.append(so_far)
+    if sent:
+        out_shape = (jax.ShapeDtypeStruct((4 * n_blocks // sent, tokens, HEAD), jnp.bfloat16),) * sent
+        out_shape += (jax.ShapeDtypeStruct((4, n_blocks, tokens, HEAD), jnp.float32),)
+    else:
+        out_shape = (jax.ShapeDtypeStruct((4, tokens, n_blocks * 2 * HEAD), jnp.float32),)
+    outs = call(
+        functools.partial(matmul_kernel, firsts, n_blocks, so_far is not None, sent),
+        out_shape,
+        in_specs=[SCALARS] + [WHOLE] * (len(args) - 1),
+        out_specs=[WHOLE] * len(out_shape),
+    )(*args)
+    return outs if sent else outs[0]
+
+
+def join_kernel(mine_ref, *refs):
+    n_blocks = mine_ref.shape[1]
+    came_refs, out_refs = refs[:-4], refs[-4:]
+    per = 4 * n_blocks // len(came_refs)
+    for p in range(4):
+        for g in range(n_blocks):
+            spot = g * 4 + p
+            came = came_refs[spot // per][spot % per].astype(jnp.float32)
+            out_refs[p][g] = (mine_ref[p, g] + came).astype(out_refs[p].dtype)
+
+
+def join(mine, *came):
+    shape = mine.shape[1:]
+    return call(
+        join_kernel,
+        (jax.ShapeDtypeStruct(shape, jnp.bfloat16),) * 3 + (jax.ShapeDtypeStruct(shape, jnp.float32),),
+        in_specs=[WHOLE] * (1 + len(came)),
+        out_specs=[WHOLE] * 4,
+    )(mine, *came)
+
+
+def summed(refs, index, scale_ref):
+    total = refs[0][index]
+    for ref in refs[1:]:
+        total += ref[index].astype(jnp.float32)
+    return total * scale_ref[...]
+
+
+def turned(block, cosine_ref, sine_ref):
+    half = HEAD // 2
+    other = jnp.concatenate([block[:, half:], block[:, :half]], axis=1)
+    return block * cosine_ref[...] + other * sine_ref[...]
+
+
+def kv_kernel(place_ref, own, r0, r1, r2, scale_ref, cosine_ref, sine_ref, out_ref):
+    block = summed((own, r0, r1, r2), 0, scale_ref)
+    spun = turned(block, cosine_ref, sine_ref)
+    out_ref[...] = jnp.where(place_ref[3] == 0, spun, block).astype(jnp.bfloat16)
+
+
+def heads_kernel(first, n_parts, place_ref, lengths_ref, *refs):
+    parts, refs = refs[:n_parts], refs[n_parts:]
+    scale_ref, cosine_ref, sine_ref, mine_ref, other_ref, *rest = refs
+    out_ref = rest[-1]
+    tokens = mine_ref.shape[0]
+    is_key = place_ref[3] == 0
+    mine, other = mine_ref[...], other_ref[...]
+    keys = jnp.where(is_key, mine, other)
+    values = jnp.where(is_key, other, mine)
+    prompt = lengths_ref[0, 0]
+    total_len = prompt + lengths_ref[0, 1]
+    at = lax.broadcasted_iota(jnp.int32, (tokens, tokens), 0)
+    key_at = lax.broadcasted_iota(jnp.int32, (tokens, tokens), 1)
+    allowed = (key_at <= at) & (key_at < total_len)
+    row = lax.broadcasted_iota(jnp.int32, (tokens, HEAD), 0)
+    keep = ((row >= prompt - 1) & (row < total_len - 1)).astype(jnp.float32)
+    before = 0
+    if len(rest) > 1:
+        before = rest[0].shape[1]
+        out_ref[:, :before] = rest[0][...]
+    for i in range(first, parts[0].shape[0]):
+        query = turned(summed(parts, i, scale_ref), cosine_ref, sine_ref).astype(jnp.bfloat16)
+        scores = lax.dot_general(
+            query, keys, (((1,), (1,)), ((), ())), preferred_element_type=jnp.float32
+        ) * HEAD ** (-0.5)
+        scores = jnp.where(allowed, scores, -1e30)
+        expo = jnp.exp(scores - jnp.max(scores, axis=-1, keepdims=True))
+        attn = (expo / jnp.sum(expo, axis=-1, keepdims=True)).astype(jnp.bfloat16)
+        mixed = jnp.dot(attn, values, preferred_element_type=jnp.float32)
+        out_ref[:, before + (i - first) * HEAD:before + (i - first + 1) * HEAD] = (mixed * keep).astype(jnp.bfloat16)
+
+
+def heads(place, lengths, parts, first, scale, cosine, sine, mine, other, *earlier):
+    tokens = mine.shape[0]
+    args = [place, lengths, *parts, scale, cosine, sine, mine, other, *earlier]
+    width = (parts[0].shape[0] - first) * HEAD + sum(e.shape[1] for e in earlier)
+    return call(
+        functools.partial(heads_kernel, first, len(parts)),
+        jax.ShapeDtypeStruct((tokens, width), jnp.bfloat16),
+        in_specs=[SCALARS] * 2 + [WHOLE] * (len(args) - 2),
+        out_specs=WHOLE,
+    )(*args)
+
+
+def staged(hidden_in, norm_gain, projection, lengths):
+    groups = lax.axis_size("groups")
+    dp = lax.axis_size("dp")
+    tensor = lax.axis_size("tensor")
+    y = lax.axis_index("groups")
+    spot = lax.axis_index("dp")
+    core = lax.axis_index("tensor")
+    place = jnp.stack([spot // 2, spot % 2, y, core]).astype(jnp.int32)
+    depth = dp // 2
+    tokens = hidden_in.shape[0]
+    part = projection.shape[1] // groups
+    heads_local = QHEADS // tensor
+
+    ring = [(i, (i + 2) % dp) for i in range(dp)]
+    over_x = swap(dp)
+    over_y = swap(groups)
+    over_core = swap(tensor)
+    across = [(g * dp + i, (g ^ 1) * dp + (i ^ 1)) for g in range(groups) for i in range(dp)]
+
+    def to_core(a):
+        return lax.ppermute(a, "tensor", over_core)
+
+    def on_ring(a):
+        return lax.ppermute(a, "dp", ring)
+
+    def back(a):
+        return lax.ppermute(a, "dp", [(j, i) for i, j in ring])
+
+    def to_plane(three):
+        return [
+            lax.ppermute(three[0], ("groups", "dp"), across),
+            lax.ppermute(three[1], "dp", over_x),
+            lax.ppermute(three[2], "groups", over_y),
+        ]
+
+    last = []
+
+    def after(*values):
+        held = lax.optimization_barrier(tuple(values) + tuple(last))[:len(values)]
+        last[:] = held[:1]
+        return held[0] if len(values) == 1 else held
+
+    blocks = [[(QHEADS + c) * HEAD for c in range(tensor)]]
+    blocks += [[(c * heads_local + i) * HEAD for c in range(tensor)] for i in range(heads_local)]
+    columns = [blocks[0] + blocks[1], blocks[2] + blocks[3]]
+    own_a, own_b = after(*select(place, projection, part, columns))
+    a1 = on_ring(own_a)
+    a3 = back(own_a)
+    pieces, squares = gate(place, after(hidden_in), norm_gain, part, depth)
+    pieces, squares = list(after(*pieces)), after(squares)
+    came = to_plane(pieces[:3])
+
+    a1 = after(a1)
+    a2 = on_ring(a1)
+    a3, own_b = after(a3, own_b)
+    b1 = on_ring(own_b)
+    a2, own_b = after(a2, own_b)
+    b3 = back(own_b)
+    b1 = after(b1)
+    b2 = on_ring(b1)
+    acts = list(after(*came)) + [pieces[3]]
+    b3 = after(b3)
+    *theirs, mine = after(*matmul(place, acts, (own_a, a1, a2, a3), (0, 1, 2, 3), sent=4))
+    swapped = after(*[to_core(t) for t in theirs])
+    *sent, own = after(*join(mine, *swapped))
+    first_parts = [own] + to_plane(sent)
+    front = after(matmul(place, acts, (own_b, b1, b3), (0, 1, 3)))
+
+    b2 = after(b2)
+    *theirs, mine = after(*matmul(place, acts, (b2,), (2,), so_far=front, sent=2))
+    swapped = [to_core(t) for t in theirs]
+    first_parts = after(*first_parts)
+    squares = after(squares)
+    squares = squares + to_core(squares)
+    scale = lax.rsqrt(jnp.sum(squares, axis=1, keepdims=True) / D + EPSILON)
+    cosine, sine = tables(tokens)
+    cosine = jnp.concatenate([cosine, cosine], axis=1)
+    sine = jnp.concatenate([-sine, sine], axis=1)
+    scale, cosine, sine = after(scale, cosine, sine)
+    kv = after(call(
+        kv_kernel,
+        jax.ShapeDtypeStruct((tokens, HEAD), jnp.bfloat16),
+        in_specs=[SCALARS] + [WHOLE] * 7,
+        out_specs=WHOLE,
+    )(place, *first_parts, scale, cosine, sine))
+    vk = to_core(kv)
+    *sent, own = after(*join(mine, *after(*swapped)))
+    parts = [own] + to_plane(sent)
+    vk = after(vk)
+    one = after(heads(place, lengths, first_parts, 1, scale, cosine, sine, kv, vk))
+    return heads(place, lengths, after(*parts), 0, scale, cosine, sine, kv, vk, one)
+
+
+def local(hidden_in, norm_gain, projection, lengths):
+    part = projection.shape[1] // lax.axis_size("groups")
+    if lax.axis_size("dp") == 8 and part % HEAD == 0:
+        return staged(hidden_in, norm_gain, projection, lengths)
+    return general(hidden_in, norm_gain, projection, lengths)
+
+
 def solution(mesh):
     in_specs = (
         P(("groups", "dp"), "tensor"),

time: 124 us -> 78.9 us (0.64)
  waiting for transfers between devices: 60.7 us -> 39.2 us
  Pallas kernels: 0 us -> 14.6 us
  other arithmetic: 14.3 us -> 0.88 us
  matrix products: 12.7 us -> 0 us
  starting transfers between devices: 29.8 us -> 21.1 us
  between operations: 2.23 us -> 0.13 us
  local copies, waits for them, and re-layouts: 4.18 us -> 2.74 us
    ppermute x34 -> x23, waiting for transfers between devices: 60.7 us -> 39.2 us  [the longest x4 17.9 us: on_ring(): return lax.ppermute(a, 'dp', ring)]
    pallas_call x0 -> x10, Pallas kernels: none -> 14.6 us  [the longest x3 6.45 us: matmul(): call(functools.partial(matmul_kernel, firsts, n_blocks, so_far is not Non...]
    dot_general x22 -> x0, matrix products: 12.7 us -> none  [the longest x16 11.4 us: local(): jnp.dot(acts[k], weights[i][k], preferred_element_type=jnp.float32)]
    ppermute x34 -> x23, starting transfers between devices: 29.8 us -> 21.1 us  [the longest x3 7.62 us: to_plane(): lax.ppermute(three[0], ('groups', 'dp'), across)]
    concatenate x7 -> x1, other arithmetic: 8.08 us -> 0.13 us  [staged(): cosine = jnp.concatenate([cosine, cosine], axis=1)]
    reduce_sum x4 -> x1, other arithmetic: 3.29 us -> 0.11 us  [staged(): scale = lax.rsqrt(jnp.sum(squares, axis=1, keepdims=True) / D + EPSILON)]
    unnamed x6, local copies, waits for them, and re-layouts: 0.01 us -> 2.6 us
    dynamic_slice x1 -> x0, local copies, waits for them, and re-layouts: 2.04 us -> none  [column(): return lax.dynamic_slice_in_dim(mine, start, HEAD, 1)]
  transfers between devices with their start and end apart: 34 -> 23, of which waited for: 14 -> 17; matrix products, arithmetic and copies ran while one was open for 21% -> 1% of each run, Pallas kernels for 0% -> 13%
where the time goes in v2:
time: 78.9 us; the launch traced here: 78.6 us
  waiting for transfers between devices  39.2 us (50%)
  starting transfers between devices  21.1 us (27%)
  Pallas kernels  14.6 us (19%)
  local copies, waits for them, and re-layouts  2.74 us (3%)
  other arithmetic  0.88 us (1%)
    ppermute x4, waiting for transfers between devices, on_ring(): return lax.ppermute(a, 'dp', ring)  17.9 us
    ppermute x3, waiting for transfers between devices, to_plane(): lax.ppermute(three[1], 'dp', over_x)  9.25 us
    ppermute x2, waiting for transfers between devices, back(): return lax.ppermute(a, 'dp', [(j, i) for i, j in ring])  7.95 us
    ppermute x3, starting transfers between devices, to_plane(): lax.ppermute(three[0], ('groups', 'dp'), across)  7.62 us
    pallas_call x3, Pallas kernels, matmul(): call(functools.partial(matmul_kernel, firsts, n_blocks, so_far is not Non...  6.45 us
    ppermute x4, starting transfers between devices, on_ring(): return lax.ppermute(a, 'dp', ring)  4.78 us
    ppermute x2, starting transfers between devices, back(): return lax.ppermute(a, 'dp', [(j, i) for i, j in ring])  3.96 us
    pallas_call x2, Pallas kernels, heads(): call(functools.partial(heads_kernel, first, len(parts)), jax.ShapeDtypeSt...  3.47 us
  transfers between devices with their start and end apart: 23, of which 17 were waited for; matrix products, arithmetic and copies ran while one was open for 1% of the time, Pallas kernels for 13%

profile of v2, /device:TPU:0, one launch (start us, length us, event | category | flops | bytes accessed | tf_op | source)
XLA Modules:
  0.0 78.6 jit_solution(18098483474313689220)
XLA Ops:
  0.1 1.8 %shard_map.46 = (bf16[384,512]{1,0:T(8,128)(2,1)S(1)}, bf16[384,512]{1,0:T(8,128)(2,1)S(1)}) custom-call(s32[4]{0:T(128)S(1)} %pad_add_fusion.place_ref, bf16[1,768,1024]{2,1,0:T(8,128)(2,1)} %rows_ref.1), custom_call_target="tpu_custom_call" | custom-call | flops 1 | bytes 1 | tf_op jit(solution)/shard_map/pallas_call | solution.py:178
  1.9 3.1 %collective-permute-start.4 = (bf16[384,512]{1,0:T(8,128)(2,1)S(1)}, bf16[384,512]{1,0:T(8,128)(2,1)S(1)}, u32[]{:S(2)}, u32[]{:S(2)}) collective-permute-start(bf16[384,512]{1,0:T(8,128)(2,1)S(1)} %get-tuple-element.83.refs_4_), channel_id=1, source_target_pairs={{0,4},{2,6},{4,8},{6,10},{8,12},{10,14},{12,0},{14,2},{1,5},{3,7},... | collective-permute-start | bytes 1179656 | tf_op jit(solution)/shard_map/ppermute | solution.py:391
  5.0 2.1 %collective-permute-start.3 = (bf16[384,512]{1,0:T(8,128)(2,1)S(1)}, bf16[384,512]{1,0:T(8,128)(2,1)S(1)}, u32[]{:S(2)}, u32[]{:S(2)}) collective-permute-start(bf16[384,512]{1,0:T(8,128)(2,1)S(1)} %get-tuple-element.83.refs_4_), channel_id=1, source_target_pairs={{4,0},{6,2},{8,4},{10,6},{12,8},{14,10},{0,12},{2,14},{5,1},{7,3},... | collective-permute-start | bytes 1179656 | tf_op jit(solution)/shard_map/ppermute | solution.py:394
  7.1 1.9 %copy-done = bf16[256,6144]{1,0:T(8,128)(2,1)S(1)} copy-done((bf16[256,6144]{1,0:T(8,128)(2,1)S(1)}, bf16[256,6144]{1,0:T(8,128)(2,1)}, u32[]{:S(2)}) %copy-start) | copy-done | bytes 3145752
  9.0 0.7 copy-done.1
  9.7 1.9 %shard_map.47 = (bf16[4,256,384]{2,1,0:T(8,128)(2,1)S(1)}, bf16[4,256,384]{2,1,0:T(8,128)(2,1)S(1)}, bf16[4,256,384]{2,1,0:T(8,128)(2,1)S(1)}, bf16[4,256,384]{2,1,0:T(8,128)(2,1)S(1)}, f32[256,128]{1,0:T(8,128)S(1)}) custom-call(s32[4]{0:T(128)S(1)} %pad_add_fusion.place_ref, bf16[256,6144]{1,0:T(8,128)(2,1)S(1)} %copy-done, bf16[6144]{0:T(1024)(128)(2,1)S(1)} %copy-done.1), custom_call_target="tpu_custom_call" | custom-call | flops 1 | bytes 1 | tf_op jit(solution)/shard_map/pallas_call | solution.py:223
  11.7 2.7 %collective-permute-start = (bf16[4,256,384]{2,1,0:T(8,128)(2,1)S(1)}, bf16[4,256,384]{2,1,0:T(8,128)(2,1)S(1)}, u32[]{:S(2)}, u32[]{:S(2)}) collective-permute-start(bf16[4,256,384]{2,1,0:T(8,128)(2,1)S(1)} %get-tuple-element.89), channel_id=1, source_target_pairs={{0,18},{2,16},{4,22},{6,20},{8,26},{10,24},{12,30},{14,28},{16,2},... | collective-permute-start | bytes 2359304 | tf_op jit(solution)/shard_map/ppermute | solution.py:398
  14.3 0.5 collective-permute-start.1
  15.2 1.8 %collective-permute-done.4.refs_5_ = bf16[384,512]{1,0:T(8,128)(2,1)S(1)} collective-permute-done((bf16[384,512]{1,0:T(8,128)(2,1)S(1)}, bf16[384,512]{1,0:T(8,128)(2,1)S(1)}, u32[]{:S(2)}, u32[]{:S(2)}) %collective-permute-start.4) | collective-permute-done | bytes 393248 | tf_op jit(solution)/shard_map/ppermute | solution.py:391
  17.0 7.2 %collective-permute-done.3.refs_7_ = bf16[384,512]{1,0:T(8,128)(2,1)S(1)} collective-permute-done((bf16[384,512]{1,0:T(8,128)(2,1)S(1)}, bf16[384,512]{1,0:T(8,128)(2,1)S(1)}, u32[]{:S(2)}, u32[]{:S(2)}) %collective-permute-start.3) | collective-permute-done | bytes 393248 | tf_op jit(solution)/shard_map/ppermute | solution.py:394
  24.2 1.7 %collective-permute-start.5 = (bf16[384,512]{1,0:T(8,128)(2,1)S(1)}, bf16[384,512]{1,0:T(8,128)(2,1)S(1)}, u32[]{:S(2)}, u32[]{:S(2)}) collective-permute-start(bf16[384,512]{1,0:T(8,128)(2,1)S(1)} %get-tuple-element.104.refs_4_), channel_id=1, source_target_pairs={{0,4},{2,6},{4,8},{6,10},{8,12},{10,14},{12,0},{14,2},{1,5},{3,7},... | collective-permute-start | bytes 1179656 | tf_op jit(solution)/shard_map/ppermute | solution.py:391
  25.9 9.6 %collective-permute-done.6.refs_6_ = bf16[384,512]{1,0:T(8,128)(2,1)S(1)} collective-permute-done((bf16[384,512]{1,0:T(8,128)(2,1)S(1)}, bf16[384,512]{1,0:T(8,128)(2,1)S(1)}, u32[]{:S(2)}, u32[]{:S(2)}) %collective-permute-start.6) | collective-permute-done | bytes 393248 | tf_op jit(solution)/shard_map/ppermute | solution.py:391
  35.5 1.9 %collective-permute-start.8 = (bf16[384,512]{1,0:T(8,128)(2,1)S(1)}, bf16[384,512]{1,0:T(8,128)(2,1)S(1)}, u32[]{:S(2)}, u32[]{:S(2)}) collective-permute-start(bf16[384,512]{1,0:T(8,128)(2,1)S(1)} %get-tuple-element.104.refs_4_), channel_id=1, source_target_pairs={{4,0},{6,2},{8,4},{10,6},{12,8},{14,10},{0,12},{2,14},{5,1},{7,3},... | collective-permute-start | bytes 1179656 | tf_op jit(solution)/shard_map/ppermute | solution.py:394
  37.4 6.4 %collective-permute-done.5.refs_5_ = bf16[384,512]{1,0:T(8,128)(2,1)S(1)} collective-permute-done((bf16[384,512]{1,0:T(8,128)(2,1)S(1)}, bf16[384,512]{1,0:T(8,128)(2,1)S(1)}, u32[]{:S(2)}, u32[]{:S(2)}) %collective-permute-start.5) | collective-permute-done | bytes 393248 | tf_op jit(solution)/shard_map/ppermute | solution.py:391
  43.9 4.7 %collective-permute-done.1.refs_1_ = bf16[4,256,384]{2,1,0:T(8,128)(2,1)S(1)} collective-permute-done((bf16[4,256,384]{2,1,0:T(8,128)(2,1)S(1)}, bf16[4,256,384]{2,1,0:T(8,128)(2,1)S(1)}, u32[]{:S(2)}, u32[]{:S(2)}) %collective-permute-start.1) | collective-permute-done | bytes 786464 | tf_op jit(solution)/shard_map/ppermute | solution.py:399
  48.6 2.9 %shard_map.49 = (bf16[2,256,128]{2,1,0:T(8,128)(2,1)S(1)}, bf16[2,256,128]{2,1,0:T(8,128)(2,1)S(1)}, bf16[2,256,128]{2,1,0:T(8,128)(2,1)S(1)}, bf16[2,256,128]{2,1,0:T(8,128)(2,1)S(1)}, f32[4,2,256,128]{3,2,1,0:T(8,128)S(1)}) custom-call(s32[4]{0:T(128)S(1)} %pad_add_fusion.place_ref, bf16[4,256,384]{2,1,0:T(8,128)(2,1)S(1)} %collective-permute-done.refs_0_, ...), custom_call_target="tpu_custom_call" | custom-call | flops 1 | bytes 1 | tf_op jit(solution)/shard_map/pallas_call | solution.py:275
  51.4 0.7 collective-permute-done.8.refs_6_
  54.3 2.5 %collective-permute-start.15 = (bf16[2,256,128]{2,1,0:T(8,128)(2,1)S(1)}, bf16[2,256,128]{2,1,0:T(8,128)(2,1)S(1)}, u32[]{:S(2)}, u32[]{:S(2)}) collective-permute-start(bf16[2,256,128]{2,1,0:T(8,128)(2,1)S(1)} %get-tuple-element.124), channel_id=1, source_target_pairs={{0,18},{2,16},{4,22},{6,20},{8,26},{10,24},{12,30},{14,28},{16,2},... | collective-permute-start | bytes 393224 | tf_op jit(solution)/shard_map/ppermute | solution.py:398
  56.8 0.5 collective-permute-start.16
  57.9 2.3 %shard_map.48.refs_5_ = f32[4,256,512]{2,1,0:T(8,128)S(1)} custom-call(s32[4]{0:T(128)S(1)} %pad_add_fusion.place_ref, bf16[4,256,384]{2,1,0:T(8,128)(2,1)S(1)} %collective-permute-done.refs_0_, bf16[4,256,384]{2,1,0:T(8,128)(2,1)S(1)} %collective-permute-done.1.refs_1_, bf16[4,256,384]{2,1,0:T(8,128)(2,1)S(1)} %collective-permute-done.2.refs_2_, ...), custom_call_target="tpu_custom_call" | custom-call | flops 1 | bytes 1 | tf_op jit(solution)/shard_map/pallas_call | solution.py:275
  60.2 1.3 %shard_map.51 = (bf16[4,256,128]{2,1,0:T(8,128)(2,1)S(1)}, bf16[4,256,128]{2,1,0:T(8,128)(2,1)S(1)}, f32[4,2,256,128]{3,2,1,0:T(8,128)S(1)}) custom-call(s32[4]{0:T(128)S(1)} %pad_add_fusion.place_ref, bf16[4,256,384]{2,1,0:T(8,128)(2,1)S(1)} %collective-permute-done.refs_0_, bf16[4,256,384]{2,1,0:T(8,128)(2,1)S(1)} %collective-permute-done.1.refs_1_, ...), custom_call_target="tpu_custom_call" | custom-call | flops 1 | bytes 1 | tf_op jit(solution)/shard_map/pallas_call | solution.py:275
  61.6 2.3 %collective-permute-done.16.r1.refs_2_ = bf16[2,256,128]{2,1,0:T(8,128)(2,1)S(1)} collective-permute-done((bf16[2,256,128]{2,1,0:T(8,128)(2,1)S(1)}, bf16[2,256,128]{2,1,0:T(8,128)(2,1)S(1)}, u32[]{:S(2)}, u32[]{:S(2)}) %collective-permute-start.16) | collective-permute-done | bytes 131104 | tf_op jit(solution)/shard_map/ppermute | solution.py:399
  64.6 0.6 collective-permute-start.13
  65.5 0.7 shard_map.52.refs_7_
  66.8 2.4 %collective-permute-start.19 = (bf16[2,256,128]{2,1,0:T(8,128)(2,1)S(1)}, bf16[2,256,128]{2,1,0:T(8,128)(2,1)S(1)}, u32[]{:S(2)}, u32[]{:S(2)}) collective-permute-start(bf16[2,256,128]{2,1,0:T(8,128)(2,1)S(1)} %get-tuple-element.152), channel_id=1, source_target_pairs={{0,18},{2,16},{4,22},{6,20},{8,26},{10,24},{12,30},{14,28},{16,2},... | collective-permute-start | bytes 393224 | tf_op jit(solution)/shard_map/ppermute | solution.py:398
  69.2 0.5 collective-permute-start.20
  69.8 0.6 collective-permute-start.21
  70.4 1.3 %collective-permute-done.22.refs_8_ = bf16[256,128]{1,0:T(8,128)(2,1)S(1)} collective-permute-done((bf16[256,128]{1,0:T(8,128)(2,1)S(1)}, bf16[256,128]{1,0:T(8,128)(2,1)S(1)}, u32[]{:S(2)}, u32[]{:S(2)}) %collective-permute-start.22) | collective-permute-done | bytes 65568 | tf_op jit(solution)/shard_map/ppermute | solution.py:388
  71.6 1.2 %shard_map.54.refs_9_ = bf16[256,128]{1,0:T(8,128)(2,1)S(1)} custom-call(s32[4]{0:T(128)S(1)} %pad_add_fusion.place_ref, s32[1,2]{1,0:T(1,128)S(1)} %copy-done.2, f32[2,256,128]{2,1,0:T(8,128)S(1)} %get-tuple-element.136.own.refs_0_, bf16[2,256,128]{2,1,0:T(8,128)(2,1)S(1)} %collective-permute-done.15.r0.refs_1_, ...), custom_call_target="tpu_custom_call" | custom-call | flops 1 | bytes 1 | tf_op jit(solution)/shard_map/pallas_call | solution.py:360
  72.8 1.3 %collective-permute-done.19.refs_1_ = bf16[2,256,128]{2,1,0:T(8,128)(2,1)S(1)} collective-permute-done((bf16[2,256,128]{2,1,0:T(8,128)(2,1)S(1)}, bf16[2,256,128]{2,1,0:T(8,128)(2,1)S(1)}, u32[]{:S(2)}, u32[]{:S(2)}) %collective-permute-start.19) | collective-permute-done | bytes 131104 | tf_op jit(solution)/shard_map/ppermute | solution.py:398
  74.1 2.2 %collective-permute-done.20.refs_2_ = bf16[2,256,128]{2,1,0:T(8,128)(2,1)S(1)} collective-permute-done((bf16[2,256,128]{2,1,0:T(8,128)(2,1)S(1)}, bf16[2,256,128]{2,1,0:T(8,128)(2,1)S(1)}, u32[]{:S(2)}, u32[]{:S(2)}) %collective-permute-start.20) | collective-permute-done | bytes 131104 | tf_op jit(solution)/shard_map/ppermute | solution.py:399
  76.3 2.3 %shard_map.55 = bf16[256,384]{1,0:T(8,128)(2,1)} custom-call(s32[4]{0:T(128)S(1)} %pad_add_fusion.place_ref, s32[1,2]{1,0:T(1,128)S(1)} %copy-done.2, f32[2,256,128]{2,1,0:T(8,128)S(1)} %get-tuple-element.157.refs_0_, bf16[2,256,128]{2,1,0:T(8,128)(2,1)S(1)} %collective-permute-done.19.refs_1_, bf16[2,256,128]{2,1,0:T(8,128)(2,1)S(1)} %collective-permute-done.20.refs_2_, ...), custom_call_target="tpu_custom_call" | custom-call | flops 1 | bytes 1 | tf_op jit(solution)/shard_map/pallas_call | solution.py:360
  (38 shorter events, 4.8 us)
Async XLA Ops:
  1.9 15.1 %collective-permute-start.4 = (bf16[384,512]{1,0:T(8,128)(2,1)S(1)}, bf16[384,512]{1,0:T(8,128)(2,1)S(1)}, u32[]{:S(2)}, u32[]{:S(2)}) collective-permute-start(bf16[384,512]{1,0:T(8,128)(2,1)S(1)} %get-tuple-element.83.refs_4_), channel_id=1, source_target_pairs={{0,4},{2,6},{4,8},{6,10},{8,12},{10,14},{12,0},{14,2},{1,5},{3,7},... | collective-permute-start | bytes 1179656 | tf_op jit(solution)/shard_map/ppermute | solution.py:391
  5.0 19.2 %collective-permute-start.3 = (bf16[384,512]{1,0:T(8,128)(2,1)S(1)}, bf16[384,512]{1,0:T(8,128)(2,1)S(1)}, u32[]{:S(2)}, u32[]{:S(2)}) collective-permute-start(bf16[384,512]{1,0:T(8,128)(2,1)S(1)} %get-tuple-element.83.refs_4_), channel_id=1, source_target_pairs={{4,0},{6,2},{8,4},{10,6},{12,8},{14,10},{0,12},{2,14},{5,1},{7,3},... | collective-permute-start | bytes 1179656 | tf_op jit(solution)/shard_map/ppermute | solution.py:394
  7.1 1.9 %copy-start = (bf16[256,6144]{1,0:T(8,128)(2,1)S(1)}, bf16[256,6144]{1,0:T(8,128)(2,1)}, u32[]{:S(2)}) copy-start(bf16[256,6144]{1,0:T(8,128)(2,1)} %hidden_ref) | copy-start | bytes 9437188
  9.0 0.7 copy-start.1
  11.7 32.2 %collective-permute-start = (bf16[4,256,384]{2,1,0:T(8,128)(2,1)S(1)}, bf16[4,256,384]{2,1,0:T(8,128)(2,1)S(1)}, u32[]{:S(2)}, u32[]{:S(2)}) collective-permute-start(bf16[4,256,384]{2,1,0:T(8,128)(2,1)S(1)} %get-tuple-element.89), channel_id=1, source_target_pairs={{0,18},{2,16},{4,22},{6,20},{8,26},{10,24},{12,30},{14,28},{16,2},... | collective-permute-start | bytes 2359304 | tf_op jit(solution)/shard_map/ppermute | solution.py:398
  14.3 34.2 %collective-permute-start.1 = (bf16[4,256,384]{2,1,0:T(8,128)(2,1)S(1)}, bf16[4,256,384]{2,1,0:T(8,128)(2,1)S(1)}, u32[]{:S(2)}, u32[]{:S(2)}) collective-permute-start(bf16[4,256,384]{2,1,0:T(8,128)(2,1)S(1)} %get-tuple-element.90), channel_id=1, source_target_pairs={{0,2},{2,0},{4,6},{6,4},{8,10},{10,8},{12,14},{14,12},{1,3},{3,1},... | collective-permute-start | bytes 2359304 | tf_op jit(solution)/shard_map/ppermute | solution.py:399
  14.9 33.7 %collective-permute-start.2 = (bf16[4,256,384]{2,1,0:T(8,128)(2,1)S(1)}, bf16[4,256,384]{2,1,0:T(8,128)(2,1)S(1)}, u32[]{:S(2)}, u32[]{:S(2)}) collective-permute-start(bf16[4,256,384]{2,1,0:T(8,128)(2,1)S(1)} %get-tuple-element.91), channel_id=1, source_target_pairs={{0,16},{16,0},{1,17},{17,1},{2,18},{18,2},{3,19},{19,3},{4,20},{20... | collective-permute-start | bytes 2359304 | tf_op jit(solution)/shard_map/ppermute | solution.py:400
  17.0 18.5 %collective-permute-start.6 = (bf16[384,512]{1,0:T(8,128)(2,1)S(1)}, bf16[384,512]{1,0:T(8,128)(2,1)S(1)}, u32[]{:S(2)}, u32[]{:S(2)}) collective-permute-start(bf16[384,512]{1,0:T(8,128)(2,1)S(1)} %collective-permute-done.4.refs_5_), channel_id=1, source_target_pairs={{0,4},{2,6},{4,8},{6,10},{8,12},{10,14},{12,0},{14,2},{1,5},{3,7},... | collective-permute-start | bytes 1179656 | tf_op jit(solution)/shard_map/ppermute | solution.py:391
  24.2 19.6 %collective-permute-start.5 = (bf16[384,512]{1,0:T(8,128)(2,1)S(1)}, bf16[384,512]{1,0:T(8,128)(2,1)S(1)}, u32[]{:S(2)}, u32[]{:S(2)}) collective-permute-start(bf16[384,512]{1,0:T(8,128)(2,1)S(1)} %get-tuple-element.104.refs_4_), channel_id=1, source_target_pairs={{0,4},{2,6},{4,8},{6,10},{8,12},{10,14},{12,0},{14,2},{1,5},{3,7},... | collective-permute-start | bytes 1179656 | tf_op jit(solution)/shard_map/ppermute | solution.py:391
  35.5 16.7 %collective-permute-start.8 = (bf16[384,512]{1,0:T(8,128)(2,1)S(1)}, bf16[384,512]{1,0:T(8,128)(2,1)S(1)}, u32[]{:S(2)}, u32[]{:S(2)}) collective-permute-start(bf16[384,512]{1,0:T(8,128)(2,1)S(1)} %get-tuple-element.104.refs_4_), channel_id=1, source_target_pairs={{4,0},{6,2},{8,4},{10,6},{12,8},{14,10},{0,12},{2,14},{5,1},{7,3},... | collective-permute-start | bytes 1179656 | tf_op jit(solution)/shard_map/ppermute | solution.py:394
  43.9 16.4 %collective-permute-start.7 = (bf16[384,512]{1,0:T(8,128)(2,1)S(1)}, bf16[384,512]{1,0:T(8,128)(2,1)S(1)}, u32[]{:S(2)}, u32[]{:S(2)}) collective-permute-start(bf16[384,512]{1,0:T(8,128)(2,1)S(1)} %collective-permute-done.5.refs_5_), channel_id=1, source_target_pairs={{0,4},{2,6},{4,8},{6,10},{8,12},{10,14},{12,0},{14,2},{1,5},{3,7},... | collective-permute-start | bytes 1179656 | tf_op jit(solution)/shard_map/ppermute | solution.py:391
  52.2 1.3 %collective-permute-start.10 = (bf16[2,256,128]{2,1,0:T(8,128)(2,1)S(1)}, bf16[2,256,128]{2,1,0:T(8,128)(2,1)S(1)}, u32[]{:S(2)}, u32[]{:S(2)}) collective-permute-start(bf16[2,256,128]{2,1,0:T(8,128)(2,1)S(1)} %get-tuple-element.113), channel_id=1, source_target_pairs={{0,1},{1,0},{2,3},{3,2},{4,5},{5,4},{6,7},{7,6},{8,9},{9,8},{10,11... | collective-permute-start | bytes 393224 | tf_op jit(solution)/shard_map/ppermute | solution.py:388
  52.2 1.5 %collective-permute-start.11 = (bf16[2,256,128]{2,1,0:T(8,128)(2,1)S(1)}, bf16[2,256,128]{2,1,0:T(8,128)(2,1)S(1)}, u32[]{:S(2)}, u32[]{:S(2)}) collective-permute-start(bf16[2,256,128]{2,1,0:T(8,128)(2,1)S(1)} %get-tuple-element.114), channel_id=1, source_target_pairs={{0,1},{1,0},{2,3},{3,2},{4,5},{5,4},{6,7},{7,6},{8,9},{9,8},{10,11... | collective-permute-start | bytes 393224 | tf_op jit(solution)/shard_map/ppermute | solution.py:388
  52.7 1.3 %collective-permute-start.12 = (bf16[2,256,128]{2,1,0:T(8,128)(2,1)S(1)}, bf16[2,256,128]{2,1,0:T(8,128)(2,1)S(1)}, u32[]{:S(2)}, u32[]{:S(2)}) collective-permute-start(bf16[2,256,128]{2,1,0:T(8,128)(2,1)S(1)} %get-tuple-element.115), channel_id=1, source_target_pairs={{0,1},{1,0},{2,3},{3,2},{4,5},{5,4},{6,7},{7,6},{8,9},{9,8},{10,11... | collective-permute-start | bytes 393224 | tf_op jit(solution)/shard_map/ppermute | solution.py:388
  52.7 1.5 %collective-permute-start.9 = (bf16[2,256,128]{2,1,0:T(8,128)(2,1)S(1)}, bf16[2,256,128]{2,1,0:T(8,128)(2,1)S(1)}, u32[]{:S(2)}, u32[]{:S(2)}) collective-permute-start(bf16[2,256,128]{2,1,0:T(8,128)(2,1)S(1)} %get-tuple-element.112), channel_id=1, source_target_pairs={{0,1},{1,0},{2,3},{3,2},{4,5},{5,4},{6,7},{7,6},{8,9},{9,8},{10,11... | collective-permute-start | bytes 393224 | tf_op jit(solution)/shard_map/ppermute | solution.py:388
  54.3 7.3 %collective-permute-start.15 = (bf16[2,256,128]{2,1,0:T(8,128)(2,1)S(1)}, bf16[2,256,128]{2,1,0:T(8,128)(2,1)S(1)}, u32[]{:S(2)}, u32[]{:S(2)}) collective-permute-start(bf16[2,256,128]{2,1,0:T(8,128)(2,1)S(1)} %get-tuple-element.124), channel_id=1, source_target_pairs={{0,18},{2,16},{4,22},{6,20},{8,26},{10,24},{12,30},{14,28},{16,2},... | collective-permute-start | bytes 393224 | tf_op jit(solution)/shard_map/ppermute | solution.py:398
  56.8 7.1 %collective-permute-start.16 = (bf16[2,256,128]{2,1,0:T(8,128)(2,1)S(1)}, bf16[2,256,128]{2,1,0:T(8,128)(2,1)S(1)}, u32[]{:S(2)}, u32[]{:S(2)}) collective-permute-start(bf16[2,256,128]{2,1,0:T(8,128)(2,1)S(1)} %get-tuple-element.134), channel_id=1, source_target_pairs={{0,2},{2,0},{4,6},{6,4},{8,10},{10,8},{12,14},{14,12},{1,3},{3,1},... | collective-permute-start | bytes 393224 | tf_op jit(solution)/shard_map/ppermute | solution.py:399
  57.4 6.5 %collective-permute-start.17 = (bf16[2,256,128]{2,1,0:T(8,128)(2,1)S(1)}, bf16[2,256,128]{2,1,0:T(8,128)(2,1)S(1)}, u32[]{:S(2)}, u32[]{:S(2)}) collective-permute-start(bf16[2,256,128]{2,1,0:T(8,128)(2,1)S(1)} %get-tuple-element.135), channel_id=1, source_target_pairs={{0,16},{16,0},{1,17},{17,1},{2,18},{18,2},{3,19},{19,3},{4,20},{20... | collective-permute-start | bytes 393224 | tf_op jit(solution)/shard_map/ppermute | solution.py:400
  61.5 10.1 %copy-start.2 = (s32[1,2]{1,0:T(1,128)S(1)}, s32[1,2]{1,0:T(1,128)}, u32[]{:S(2)}) copy-start(s32[1,2]{1,0:T(1,128)} %lengths_ref.3) | copy-start | bytes 28
  63.9 1.3 %collective-permute-start.18 = (f32[256,128]{1,0:T(8,128)S(1)}, f32[256,128]{1,0:T(8,128)S(1)}, u32[]{:S(2)}, u32[]{:S(2)}) collective-permute-start(f32[256,128]{1,0:T(8,128)S(1)} %get-tuple-element.140), channel_id=1, source_target_pairs={{0,1},{1,0},{2,3},{3,2},{4,5},{5,4},{6,7},{7,6},{8,9},{9,8},{10,11... | collective-permute-start | bytes 393224 | tf_op jit(solution)/shard_map/ppermute | solution.py:388
  64.6 1.7 %collective-permute-start.13 = (bf16[4,256,128]{2,1,0:T(8,128)(2,1)S(1)}, bf16[4,256,128]{2,1,0:T(8,128)(2,1)S(1)}, u32[]{:S(2)}, u32[]{:S(2)}) collective-permute-start(bf16[4,256,128]{2,1,0:T(8,128)(2,1)S(1)} %get-tuple-element.131), channel_id=1, source_target_pairs={{0,1},{1,0},{2,3},{3,2},{4,5},{5,4},{6,7},{7,6},{8,9},{9,8},{10,11... | collective-permute-start | bytes 786440 | tf_op jit(solution)/shard_map/ppermute | solution.py:388
  65.2 1.5 %collective-permute-start.14 = (bf16[4,256,128]{2,1,0:T(8,128)(2,1)S(1)}, bf16[4,256,128]{2,1,0:T(8,128)(2,1)S(1)}, u32[]{:S(2)}, u32[]{:S(2)}) collective-permute-start(bf16[4,256,128]{2,1,0:T(8,128)(2,1)S(1)} %get-tuple-element.132), channel_id=1, source_target_pairs={{0,1},{1,0},{2,3},{3,2},{4,5},{5,4},{6,7},{7,6},{8,9},{9,8},{10,11... | collective-permute-start | bytes 786440 | tf_op jit(solution)/shard_map/ppermute | solution.py:388
  66.8 7.3 %collective-permute-start.19 = (bf16[2,256,128]{2,1,0:T(8,128)(2,1)S(1)}, bf16[2,256,128]{2,1,0:T(8,128)(2,1)S(1)}, u32[]{:S(2)}, u32[]{:S(2)}) collective-permute-start(bf16[2,256,128]{2,1,0:T(8,128)(2,1)S(1)} %get-tuple-element.152), channel_id=1, source_target_pairs={{0,18},{2,16},{4,22},{6,20},{8,26},{10,24},{12,30},{14,28},{16,2},... | collective-permute-start | bytes 393224 | tf_op jit(solution)/shard_map/ppermute | solution.py:398
  69.2 7.1 %collective-permute-start.20 = (bf16[2,256,128]{2,1,0:T(8,128)(2,1)S(1)}, bf16[2,256,128]{2,1,0:T(8,128)(2,1)S(1)}, u32[]{:S(2)}, u32[]{:S(2)}) collective-permute-start(bf16[2,256,128]{2,1,0:T(8,128)(2,1)S(1)} %get-tuple-element.153), channel_id=1, source_target_pairs={{0,2},{2,0},{4,6},{6,4},{8,10},{10,8},{12,14},{14,12},{1,3},{3,1},... | collective-permute-start | bytes 393224 | tf_op jit(solution)/shard_map/ppermute | solution.py:399
  69.8 6.6 %collective-permute-start.21 = (bf16[2,256,128]{2,1,0:T(8,128)(2,1)S(1)}, bf16[2,256,128]{2,1,0:T(8,128)(2,1)S(1)}, u32[]{:S(2)}, u32[]{:S(2)}) collective-permute-start(bf16[2,256,128]{2,1,0:T(8,128)(2,1)S(1)} %get-tuple-element.154), channel_id=1, source_target_pairs={{0,16},{16,0},{1,17},{17,1},{2,18},{18,2},{3,19},{19,3},{4,20},{20... | collective-permute-start | bytes 393224 | tf_op jit(solution)/shard_map/ppermute | solution.py:400
  70.4 1.3 %collective-permute-start.22 = (bf16[256,128]{1,0:T(8,128)(2,1)S(1)}, bf16[256,128]{1,0:T(8,128)(2,1)S(1)}, u32[]{:S(2)}, u32[]{:S(2)}) collective-permute-start(bf16[256,128]{1,0:T(8,128)(2,1)S(1)} %shard_map.52.refs_7_), channel_id=1, source_target_pairs={{0,1},{1,0},{2,3},{3,2},{4,5},{5,4},{6,7},{7,6},{8,9},{9,8},{10,11... | collective-permute-start | bytes 196616 | tf_op jit(solution)/shard_map/ppermute | solution.py:388

commit v3 on v2

v3 whole, which is shorter than its diff:
```python
import functools
import math

import jax
import jax.numpy as jnp
from jax import lax
from jax.experimental import pallas as pl
from jax.experimental.pallas import tpu as pltpu
from jax.sharding import PartitionSpec as P

D = 12288
HEAD = 128
QHEADS = 6
ROPE_BASE = 1000000.0
EPSILON = 1e-05


def angles(seq_len):
    half = HEAD // 2
    positions = jnp.arange(seq_len, dtype=jnp.int32)
    freq = ROPE_BASE ** (-(jnp.arange(half, dtype=jnp.float32) * 2.0 / HEAD))
    angle = positions.astype(jnp.float32)[:, None] * freq[None, :]
    return jnp.cos(angle), jnp.sin(angle)


def rotate(block, cosine, sine):
    half = HEAD // 2
    first = block[:, :half]
    second = block[:, half:]
    return jnp.concatenate([first * cosine - second * sine, second * cosine + first * sine], axis=-1)


def attend_head(query, keys, values, allowed, keep):
    scores = lax.dot_general(
        query, keys, (((1,), (1,)), ((), ())), preferred_element_type=jnp.float32
    ) * HEAD ** (-0.5)
    scores = jnp.where(allowed, scores, -1e30)
    largest = jnp.max(scores, axis=-1, keepdims=True)
    expo = jnp.exp(scores - largest)
    attn = (expo / jnp.sum(expo, axis=-1, keepdims=True)).astype(jnp.bfloat16)
    mixed = jnp.dot(attn, values, preferred_element_type=jnp.float32)
    return (mixed * keep).astype(jnp.bfloat16)


def swap(size):
    return [(i, i ^ 1) for i in range(size)]


def general(hidden_in, norm_gain, projection, lengths):
    groups = lax.axis_size("groups")
    dp = lax.axis_size("dp")
    tensor = lax.axis_size("tensor")
    y = lax.axis_index("groups")
    place = lax.axis_index("dp")
    core = lax.axis_index("tensor")
    x = place % 2
    z = place // 2
    depth = dp // 2
    tokens = hidden_in.shape[0]
    rows = projection.shape[1]
    part = rows // groups
    heads_local = QHEADS // tensor

    ring = [(i, (i + 2) % dp) for i in range(dp)]
    over_x = swap(dp)
    over_y = swap(groups)
    over_core = swap(tensor)
    across = [(g * dp + i, (g ^ 1) * dp + (i ^ 1)) for g in range(groups) for i in range(dp)]

    mine = lax.dynamic_slice_in_dim(projection[0], y * part, part, 0)

    def column(owner, index):
        start = (QHEADS + owner) * HEAD if index == 0 else (owner * heads_local + index - 1) * HEAD
        return lax.dynamic_slice_in_dim(mine, start, HEAD, 1)

    n_cols = heads_local + 1
    theirs = jnp.concatenate([column(1 - core, i) for i in range(n_cols)], axis=1)
    other = lax.ppermute(theirs, "tensor", over_core)
    weights = []
    for i in range(n_cols):
        slot = jnp.concatenate([column(core, i), other[:, i * HEAD:(i + 1) * HEAD]], axis=0)
        weights.append([slot])
    for _ in range(depth - 1):
        for i in range(n_cols):
            weights[i].append(lax.ppermute(weights[i][-1], "dp", ring))

    wide32 = hidden_in.astype(jnp.float32)
    gated = (wide32 * norm_gain.astype(jnp.float32)[None, :]).astype(jnp.bfloat16)
    local_sq = jnp.sum(wide32 * wide32, axis=1)
    total_sq = local_sq + lax.ppermute(local_sq, "tensor", over_core)
    inv_rms = lax.rsqrt(total_sq / D + EPSILON)[:, None]

    def piece(dx, dy):
        slabs = []
        for k in range(depth):
            shard = ((z - k + depth) % depth) * 2 + (x ^ dx)
            slabs.append(lax.dynamic_slice_in_dim(gated, shard * rows + (y ^ dy) * part, part, 1))
        return jnp.stack(slabs)

    sent = [piece(1, 1), piece(1, 0), piece(0, 1)]
    held = [
        lax.ppermute(sent[0], ("groups", "dp"), across),
        lax.ppermute(sent[1], "dp", over_x),
        lax.ppermute(sent[2], "groups", over_y),
        piece(0, 0),
    ]
    acts = []
    for h in held:
        acts.append(jnp.concatenate([h, lax.ppermute(h, "tensor", over_core)], axis=2))
    acts = jnp.concatenate(acts, axis=1)

    cosine, sine = angles(tokens)
    positions = jnp.arange(tokens, dtype=jnp.int32)
    prompt = lengths[0, 0]
    total_len = prompt + lengths[0, 1]
    allowed = (positions[None, :] <= positions[:, None]) & (positions[None, :] < total_len)
    keep = ((positions >= prompt - 1) & (positions < total_len - 1)).astype(jnp.float32)[:, None]

    outs = []
    keys = values = None
    for i in range(n_cols):
        partial = sum(
            jnp.dot(acts[k], weights[i][k], preferred_element_type=jnp.float32) for k in range(depth)
        )
        blocks = partial.reshape(4, tokens, HEAD)
        low = blocks[:3].astype(jnp.bfloat16)
        summed = blocks[3]
        summed = summed + lax.ppermute(low[0], ("groups", "dp"), across).astype(jnp.float32)
        summed = summed + lax.ppermute(low[1], "dp", over_x).astype(jnp.float32)
        summed = summed + lax.ppermute(low[2], "groups", over_y).astype(jnp.float32)
        scaled = summed * inv_rms
        if i == 0:
            turned = rotate(scaled, cosine, sine)
            kv = jnp.where(core == 0, turned, scaled).astype(jnp.bfloat16)
            vk = lax.ppermute(kv, "tensor", over_core)
            keys = jnp.where(core == 0, kv, vk)
            values = jnp.where(core == 0, vk, kv)
        else:
            query = rotate(scaled, cosine, sine).astype(jnp.bfloat16)
            outs.append(attend_head(query, keys, values, allowed, keep))
    return jnp.concatenate(outs, axis=1)


VMEM = pltpu.VMEM
PLANE = ((1, 1), (1, 0), (0, 1), (0, 0))
WHOLE = pl.BlockSpec(memory_space=VMEM)
SCALARS = pl.BlockSpec(memory_space=pltpu.SMEM)


def call(kernel, out_shape, limit=12, result=False, **kwargs):
    if not result:
        out_shape = jax.tree.map(lambda s: pltpu.VMEM(s.shape, s.dtype), out_shape)
    return pl.pallas_call(
        kernel,
        out_shape=out_shape,
        compiler_params=pltpu.CompilerParams(vmem_limit_bytes=limit * 2**20),
        cost_estimate=pl.CostEstimate(flops=1, bytes_accessed=1, transcendentals=0),
        **kwargs,
    )


def select_kernel(columns, part, rows_ref, *refs):
    out_refs, sems = refs[:len(columns)], refs[-1]
    rows = pl.ds(pl.multiple_of(lax.axis_index("groups") * part, HEAD), part)
    copies = []
    for starts, out_ref in zip(columns, out_refs):
        at = 0
        while at < len(starts):
            more = 1
            while at + more < len(starts) and starts[at + more] == starts[at] + more * HEAD:
                more += 1
            copies.append(pltpu.make_async_copy(
                rows_ref.at[0, rows, pl.ds(starts[at], more * HEAD)],
                out_ref.at[:, pl.ds(at * HEAD, more * HEAD)],
                sems.at[len(copies)],
            ))
            at += more
    for copy in copies:
        copy.start()
    for copy in copies:
        copy.wait()


def select(projection, part, columns):
    chunk = jax.ShapeDtypeStruct((part, len(columns[0]) * HEAD), projection.dtype)
    out_shape = (chunk,) * len(columns)
    return call(
        functools.partial(select_kernel, columns, part),
        out_shape,
        in_specs=[pl.BlockSpec(memory_space=pltpu.HBM)],
        out_specs=[WHOLE] * len(out_shape),
        scratch_shapes=[pltpu.SemaphoreType.DMA((len(columns) * len(columns[0]),))],
    )(pltpu.with_memory_space_constraint(projection, pltpu.HBM))


def gate_kernel(part, depth, plane, squares, place_ref, hidden_ref, gain_ref, *refs):
    piece_refs, row_ref = refs[:len(plane)], refs[-1]
    x, y = place_ref[1], place_ref[2]
    base = lax.rem(place_ref[0] - pl.program_id(0) + depth, depth) * 4 * part

    @pl.when(pl.program_id(0) == 0)
    def _():
        row_ref[0, :] = gain_ref[...].astype(jnp.float32)

    for piece_ref, (dx, dy) in zip(piece_refs, plane):
        start = pl.multiple_of(((x ^ dx) * 2 + (y ^ dy)) * part, HEAD)
        wide = hidden_ref[:, pl.ds(start, part)].astype(jnp.float32)
        gain = row_ref[:, pl.ds(pl.multiple_of(base + start, HEAD), part)]
        piece_ref[0] = (wide * gain).astype(jnp.bfloat16)
    if not squares:
        return
    sq_ref = refs[len(plane)]
    total = jnp.zeros(sq_ref.shape, jnp.float32)
    for j in range(0, hidden_ref.shape[1], HEAD):
        wide = hidden_ref[:, j:j + HEAD].astype(jnp.float32)
        total += wide * wide

    @pl.when(pl.program_id(0) == 0)
    def _():
        sq_ref[...] = total

    @pl.when(pl.program_id(0) > 0)
    def _():
        sq_ref[...] += total


def gate(place, hidden_in, norm_gain, part, depth, plane=PLANE, squares=True):
    tokens = hidden_in.shape[0]
    wide = 4 * part
    out_shape = (jax.ShapeDtypeStruct((depth, tokens, part), jnp.bfloat16),) * len(plane)
    out_specs = [pl.BlockSpec((1, tokens, part), lambda k, place: (k, 0, 0))] * len(plane)
    if squares:
        out_shape += (jax.ShapeDtypeStruct((tokens, HEAD), jnp.float32),)
        out_specs.append(pl.BlockSpec((tokens, HEAD), lambda k, place: (0, 0)))

    def shard(k, place):
        return (0, lax.rem(place[0] - k + depth, depth))

    return call(
        functools.partial(gate_kernel, part, depth, plane, squares),
        out_shape,
        grid_spec=pltpu.PrefetchScalarGridSpec(
            num_scalar_prefetch=1,
            grid=(depth,),
            in_specs=[
                pl.BlockSpec((tokens, wide), shard),
                pl.BlockSpec(norm_gain.shape, lambda k, place: (0,)),
            ],
            out_specs=out_specs,
            scratch_shapes=[pltpu.VMEM((1, norm_gain.shape[0]), jnp.float32)],
        ),
    )(place, *(pltpu.with_memory_space_constraint(a, pltpu.HBM) for a in (hidden_in, norm_gain)))


def matmul_kernel(firsts, n_acts, n_more, sent, *refs):
    is_first = lax.axis_index("tensor") == 0
    acts, refs = refs[:n_acts], refs[n_acts:]
    slots, refs = refs[:len(firsts)], refs[len(firsts):]
    more, out_refs = refs[:n_more], refs[n_more:]
    more = [(ref, i) for ref in more for i in range(ref.shape[0])]
    right = [slot[...] for slot in slots]
    wide = 2 * HEAD
    for p in range(n_acts):
        total = jnp.dot(acts[p][firsts[0]], right[0], preferred_element_type=jnp.float32)
        for k in range(1, len(firsts)):
            total += jnp.dot(acts[p][firsts[k]], right[k], preferred_element_type=jnp.float32)
        if more:
            ref, i = more[p]
            total += ref[i]
        if not sent:
            out_refs[0][p] = total
            continue
        theirs_refs, mine_ref = out_refs[:-1], out_refs[-1]
        n_blocks = mine_ref.shape[1]
        per = n_acts * n_blocks // sent
        for g in range(n_blocks):
            low = total[:, g * wide:g * wide + HEAD]
            high = total[:, g * wide + HEAD:(g + 1) * wide]
            spot = p * n_blocks + g
            theirs_refs[spot // per][spot % per] = jnp.where(is_first, high, low).astype(jnp.bfloat16)
            mine_ref[p, g] = jnp.where(is_first, low, high)


def matmul(acts, slots, firsts, so_far=(), sent=0):
    n_blocks = slots[0].shape[1] // (2 * HEAD)
    tokens = acts[0].shape[1]
    args = [*acts, *slots, *so_far]
    if sent:
        out_shape = (jax.ShapeDtypeStruct((len(acts) * n_blocks // sent, tokens, HEAD), jnp.bfloat16),) * sent
        out_shape += (jax.ShapeDtypeStruct((len(acts), n_blocks, tokens, HEAD), jnp.float32),)
    else:
        out_shape = (jax.ShapeDtypeStruct((len(acts), tokens, n_blocks * 2 * HEAD), jnp.float32),)
    outs = call(
        functools.partial(matmul_kernel, firsts, len(acts), len(so_far), sent),
        out_shape,
        in_specs=[WHOLE] * len(args),
        out_specs=[WHOLE] * len(out_shape),
    )(*args)
    return outs if sent else outs[0]


def join_kernel(n_came, mine_ref, *refs):
    came_refs, out_refs = refs[:n_came], refs[n_came:]
    n_blocks = mine_ref.shape[1]
    per = len(out_refs) * n_blocks // n_came
    for p, out_ref in enumerate(out_refs):
        for g in range(n_blocks):
            spot = p * n_blocks + g
            came = came_refs[spot // per][spot % per].astype(jnp.float32)
            out_ref[g] = (mine_ref[p, g] + came).astype(out_ref.dtype)


def join(mine, came, types):
    return call(
        functools.partial(join_kernel, len(came)),
        tuple(jax.ShapeDtypeStruct(mine.shape[1:], t) for t in types),
        in_specs=[WHOLE] * (1 + len(came)),
        out_specs=[WHOLE] * len(types),
    )(mine, *came)


def tables_kernel(lengths_ref, _, cosine_ref, sine_ref, allowed_ref, keep_ref):
    at = lax.broadcasted_iota(jnp.int32, cosine_ref.shape, 0)
    lane = lax.broadcasted_iota(jnp.int32, cosine_ref.shape, 1)
    pair = lax.rem(lane, HEAD // 2).astype(jnp.float32)
    angle = at.astype(jnp.float32) * jnp.exp(pair * (-2.0 * math.log(ROPE_BASE) / HEAD))
    cosine_ref[...] = jnp.cos(angle)
    sine_ref[...] = jnp.where(lane < HEAD // 2, -jnp.sin(angle), jnp.sin(angle))
    prompt = lengths_ref[0, 0]
    total_len = prompt + lengths_ref[0, 1]
    keep_ref[...] = ((at >= prompt - 1) & (at < total_len - 1)).astype(jnp.float32)
    query_at = lax.broadcasted_iota(jnp.int32, allowed_ref.shape, 0)
    key_at = lax.broadcasted_iota(jnp.int32, allowed_ref.shape, 1)
    allowed_ref[...] = ((key_at <= query_at) & (key_at < total_len)).astype(jnp.float32)


def tables(tokens, lengths, later_than):
    table = jax.ShapeDtypeStruct((tokens, HEAD), jnp.float32)
    allowed = jax.ShapeDtypeStruct((tokens, tokens), jnp.float32)
    return call(
        tables_kernel,
        (table, table, allowed, table),
        in_specs=[SCALARS, pl.BlockSpec(memory_space=pl.ANY)],
        out_specs=[WHOLE] * 4,
    )(lengths, later_than)


def scale_kernel(own_ref, other_ref, out_ref):
    squares = jnp.sum(own_ref[...] + other_ref[...], axis=1, keepdims=True)
    out_ref[...] = jnp.broadcast_to(lax.rsqrt(squares / D + EPSILON), out_ref.shape)


def inv_rms(own, other):
    return call(
        scale_kernel,
        jax.ShapeDtypeStruct(own.shape, jnp.float32),
        in_specs=[WHOLE] * 2,
        out_specs=WHOLE,
    )(own, other)


def summed(refs, index, scale_ref):
    total = refs[0][index]
    for ref in refs[1:]:
        total += ref[index].astype(jnp.float32)
    return total * scale_ref[...]


def turned(block, cosine_ref, sine_ref):
    half = HEAD // 2
    other = jnp.concatenate([block[:, half:], block[:, :half]], axis=1)
    return block * cosine_ref[...] + other * sine_ref[...]


def kv_kernel(own, r0, r1, r2, scale_ref, cosine_ref, sine_ref, out_ref):
    block = summed((own, r0, r1, r2), 0, scale_ref)
    spun = turned(block, cosine_ref, sine_ref)
    out_ref[...] = jnp.where(lax.axis_index("tensor") == 0, spun, block).astype(jnp.bfloat16)


def heads_kernel(first, n_parts, *refs):
    parts, refs = refs[:n_parts], refs[n_parts:]
    scale_ref, cosine_ref, sine_ref, allowed_ref, keep_ref, mine_ref, other_ref, *rest = refs
    out_ref = rest[-1]
    is_key = lax.axis_index("tensor") == 0
    mine, other = mine_ref[...], other_ref[...]
    keys = jnp.where(is_key, mine, other)
    values = jnp.where(is_key, other, mine)
    before = 0
    if len(rest) > 1:
        before = rest[0].shape[1]
        out_ref[:, :before] = rest[0][...]
    for i in range(first, parts[0].shape[0]):
        query = turned(summed(parts, i, scale_ref), cosine_ref, sine_ref).astype(jnp.bfloat16)
        scores = lax.dot_general(
            query, keys, (((1,), (1,)), ((), ())), preferred_element_type=jnp.float32
        ) * HEAD ** (-0.5)
        scores = jnp.where(allowed_ref[...] > 0.0, scores, -1e30)
        expo = jnp.exp(scores - jnp.max(scores, axis=-1, keepdims=True))
        attn = (expo / jnp.sum(expo, axis=-1, keepdims=True)).astype(jnp.bfloat16)
        mixed = jnp.dot(attn, values, preferred_element_type=jnp.float32)
        at = before + (i - first) * HEAD
        out_ref[:, at:at + HEAD] = (mixed * keep_ref[...]).astype(jnp.bfloat16)


def heads(parts, first, scale, tabled, mine, other, *earlier):
    args = [*parts, scale, *tabled, mine, other, *earlier]
    width = (parts[0].shape[0] - first) * HEAD + sum(e.shape[1] for e in earlier)
    return call(
        functools.partial(heads_kernel, first, len(parts)),
        jax.ShapeDtypeStruct((mine.shape[0], width), jnp.bfloat16),
        result=bool(earlier),
        in_specs=[WHOLE] * len(args),
        out_specs=WHOLE,
    )(*args)


def staged(hidden_in, norm_gain, projection, lengths):
    groups = lax.axis_size("groups")
    dp = lax.axis_size("dp")
    tensor = lax.axis_size("tensor")
    y = lax.axis_index("groups")
    spot = lax.axis_index("dp")
    core = lax.axis_index("tensor")
    place = jnp.stack([spot // 2, spot % 2, y, core]).astype(jnp.int32)
    depth = dp // 2
    tokens = hidden_in.shape[0]
    part = projection.shape[1] // groups
    heads_local = QHEADS // tensor

    ring = [(i, (i + 2) % dp) for i in range(dp)]
    over_x = swap(dp)
    over_y = swap(groups)
    over_core = swap(tensor)
    across = [(g * dp + i, (g ^ 1) * dp + (i ^ 1)) for g in range(groups) for i in range(dp)]

    def to_core(a):
        return lax.ppermute(a, "tensor", over_core)

    def on_ring(a):
        return lax.ppermute(a, "dp", ring)

    def back(a):
        return lax.ppermute(a, "dp", [(j, i) for i, j in ring])

    def to_far(a):
        return lax.ppermute(a, ("groups", "dp"), across)

    def to_x(a):
        return lax.ppermute(a, "dp", over_x)

    def to_y(a):
        return lax.ppermute(a, "groups", over_y)

    def to_plane(three):
        return [to_far(three[0]), to_x(three[1]), to_y(three[2])]

    last = []

    def after(*values):
        held = lax.optimization_barrier(tuple(values) + tuple(last))[:len(values)]
        last[:] = held[:1]
        return held[0] if len(values) == 1 else held

    blocks = [[(QHEADS + c) * HEAD for c in range(tensor)]]
    blocks += [[(c * heads_local + i) * HEAD for c in range(tensor)] for i in range(heads_local)]
    columns = [blocks[0] + blocks[1], blocks[2] + blocks[3]]
    a0, = select(projection, part, columns[:1])
    a0 = after(a0)
    a1 = on_ring(a0)
    a3 = back(a0)
    far, near_x, near_y, own, squares = after(*gate(place, after(hidden_in), norm_gain, part, depth))
    far = to_far(far)
    near_x = to_x(near_x)
    near_y = to_y(near_y)
    b0, = select(after(projection), part, columns[1:])
    tabled = after(*tables(tokens, lengths, after(squares)))

    a1 = after(a1)
    a2 = on_ring(a1)
    a3, b0 = after(a3, b0)
    b1 = on_ring(b0)
    a2, b0 = after(a2, b0)
    b3 = back(b0)
    set_a = (a0, a1, a2, a3)

    far = after(far)
    *theirs, mine = after(*matmul((far, own), set_a, (0, 1, 2, 3), sent=2))
    swapped = [to_core(t) for t in theirs]
    b1 = after(b1)
    b2 = on_ring(b1)
    sums_far, sums = after(*join(mine, after(*swapped), (jnp.bfloat16, jnp.float32)))
    sums_far = to_far(sums_far)
    near_x, near_y = after(near_x, near_y)
    acts = (far, own, near_x, near_y)
    *theirs, mine = after(*matmul((near_x, near_y), set_a, (0, 1, 2, 3), sent=2))
    swapped = [to_core(t) for t in theirs]
    squares = after(squares)
    other_norm = to_core(squares)
    b3 = after(b3)
    *swapped, other_norm = after(*swapped, other_norm)
    scale = inv_rms(squares, other_norm)
    sums_x, sums_y = after(*join(mine, swapped, (jnp.bfloat16, jnp.bfloat16)))
    sums_x = to_x(sums_x)
    sums_y = to_y(sums_y)
    front = after(matmul(acts, (b0, b1, b3), (0, 1, 3)))

    b2 = after(b2)
    parts_a = after(sums, sums_far, sums_x, sums_y)
    *theirs, mine = after(*matmul(acts, (b2,), (2,), (front,), sent=2))
    swapped = [to_core(t) for t in theirs]
    kv = after(call(
        kv_kernel,
        jax.ShapeDtypeStruct((tokens, HEAD), jnp.bfloat16),
        in_specs=[WHOLE] * 7,
        out_specs=WHOLE,
    )(*parts_a, scale, *tabled[:2]))
    vk = to_core(kv)
    types = (jnp.bfloat16, jnp.float32, jnp.bfloat16, jnp.bfloat16)
    sums_far, sums, sums_x, sums_y = after(*join(mine, after(*swapped), types))
    parts_b = (sums, to_far(sums_far), to_x(sums_x), to_y(sums_y))
    vk = after(vk)
    one = after(heads(parts_a, 1, scale, tabled, kv, vk))
    return heads(after(*parts_b), 0, scale, tabled, kv, vk, one)


def local(hidden_in, norm_gain, projection, lengths):
    part = projection.shape[1] // lax.axis_size("groups")
    if lax.axis_size("dp") == 8 and part % HEAD == 0:
        return staged(hidden_in, norm_gain, projection, lengths)
    return general(hidden_in, norm_gain, projection, lengths)


def solution(mesh):
    in_specs = (
        P(("groups", "dp"), "tensor"),
        P("tensor"),
        P("tensor", "dp", None),
        P(("groups", "dp"), None),
    )
    out_specs = P(("groups", "dp"), "tensor")
    return jax.shard_map(local, mesh=mesh, in_specs=in_specs, out_specs=out_specs, check_vma=False)
```

time: 78.9 us -> 74 us (0.938)
  local copies, waits for them, and re-layouts: 2.74 us -> 0.01 us
  starting transfers between devices: 21.1 us -> 19.6 us
  other arithmetic: 0.88 us -> 0.08 us
    ppermute x9, waiting for transfers between devices: 10.6 us -> 5.8 us  [the longest x3 4.18 us: to_y(): return lax.ppermute(a, 'groups', over_y)]
    unnamed x6 -> x2, local copies, waits for them, and re-layouts: 2.6 us -> 0.01 us
    pallas_call x7 -> x12, Pallas kernels: 10.4 us -> 12.4 us  [the longest x4 4.95 us: matmul(): call(functools.partial(matmul_kernel, firsts, len(acts), len(so_far), sen...]
    ppermute x4, waiting for transfers between devices: 17.9 us -> 19.8 us  [on_ring(): return lax.ppermute(a, 'dp', ring)]
    ppermute x2, waiting for transfers between devices: 7.95 us -> 9.78 us  [back(): return lax.ppermute(a, 'dp', [(j, i) for i, j in ring])]
    pallas_call x2, Pallas kernels: 3.47 us -> 2.25 us  [heads(): call(functools.partial(heads_kernel, first, len(parts)), jax.ShapeDtypeSt...]
    ppermute x4, starting transfers between devices: 4.78 us -> 3.65 us  [on_ring(): return lax.ppermute(a, 'dp', ring)]
    ppermute x8, waiting for transfers between devices: 2.73 us -> 3.76 us  [to_core(): return lax.ppermute(a, 'tensor', over_core)]
  transfers between devices with their start and end apart: 23 -> 23, of which waited for: 17 -> 13; matrix products, arithmetic and copies ran while one was open for 1% -> 0% of each run, Pallas kernels for 13% -> 16%
where the time goes in v3:
time: 74 us; the launch traced here: 73.8 us
  waiting for transfers between devices  39.1 us (53%)
  starting transfers between devices  19.6 us (26%)
  Pallas kernels  14.8 us (20%)
    ppermute x4, waiting for transfers between devices, on_ring(): return lax.ppermute(a, 'dp', ring)  19.8 us
    ppermute x2, waiting for transfers between devices, back(): return lax.ppermute(a, 'dp', [(j, i) for i, j in ring])  9.78 us
    ppermute x3, starting transfers between devices, to_far(): return lax.ppermute(a, ('groups', 'dp'), across)  5.17 us
    pallas_call x4, Pallas kernels, matmul(): call(functools.partial(matmul_kernel, firsts, len(acts), len(so_far), sen...  4.95 us
    ppermute x3, waiting for transfers between devices, to_y(): return lax.ppermute(a, 'groups', over_y)  4.18 us
    ppermute x2, starting transfers between devices, back(): return lax.ppermute(a, 'dp', [(j, i) for i, j in ring])  4.11 us
    pallas_call x1, Pallas kernels, gate(): call(functools.partial(gate_kernel, part, depth, plane, squares), out_sha...  3.96 us
    ppermute x8, waiting for transfers between devices, to_core(): return lax.ppermute(a, 'tensor', over_core)  3.76 us
  transfers between devices with their start and end apart: 23, of which 13 were waited for; matrix products, arithmetic and copies ran while one was open for 0% of the time, Pallas kernels for 16%

profile of v3, /device:TPU:0, one launch (start us, length us, event | category | flops | bytes accessed | tf_op | source)
XLA Modules:
  0.0 73.8 jit_solution(8149904287315718683)
XLA Ops:
  0.0 1.1 %shard_map.46.refs_2_ = bf16[384,512]{1,0:T(8,128)(2,1)S(1)} custom-call(bf16[1,768,1024]{2,1,0:T(8,128)(2,1)} %rows_ref.2), custom_call_target="tpu_custom_call" | custom-call | flops 1 | bytes 1 | tf_op jit(solution)/shard_map/pallas_call | solution.py:187
  1.1 3.1 %collective-permute-start.1 = (bf16[384,512]{1,0:T(8,128)(2,1)S(1)}, bf16[384,512]{1,0:T(8,128)(2,1)S(1)}, u32[]{:S(2)}, u32[]{:S(2)}) collective-permute-start(bf16[384,512]{1,0:T(8,128)(2,1)S(1)} %shard_map.46.refs_2_), channel_id=1, source_target_pairs={{0,4},{2,6},{4,8},{6,10},{8,12},{10,14},{12,0},{14,2},{1,5},{3,7},... | collective-permute-start | bytes 1179656 | tf_op jit(solution)/shard_map/ppermute | solution.py:441
  4.3 4.0 %shard_map.47 = (bf16[4,256,384]{2,1,0:T(8,128)(2,1)S(1)}, bf16[4,256,384]{2,1,0:T(8,128)(2,1)S(1)}, bf16[4,256,384]{2,1,0:T(8,128)(2,1)S(1)}, bf16[4,256,384]{2,1,0:T(8,128)(2,1)S(1)}, f32[256,128]{1,0:T(8,128)S(1)}) custom-call(s32[4]{0:T(128)S(1)} %pad_add_fusion.place_ref, bf16[256,6144]{1,0:T(8,128)(2,1)} %hidden_ref, bf16[6144]{0:T(1024)(128)(2,1)} %gain_ref.1), custom_call_target="tpu_custom_call" | custom-call | flops 1 | bytes 1 | tf_op jit(solution)/shard_map/pallas_call | solution.py:239
  8.2 2.5 %collective-permute-start = (bf16[4,256,384]{2,1,0:T(8,128)(2,1)S(1)}, bf16[4,256,384]{2,1,0:T(8,128)(2,1)S(1)}, u32[]{:S(2)}, u32[]{:S(2)}) collective-permute-start(bf16[4,256,384]{2,1,0:T(8,128)(2,1)S(1)} %get-tuple-element.97), channel_id=1, source_target_pairs={{0,18},{2,16},{4,22},{6,20},{8,26},{10,24},{12,30},{14,28},{16,2},... | collective-permute-start | bytes 2359304 | tf_op jit(solution)/shard_map/ppermute | solution.py:447
  10.7 2.2 %collective-permute-start.3 = (bf16[384,512]{1,0:T(8,128)(2,1)S(1)}, bf16[384,512]{1,0:T(8,128)(2,1)S(1)}, u32[]{:S(2)}, u32[]{:S(2)}) collective-permute-start(bf16[384,512]{1,0:T(8,128)(2,1)S(1)} %shard_map.46.refs_2_), channel_id=1, source_target_pairs={{4,0},{6,2},{8,4},{10,6},{12,8},{14,10},{0,12},{2,14},{5,1},{7,3},... | collective-permute-start | bytes 1179656 | tf_op jit(solution)/shard_map/ppermute | solution.py:444
  13.0 0.5 collective-permute-start.4
  13.8 1.1 %shard_map.48 = (f32[256,128]{1,0:T(8,128)S(1)}, f32[256,128]{1,0:T(8,128)S(1)}, f32[256,256]{1,0:T(8,128)S(1)}, f32[256,128]{1,0:T(8,128)S(1)}) custom-call(s32[1,2]{1,0:T(1,128)S(1)} %copy-done, f32[256,128]{1,0:T(8,128)S(1)} %get-tuple-element.133._.own_ref), custom_call_target="tpu_custom_call" | custom-call | flops 1 | bytes 1 | tf_op jit(solution)/shard_map/pallas_call | solution.py:340
  14.9 1.0 %collective-permute-done.1.refs_3_ = bf16[384,512]{1,0:T(8,128)(2,1)S(1)} collective-permute-done((bf16[384,512]{1,0:T(8,128)(2,1)S(1)}, bf16[384,512]{1,0:T(8,128)(2,1)S(1)}, u32[]{:S(2)}, u32[]{:S(2)}) %collective-permute-start.1) | collective-permute-done | bytes 393248 | tf_op jit(solution)/shard_map/ppermute | solution.py:441
  15.9 1.1 %shard_map.49.refs_4_ = bf16[384,512]{1,0:T(8,128)(2,1)S(1)} custom-call(bf16[1,768,1024]{2,1,0:T(8,128)(2,1)} %rows_ref.2), custom_call_target="tpu_custom_call" | custom-call | flops 1 | bytes 1 | tf_op jit(solution)/shard_map/pallas_call | solution.py:187
  17.0 7.8 %collective-permute-done.3.refs_5_ = bf16[384,512]{1,0:T(8,128)(2,1)S(1)} collective-permute-done((bf16[384,512]{1,0:T(8,128)(2,1)S(1)}, bf16[384,512]{1,0:T(8,128)(2,1)S(1)}, u32[]{:S(2)}, u32[]{:S(2)}) %collective-permute-start.3) | collective-permute-done | bytes 393248 | tf_op jit(solution)/shard_map/ppermute | solution.py:444
  24.8 0.6 collective-permute-start.8
  25.4 9.0 %collective-permute-done.2.refs_4_ = bf16[384,512]{1,0:T(8,128)(2,1)S(1)} collective-permute-done((bf16[384,512]{1,0:T(8,128)(2,1)S(1)}, bf16[384,512]{1,0:T(8,128)(2,1)S(1)}, u32[]{:S(2)}, u32[]{:S(2)}) %collective-permute-start.2) | collective-permute-done | bytes 393248 | tf_op jit(solution)/shard_map/ppermute | solution.py:441
  34.3 1.9 %collective-permute-start.10 = (bf16[384,512]{1,0:T(8,128)(2,1)S(1)}, bf16[384,512]{1,0:T(8,128)(2,1)S(1)}, u32[]{:S(2)}, u32[]{:S(2)}) collective-permute-start(bf16[384,512]{1,0:T(8,128)(2,1)S(1)} %shard_map.49.refs_4_), channel_id=1, source_target_pairs={{4,0},{6,2},{8,4},{10,6},{12,8},{14,10},{0,12},{2,14},{5,1},{7,3},... | collective-permute-start | bytes 1179656 | tf_op jit(solution)/shard_map/ppermute | solution.py:444
  36.2 1.2 %shard_map.50 = (bf16[2,256,128]{2,1,0:T(8,128)(2,1)S(1)}, bf16[2,256,128]{2,1,0:T(8,128)(2,1)S(1)}, f32[2,2,256,128]{3,2,1,0:T(8,128)S(1)}) custom-call(bf16[4,256,384]{2,1,0:T(8,128)(2,1)S(1)} %collective-permute-done.refs_0_, bf16[4,256,384]{2,1,0:T(8,128)(2,1)S(1)} %get-tuple-element.111.refs_1_, bf16[384,512]{1,0:T(8,128)(2,1)S(1)} %shard_map.46.refs_2_, ...), custom_call_target="tpu_custom_call" | custom-call | flops 1 | bytes 1 | tf_op jit(solution)/shard_map/pallas_call | solution.py:293
  37.5 5.1 %collective-permute-done.8.refs_5_ = bf16[384,512]{1,0:T(8,128)(2,1)S(1)} collective-permute-done((bf16[384,512]{1,0:T(8,128)(2,1)S(1)}, bf16[384,512]{1,0:T(8,128)(2,1)S(1)}, u32[]{:S(2)}, u32[]{:S(2)}) %collective-permute-start.8) | collective-permute-done | bytes 393248 | tf_op jit(solution)/shard_map/ppermute | solution.py:441
  42.7 1.3 %collective-permute-done.6.refs_0_ = bf16[2,256,128]{2,1,0:T(8,128)(2,1)S(1)} collective-permute-done((bf16[2,256,128]{2,1,0:T(8,128)(2,1)S(1)}, bf16[2,256,128]{2,1,0:T(8,128)(2,1)S(1)}, u32[]{:S(2)}, u32[]{:S(2)}) %collective-permute-start.6) | collective-permute-done | bytes 131104 | tf_op jit(solution)/shard_map/ppermute | solution.py:438
  44.0 1.1 %collective-permute-done.4.refs_0_.refs_2_ = bf16[4,256,384]{2,1,0:T(8,128)(2,1)S(1)} collective-permute-done((bf16[4,256,384]{2,1,0:T(8,128)(2,1)S(1)}, bf16[4,256,384]{2,1,0:T(8,128)(2,1)S(1)}, u32[]{:S(2)}, u32[]{:S(2)}) %collective-permute-start.4) | collective-permute-done | bytes 786464 | tf_op jit(solution)/shard_map/ppermute | solution.py:450
  45.1 1.2 %shard_map.52 = (bf16[2,256,128]{2,1,0:T(8,128)(2,1)S(1)}, bf16[2,256,128]{2,1,0:T(8,128)(2,1)S(1)}, f32[2,2,256,128]{3,2,1,0:T(8,128)S(1)}) custom-call(bf16[4,256,384]{2,1,0:T(8,128)(2,1)S(1)} %collective-permute-done.4.refs_0_.refs_2_, bf16[4,256,384]{2,1,0:T(8,128)(2,1)S(1)} %collective-permute-done.5.refs_1_.refs_3_, ...), custom_call_target="tpu_custom_call" | custom-call | flops 1 | bytes 1 | tf_op jit(solution)/shard_map/pallas_call | solution.py:293
  47.0 2.0 %collective-permute-done.10.refs_6_ = bf16[384,512]{1,0:T(8,128)(2,1)S(1)} collective-permute-done((bf16[384,512]{1,0:T(8,128)(2,1)S(1)}, bf16[384,512]{1,0:T(8,128)(2,1)S(1)}, u32[]{:S(2)}, u32[]{:S(2)}) %collective-permute-start.10) | collective-permute-done | bytes 393248 | tf_op jit(solution)/shard_map/ppermute | solution.py:444
  49.0 2.5 %collective-permute-start.14 = (bf16[2,256,128]{2,1,0:T(8,128)(2,1)S(1)}, bf16[2,256,128]{2,1,0:T(8,128)(2,1)S(1)}, u32[]{:S(2)}, u32[]{:S(2)}) collective-permute-start(bf16[2,256,128]{2,1,0:T(8,128)(2,1)S(1)} %get-tuple-element.125), channel_id=1, source_target_pairs={{0,18},{2,16},{4,22},{6,20},{8,26},{10,24},{12,30},{14,28},{16,2},... | collective-permute-start | bytes 393224 | tf_op jit(solution)/shard_map/ppermute | solution.py:447
  51.6 0.5 collective-permute-start.16
  52.1 0.6 collective-permute-start.15
  52.7 1.8 %shard_map.53.refs_5_ = f32[4,256,512]{2,1,0:T(8,128)S(1)} custom-call(bf16[4,256,384]{2,1,0:T(8,128)(2,1)S(1)} %collective-permute-done.refs_0_, bf16[4,256,384]{2,1,0:T(8,128)(2,1)S(1)} %get-tuple-element.111.refs_1_, bf16[4,256,384]{2,1,0:T(8,128)(2,1)S(1)} %collective-permute-done.4.refs_0_.refs_2_, ...), custom_call_target="tpu_custom_call" | custom-call | flops 1 | bytes 1 | tf_op jit(solution)/shard_map/pallas_call | solution.py:293
  54.4 4.7 %collective-permute-done.9.refs_4_ = bf16[384,512]{1,0:T(8,128)(2,1)S(1)} collective-permute-done((bf16[384,512]{1,0:T(8,128)(2,1)S(1)}, bf16[384,512]{1,0:T(8,128)(2,1)S(1)}, u32[]{:S(2)}, u32[]{:S(2)}) %collective-permute-start.9) | collective-permute-done | bytes 393248 | tf_op jit(solution)/shard_map/ppermute | solution.py:441
  59.2 0.7 shard_map.55
  60.7 0.8 %collective-permute-done.18.refs_1_ = bf16[4,256,128]{2,1,0:T(8,128)(2,1)S(1)} collective-permute-done((bf16[4,256,128]{2,1,0:T(8,128)(2,1)S(1)}, bf16[4,256,128]{2,1,0:T(8,128)(2,1)S(1)}, u32[]{:S(2)}, u32[]{:S(2)}) %collective-permute-start.18) | collective-permute-done | bytes 262176 | tf_op jit(solution)/shard_map/ppermute | solution.py:438
  62.0 2.1 %collective-permute-start.20 = (bf16[2,256,128]{2,1,0:T(8,128)(2,1)S(1)}, bf16[2,256,128]{2,1,0:T(8,128)(2,1)S(1)}, u32[]{:S(2)}, u32[]{:S(2)}) collective-permute-start(bf16[2,256,128]{2,1,0:T(8,128)(2,1)S(1)} %get-tuple-element.167), channel_id=1, source_target_pairs={{0,2},{2,0},{4,6},{6,4},{8,10},{10,8},{12,14},{14,12},{1,3},{3,1},... | collective-permute-start | bytes 393224 | tf_op jit(solution)/shard_map/ppermute | solution.py:450
  64.1 1.3 %collective-permute-start.21 = (bf16[2,256,128]{2,1,0:T(8,128)(2,1)S(1)}, bf16[2,256,128]{2,1,0:T(8,128)(2,1)S(1)}, u32[]{:S(2)}, u32[]{:S(2)}) collective-permute-start(bf16[2,256,128]{2,1,0:T(8,128)(2,1)S(1)} %get-tuple-element.168), channel_id=1, source_target_pairs={{0,16},{16,0},{1,17},{17,1},{2,18},{18,2},{3,19},{19,3},{4,20},{20... | collective-permute-start | bytes 393224 | tf_op jit(solution)/shard_map/ppermute | solution.py:453
  65.6 1.3 %collective-permute-done.22.refs_10_ = bf16[256,128]{1,0:T(8,128)(2,1)S(1)} collective-permute-done((bf16[256,128]{1,0:T(8,128)(2,1)S(1)}, bf16[256,128]{1,0:T(8,128)(2,1)S(1)}, u32[]{:S(2)}, u32[]{:S(2)}) %collective-permute-start.22) | collective-permute-done | bytes 65568 | tf_op jit(solution)/shard_map/ppermute | solution.py:438
  66.9 0.6 shard_map.59.refs_11_
  68.0 4.2 %collective-permute-done.21.refs_3_ = bf16[2,256,128]{2,1,0:T(8,128)(2,1)S(1)} collective-permute-done((bf16[2,256,128]{2,1,0:T(8,128)(2,1)S(1)}, bf16[2,256,128]{2,1,0:T(8,128)(2,1)S(1)}, u32[]{:S(2)}, u32[]{:S(2)}) %collective-permute-start.21) | collective-permute-done | bytes 131104 | tf_op jit(solution)/shard_map/ppermute | solution.py:453
  72.1 1.7 %shard_map.60 = bf16[256,384]{1,0:T(8,128)(2,1)} custom-call(f32[2,256,128]{2,1,0:T(8,128)S(1)} %get-tuple-element.173.refs_0_, bf16[2,256,128]{2,1,0:T(8,128)(2,1)S(1)} %collective-permute-done.19.refs_1_, bf16[2,256,128]{2,1,0:T(8,128)(2,1)S(1)} %collective-permute-done.20.refs_2_, bf16[2,256,128]{2,1,0:T(8,128)(2,1)S(1)} %collective-permute-done.21.refs_3_, ...), custom_call_target="tpu_custom_call" | custom-call | flops 1 | bytes 1 | tf_op jit(solution)/shard_map/pallas_call | solution.py:409
  (32 shorter events, 3.2 us)
Async XLA Ops:
  1.1 12.8 %copy-start = (s32[1,2]{1,0:T(1,128)S(1)}, s32[1,2]{1,0:T(1,128)}, u32[]{:S(2)}) copy-start(s32[1,2]{1,0:T(1,128)} %lengths_ref.1) | copy-start | bytes 28
  1.1 14.8 %collective-permute-start.1 = (bf16[384,512]{1,0:T(8,128)(2,1)S(1)}, bf16[384,512]{1,0:T(8,128)(2,1)S(1)}, u32[]{:S(2)}, u32[]{:S(2)}) collective-permute-start(bf16[384,512]{1,0:T(8,128)(2,1)S(1)} %shard_map.46.refs_2_), channel_id=1, source_target_pairs={{0,4},{2,6},{4,8},{6,10},{8,12},{10,14},{12,0},{14,2},{1,5},{3,7},... | collective-permute-start | bytes 1179656 | tf_op jit(solution)/shard_map/ppermute | solution.py:441
  8.2 28.0 %collective-permute-start = (bf16[4,256,384]{2,1,0:T(8,128)(2,1)S(1)}, bf16[4,256,384]{2,1,0:T(8,128)(2,1)S(1)}, u32[]{:S(2)}, u32[]{:S(2)}) collective-permute-start(bf16[4,256,384]{2,1,0:T(8,128)(2,1)S(1)} %get-tuple-element.97), channel_id=1, source_target_pairs={{0,18},{2,16},{4,22},{6,20},{8,26},{10,24},{12,30},{14,28},{16,2},... | collective-permute-start | bytes 2359304 | tf_op jit(solution)/shard_map/ppermute | solution.py:447
  10.7 14.1 %collective-permute-start.3 = (bf16[384,512]{1,0:T(8,128)(2,1)S(1)}, bf16[384,512]{1,0:T(8,128)(2,1)S(1)}, u32[]{:S(2)}, u32[]{:S(2)}) collective-permute-start(bf16[384,512]{1,0:T(8,128)(2,1)S(1)} %shard_map.46.refs_2_), channel_id=1, source_target_pairs={{4,0},{6,2},{8,4},{10,6},{12,8},{14,10},{0,12},{2,14},{5,1},{7,3},... | collective-permute-start | bytes 1179656 | tf_op jit(solution)/shard_map/ppermute | solution.py:444
  13.0 32.2 %collective-permute-start.4 = (bf16[4,256,384]{2,1,0:T(8,128)(2,1)S(1)}, bf16[4,256,384]{2,1,0:T(8,128)(2,1)S(1)}, u32[]{:S(2)}, u32[]{:S(2)}) collective-permute-start(bf16[4,256,384]{2,1,0:T(8,128)(2,1)S(1)} %get-tuple-element.112), channel_id=1, source_target_pairs={{0,2},{2,0},{4,6},{6,4},{8,10},{10,8},{12,14},{14,12},{1,3},{3,1},... | collective-permute-start | bytes 2359304 | tf_op jit(solution)/shard_map/ppermute | solution.py:450
  13.5 31.6 %collective-permute-start.5 = (bf16[4,256,384]{2,1,0:T(8,128)(2,1)S(1)}, bf16[4,256,384]{2,1,0:T(8,128)(2,1)S(1)}, u32[]{:S(2)}, u32[]{:S(2)}) collective-permute-start(bf16[4,256,384]{2,1,0:T(8,128)(2,1)S(1)} %get-tuple-element.113), channel_id=1, source_target_pairs={{0,16},{16,0},{1,17},{17,1},{2,18},{18,2},{3,19},{19,3},{4,20},{20... | collective-permute-start | bytes 2359304 | tf_op jit(solution)/shard_map/ppermute | solution.py:453
  15.9 18.4 %collective-permute-start.2 = (bf16[384,512]{1,0:T(8,128)(2,1)S(1)}, bf16[384,512]{1,0:T(8,128)(2,1)S(1)}, u32[]{:S(2)}, u32[]{:S(2)}) collective-permute-start(bf16[384,512]{1,0:T(8,128)(2,1)S(1)} %collective-permute-done.1.refs_3_), channel_id=1, source_target_pairs={{0,4},{2,6},{4,8},{6,10},{8,12},{10,14},{12,0},{14,2},{1,5},{3,7},... | collective-permute-start | bytes 1179656 | tf_op jit(solution)/shard_map/ppermute | solution.py:441
  24.8 17.8 %collective-permute-start.8 = (bf16[384,512]{1,0:T(8,128)(2,1)S(1)}, bf16[384,512]{1,0:T(8,128)(2,1)S(1)}, u32[]{:S(2)}, u32[]{:S(2)}) collective-permute-start(bf16[384,512]{1,0:T(8,128)(2,1)S(1)} %shard_map.49.refs_4_), channel_id=1, source_target_pairs={{0,4},{2,6},{4,8},{6,10},{8,12},{10,14},{12,0},{14,2},{1,5},{3,7},... | collective-permute-start | bytes 1179656 | tf_op jit(solution)/shard_map/ppermute | solution.py:441
  34.3 14.7 %collective-permute-start.10 = (bf16[384,512]{1,0:T(8,128)(2,1)S(1)}, bf16[384,512]{1,0:T(8,128)(2,1)S(1)}, u32[]{:S(2)}, u32[]{:S(2)}) collective-permute-start(bf16[384,512]{1,0:T(8,128)(2,1)S(1)} %shard_map.49.refs_4_), channel_id=1, source_target_pairs={{4,0},{6,2},{8,4},{10,6},{12,8},{14,10},{0,12},{2,14},{5,1},{7,3},... | collective-permute-start | bytes 1179656 | tf_op jit(solution)/shard_map/ppermute | solution.py:444
  37.4 5.2 %collective-permute-start.7 = (bf16[2,256,128]{2,1,0:T(8,128)(2,1)S(1)}, bf16[2,256,128]{2,1,0:T(8,128)(2,1)S(1)}, u32[]{:S(2)}, u32[]{:S(2)}) collective-permute-start(bf16[2,256,128]{2,1,0:T(8,128)(2,1)S(1)} %get-tuple-element.119), channel_id=1, source_target_pairs={{0,1},{1,0},{2,3},{3,2},{4,5},{5,4},{6,7},{7,6},{8,9},{9,8},{10,11... | collective-permute-start | bytes 393224 | tf_op jit(solution)/shard_map/ppermute | solution.py:438
  42.6 1.3 %collective-permute-start.6 = (bf16[2,256,128]{2,1,0:T(8,128)(2,1)S(1)}, bf16[2,256,128]{2,1,0:T(8,128)(2,1)S(1)}, u32[]{:S(2)}, u32[]{:S(2)}) collective-permute-start(bf16[2,256,128]{2,1,0:T(8,128)(2,1)S(1)} %get-tuple-element.118), channel_id=1, source_target_pairs={{0,1},{1,0},{2,3},{3,2},{4,5},{5,4},{6,7},{7,6},{8,9},{9,8},{10,11... | collective-permute-start | bytes 393224 | tf_op jit(solution)/shard_map/ppermute | solution.py:438
  42.6 16.5 %collective-permute-start.9 = (bf16[384,512]{1,0:T(8,128)(2,1)S(1)}, bf16[384,512]{1,0:T(8,128)(2,1)S(1)}, u32[]{:S(2)}, u32[]{:S(2)}) collective-permute-start(bf16[384,512]{1,0:T(8,128)(2,1)S(1)} %collective-permute-done.8.refs_5_), channel_id=1, source_target_pairs={{0,4},{2,6},{4,8},{6,10},{8,12},{10,14},{12,0},{14,2},{1,5},{3,7},... | collective-permute-start | bytes 1179656 | tf_op jit(solution)/shard_map/ppermute | solution.py:441
  46.4 5.1 %collective-permute-start.13 = (f32[256,128]{1,0:T(8,128)S(1)}, f32[256,128]{1,0:T(8,128)S(1)}, u32[]{:S(2)}, u32[]{:S(2)}) collective-permute-start(f32[256,128]{1,0:T(8,128)S(1)} %get-tuple-element.133._.own_ref), channel_id=1, source_target_pairs={{0,1},{1,0},{2,3},{3,2},{4,5},{5,4},{6,7},{7,6},{8,9},{9,8},{10,11... | collective-permute-start | bytes 393224 | tf_op jit(solution)/shard_map/ppermute | solution.py:438
  46.5 5.1 %collective-permute-start.12 = (bf16[2,256,128]{2,1,0:T(8,128)(2,1)S(1)}, bf16[2,256,128]{2,1,0:T(8,128)(2,1)S(1)}, u32[]{:S(2)}, u32[]{:S(2)}) collective-permute-start(bf16[2,256,128]{2,1,0:T(8,128)(2,1)S(1)} %get-tuple-element.136), channel_id=1, source_target_pairs={{0,1},{1,0},{2,3},{3,2},{4,5},{5,4},{6,7},{7,6},{8,9},{9,8},{10,11... | collective-permute-start | bytes 393224 | tf_op jit(solution)/shard_map/ppermute | solution.py:438
  47.0 4.6 %collective-permute-start.11 = (bf16[2,256,128]{2,1,0:T(8,128)(2,1)S(1)}, bf16[2,256,128]{2,1,0:T(8,128)(2,1)S(1)}, u32[]{:S(2)}, u32[]{:S(2)}) collective-permute-start(bf16[2,256,128]{2,1,0:T(8,128)(2,1)S(1)} %get-tuple-element.132), channel_id=1, source_target_pairs={{0,1},{1,0},{2,3},{3,2},{4,5},{5,4},{6,7},{7,6},{8,9},{9,8},{10,11... | collective-permute-start | bytes 393224 | tf_op jit(solution)/shard_map/ppermute | solution.py:438
  49.0 10.8 %collective-permute-start.14 = (bf16[2,256,128]{2,1,0:T(8,128)(2,1)S(1)}, bf16[2,256,128]{2,1,0:T(8,128)(2,1)S(1)}, u32[]{:S(2)}, u32[]{:S(2)}) collective-permute-start(bf16[2,256,128]{2,1,0:T(8,128)(2,1)S(1)} %get-tuple-element.125), channel_id=1, source_target_pairs={{0,18},{2,16},{4,22},{6,20},{8,26},{10,24},{12,30},{14,28},{16,2},... | collective-permute-start | bytes 393224 | tf_op jit(solution)/shard_map/ppermute | solution.py:447
  51.6 8.3 %collective-permute-start.16 = (bf16[2,256,128]{2,1,0:T(8,128)(2,1)S(1)}, bf16[2,256,128]{2,1,0:T(8,128)(2,1)S(1)}, u32[]{:S(2)}, u32[]{:S(2)}) collective-permute-start(bf16[2,256,128]{2,1,0:T(8,128)(2,1)S(1)} %get-tuple-element.148), channel_id=1, source_target_pairs={{0,16},{16,0},{1,17},{17,1},{2,18},{18,2},{3,19},{19,3},{4,20},{20... | collective-permute-start | bytes 393224 | tf_op jit(solution)/shard_map/ppermute | solution.py:453
  52.1 7.8 %collective-permute-start.15 = (bf16[2,256,128]{2,1,0:T(8,128)(2,1)S(1)}, bf16[2,256,128]{2,1,0:T(8,128)(2,1)S(1)}, u32[]{:S(2)}, u32[]{:S(2)}) collective-permute-start(bf16[2,256,128]{2,1,0:T(8,128)(2,1)S(1)} %get-tuple-element.141), channel_id=1, source_target_pairs={{0,2},{2,0},{4,6},{6,4},{8,10},{10,8},{12,14},{14,12},{1,3},{3,1},... | collective-permute-start | bytes 393224 | tf_op jit(solution)/shard_map/ppermute | solution.py:450
  59.9 1.6 %collective-permute-start.18 = (bf16[4,256,128]{2,1,0:T(8,128)(2,1)S(1)}, bf16[4,256,128]{2,1,0:T(8,128)(2,1)S(1)}, u32[]{:S(2)}, u32[]{:S(2)}) collective-permute-start(bf16[4,256,128]{2,1,0:T(8,128)(2,1)S(1)} %get-tuple-element.152), channel_id=1, source_target_pairs={{0,1},{1,0},{2,3},{3,2},{4,5},{5,4},{6,7},{7,6},{8,9},{9,8},{10,11... | collective-permute-start | bytes 786440 | tf_op jit(solution)/shard_map/ppermute | solution.py:438
  60.0 1.9 %collective-permute-start.17 = (bf16[4,256,128]{2,1,0:T(8,128)(2,1)S(1)}, bf16[4,256,128]{2,1,0:T(8,128)(2,1)S(1)}, u32[]{:S(2)}, u32[]{:S(2)}) collective-permute-start(bf16[4,256,128]{2,1,0:T(8,128)(2,1)S(1)} %get-tuple-element.151), channel_id=1, source_target_pairs={{0,1},{1,0},{2,3},{3,2},{4,5},{5,4},{6,7},{7,6},{8,9},{9,8},{10,11... | collective-permute-start | bytes 786440 | tf_op jit(solution)/shard_map/ppermute | solution.py:438
  62.0 6.0 %collective-permute-start.20 = (bf16[2,256,128]{2,1,0:T(8,128)(2,1)S(1)}, bf16[2,256,128]{2,1,0:T(8,128)(2,1)S(1)}, u32[]{:S(2)}, u32[]{:S(2)}) collective-permute-start(bf16[2,256,128]{2,1,0:T(8,128)(2,1)S(1)} %get-tuple-element.167), channel_id=1, source_target_pairs={{0,2},{2,0},{4,6},{6,4},{8,10},{10,8},{12,14},{14,12},{1,3},{3,1},... | collective-permute-start | bytes 393224 | tf_op jit(solution)/shard_map/ppermute | solution.py:450
  64.1 8.1 %collective-permute-start.21 = (bf16[2,256,128]{2,1,0:T(8,128)(2,1)S(1)}, bf16[2,256,128]{2,1,0:T(8,128)(2,1)S(1)}, u32[]{:S(2)}, u32[]{:S(2)}) collective-permute-start(bf16[2,256,128]{2,1,0:T(8,128)(2,1)S(1)} %get-tuple-element.168), channel_id=1, source_target_pairs={{0,16},{16,0},{1,17},{17,1},{2,18},{18,2},{3,19},{19,3},{4,20},{20... | collective-permute-start | bytes 393224 | tf_op jit(solution)/shard_map/ppermute | solution.py:453
  65.4 6.7 %collective-permute-start.19 = (bf16[2,256,128]{2,1,0:T(8,128)(2,1)S(1)}, bf16[2,256,128]{2,1,0:T(8,128)(2,1)S(1)}, u32[]{:S(2)}, u32[]{:S(2)}) collective-permute-start(bf16[2,256,128]{2,1,0:T(8,128)(2,1)S(1)} %get-tuple-element.166), channel_id=1, source_target_pairs={{0,18},{2,16},{4,22},{6,20},{8,26},{10,24},{12,30},{14,28},{16,2},... | collective-permute-start | bytes 393224 | tf_op jit(solution)/shard_map/ppermute | solution.py:447
  65.6 1.3 %collective-permute-start.22 = (bf16[256,128]{1,0:T(8,128)(2,1)S(1)}, bf16[256,128]{1,0:T(8,128)(2,1)S(1)}, u32[]{:S(2)}, u32[]{:S(2)}) collective-permute-start(bf16[256,128]{1,0:T(8,128)(2,1)S(1)} %shard_map.57.refs_9_), channel_id=1, source_target_pairs={{0,1},{1,0},{2,3},{3,2},{4,5},{5,4},{6,7},{7,6},{8,9},{9,8},{10,11... | collective-permute-start | bytes 196616 | tf_op jit(solution)/shard_map/ppermute | solution.py:438

commit v4 on v3

--- a/solution.py
+++ b/solution.py
@@ -193,63 +193,49 @@
     )(pltpu.with_memory_space_constraint(projection, pltpu.HBM))
 
 
-def gate_kernel(part, depth, plane, squares, place_ref, hidden_ref, gain_ref, *refs):
-    piece_refs, row_ref = refs[:len(plane)], refs[-1]
-    x, y = place_ref[1], place_ref[2]
-    base = lax.rem(place_ref[0] - pl.program_id(0) + depth, depth) * 4 * part
-
-    @pl.when(pl.program_id(0) == 0)
-    def _():
-        row_ref[0, :] = gain_ref[...].astype(jnp.float32)
-
-    for piece_ref, (dx, dy) in zip(piece_refs, plane):
-        start = pl.multiple_of(((x ^ dx) * 2 + (y ^ dy)) * part, HEAD)
-        wide = hidden_ref[:, pl.ds(start, part)].astype(jnp.float32)
-        gain = row_ref[:, pl.ds(pl.multiple_of(base + start, HEAD), part)]
-        piece_ref[0] = (wide * gain).astype(jnp.bfloat16)
-    if not squares:
-        return
-    sq_ref = refs[len(plane)]
-    total = jnp.zeros(sq_ref.shape, jnp.float32)
-    for j in range(0, hidden_ref.shape[1], HEAD):
-        wide = hidden_ref[:, j:j + HEAD].astype(jnp.float32)
-        total += wide * wide
-
-    @pl.when(pl.program_id(0) == 0)
-    def _():
-        sq_ref[...] = total
-
-    @pl.when(pl.program_id(0) > 0)
-    def _():
-        sq_ref[...] += total
-
-
-def gate(place, hidden_in, norm_gain, part, depth, plane=PLANE, squares=True):
+def gate_kernel(part, depth, hidden_ref, gain_ref, *refs):
+    piece_refs, (sq_ref, slab_ref, row_ref, sems) = refs[:4], refs[4:]
+    place = lax.axis_index("dp")
+    x, z, y = place % 2, place // 2, lax.axis_index("groups")
+    wide = 4 * part
+    columns = [pl.ds(pl.multiple_of(lax.rem(z - k + depth, depth) * wide, HEAD), wide) for k in range(depth)]
+    copies = [pltpu.make_async_copy(hidden_ref.at[:, c], slab_ref.at[k], sems.at[k]) for k, c in enumerate(columns)]
+    for copy in copies:
+        copy.start()
+    row_ref[0, :] = gain_ref[...].astype(jnp.float32)
+    tokens = hidden_ref.shape[0]
+    height = 64
+    for k, copy in enumerate(copies):
+        copy.wait()
+        for top in range(0, tokens, height):
+            rows = slice(top, top + height)
+            total = jnp.zeros((height, HEAD), jnp.float32)
+            for piece_ref, (dx, dy) in zip(piece_refs, PLANE):
+                start = ((x ^ dx) * 2 + (y ^ dy)) * part
+                whole = slab_ref[k, rows, pl.ds(pl.multiple_of(start, HEAD), part)].astype(jnp.float32)
+                at = lax.rem(z - k + depth, depth) * wide + start
+                gain = row_ref[:, pl.ds(pl.multiple_of(at, HEAD), part)]
+                piece_ref[k, rows] = (whole * gain).astype(jnp.bfloat16)
+                square = whole * whole
+                for j in range(0, part, HEAD):
+                    total += square[:, j:j + HEAD]
+            sq_ref[rows] = total if k == 0 else sq_ref[rows] + total
+
+
+def gate(hidden_in, norm_gain, part, depth):
     tokens = hidden_in.shape[0]
-    wide = 4 * part
-    out_shape = (jax.ShapeDtypeStruct((depth, tokens, part), jnp.bfloat16),) * len(plane)
-    out_specs = [pl.BlockSpec((1, tokens, part), lambda k, place: (k, 0, 0))] * len(plane)
-    if squares:
-        out_shape += (jax.ShapeDtypeStruct((tokens, HEAD), jnp.float32),)
-        out_specs.append(pl.BlockSpec((tokens, HEAD), lambda k, place: (0, 0)))
-
-    def shard(k, place):
-        return (0, lax.rem(place[0] - k + depth, depth))
-
+    piece = jax.ShapeDtypeStruct((depth, tokens, part), jnp.bfloat16)
     return call(
-        functools.partial(gate_kernel, part, depth, plane, squares),
-        out_shape,
-        grid_spec=pltpu.PrefetchScalarGridSpec(
-            num_scalar_prefetch=1,
-            grid=(depth,),
-            in_specs=[
-                pl.BlockSpec((tokens, wide), shard),
-                pl.BlockSpec(norm_gain.shape, lambda k, place: (0,)),
-            ],
-            out_specs=out_specs,
-            scratch_shapes=[pltpu.VMEM((1, norm_gain.shape[0]), jnp.float32)],
-        ),
-    )(place, *(pltpu.with_memory_space_constraint(a, pltpu.HBM) for a in (hidden_in, norm_gain)))
+        functools.partial(gate_kernel, part, depth),
+        (piece,) * 4 + (jax.ShapeDtypeStruct((tokens, HEAD), jnp.float32),),
+        in_specs=[pl.BlockSpec(memory_space=pltpu.HBM), WHOLE],
+        out_specs=[WHOLE] * 5,
+        scratch_shapes=[
+            pltpu.VMEM((depth, tokens, 4 * part), jnp.bfloat16),
+            pltpu.VMEM((1, norm_gain.shape[0]), jnp.float32),
+            pltpu.SemaphoreType.DMA((depth,)),
+        ],
+    )(pltpu.with_memory_space_constraint(hidden_in, pltpu.HBM), norm_gain)
 
 
 def matmul_kernel(firsts, n_acts, n_more, sent, *refs):
@@ -299,7 +285,7 @@
     return outs if sent else outs[0]
 
 
-def join_kernel(n_came, mine_ref, *refs):
+def join_kernel(n_came, first, mine_ref, *refs):
     came_refs, out_refs = refs[:n_came], refs[n_came:]
     n_blocks = mine_ref.shape[1]
     per = len(out_refs) * n_blocks // n_came
@@ -307,12 +293,12 @@
         for g in range(n_blocks):
             spot = p * n_blocks + g
             came = came_refs[spot // per][spot % per].astype(jnp.float32)
-            out_ref[g] = (mine_ref[p, g] + came).astype(out_ref.dtype)
-
-
-def join(mine, came, types):
+            out_ref[g] = (mine_ref[first + p, g] + came).astype(out_ref.dtype)
+
+
+def join(mine, came, types, first=0):
     return call(
-        functools.partial(join_kernel, len(came)),
+        functools.partial(join_kernel, len(came), first),
         tuple(jax.ShapeDtypeStruct(mine.shape[1:], t) for t in types),
         in_specs=[WHOLE] * (1 + len(came)),
         out_specs=[WHOLE] * len(types),
@@ -419,10 +405,6 @@
     groups = lax.axis_size("groups")
     dp = lax.axis_size("dp")
     tensor = lax.axis_size("tensor")
-    y = lax.axis_index("groups")
-    spot = lax.axis_index("dp")
-    core = lax.axis_index("tensor")
-    place = jnp.stack([spot // 2, spot % 2, y, core]).astype(jnp.int32)
     depth = dp // 2
     tokens = hidden_in.shape[0]
     part = projection.shape[1] // groups
@@ -468,46 +450,51 @@
     a0, = select(projection, part, columns[:1])
     a0 = after(a0)
     a1 = on_ring(a0)
-    a3 = back(a0)
-    far, near_x, near_y, own, squares = after(*gate(place, after(hidden_in), norm_gain, part, depth))
-    far = to_far(far)
+    far, near_x, near_y, own, squares = after(*gate(after(hidden_in), norm_gain, part, depth))
     near_x = to_x(near_x)
     near_y = to_y(near_y)
     b0, = select(after(projection), part, columns[1:])
+    b0, a0 = after(b0, a0)
+    a3 = back(a0)
     tabled = after(*tables(tokens, lengths, after(squares)))
 
-    a1 = after(a1)
+    a1, b0, far = after(a1, b0, far)
+    b1 = on_ring(b0)
+    far = to_far(far)
+    a3, a1 = after(a3, a1)
     a2 = on_ring(a1)
-    a3, b0 = after(a3, b0)
-    b1 = on_ring(b0)
+    b1 = after(b1)
+    b2 = on_ring(b1)
+    near_y = after(near_y)
+    near_x = after(near_x)
     a2, b0 = after(a2, b0)
     b3 = back(b0)
     set_a = (a0, a1, a2, a3)
 
+    early = (near_x, near_y, own)
+    *theirs, mine = after(*matmul(early, set_a, (0, 1, 2, 3), sent=2))
+    swapped = [to_core(t) for t in theirs]
     far = after(far)
-    *theirs, mine = after(*matmul((far, own), set_a, (0, 1, 2, 3), sent=2))
-    swapped = [to_core(t) for t in theirs]
-    b1 = after(b1)
-    b2 = on_ring(b1)
-    sums_far, sums = after(*join(mine, after(*swapped), (jnp.bfloat16, jnp.float32)))
-    sums_far = to_far(sums_far)
-    near_x, near_y = after(near_x, near_y)
+    sums_x, sums_y, sums = after(*join(mine, after(*swapped), (jnp.bfloat16, jnp.bfloat16, jnp.float32)))
+    sums_x = to_x(sums_x)
+    sums_y = to_y(sums_y)
     acts = (far, own, near_x, near_y)
-    *theirs, mine = after(*matmul((near_x, near_y), set_a, (0, 1, 2, 3), sent=2))
+    *theirs, mine = after(*matmul((far,), set_a, (0, 1, 2, 3), sent=1))
     swapped = [to_core(t) for t in theirs]
     squares = after(squares)
     other_norm = to_core(squares)
-    b3 = after(b3)
+    b2 = after(b2)
     *swapped, other_norm = after(*swapped, other_norm)
     scale = inv_rms(squares, other_norm)
-    sums_x, sums_y = after(*join(mine, swapped, (jnp.bfloat16, jnp.bfloat16)))
-    sums_x = to_x(sums_x)
-    sums_y = to_y(sums_y)
-    front = after(matmul(acts, (b0, b1, b3), (0, 1, 3)))
-
-    b2 = after(b2)
+    sums_far = after(*join(mine, swapped, (jnp.bfloat16,)))
+    sums_far = to_far(sums_far)
+    sums_y = after(sums_y)
+    sums_x = after(sums_x)
+    front = after(matmul(acts, (b0, b1, b2), (0, 1, 2)))
+
+    b3 = after(b3)
     parts_a = after(sums, sums_far, sums_x, sums_y)
-    *theirs, mine = after(*matmul(acts, (b2,), (2,), (front,), sent=2))
+    *theirs, mine = after(*matmul(acts, (b3,), (3,), (front,), sent=2))
     swapped = [to_core(t) for t in theirs]
     kv = after(call(
         kv_kernel,
@@ -516,12 +503,16 @@
         out_specs=WHOLE,
     )(*parts_a, scale, *tabled[:2]))
     vk = to_core(kv)
-    types = (jnp.bfloat16, jnp.float32, jnp.bfloat16, jnp.bfloat16)
-    sums_far, sums, sums_x, sums_y = after(*join(mine, after(*swapped), types))
-    parts_b = (sums, to_far(sums_far), to_x(sums_x), to_y(sums_y))
+    sums_far, sums = after(*join(mine, (after(swapped[0]),), (jnp.bfloat16, jnp.float32)))
+    sums_far = to_far(sums_far)
+    sums_x, sums_y = after(*join(mine, (after(swapped[1]),), (jnp.bfloat16, jnp.bfloat16), first=2))
+    sums_x = to_x(sums_x)
+    sums_y = to_y(sums_y)
     vk = after(vk)
     one = after(heads(parts_a, 1, scale, tabled, kv, vk))
-    return heads(after(*parts_b), 0, scale, tabled, kv, vk, one)
+    sums_far = after(sums_far)
+    sums_x, sums_y = after(sums_x, sums_y)
+    return heads((sums, sums_far, sums_x, sums_y), 0, scale, tabled, kv, vk, one)
 
 
 def local(hidden_in, norm_gain, projection, lengths):

time: 74 us -> 72.6 us (0.981)
  waiting for transfers between devices: 39.1 us -> 35.2 us
  starting transfers between devices: 19.6 us -> 23.3 us
  Pallas kernels: 14.8 us -> 13 us
    ppermute x2, waiting for transfers between devices: 9.78 us -> 5.95 us  [back(): return lax.ppermute(a, 'dp', [(j, i) for i, j in ring])]
    ppermute x3, waiting for transfers between devices: 0.01 us -> 2.35 us  [to_far(): return lax.ppermute(a, ('groups', 'dp'), across)]
    ppermute x3, starting transfers between devices: 2.2 us -> 4.54 us  [to_y(): return lax.ppermute(a, 'groups', over_y)]
    ppermute x3, waiting for transfers between devices: 4.18 us -> 2.11 us  [to_y(): return lax.ppermute(a, 'groups', over_y)]
    pallas_call x4 -> x5, Pallas kernels: 4.13 us -> 2.34 us  [the longest x1 2.16 us: gate(): call(functools.partial(gate_kernel, part, depth), (piece,) * 4 + (jax.Sha...]
    ppermute x8 -> x7, waiting for transfers between devices: 3.76 us -> 2.05 us  [to_core(): return lax.ppermute(a, 'tensor', over_core)]
    ppermute x4, starting transfers between devices: 3.65 us -> 4.94 us  [on_ring(): return lax.ppermute(a, 'dp', ring)]
    ppermute x3, waiting for transfers between devices: 1.62 us -> 2.51 us  [to_x(): return lax.ppermute(a, 'dp', over_x)]
  transfers between devices with their start and end apart: 23 -> 22, of which waited for: 13 -> 13; matrix products, arithmetic and copies ran while one was open for 0% -> 0% of each run, Pallas kernels for 16% -> 14%
where the time goes in v4:
time: 72.6 us; the launch traced here: 72.4 us
  waiting for transfers between devices  35.2 us (48%)
  starting transfers between devices  23.3 us (32%)
  Pallas kernels  13 us (18%)
    ppermute x4, waiting for transfers between devices, on_ring(): return lax.ppermute(a, 'dp', ring)  20.2 us
    ppermute x2, waiting for transfers between devices, back(): return lax.ppermute(a, 'dp', [(j, i) for i, j in ring])  5.95 us
    ppermute x3, starting transfers between devices, to_far(): return lax.ppermute(a, ('groups', 'dp'), across)  5.75 us
    pallas_call x4, Pallas kernels, matmul(): call(functools.partial(matmul_kernel, firsts, len(acts), len(so_far), sen...  4.95 us
    ppermute x4, starting transfers between devices, on_ring(): return lax.ppermute(a, 'dp', ring)  4.94 us
    ppermute x3, starting transfers between devices, to_y(): return lax.ppermute(a, 'groups', over_y)  4.54 us
    ppermute x2, starting transfers between devices, back(): return lax.ppermute(a, 'dp', [(j, i) for i, j in ring])  3.8 us
    ppermute x3, starting transfers between devices, to_x(): return lax.ppermute(a, 'dp', over_x)  2.65 us
  transfers between devices with their start and end apart: 22, of which 13 were waited for; matrix products, arithmetic and copies ran while one was open for 0% of the time, Pallas kernels for 14%

profile of v4, /device:TPU:0, one launch (start us, length us, event | category | flops | bytes accessed | tf_op | source)
XLA Modules:
  0.0 72.4 jit_solution(882605181041478502)
XLA Ops:
  0.0 1.1 %shard_map.46.refs_3_.refs_1_ = bf16[384,512]{1,0:T(8,128)(2,1)S(1)} custom-call(bf16[1,768,1024]{2,1,0:T(8,128)(2,1)} %rows_ref.2), custom_call_target="tpu_custom_call" | custom-call | flops 1 | bytes 1 | tf_op jit(solution)/shard_map/pallas_call | solution.py:187
  1.1 3.1 %collective-permute-start = (bf16[384,512]{1,0:T(8,128)(2,1)S(1)}, bf16[384,512]{1,0:T(8,128)(2,1)S(1)}, u32[]{:S(2)}, u32[]{:S(2)}) collective-permute-start(bf16[384,512]{1,0:T(8,128)(2,1)S(1)} %shard_map.46.refs_3_.refs_1_), channel_id=1, source_target_pairs={{0,4},{2,6},{4,8},{6,10},{8,12},{10,14},{12,0},{14,2},{1,5},{3,7},... | collective-permute-start | bytes 1179656 | tf_op jit(solution)/shard_map/ppermute | solution.py:423
  4.2 0.7 copy-done
  4.9 2.2 %shard_map.47 = (bf16[4,256,384]{2,1,0:T(8,128)(2,1)S(1)}, bf16[4,256,384]{2,1,0:T(8,128)(2,1)S(1)}, bf16[4,256,384]{2,1,0:T(8,128)(2,1)S(1)}, bf16[4,256,384]{2,1,0:T(8,128)(2,1)S(1)}, f32[256,128]{1,0:T(8,128)S(1)}) custom-call(bf16[256,6144]{1,0:T(8,128)(2,1)} %hidden_ref, bf16[6144]{0:T(1024)(128)(2,1)S(1)} %copy-done), custom_call_target="tpu_custom_call" | custom-call | flops 1 | bytes 1 | tf_op jit(solution)/shard_map/pallas_call | solution.py:228
  7.0 1.6 %collective-permute-start.3 = (bf16[4,256,384]{2,1,0:T(8,128)(2,1)S(1)}, bf16[4,256,384]{2,1,0:T(8,128)(2,1)S(1)}, u32[]{:S(2)}, u32[]{:S(2)}) collective-permute-start(bf16[4,256,384]{2,1,0:T(8,128)(2,1)S(1)} %get-tuple-element.110), channel_id=1, source_target_pairs={{0,16},{16,0},{1,17},{17,1},{2,18},{18,2},{3,19},{19,3},{4,20},{20... | collective-permute-start | bytes 2359304 | tf_op jit(solution)/shard_map/ppermute | solution.py:435
  8.6 1.1 %shard_map.48.refs_4_ = bf16[384,512]{1,0:T(8,128)(2,1)S(1)} custom-call(bf16[1,768,1024]{2,1,0:T(8,128)(2,1)} %rows_ref.2), custom_call_target="tpu_custom_call" | custom-call | flops 1 | bytes 1 | tf_op jit(solution)/shard_map/pallas_call | solution.py:187
  9.7 2.3 %collective-permute-start.5 = (bf16[384,512]{1,0:T(8,128)(2,1)S(1)}, bf16[384,512]{1,0:T(8,128)(2,1)S(1)}, u32[]{:S(2)}, u32[]{:S(2)}) collective-permute-start(bf16[384,512]{1,0:T(8,128)(2,1)S(1)} %shard_map.46.refs_3_.refs_1_), channel_id=1, source_target_pairs={{4,0},{6,2},{8,4},{10,6},{12,8},{14,10},{0,12},{2,14},{5,1},{7,3},... | collective-permute-start | bytes 1179656 | tf_op jit(solution)/shard_map/ppermute | solution.py:426
  12.0 1.5 %collective-permute-start.2 = (bf16[4,256,384]{2,1,0:T(8,128)(2,1)S(1)}, bf16[4,256,384]{2,1,0:T(8,128)(2,1)S(1)}, u32[]{:S(2)}, u32[]{:S(2)}) collective-permute-start(bf16[4,256,384]{2,1,0:T(8,128)(2,1)S(1)} %get-tuple-element.109), channel_id=1, source_target_pairs={{0,2},{2,0},{4,6},{6,4},{8,10},{10,8},{12,14},{14,12},{1,3},{3,1},... | collective-permute-start | bytes 2359304 | tf_op jit(solution)/shard_map/ppermute | solution.py:432
  13.5 1.1 %shard_map.49 = (f32[256,128]{1,0:T(8,128)S(1)}, f32[256,128]{1,0:T(8,128)S(1)}, f32[256,256]{1,0:T(8,128)S(1)}, f32[256,128]{1,0:T(8,128)S(1)}) custom-call(s32[1,2]{1,0:T(1,128)S(1)} %copy-done.1, f32[256,128]{1,0:T(8,128)S(1)} %get-tuple-element.138._.own_ref), custom_call_target="tpu_custom_call" | custom-call | flops 1 | bytes 1 | tf_op jit(solution)/shard_map/pallas_call | solution.py:326
  14.6 1.6 %collective-permute-done.refs_4_.refs_2_ = bf16[384,512]{1,0:T(8,128)(2,1)S(1)} collective-permute-done((bf16[384,512]{1,0:T(8,128)(2,1)S(1)}, bf16[384,512]{1,0:T(8,128)(2,1)S(1)}, u32[]{:S(2)}, u32[]{:S(2)}) %collective-permute-start) | collective-permute-done | bytes 393248 | tf_op jit(solution)/shard_map/ppermute | solution.py:423
  16.2 2.7 %collective-permute-start.1 = (bf16[4,256,384]{2,1,0:T(8,128)(2,1)S(1)}, bf16[4,256,384]{2,1,0:T(8,128)(2,1)S(1)}, u32[]{:S(2)}, u32[]{:S(2)}) collective-permute-start(bf16[4,256,384]{2,1,0:T(8,128)(2,1)S(1)} %get-tuple-element.108), channel_id=1, source_target_pairs={{0,18},{2,16},{4,22},{6,20},{8,26},{10,24},{12,30},{14,28},{16,2},... | collective-permute-start | bytes 2359304 | tf_op jit(solution)/shard_map/ppermute | solution.py:429
  18.9 5.6 %collective-permute-done.5.refs_6_.refs_4_ = bf16[384,512]{1,0:T(8,128)(2,1)S(1)} collective-permute-done((bf16[384,512]{1,0:T(8,128)(2,1)S(1)}, bf16[384,512]{1,0:T(8,128)(2,1)S(1)}, u32[]{:S(2)}, u32[]{:S(2)}) %collective-permute-start.5) | collective-permute-done | bytes 393248 | tf_op jit(solution)/shard_map/ppermute | solution.py:426
  24.5 1.9 %collective-permute-start.6 = (bf16[384,512]{1,0:T(8,128)(2,1)S(1)}, bf16[384,512]{1,0:T(8,128)(2,1)S(1)}, u32[]{:S(2)}, u32[]{:S(2)}) collective-permute-start(bf16[384,512]{1,0:T(8,128)(2,1)S(1)} %collective-permute-done.refs_4_.refs_2_), channel_id=1, source_target_pairs={{0,4},{2,6},{4,8},{6,10},{8,12},{10,14},{12,0},{14,2},{1,5},{3,7},... | collective-permute-start | bytes 1179656 | tf_op jit(solution)/shard_map/ppermute | solution.py:423
  26.4 10.2 %collective-permute-done.4.refs_5_ = bf16[384,512]{1,0:T(8,128)(2,1)S(1)} collective-permute-done((bf16[384,512]{1,0:T(8,128)(2,1)S(1)}, bf16[384,512]{1,0:T(8,128)(2,1)S(1)}, u32[]{:S(2)}, u32[]{:S(2)}) %collective-permute-start.4) | collective-permute-done | bytes 393248 | tf_op jit(solution)/shard_map/ppermute | solution.py:423
  36.6 8.4 %collective-permute-done.6.refs_5_.refs_3_ = bf16[384,512]{1,0:T(8,128)(2,1)S(1)} collective-permute-done((bf16[384,512]{1,0:T(8,128)(2,1)S(1)}, bf16[384,512]{1,0:T(8,128)(2,1)S(1)}, u32[]{:S(2)}, u32[]{:S(2)}) %collective-permute-start.6) | collective-permute-done | bytes 393248 | tf_op jit(solution)/shard_map/ppermute | solution.py:423
  45.0 1.8 %shard_map.50 = (bf16[3,256,128]{2,1,0:T(8,128)(2,1)S(1)}, bf16[3,256,128]{2,1,0:T(8,128)(2,1)S(1)}, f32[3,2,256,128]{3,2,1,0:T(8,128)S(1)}) custom-call(bf16[4,256,384]{2,1,0:T(8,128)(2,1)S(1)} %collective-permute-done.2.refs_0_.refs_2_, bf16[4,256,384]{2,1,0:T(8,128)(2,1)S(1)} %collective-permute-done.3.refs_1_.refs_3_, ...), custom_call_target="tpu_custom_call" | custom-call | flops 1 | bytes 1 | tf_op jit(solution)/shard_map/pallas_call | solution.py:279
  47.4 1.5 %collective-permute-start.7 = (bf16[384,512]{1,0:T(8,128)(2,1)S(1)}, bf16[384,512]{1,0:T(8,128)(2,1)S(1)}, u32[]{:S(2)}, u32[]{:S(2)}) collective-permute-start(bf16[384,512]{1,0:T(8,128)(2,1)S(1)} %shard_map.48.refs_4_), channel_id=1, source_target_pairs={{4,0},{6,2},{8,4},{10,6},{12,8},{14,10},{0,12},{2,14},{5,1},{7,3},... | collective-permute-start | bytes 1179656 | tf_op jit(solution)/shard_map/ppermute | solution.py:426
  48.9 0.7 shard_map.51
  50.3 1.5 %collective-permute-start.12 = (bf16[2,256,128]{2,1,0:T(8,128)(2,1)S(1)}, bf16[2,256,128]{2,1,0:T(8,128)(2,1)S(1)}, u32[]{:S(2)}, u32[]{:S(2)}) collective-permute-start(bf16[2,256,128]{2,1,0:T(8,128)(2,1)S(1)} %get-tuple-element.140), channel_id=1, source_target_pairs={{0,16},{16,0},{1,17},{17,1},{2,18},{18,2},{3,19},{19,3},{4,20},{20... | collective-permute-start | bytes 393224 | tf_op jit(solution)/shard_map/ppermute | solution.py:435
  52.4 1.5 %collective-permute-start.15 = (bf16[2,256,128]{2,1,0:T(8,128)(2,1)S(1)}, bf16[2,256,128]{2,1,0:T(8,128)(2,1)S(1)}, u32[]{:S(2)}, u32[]{:S(2)}) collective-permute-start(bf16[2,256,128]{2,1,0:T(8,128)(2,1)S(1)} %shard_map.54), channel_id=1, source_target_pairs={{0,18},{2,16},{4,22},{6,20},{8,26},{10,24},{12,30},{14,28},{16,2},... | collective-permute-start | bytes 393224 | tf_op jit(solution)/shard_map/ppermute | solution.py:429
  53.9 1.8 %shard_map.53.refs_5_ = f32[4,256,512]{2,1,0:T(8,128)S(1)} custom-call(bf16[4,256,384]{2,1,0:T(8,128)(2,1)S(1)} %collective-permute-done.1.refs_0_, bf16[4,256,384]{2,1,0:T(8,128)(2,1)S(1)} %get-tuple-element.118.refs_2_.refs_1_, bf16[4,256,384]{2,1,0:T(8,128)(2,1)S(1)} %collective-permute-done.2.refs_0_.refs_2_, ...), custom_call_target="tpu_custom_call" | custom-call | flops 1 | bytes 1 | tf_op jit(solution)/shard_map/pallas_call | solution.py:279
  55.8 2.4 %collective-permute-done.11.r1.refs_2_ = bf16[2,256,128]{2,1,0:T(8,128)(2,1)S(1)} collective-permute-done((bf16[2,256,128]{2,1,0:T(8,128)(2,1)S(1)}, bf16[2,256,128]{2,1,0:T(8,128)(2,1)S(1)}, u32[]{:S(2)}, u32[]{:S(2)}) %collective-permute-start.11) | collective-permute-done | bytes 131104 | tf_op jit(solution)/shard_map/ppermute | solution.py:432
  58.5 0.7 shard_map.55
  60.5 0.8 %collective-permute-done.16.refs_0_ = bf16[4,256,128]{2,1,0:T(8,128)(2,1)S(1)} collective-permute-done((bf16[4,256,128]{2,1,0:T(8,128)(2,1)S(1)}, bf16[4,256,128]{2,1,0:T(8,128)(2,1)S(1)}, u32[]{:S(2)}, u32[]{:S(2)}) %collective-permute-start.16) | collective-permute-done | bytes 262176 | tf_op jit(solution)/shard_map/ppermute | solution.py:420
  61.3 1.6 %collective-permute-start.17 = (bf16[2,256,128]{2,1,0:T(8,128)(2,1)S(1)}, bf16[2,256,128]{2,1,0:T(8,128)(2,1)S(1)}, u32[]{:S(2)}, u32[]{:S(2)}) collective-permute-start(bf16[2,256,128]{2,1,0:T(8,128)(2,1)S(1)} %get-tuple-element.165), channel_id=1, source_target_pairs={{0,18},{2,16},{4,22},{6,20},{8,26},{10,24},{12,30},{14,28},{16,2},... | collective-permute-start | bytes 393224 | tf_op jit(solution)/shard_map/ppermute | solution.py:429
  63.0 1.4 %collective-permute-start.21 = (bf16[2,256,128]{2,1,0:T(8,128)(2,1)S(1)}, bf16[2,256,128]{2,1,0:T(8,128)(2,1)S(1)}, u32[]{:S(2)}, u32[]{:S(2)}) collective-permute-start(bf16[2,256,128]{2,1,0:T(8,128)(2,1)S(1)} %get-tuple-element.176), channel_id=1, source_target_pairs={{0,16},{16,0},{1,17},{17,1},{2,18},{18,2},{3,19},{19,3},{4,20},{20... | collective-permute-start | bytes 393224 | tf_op jit(solution)/shard_map/ppermute | solution.py:435
  64.4 0.6 collective-permute-start.20
  65.0 1.3 %collective-permute-done.18.refs_10_ = bf16[256,128]{1,0:T(8,128)(2,1)S(1)} collective-permute-done((bf16[256,128]{1,0:T(8,128)(2,1)S(1)}, bf16[256,128]{1,0:T(8,128)(2,1)S(1)}, u32[]{:S(2)}, u32[]{:S(2)}) %collective-permute-start.18) | collective-permute-done | bytes 65568 | tf_op jit(solution)/shard_map/ppermute | solution.py:420
  66.3 0.6 shard_map.60.refs_11_
  66.9 1.8 %collective-permute-done.17.refs_1_ = bf16[2,256,128]{2,1,0:T(8,128)(2,1)S(1)} collective-permute-done((bf16[2,256,128]{2,1,0:T(8,128)(2,1)S(1)}, bf16[2,256,128]{2,1,0:T(8,128)(2,1)S(1)}, u32[]{:S(2)}, u32[]{:S(2)}) %collective-permute-start.17) | collective-permute-done | bytes 131104 | tf_op jit(solution)/shard_map/ppermute | solution.py:429
  68.7 2.0 %collective-permute-done.21.refs_3_ = bf16[2,256,128]{2,1,0:T(8,128)(2,1)S(1)} collective-permute-done((bf16[2,256,128]{2,1,0:T(8,128)(2,1)S(1)}, bf16[2,256,128]{2,1,0:T(8,128)(2,1)S(1)}, u32[]{:S(2)}, u32[]{:S(2)}) %collective-permute-start.21) | collective-permute-done | bytes 131104 | tf_op jit(solution)/shard_map/ppermute | solution.py:435
  70.7 1.7 %shard_map.61 = bf16[256,384]{1,0:T(8,128)(2,1)} custom-call(f32[2,256,128]{2,1,0:T(8,128)S(1)} %get-tuple-element.164.refs_0_, bf16[2,256,128]{2,1,0:T(8,128)(2,1)S(1)} %collective-permute-done.17.refs_1_, bf16[2,256,128]{2,1,0:T(8,128)(2,1)S(1)} %collective-permute-done.20.refs_2_, bf16[2,256,128]{2,1,0:T(8,128)(2,1)S(1)} %collective-permute-done.21.refs_3_, ...), custom_call_target="tpu_custom_call" | custom-call | flops 1 | bytes 1 | tf_op jit(solution)/shard_map/pallas_call | solution.py:395
  (32 shorter events, 3.7 us)
Async XLA Ops:
  1.1 15.1 %collective-permute-start = (bf16[384,512]{1,0:T(8,128)(2,1)S(1)}, bf16[384,512]{1,0:T(8,128)(2,1)S(1)}, u32[]{:S(2)}, u32[]{:S(2)}) collective-permute-start(bf16[384,512]{1,0:T(8,128)(2,1)S(1)} %shard_map.46.refs_3_.refs_1_), channel_id=1, source_target_pairs={{0,4},{2,6},{4,8},{6,10},{8,12},{10,14},{12,0},{14,2},{1,5},{3,7},... | collective-permute-start | bytes 1179656 | tf_op jit(solution)/shard_map/ppermute | solution.py:423
  4.2 0.7 copy-start
  4.9 8.6 %copy-start.1 = (s32[1,2]{1,0:T(1,128)S(1)}, s32[1,2]{1,0:T(1,128)}, u32[]{:S(2)}) copy-start(s32[1,2]{1,0:T(1,128)} %lengths_ref.1) | copy-start | bytes 28
  7.0 29.6 %collective-permute-start.3 = (bf16[4,256,384]{2,1,0:T(8,128)(2,1)S(1)}, bf16[4,256,384]{2,1,0:T(8,128)(2,1)S(1)}, u32[]{:S(2)}, u32[]{:S(2)}) collective-permute-start(bf16[4,256,384]{2,1,0:T(8,128)(2,1)S(1)} %get-tuple-element.110), channel_id=1, source_target_pairs={{0,16},{16,0},{1,17},{17,1},{2,18},{18,2},{3,19},{19,3},{4,20},{20... | collective-permute-start | bytes 2359304 | tf_op jit(solution)/shard_map/ppermute | solution.py:435
  9.7 14.8 %collective-permute-start.5 = (bf16[384,512]{1,0:T(8,128)(2,1)S(1)}, bf16[384,512]{1,0:T(8,128)(2,1)S(1)}, u32[]{:S(2)}, u32[]{:S(2)}) collective-permute-start(bf16[384,512]{1,0:T(8,128)(2,1)S(1)} %shard_map.46.refs_3_.refs_1_), channel_id=1, source_target_pairs={{4,0},{6,2},{8,4},{10,6},{12,8},{14,10},{0,12},{2,14},{5,1},{7,3},... | collective-permute-start | bytes 1179656 | tf_op jit(solution)/shard_map/ppermute | solution.py:426
  12.0 24.6 %collective-permute-start.2 = (bf16[4,256,384]{2,1,0:T(8,128)(2,1)S(1)}, bf16[4,256,384]{2,1,0:T(8,128)(2,1)S(1)}, u32[]{:S(2)}, u32[]{:S(2)}) collective-permute-start(bf16[4,256,384]{2,1,0:T(8,128)(2,1)S(1)} %get-tuple-element.109), channel_id=1, source_target_pairs={{0,2},{2,0},{4,6},{6,4},{8,10},{10,8},{12,14},{14,12},{1,3},{3,1},... | collective-permute-start | bytes 2359304 | tf_op jit(solution)/shard_map/ppermute | solution.py:432
  16.2 32.7 %collective-permute-start.1 = (bf16[4,256,384]{2,1,0:T(8,128)(2,1)S(1)}, bf16[4,256,384]{2,1,0:T(8,128)(2,1)S(1)}, u32[]{:S(2)}, u32[]{:S(2)}) collective-permute-start(bf16[4,256,384]{2,1,0:T(8,128)(2,1)S(1)} %get-tuple-element.108), channel_id=1, source_target_pairs={{0,18},{2,16},{4,22},{6,20},{8,26},{10,24},{12,30},{14,28},{16,2},... | collective-permute-start | bytes 2359304 | tf_op jit(solution)/shard_map/ppermute | solution.py:429
  18.9 17.7 %collective-permute-start.4 = (bf16[384,512]{1,0:T(8,128)(2,1)S(1)}, bf16[384,512]{1,0:T(8,128)(2,1)S(1)}, u32[]{:S(2)}, u32[]{:S(2)}) collective-permute-start(bf16[384,512]{1,0:T(8,128)(2,1)S(1)} %shard_map.48.refs_4_), channel_id=1, source_target_pairs={{0,4},{2,6},{4,8},{6,10},{8,12},{10,14},{12,0},{14,2},{1,5},{3,7},... | collective-permute-start | bytes 1179656 | tf_op jit(solution)/shard_map/ppermute | solution.py:423
  24.5 20.5 %collective-permute-start.6 = (bf16[384,512]{1,0:T(8,128)(2,1)S(1)}, bf16[384,512]{1,0:T(8,128)(2,1)S(1)}, u32[]{:S(2)}, u32[]{:S(2)}) collective-permute-start(bf16[384,512]{1,0:T(8,128)(2,1)S(1)} %collective-permute-done.refs_4_.refs_2_), channel_id=1, source_target_pairs={{0,4},{2,6},{4,8},{6,10},{8,12},{10,14},{12,0},{14,2},{1,5},{3,7},... | collective-permute-start | bytes 1179656 | tf_op jit(solution)/shard_map/ppermute | solution.py:423
  36.6 15.2 %collective-permute-start.8 = (bf16[384,512]{1,0:T(8,128)(2,1)S(1)}, bf16[384,512]{1,0:T(8,128)(2,1)S(1)}, u32[]{:S(2)}, u32[]{:S(2)}) collective-permute-start(bf16[384,512]{1,0:T(8,128)(2,1)S(1)} %collective-permute-done.4.refs_5_), channel_id=1, source_target_pairs={{0,4},{2,6},{4,8},{6,10},{8,12},{10,14},{12,0},{14,2},{1,5},{3,7},... | collective-permute-start | bytes 1179656 | tf_op jit(solution)/shard_map/ppermute | solution.py:423
  46.8 2.8 %collective-permute-start.10 = (bf16[3,256,128]{2,1,0:T(8,128)(2,1)S(1)}, bf16[3,256,128]{2,1,0:T(8,128)(2,1)S(1)}, u32[]{:S(2)}, u32[]{:S(2)}) collective-permute-start(bf16[3,256,128]{2,1,0:T(8,128)(2,1)S(1)} %get-tuple-element.130), channel_id=1, source_target_pairs={{0,1},{1,0},{2,3},{3,2},{4,5},{5,4},{6,7},{7,6},{8,9},{9,8},{10,11... | collective-permute-start | bytes 589832 | tf_op jit(solution)/shard_map/ppermute | solution.py:420
  46.9 2.7 %collective-permute-start.9 = (bf16[3,256,128]{2,1,0:T(8,128)(2,1)S(1)}, bf16[3,256,128]{2,1,0:T(8,128)(2,1)S(1)}, u32[]{:S(2)}, u32[]{:S(2)}) collective-permute-start(bf16[3,256,128]{2,1,0:T(8,128)(2,1)S(1)} %get-tuple-element.124), channel_id=1, source_target_pairs={{0,1},{1,0},{2,3},{3,2},{4,5},{5,4},{6,7},{7,6},{8,9},{9,8},{10,11... | collective-permute-start | bytes 589832 | tf_op jit(solution)/shard_map/ppermute | solution.py:420
  47.4 11.1 %collective-permute-start.7 = (bf16[384,512]{1,0:T(8,128)(2,1)S(1)}, bf16[384,512]{1,0:T(8,128)(2,1)S(1)}, u32[]{:S(2)}, u32[]{:S(2)}) collective-permute-start(bf16[384,512]{1,0:T(8,128)(2,1)S(1)} %shard_map.48.refs_4_), channel_id=1, source_target_pairs={{4,0},{6,2},{8,4},{10,6},{12,8},{14,10},{0,12},{2,14},{5,1},{7,3},... | collective-permute-start | bytes 1179656 | tf_op jit(solution)/shard_map/ppermute | solution.py:426
  49.7 2.7 %collective-permute-start.14 = (f32[256,128]{1,0:T(8,128)S(1)}, f32[256,128]{1,0:T(8,128)S(1)}, u32[]{:S(2)}, u32[]{:S(2)}) collective-permute-start(f32[256,128]{1,0:T(8,128)S(1)} %get-tuple-element.138._.own_ref), channel_id=1, source_target_pairs={{0,1},{1,0},{2,3},{3,2},{4,5},{5,4},{6,7},{7,6},{8,9},{9,8},{10,11... | collective-permute-start | bytes 393224 | tf_op jit(solution)/shard_map/ppermute | solution.py:420
  49.8 2.6 %collective-permute-start.13 = (bf16[2,256,128]{2,1,0:T(8,128)(2,1)S(1)}, bf16[2,256,128]{2,1,0:T(8,128)(2,1)S(1)}, u32[]{:S(2)}, u32[]{:S(2)}) collective-permute-start(bf16[2,256,128]{2,1,0:T(8,128)(2,1)S(1)} %get-tuple-element.137), channel_id=1, source_target_pairs={{0,1},{1,0},{2,3},{3,2},{4,5},{5,4},{6,7},{7,6},{8,9},{9,8},{10,11... | collective-permute-start | bytes 393224 | tf_op jit(solution)/shard_map/ppermute | solution.py:420
  50.3 5.5 %collective-permute-start.12 = (bf16[2,256,128]{2,1,0:T(8,128)(2,1)S(1)}, bf16[2,256,128]{2,1,0:T(8,128)(2,1)S(1)}, u32[]{:S(2)}, u32[]{:S(2)}) collective-permute-start(bf16[2,256,128]{2,1,0:T(8,128)(2,1)S(1)} %get-tuple-element.140), channel_id=1, source_target_pairs={{0,16},{16,0},{1,17},{17,1},{2,18},{18,2},{3,19},{19,3},{4,20},{20... | collective-permute-start | bytes 393224 | tf_op jit(solution)/shard_map/ppermute | solution.py:435
  51.8 6.4 %collective-permute-start.11 = (bf16[2,256,128]{2,1,0:T(8,128)(2,1)S(1)}, bf16[2,256,128]{2,1,0:T(8,128)(2,1)S(1)}, u32[]{:S(2)}, u32[]{:S(2)}) collective-permute-start(bf16[2,256,128]{2,1,0:T(8,128)(2,1)S(1)} %get-tuple-element.136), channel_id=1, source_target_pairs={{0,2},{2,0},{4,6},{6,4},{8,10},{10,8},{12,14},{14,12},{1,3},{3,1},... | collective-permute-start | bytes 393224 | tf_op jit(solution)/shard_map/ppermute | solution.py:432
  52.4 7.4 %collective-permute-start.15 = (bf16[2,256,128]{2,1,0:T(8,128)(2,1)S(1)}, bf16[2,256,128]{2,1,0:T(8,128)(2,1)S(1)}, u32[]{:S(2)}, u32[]{:S(2)}) collective-permute-start(bf16[2,256,128]{2,1,0:T(8,128)(2,1)S(1)} %shard_map.54), channel_id=1, source_target_pairs={{0,18},{2,16},{4,22},{6,20},{8,26},{10,24},{12,30},{14,28},{16,2},... | collective-permute-start | bytes 393224 | tf_op jit(solution)/shard_map/ppermute | solution.py:429
  59.8 1.5 %collective-permute-start.16 = (bf16[4,256,128]{2,1,0:T(8,128)(2,1)S(1)}, bf16[4,256,128]{2,1,0:T(8,128)(2,1)S(1)}, u32[]{:S(2)}, u32[]{:S(2)}) collective-permute-start(bf16[4,256,128]{2,1,0:T(8,128)(2,1)S(1)} %get-tuple-element.154), channel_id=1, source_target_pairs={{0,1},{1,0},{2,3},{3,2},{4,5},{5,4},{6,7},{7,6},{8,9},{9,8},{10,11... | collective-permute-start | bytes 786440 | tf_op jit(solution)/shard_map/ppermute | solution.py:420
  59.8 3.2 %collective-permute-start.19 = (bf16[4,256,128]{2,1,0:T(8,128)(2,1)S(1)}, bf16[4,256,128]{2,1,0:T(8,128)(2,1)S(1)}, u32[]{:S(2)}, u32[]{:S(2)}) collective-permute-start(bf16[4,256,128]{2,1,0:T(8,128)(2,1)S(1)} %get-tuple-element.168), channel_id=1, source_target_pairs={{0,1},{1,0},{2,3},{3,2},{4,5},{5,4},{6,7},{7,6},{8,9},{9,8},{10,11... | collective-permute-start | bytes 786440 | tf_op jit(solution)/shard_map/ppermute | solution.py:420
  61.3 7.3 %collective-permute-start.17 = (bf16[2,256,128]{2,1,0:T(8,128)(2,1)S(1)}, bf16[2,256,128]{2,1,0:T(8,128)(2,1)S(1)}, u32[]{:S(2)}, u32[]{:S(2)}) collective-permute-start(bf16[2,256,128]{2,1,0:T(8,128)(2,1)S(1)} %get-tuple-element.165), channel_id=1, source_target_pairs={{0,18},{2,16},{4,22},{6,20},{8,26},{10,24},{12,30},{14,28},{16,2},... | collective-permute-start | bytes 393224 | tf_op jit(solution)/shard_map/ppermute | solution.py:429
  63.0 7.7 %collective-permute-start.21 = (bf16[2,256,128]{2,1,0:T(8,128)(2,1)S(1)}, bf16[2,256,128]{2,1,0:T(8,128)(2,1)S(1)}, u32[]{:S(2)}, u32[]{:S(2)}) collective-permute-start(bf16[2,256,128]{2,1,0:T(8,128)(2,1)S(1)} %get-tuple-element.176), channel_id=1, source_target_pairs={{0,16},{16,0},{1,17},{17,1},{2,18},{18,2},{3,19},{19,3},{4,20},{20... | collective-permute-start | bytes 393224 | tf_op jit(solution)/shard_map/ppermute | solution.py:435
  64.4 6.3 %collective-permute-start.20 = (bf16[2,256,128]{2,1,0:T(8,128)(2,1)S(1)}, bf16[2,256,128]{2,1,0:T(8,128)(2,1)S(1)}, u32[]{:S(2)}, u32[]{:S(2)}) collective-permute-start(bf16[2,256,128]{2,1,0:T(8,128)(2,1)S(1)} %get-tuple-element.172), channel_id=1, source_target_pairs={{0,2},{2,0},{4,6},{6,4},{8,10},{10,8},{12,14},{14,12},{1,3},{3,1},... | collective-permute-start | bytes 393224 | tf_op jit(solution)/shard_map/ppermute | solution.py:432
  65.0 1.3 %collective-permute-start.18 = (bf16[256,128]{1,0:T(8,128)(2,1)S(1)}, bf16[256,128]{1,0:T(8,128)(2,1)S(1)}, u32[]{:S(2)}, u32[]{:S(2)}) collective-permute-start(bf16[256,128]{1,0:T(8,128)(2,1)S(1)} %shard_map.57.refs_9_), channel_id=1, source_target_pairs={{0,1},{1,0},{2,3},{3,2},{4,5},{5,4},{6,7},{7,6},{8,9},{9,8},{10,11... | collective-permute-start | bytes 196616 | tf_op jit(solution)/shard_map/ppermute | solution.py:420

commit v5 on v4

--- a/solution.py
+++ b/solution.py
@@ -367,15 +367,24 @@
 def heads_kernel(first, n_parts, *refs):
     parts, refs = refs[:n_parts], refs[n_parts:]
     scale_ref, cosine_ref, sine_ref, allowed_ref, keep_ref, mine_ref, other_ref, *rest = refs
-    out_ref = rest[-1]
+    earlier_refs, out_ref, scratch = rest[:-1], rest[-1], None
+    if len(rest) > 1:
+        earlier_ref, out_ref, scratch, sems = rest
+        earlier_refs = [earlier_ref]
+    copies = []
+
+    def put(source, at):
+        copies.append(pltpu.make_async_copy(source, out_ref.at[:, pl.ds(at, source.shape[1])], sems.at[len(copies)]))
+        copies[-1].start()
+
     is_key = lax.axis_index("tensor") == 0
     mine, other = mine_ref[...], other_ref[...]
     keys = jnp.where(is_key, mine, other)
     values = jnp.where(is_key, other, mine)
     before = 0
-    if len(rest) > 1:
-        before = rest[0].shape[1]
-        out_ref[:, :before] = rest[0][...]
+    for earlier_ref in earlier_refs:
+        put(earlier_ref, before)
+        before += earlier_ref.shape[1]
     for i in range(first, parts[0].shape[0]):
         query = turned(summed(parts, i, scale_ref), cosine_ref, sine_ref).astype(jnp.bfloat16)
         scores = lax.dot_general(
@@ -385,19 +394,29 @@
         expo = jnp.exp(scores - jnp.max(scores, axis=-1, keepdims=True))
         attn = (expo / jnp.sum(expo, axis=-1, keepdims=True)).astype(jnp.bfloat16)
         mixed = jnp.dot(attn, values, preferred_element_type=jnp.float32)
-        at = before + (i - first) * HEAD
-        out_ref[:, at:at + HEAD] = (mixed * keep_ref[...]).astype(jnp.bfloat16)
+        done = (mixed * keep_ref[...]).astype(jnp.bfloat16)
+        if scratch is None:
+            out_ref[:, (i - first) * HEAD:(i - first + 1) * HEAD] = done
+        else:
+            scratch[i - first] = done
+            put(scratch.at[i - first], before + (i - first) * HEAD)
+    for copy in copies:
+        copy.wait()
 
 
 def heads(parts, first, scale, tabled, mine, other, *earlier):
     args = [*parts, scale, *tabled, mine, other, *earlier]
-    width = (parts[0].shape[0] - first) * HEAD + sum(e.shape[1] for e in earlier)
+    tokens = mine.shape[0]
+    count = parts[0].shape[0] - first
+    out_shape = jax.ShapeDtypeStruct((tokens, count * HEAD + sum(e.shape[1] for e in earlier)), jnp.bfloat16)
+    scratch = [pltpu.VMEM((count, tokens, HEAD), jnp.bfloat16), pltpu.SemaphoreType.DMA((count + len(earlier),))]
     return call(
         functools.partial(heads_kernel, first, len(parts)),
-        jax.ShapeDtypeStruct((mine.shape[0], width), jnp.bfloat16),
+        out_shape,
         result=bool(earlier),
         in_specs=[WHOLE] * len(args),
-        out_specs=WHOLE,
+        out_specs=pl.BlockSpec(memory_space=pltpu.HBM) if earlier else WHOLE,
+        scratch_shapes=scratch if earlier else [],
     )(*args)
 
 
@@ -456,23 +475,26 @@
     b0, = select(after(projection), part, columns[1:])
     b0, a0 = after(b0, a0)
     a3 = back(a0)
+    other_squares = to_core(squares)
     tabled = after(*tables(tokens, lengths, after(squares)))
+    scale = after(inv_rms(squares, after(other_squares)))
 
     a1, b0, far = after(a1, b0, far)
     b1 = on_ring(b0)
     far = to_far(far)
     a3, a1 = after(a3, a1)
     a2 = on_ring(a1)
+    near_y = after(near_y)
+    near_x = after(near_x)
     b1 = after(b1)
     b2 = on_ring(b1)
-    near_y = after(near_y)
-    near_x = after(near_x)
+    early = (near_x, near_y, own)
+    front = after(matmul(early, (a0, a1, a3), (0, 1, 3)))
     a2, b0 = after(a2, b0)
     b3 = back(b0)
     set_a = (a0, a1, a2, a3)
 
-    early = (near_x, near_y, own)
-    *theirs, mine = after(*matmul(early, set_a, (0, 1, 2, 3), sent=2))
+    *theirs, mine = after(*matmul(early, (a2,), (2,), (front,), sent=2))
     swapped = [to_core(t) for t in theirs]
     far = after(far)
     sums_x, sums_y, sums = after(*join(mine, after(*swapped), (jnp.bfloat16, jnp.bfloat16, jnp.float32)))
@@ -481,11 +503,8 @@
     acts = (far, own, near_x, near_y)
     *theirs, mine = after(*matmul((far,), set_a, (0, 1, 2, 3), sent=1))
     swapped = [to_core(t) for t in theirs]
-    squares = after(squares)
-    other_norm = to_core(squares)
     b2 = after(b2)
-    *swapped, other_norm = after(*swapped, other_norm)
-    scale = inv_rms(squares, other_norm)
+    swapped = [after(t) for t in swapped]
     sums_far = after(*join(mine, swapped, (jnp.bfloat16,)))
     sums_far = to_far(sums_far)
     sums_y = after(sums_y)

time: 72.6 us -> 73 us (level)
  the two profiles are of different devices: /device:TPU:0 before, /device:TPU:31 now
where the time goes in v5:
time: 73 us; the launch traced here: 72.8 us
  starting transfers between devices  32.5 us (45%)
  waiting for transfers between devices  26.4 us (36%)
  Pallas kernels  13.1 us (18%)
    ppermute x7, starting transfers between devices, to_core(): return lax.ppermute(a, 'tensor', over_core)  15.9 us
    ppermute x4, waiting for transfers between devices, on_ring(): return lax.ppermute(a, 'dp', ring)  9.24 us
    ppermute x2, waiting for transfers between devices, back(): return lax.ppermute(a, 'dp', [(j, i) for i, j in ring])  9.17 us
    ppermute x4, starting transfers between devices, on_ring(): return lax.ppermute(a, 'dp', ring)  7.86 us
    pallas_call x5, Pallas kernels, matmul(): call(functools.partial(matmul_kernel, firsts, len(acts), len(so_far), sen...  5.11 us
    ppermute x3, starting transfers between devices, to_y(): return lax.ppermute(a, 'groups', over_y)  4.42 us
    ppermute x3, waiting for transfers between devices, to_y(): return lax.ppermute(a, 'groups', over_y)  4.14 us
    ppermute x7, waiting for transfers between devices, to_core(): return lax.ppermute(a, 'tensor', over_core)  2.81 us
  transfers between devices with their start and end apart: 22, of which 14 were waited for; matrix products, arithmetic and copies ran while one was open for 0% of the time, Pallas kernels for 14%

profile of v5, /device:TPU:31, one launch (start us, length us, event | category | flops | bytes accessed | tf_op | source)
XLA Modules:
  0.0 72.8 jit_solution(11488359056307850965)
XLA Ops:
  0.0 1.1 %shard_map.46.refs_3_.refs_1_ = bf16[384,512]{1,0:T(8,128)(2,1)S(1)} custom-call(bf16[1,768,1024]{2,1,0:T(8,128)(2,1)} %rows_ref.2), custom_call_target="tpu_custom_call" | custom-call | flops 1 | bytes 1 | tf_op jit(solution)/shard_map/pallas_call | solution.py:187
  1.2 0.7 copy-done
  1.9 2.2 %shard_map.47 = (bf16[4,256,384]{2,1,0:T(8,128)(2,1)S(1)}, bf16[4,256,384]{2,1,0:T(8,128)(2,1)S(1)}, bf16[4,256,384]{2,1,0:T(8,128)(2,1)S(1)}, bf16[4,256,384]{2,1,0:T(8,128)(2,1)S(1)}, f32[256,128]{1,0:T(8,128)S(1)}) custom-call(bf16[256,6144]{1,0:T(8,128)(2,1)} %hidden_ref, bf16[6144]{0:T(1024)(128)(2,1)S(1)} %copy-done), custom_call_target="tpu_custom_call" | custom-call | flops 1 | bytes 1 | tf_op jit(solution)/shard_map/pallas_call | solution.py:228
  4.6 1.1 %shard_map.48.refs_4_ = bf16[384,512]{1,0:T(8,128)(2,1)S(1)} custom-call(bf16[1,768,1024]{2,1,0:T(8,128)(2,1)} %rows_ref.2), custom_call_target="tpu_custom_call" | custom-call | flops 1 | bytes 1 | tf_op jit(solution)/shard_map/pallas_call | solution.py:187
  5.7 1.5 %collective-permute-start.5 = (bf16[384,512]{1,0:T(8,128)(2,1)S(1)}, bf16[384,512]{1,0:T(8,128)(2,1)S(1)}, u32[]{:S(2)}, u32[]{:S(2)}) collective-permute-start(bf16[384,512]{1,0:T(8,128)(2,1)S(1)} %shard_map.46.refs_3_.refs_1_), channel_id=1, source_target_pairs={{4,0},{6,2},{8,4},{10,6},{12,8},{14,10},{0,12},{2,14},{5,1},{7,3},... | collective-permute-start | bytes 1179656 | tf_op jit(solution)/shard_map/ppermute | solution.py:445
  7.2 1.8 %collective-permute-start.1 = (f32[256,128]{1,0:T(8,128)S(1)}, f32[256,128]{1,0:T(8,128)S(1)}, u32[]{:S(2)}, u32[]{:S(2)}) collective-permute-start(f32[256,128]{1,0:T(8,128)S(1)} %get-tuple-element.103._.own_ref), channel_id=1, source_target_pairs={{0,1},{1,0},{2,3},{3,2},{4,5},{5,4},{6,7},{7,6},{8,9},{9,8},{10,11... | collective-permute-start | bytes 393224 | tf_op jit(solution)/shard_map/ppermute | solution.py:439
  9.0 1.1 %shard_map.49 = (f32[256,128]{1,0:T(8,128)S(1)}, f32[256,128]{1,0:T(8,128)S(1)}, f32[256,256]{1,0:T(8,128)S(1)}, f32[256,128]{1,0:T(8,128)S(1)}) custom-call(s32[1,2]{1,0:T(1,128)S(1)} %copy-done.1, f32[256,128]{1,0:T(8,128)S(1)} %get-tuple-element.103._.own_ref), custom_call_target="tpu_custom_call" | custom-call | flops 1 | bytes 1 | tf_op jit(solution)/shard_map/pallas_call | solution.py:326
  10.2 1.2 %collective-permute-done.refs_4_.refs_2_ = bf16[384,512]{1,0:T(8,128)(2,1)S(1)} collective-permute-done((bf16[384,512]{1,0:T(8,128)(2,1)S(1)}, bf16[384,512]{1,0:T(8,128)(2,1)S(1)}, u32[]{:S(2)}, u32[]{:S(2)}) %collective-permute-start) | collective-permute-done | bytes 393248 | tf_op jit(solution)/shard_map/ppermute | solution.py:442
  11.3 1.1 %collective-permute-start.2 = (bf16[4,256,384]{2,1,0:T(8,128)(2,1)S(1)}, bf16[4,256,384]{2,1,0:T(8,128)(2,1)S(1)}, u32[]{:S(2)}, u32[]{:S(2)}) collective-permute-start(bf16[4,256,384]{2,1,0:T(8,128)(2,1)S(1)} %get-tuple-element.111), channel_id=1, source_target_pairs={{0,18},{2,16},{4,22},{6,20},{8,26},{10,24},{12,30},{14,28},{16,2},... | collective-permute-start | bytes 2359304 | tf_op jit(solution)/shard_map/ppermute | solution.py:448
  12.4 1.7 %collective-permute-start.7 = (bf16[384,512]{1,0:T(8,128)(2,1)S(1)}, bf16[384,512]{1,0:T(8,128)(2,1)S(1)}, u32[]{:S(2)}, u32[]{:S(2)}) collective-permute-start(bf16[384,512]{1,0:T(8,128)(2,1)S(1)} %shard_map.48.refs_4_), channel_id=1, source_target_pairs={{0,4},{2,6},{4,8},{6,10},{8,12},{10,14},{12,0},{14,2},{1,5},{3,7},... | collective-permute-start | bytes 1179656 | tf_op jit(solution)/shard_map/ppermute | solution.py:442
  14.2 5.2 %collective-permute-done.5.refs_5_.refs_4_ = bf16[384,512]{1,0:T(8,128)(2,1)S(1)} collective-permute-done((bf16[384,512]{1,0:T(8,128)(2,1)S(1)}, bf16[384,512]{1,0:T(8,128)(2,1)S(1)}, u32[]{:S(2)}, u32[]{:S(2)}) %collective-permute-start.5) | collective-permute-done | bytes 393248 | tf_op jit(solution)/shard_map/ppermute | solution.py:445
  19.4 3.9 %collective-permute-start.6 = (bf16[384,512]{1,0:T(8,128)(2,1)S(1)}, bf16[384,512]{1,0:T(8,128)(2,1)S(1)}, u32[]{:S(2)}, u32[]{:S(2)}) collective-permute-start(bf16[384,512]{1,0:T(8,128)(2,1)S(1)} %collective-permute-done.refs_4_.refs_2_), channel_id=1, source_target_pairs={{0,4},{2,6},{4,8},{6,10},{8,12},{10,14},{12,0},{14,2},{1,5},{3,7},... | collective-permute-start | bytes 1179656 | tf_op jit(solution)/shard_map/ppermute | solution.py:442
  23.3 3.2 %collective-permute-done.7.refs_5_ = bf16[384,512]{1,0:T(8,128)(2,1)S(1)} collective-permute-done((bf16[384,512]{1,0:T(8,128)(2,1)S(1)}, bf16[384,512]{1,0:T(8,128)(2,1)S(1)}, u32[]{:S(2)}, u32[]{:S(2)}) %collective-permute-start.7) | collective-permute-done | bytes 393248 | tf_op jit(solution)/shard_map/ppermute | solution.py:442
  26.5 2.2 %collective-permute-start.9 = (bf16[384,512]{1,0:T(8,128)(2,1)S(1)}, bf16[384,512]{1,0:T(8,128)(2,1)S(1)}, u32[]{:S(2)}, u32[]{:S(2)}) collective-permute-start(bf16[384,512]{1,0:T(8,128)(2,1)S(1)} %collective-permute-done.7.refs_5_), channel_id=1, source_target_pairs={{0,4},{2,6},{4,8},{6,10},{8,12},{10,14},{12,0},{14,2},{1,5},{3,7},... | collective-permute-start | bytes 1179656 | tf_op jit(solution)/shard_map/ppermute | solution.py:442
  28.6 1.4 %shard_map.51.refs_4_ = f32[3,256,512]{2,1,0:T(8,128)S(1)} custom-call(bf16[4,256,384]{2,1,0:T(8,128)(2,1)S(1)} %collective-permute-done.3.refs_0_.refs_2_, bf16[4,256,384]{2,1,0:T(8,128)(2,1)S(1)} %collective-permute-done.4.refs_1_.refs_3_, bf16[4,256,384]{2,1,0:T(8,128)(2,1)S(1)} %get-tuple-element.119.refs_2_.refs_1_, ...), custom_call_target="tpu_custom_call" | custom-call | flops 1 | bytes 1 | tf_op jit(solution)/shard_map/pallas_call | solution.py:279
  30.0 4.9 %collective-permute-done.6.refs_3_ = bf16[384,512]{1,0:T(8,128)(2,1)S(1)} collective-permute-done((bf16[384,512]{1,0:T(8,128)(2,1)S(1)}, bf16[384,512]{1,0:T(8,128)(2,1)S(1)}, u32[]{:S(2)}, u32[]{:S(2)}) %collective-permute-start.6) | collective-permute-done | bytes 393248 | tf_op jit(solution)/shard_map/ppermute | solution.py:442
  35.5 5.8 %collective-permute-start.10 = (bf16[3,256,128]{2,1,0:T(8,128)(2,1)S(1)}, bf16[3,256,128]{2,1,0:T(8,128)(2,1)S(1)}, u32[]{:S(2)}, u32[]{:S(2)}) collective-permute-start(bf16[3,256,128]{2,1,0:T(8,128)(2,1)S(1)} %get-tuple-element.128), channel_id=1, source_target_pairs={{0,1},{1,0},{2,3},{3,2},{4,5},{5,4},{6,7},{7,6},{8,9},{9,8},{10,11... | collective-permute-start | bytes 589832 | tf_op jit(solution)/shard_map/ppermute | solution.py:439
  41.4 0.7 shard_map.53
  43.1 1.8 %collective-permute-start.13 = (bf16[2,256,128]{2,1,0:T(8,128)(2,1)S(1)}, bf16[2,256,128]{2,1,0:T(8,128)(2,1)S(1)}, u32[]{:S(2)}, u32[]{:S(2)}) collective-permute-start(bf16[2,256,128]{2,1,0:T(8,128)(2,1)S(1)} %get-tuple-element.143), channel_id=1, source_target_pairs={{0,16},{16,0},{1,17},{17,1},{2,18},{18,2},{3,19},{19,3},{4,20},{20... | collective-permute-start | bytes 393224 | tf_op jit(solution)/shard_map/ppermute | solution.py:454
  45.2 0.9 %collective-permute-start.15 = (bf16[2,256,128]{2,1,0:T(8,128)(2,1)S(1)}, bf16[2,256,128]{2,1,0:T(8,128)(2,1)S(1)}, u32[]{:S(2)}, u32[]{:S(2)}) collective-permute-start(bf16[2,256,128]{2,1,0:T(8,128)(2,1)S(1)} %shard_map.56), channel_id=1, source_target_pairs={{0,18},{2,16},{4,22},{6,20},{8,26},{10,24},{12,30},{14,28},{16,2},... | collective-permute-start | bytes 393224 | tf_op jit(solution)/shard_map/ppermute | solution.py:448
  46.2 1.8 %shard_map.55.refs_5_ = f32[4,256,512]{2,1,0:T(8,128)S(1)} custom-call(bf16[4,256,384]{2,1,0:T(8,128)(2,1)S(1)} %collective-permute-done.2.refs_0_, bf16[4,256,384]{2,1,0:T(8,128)(2,1)S(1)} %get-tuple-element.119.refs_2_.refs_1_, bf16[4,256,384]{2,1,0:T(8,128)(2,1)S(1)} %collective-permute-done.3.refs_0_.refs_2_, ...), custom_call_target="tpu_custom_call" | custom-call | flops 1 | bytes 1 | tf_op jit(solution)/shard_map/pallas_call | solution.py:279
  47.9 0.7 collective-permute-done.13.r2.refs_3_
  48.6 0.8 %collective-permute-done.12.r1.refs_2_ = bf16[2,256,128]{2,1,0:T(8,128)(2,1)S(1)} collective-permute-done((bf16[2,256,128]{2,1,0:T(8,128)(2,1)S(1)}, bf16[2,256,128]{2,1,0:T(8,128)(2,1)S(1)}, u32[]{:S(2)}, u32[]{:S(2)}) %collective-permute-start.12) | collective-permute-done | bytes 131104 | tf_op jit(solution)/shard_map/ppermute | solution.py:451
  49.4 4.0 %collective-permute-done.8.refs_4_ = bf16[384,512]{1,0:T(8,128)(2,1)S(1)} collective-permute-done((bf16[384,512]{1,0:T(8,128)(2,1)S(1)}, bf16[384,512]{1,0:T(8,128)(2,1)S(1)}, u32[]{:S(2)}, u32[]{:S(2)}) %collective-permute-start.8) | collective-permute-done | bytes 393248 | tf_op jit(solution)/shard_map/ppermute | solution.py:445
  53.4 0.7 shard_map.57
  54.1 6.7 %collective-permute-start.16 = (bf16[4,256,128]{2,1,0:T(8,128)(2,1)S(1)}, bf16[4,256,128]{2,1,0:T(8,128)(2,1)S(1)}, u32[]{:S(2)}, u32[]{:S(2)}) collective-permute-start(bf16[4,256,128]{2,1,0:T(8,128)(2,1)S(1)} %get-tuple-element.157), channel_id=1, source_target_pairs={{0,1},{1,0},{2,3},{3,2},{4,5},{5,4},{6,7},{7,6},{8,9},{9,8},{10,11... | collective-permute-start | bytes 786440 | tf_op jit(solution)/shard_map/ppermute | solution.py:439
  60.9 1.0 %collective-permute-done.16.refs_0_ = bf16[4,256,128]{2,1,0:T(8,128)(2,1)S(1)} collective-permute-done((bf16[4,256,128]{2,1,0:T(8,128)(2,1)S(1)}, bf16[4,256,128]{2,1,0:T(8,128)(2,1)S(1)}, u32[]{:S(2)}, u32[]{:S(2)}) %collective-permute-start.16) | collective-permute-done | bytes 262176 | tf_op jit(solution)/shard_map/ppermute | solution.py:439
  62.4 2.4 %collective-permute-start.21 = (bf16[2,256,128]{2,1,0:T(8,128)(2,1)S(1)}, bf16[2,256,128]{2,1,0:T(8,128)(2,1)S(1)}, u32[]{:S(2)}, u32[]{:S(2)}) collective-permute-start(bf16[2,256,128]{2,1,0:T(8,128)(2,1)S(1)} %get-tuple-element.178), channel_id=1, source_target_pairs={{0,16},{16,0},{1,17},{17,1},{2,18},{18,2},{3,19},{19,3},{4,20},{20... | collective-permute-start | bytes 393224 | tf_op jit(solution)/shard_map/ppermute | solution.py:454
  64.8 1.2 %collective-permute-start.18 = (bf16[256,128]{1,0:T(8,128)(2,1)S(1)}, bf16[256,128]{1,0:T(8,128)(2,1)S(1)}, u32[]{:S(2)}, u32[]{:S(2)}) collective-permute-start(bf16[256,128]{1,0:T(8,128)(2,1)S(1)} %shard_map.58.refs_9_), channel_id=1, source_target_pairs={{0,1},{1,0},{2,3},{3,2},{4,5},{5,4},{6,7},{7,6},{8,9},{9,8},{10,11... | collective-permute-start | bytes 196616 | tf_op jit(solution)/shard_map/ppermute | solution.py:439
  66.0 0.9 %collective-permute-done.18.refs_10_ = bf16[256,128]{1,0:T(8,128)(2,1)S(1)} collective-permute-done((bf16[256,128]{1,0:T(8,128)(2,1)S(1)}, bf16[256,128]{1,0:T(8,128)(2,1)S(1)}, u32[]{:S(2)}, u32[]{:S(2)}) %collective-permute-start.18) | collective-permute-done | bytes 65568 | tf_op jit(solution)/shard_map/ppermute | solution.py:439
  67.7 3.5 %collective-permute-done.21.refs_3_ = bf16[2,256,128]{2,1,0:T(8,128)(2,1)S(1)} collective-permute-done((bf16[2,256,128]{2,1,0:T(8,128)(2,1)S(1)}, bf16[2,256,128]{2,1,0:T(8,128)(2,1)S(1)}, u32[]{:S(2)}, u32[]{:S(2)}) %collective-permute-start.21) | collective-permute-done | bytes 131104 | tf_op jit(solution)/shard_map/ppermute | solution.py:454
  71.2 1.6 %shard_map.62 = bf16[256,384]{1,0:T(8,128)(2,1)} custom-call(f32[2,256,128]{2,1,0:T(8,128)S(1)} %get-tuple-element.166.refs_0_, bf16[2,256,128]{2,1,0:T(8,128)(2,1)S(1)} %collective-permute-done.17.refs_1_, bf16[2,256,128]{2,1,0:T(8,128)(2,1)S(1)} %collective-permute-done.20.refs_2_, bf16[2,256,128]{2,1,0:T(8,128)(2,1)S(1)} %collective-permute-done.21.refs_3_, ...), custom_call_target="tpu_custom_call" | custom-call | flops 1 | bytes 1 | tf_op jit(solution)/shard_map/pallas_call | solution.py:413
  (33 shorter events, 4.1 us)
Async XLA Ops:
  1.1 10.2 %collective-permute-start = (bf16[384,512]{1,0:T(8,128)(2,1)S(1)}, bf16[384,512]{1,0:T(8,128)(2,1)S(1)}, u32[]{:S(2)}, u32[]{:S(2)}) collective-permute-start(bf16[384,512]{1,0:T(8,128)(2,1)S(1)} %shard_map.46.refs_3_.refs_1_), channel_id=1, source_target_pairs={{0,4},{2,6},{4,8},{6,10},{8,12},{10,14},{12,0},{14,2},{1,5},{3,7},... | collective-permute-start | bytes 1179656 | tf_op jit(solution)/shard_map/ppermute | solution.py:442
  1.2 0.7 copy-start
  1.9 7.1 %copy-start.1 = (s32[1,2]{1,0:T(1,128)S(1)}, s32[1,2]{1,0:T(1,128)}, u32[]{:S(2)}) copy-start(s32[1,2]{1,0:T(1,128)} %lengths_ref.1) | copy-start | bytes 28
  4.0 19.2 %collective-permute-start.4 = (bf16[4,256,384]{2,1,0:T(8,128)(2,1)S(1)}, bf16[4,256,384]{2,1,0:T(8,128)(2,1)S(1)}, u32[]{:S(2)}, u32[]{:S(2)}) collective-permute-start(bf16[4,256,384]{2,1,0:T(8,128)(2,1)S(1)} %get-tuple-element.113), channel_id=1, source_target_pairs={{0,16},{16,0},{1,17},{17,1},{2,18},{18,2},{3,19},{19,3},{4,20},{20... | collective-permute-start | bytes 2359304 | tf_op jit(solution)/shard_map/ppermute | solution.py:454
  4.3 18.9 %collective-permute-start.3 = (bf16[4,256,384]{2,1,0:T(8,128)(2,1)S(1)}, bf16[4,256,384]{2,1,0:T(8,128)(2,1)S(1)}, u32[]{:S(2)}, u32[]{:S(2)}) collective-permute-start(bf16[4,256,384]{2,1,0:T(8,128)(2,1)S(1)} %get-tuple-element.112), channel_id=1, source_target_pairs={{0,2},{2,0},{4,6},{6,4},{8,10},{10,8},{12,14},{14,12},{1,3},{3,1},... | collective-permute-start | bytes 2359304 | tf_op jit(solution)/shard_map/ppermute | solution.py:451
  5.7 13.7 %collective-permute-start.5 = (bf16[384,512]{1,0:T(8,128)(2,1)S(1)}, bf16[384,512]{1,0:T(8,128)(2,1)S(1)}, u32[]{:S(2)}, u32[]{:S(2)}) collective-permute-start(bf16[384,512]{1,0:T(8,128)(2,1)S(1)} %shard_map.46.refs_3_.refs_1_), channel_id=1, source_target_pairs={{4,0},{6,2},{8,4},{10,6},{12,8},{14,10},{0,12},{2,14},{5,1},{7,3},... | collective-permute-start | bytes 1179656 | tf_op jit(solution)/shard_map/ppermute | solution.py:445
  7.2 2.9 %collective-permute-start.1 = (f32[256,128]{1,0:T(8,128)S(1)}, f32[256,128]{1,0:T(8,128)S(1)}, u32[]{:S(2)}, u32[]{:S(2)}) collective-permute-start(f32[256,128]{1,0:T(8,128)S(1)} %get-tuple-element.103._.own_ref), channel_id=1, source_target_pairs={{0,1},{1,0},{2,3},{3,2},{4,5},{5,4},{6,7},{7,6},{8,9},{9,8},{10,11... | collective-permute-start | bytes 393224 | tf_op jit(solution)/shard_map/ppermute | solution.py:439
  11.3 30.0 %collective-permute-start.2 = (bf16[4,256,384]{2,1,0:T(8,128)(2,1)S(1)}, bf16[4,256,384]{2,1,0:T(8,128)(2,1)S(1)}, u32[]{:S(2)}, u32[]{:S(2)}) collective-permute-start(bf16[4,256,384]{2,1,0:T(8,128)(2,1)S(1)} %get-tuple-element.111), channel_id=1, source_target_pairs={{0,18},{2,16},{4,22},{6,20},{8,26},{10,24},{12,30},{14,28},{16,2},... | collective-permute-start | bytes 2359304 | tf_op jit(solution)/shard_map/ppermute | solution.py:448
  12.4 14.0 %collective-permute-start.7 = (bf16[384,512]{1,0:T(8,128)(2,1)S(1)}, bf16[384,512]{1,0:T(8,128)(2,1)S(1)}, u32[]{:S(2)}, u32[]{:S(2)}) collective-permute-start(bf16[384,512]{1,0:T(8,128)(2,1)S(1)} %shard_map.48.refs_4_), channel_id=1, source_target_pairs={{0,4},{2,6},{4,8},{6,10},{8,12},{10,14},{12,0},{14,2},{1,5},{3,7},... | collective-permute-start | bytes 1179656 | tf_op jit(solution)/shard_map/ppermute | solution.py:442
  19.4 15.5 %collective-permute-start.6 = (bf16[384,512]{1,0:T(8,128)(2,1)S(1)}, bf16[384,512]{1,0:T(8,128)(2,1)S(1)}, u32[]{:S(2)}, u32[]{:S(2)}) collective-permute-start(bf16[384,512]{1,0:T(8,128)(2,1)S(1)} %collective-permute-done.refs_4_.refs_2_), channel_id=1, source_target_pairs={{0,4},{2,6},{4,8},{6,10},{8,12},{10,14},{12,0},{14,2},{1,5},{3,7},... | collective-permute-start | bytes 1179656 | tf_op jit(solution)/shard_map/ppermute | solution.py:442
  26.5 18.7 %collective-permute-start.9 = (bf16[384,512]{1,0:T(8,128)(2,1)S(1)}, bf16[384,512]{1,0:T(8,128)(2,1)S(1)}, u32[]{:S(2)}, u32[]{:S(2)}) collective-permute-start(bf16[384,512]{1,0:T(8,128)(2,1)S(1)} %collective-permute-done.7.refs_5_), channel_id=1, source_target_pairs={{0,4},{2,6},{4,8},{6,10},{8,12},{10,14},{12,0},{14,2},{1,5},{3,7},... | collective-permute-start | bytes 1179656 | tf_op jit(solution)/shard_map/ppermute | solution.py:442
  35.5 6.9 %collective-permute-start.10 = (bf16[3,256,128]{2,1,0:T(8,128)(2,1)S(1)}, bf16[3,256,128]{2,1,0:T(8,128)(2,1)S(1)}, u32[]{:S(2)}, u32[]{:S(2)}) collective-permute-start(bf16[3,256,128]{2,1,0:T(8,128)(2,1)S(1)} %get-tuple-element.128), channel_id=1, source_target_pairs={{0,1},{1,0},{2,3},{3,2},{4,5},{5,4},{6,7},{7,6},{8,9},{9,8},{10,11... | collective-permute-start | bytes 589832 | tf_op jit(solution)/shard_map/ppermute | solution.py:439
  41.3 1.4 %collective-permute-start.11 = (bf16[3,256,128]{2,1,0:T(8,128)(2,1)S(1)}, bf16[3,256,128]{2,1,0:T(8,128)(2,1)S(1)}, u32[]{:S(2)}, u32[]{:S(2)}) collective-permute-start(bf16[3,256,128]{2,1,0:T(8,128)(2,1)S(1)} %get-tuple-element.134), channel_id=1, source_target_pairs={{0,1},{1,0},{2,3},{3,2},{4,5},{5,4},{6,7},{7,6},{8,9},{9,8},{10,11... | collective-permute-start | bytes 589832 | tf_op jit(solution)/shard_map/ppermute | solution.py:439
  41.3 12.1 %collective-permute-start.8 = (bf16[384,512]{1,0:T(8,128)(2,1)S(1)}, bf16[384,512]{1,0:T(8,128)(2,1)S(1)}, u32[]{:S(2)}, u32[]{:S(2)}) collective-permute-start(bf16[384,512]{1,0:T(8,128)(2,1)S(1)} %shard_map.48.refs_4_), channel_id=1, source_target_pairs={{4,0},{6,2},{8,4},{10,6},{12,8},{14,10},{0,12},{2,14},{5,1},{7,3},... | collective-permute-start | bytes 1179656 | tf_op jit(solution)/shard_map/ppermute | solution.py:445
  42.8 2.4 %collective-permute-start.14 = (bf16[2,256,128]{2,1,0:T(8,128)(2,1)S(1)}, bf16[2,256,128]{2,1,0:T(8,128)(2,1)S(1)}, u32[]{:S(2)}, u32[]{:S(2)}) collective-permute-start(bf16[2,256,128]{2,1,0:T(8,128)(2,1)S(1)} %get-tuple-element.141), channel_id=1, source_target_pairs={{0,1},{1,0},{2,3},{3,2},{4,5},{5,4},{6,7},{7,6},{8,9},{9,8},{10,11... | collective-permute-start | bytes 393224 | tf_op jit(solution)/shard_map/ppermute | solution.py:439
  43.1 5.5 %collective-permute-start.13 = (bf16[2,256,128]{2,1,0:T(8,128)(2,1)S(1)}, bf16[2,256,128]{2,1,0:T(8,128)(2,1)S(1)}, u32[]{:S(2)}, u32[]{:S(2)}) collective-permute-start(bf16[2,256,128]{2,1,0:T(8,128)(2,1)S(1)} %get-tuple-element.143), channel_id=1, source_target_pairs={{0,16},{16,0},{1,17},{17,1},{2,18},{18,2},{3,19},{19,3},{4,20},{20... | collective-permute-start | bytes 393224 | tf_op jit(solution)/shard_map/ppermute | solution.py:454
  44.9 4.6 %collective-permute-start.12 = (bf16[2,256,128]{2,1,0:T(8,128)(2,1)S(1)}, bf16[2,256,128]{2,1,0:T(8,128)(2,1)S(1)}, u32[]{:S(2)}, u32[]{:S(2)}) collective-permute-start(bf16[2,256,128]{2,1,0:T(8,128)(2,1)S(1)} %get-tuple-element.140), channel_id=1, source_target_pairs={{0,2},{2,0},{4,6},{6,4},{8,10},{10,8},{12,14},{14,12},{1,3},{3,1},... | collective-permute-start | bytes 393224 | tf_op jit(solution)/shard_map/ppermute | solution.py:451
  45.2 8.9 %collective-permute-start.15 = (bf16[2,256,128]{2,1,0:T(8,128)(2,1)S(1)}, bf16[2,256,128]{2,1,0:T(8,128)(2,1)S(1)}, u32[]{:S(2)}, u32[]{:S(2)}) collective-permute-start(bf16[2,256,128]{2,1,0:T(8,128)(2,1)S(1)} %shard_map.56), channel_id=1, source_target_pairs={{0,18},{2,16},{4,22},{6,20},{8,26},{10,24},{12,30},{14,28},{16,2},... | collective-permute-start | bytes 393224 | tf_op jit(solution)/shard_map/ppermute | solution.py:448
  54.1 7.8 %collective-permute-start.16 = (bf16[4,256,128]{2,1,0:T(8,128)(2,1)S(1)}, bf16[4,256,128]{2,1,0:T(8,128)(2,1)S(1)}, u32[]{:S(2)}, u32[]{:S(2)}) collective-permute-start(bf16[4,256,128]{2,1,0:T(8,128)(2,1)S(1)} %get-tuple-element.157), channel_id=1, source_target_pairs={{0,1},{1,0},{2,3},{3,2},{4,5},{5,4},{6,7},{7,6},{8,9},{9,8},{10,11... | collective-permute-start | bytes 786440 | tf_op jit(solution)/shard_map/ppermute | solution.py:439
  60.8 1.5 %collective-permute-start.19 = (bf16[4,256,128]{2,1,0:T(8,128)(2,1)S(1)}, bf16[4,256,128]{2,1,0:T(8,128)(2,1)S(1)}, u32[]{:S(2)}, u32[]{:S(2)}) collective-permute-start(bf16[4,256,128]{2,1,0:T(8,128)(2,1)S(1)} %get-tuple-element.170), channel_id=1, source_target_pairs={{0,1},{1,0},{2,3},{3,2},{4,5},{5,4},{6,7},{7,6},{8,9},{9,8},{10,11... | collective-permute-start | bytes 786440 | tf_op jit(solution)/shard_map/ppermute | solution.py:439
  62.0 5.7 %collective-permute-start.17 = (bf16[2,256,128]{2,1,0:T(8,128)(2,1)S(1)}, bf16[2,256,128]{2,1,0:T(8,128)(2,1)S(1)}, u32[]{:S(2)}, u32[]{:S(2)}) collective-permute-start(bf16[2,256,128]{2,1,0:T(8,128)(2,1)S(1)} %get-tuple-element.167), channel_id=1, source_target_pairs={{0,18},{2,16},{4,22},{6,20},{8,26},{10,24},{12,30},{14,28},{16,2},... | collective-permute-start | bytes 393224 | tf_op jit(solution)/shard_map/ppermute | solution.py:448
  62.4 5.3 %collective-permute-start.20 = (bf16[2,256,128]{2,1,0:T(8,128)(2,1)S(1)}, bf16[2,256,128]{2,1,0:T(8,128)(2,1)S(1)}, u32[]{:S(2)}, u32[]{:S(2)}) collective-permute-start(bf16[2,256,128]{2,1,0:T(8,128)(2,1)S(1)} %get-tuple-element.174), channel_id=1, source_target_pairs={{0,2},{2,0},{4,6},{6,4},{8,10},{10,8},{12,14},{14,12},{1,3},{3,1},... | collective-permute-start | bytes 393224 | tf_op jit(solution)/shard_map/ppermute | solution.py:451
  62.4 8.7 %collective-permute-start.21 = (bf16[2,256,128]{2,1,0:T(8,128)(2,1)S(1)}, bf16[2,256,128]{2,1,0:T(8,128)(2,1)S(1)}, u32[]{:S(2)}, u32[]{:S(2)}) collective-permute-start(bf16[2,256,128]{2,1,0:T(8,128)(2,1)S(1)} %get-tuple-element.178), channel_id=1, source_target_pairs={{0,16},{16,0},{1,17},{17,1},{2,18},{18,2},{3,19},{19,3},{4,20},{20... | collective-permute-start | bytes 393224 | tf_op jit(solution)/shard_map/ppermute | solution.py:454
  64.8 2.1 %collective-permute-start.18 = (bf16[256,128]{1,0:T(8,128)(2,1)S(1)}, bf16[256,128]{1,0:T(8,128)(2,1)S(1)}, u32[]{:S(2)}, u32[]{:S(2)}) collective-permute-start(bf16[256,128]{1,0:T(8,128)(2,1)S(1)} %shard_map.58.refs_9_), channel_id=1, source_target_pairs={{0,1},{1,0},{2,3},{3,2},{4,5},{5,4},{6,7},{7,6},{8,9},{9,8},{10,11... | collective-permute-start | bytes 196616 | tf_op jit(solution)/shard_map/ppermute | solution.py:439

commit v6 on v5

--- a/solution.py
+++ b/solution.py
@@ -385,21 +385,24 @@
     for earlier_ref in earlier_refs:
         put(earlier_ref, before)
         before += earlier_ref.shape[1]
-    for i in range(first, parts[0].shape[0]):
-        query = turned(summed(parts, i, scale_ref), cosine_ref, sine_ref).astype(jnp.bfloat16)
-        scores = lax.dot_general(
-            query, keys, (((1,), (1,)), ((), ())), preferred_element_type=jnp.float32
-        ) * HEAD ** (-0.5)
-        scores = jnp.where(allowed_ref[...] > 0.0, scores, -1e30)
-        expo = jnp.exp(scores - jnp.max(scores, axis=-1, keepdims=True))
-        attn = (expo / jnp.sum(expo, axis=-1, keepdims=True)).astype(jnp.bfloat16)
-        mixed = jnp.dot(attn, values, preferred_element_type=jnp.float32)
-        done = (mixed * keep_ref[...]).astype(jnp.bfloat16)
+    tokens = mine.shape[0]
+    count = parts[0].shape[0] - first
+    query = [turned(summed(parts, first + i, scale_ref), cosine_ref, sine_ref).astype(jnp.bfloat16) for i in range(count)]
+    scores = lax.dot_general(
+        jnp.concatenate(query, axis=0), keys, (((1,), (1,)), ((), ())), preferred_element_type=jnp.float32
+    ) * HEAD ** (-0.5)
+    allowed = jnp.concatenate([allowed_ref[...] > 0.0] * count, axis=0)
+    scores = jnp.where(allowed, scores, -1e30)
+    expo = jnp.exp(scores - jnp.max(scores, axis=-1, keepdims=True))
+    attn = (expo * (1.0 / jnp.sum(expo, axis=-1, keepdims=True))).astype(jnp.bfloat16)
+    mixed = jnp.dot(attn, values, preferred_element_type=jnp.float32)
+    for i in range(count):
+        done = (mixed[i * tokens:(i + 1) * tokens] * keep_ref[...]).astype(jnp.bfloat16)
         if scratch is None:
-            out_ref[:, (i - first) * HEAD:(i - first + 1) * HEAD] = done
+            out_ref[:, i * HEAD:(i + 1) * HEAD] = done
         else:
-            scratch[i - first] = done
-            put(scratch.at[i - first], before + (i - first) * HEAD)
+            scratch[i] = done
+            put(scratch.at[i], before + i * HEAD)
     for copy in copies:
         copy.wait()
 
@@ -490,13 +493,13 @@
     b2 = on_ring(b1)
     early = (near_x, near_y, own)
     front = after(matmul(early, (a0, a1, a3), (0, 1, 3)))
-    a2, b0 = after(a2, b0)
-    b3 = back(b0)
+    a2 = after(a2)
     set_a = (a0, a1, a2, a3)
 
     *theirs, mine = after(*matmul(early, (a2,), (2,), (front,), sent=2))
     swapped = [to_core(t) for t in theirs]
-    far = after(far)
+    far, b0 = after(far, b0)
+    b3 = back(b0)
     sums_x, sums_y, sums = after(*join(mine, after(*swapped), (jnp.bfloat16, jnp.bfloat16, jnp.float32)))
     sums_x = to_x(sums_x)
     sums_y = to_y(sums_y)

time: 73 us -> 72 us (0.986)
  the two profiles are of different devices: /device:TPU:31 before, /device:TPU:0 now
where the time goes in v6:
time: 72 us; the launch traced here: 71.8 us
  waiting for transfers between devices  32.8 us (46%)
  starting transfers between devices  25.3 us (35%)
  Pallas kernels  12.8 us (18%)
    ppermute x4, waiting for transfers between devices, on_ring(): return lax.ppermute(a, 'dp', ring)  16 us
    ppermute x2, waiting for transfers between devices, back(): return lax.ppermute(a, 'dp', [(j, i) for i, j in ring])  6.79 us
    ppermute x3, starting transfers between devices, to_far(): return lax.ppermute(a, ('groups', 'dp'), across)  6.47 us
    ppermute x4, starting transfers between devices, on_ring(): return lax.ppermute(a, 'dp', ring)  6.08 us
    pallas_call x5, Pallas kernels, matmul(): call(functools.partial(matmul_kernel, firsts, len(acts), len(so_far), sen...  5.11 us
    ppermute x2, starting transfers between devices, back(): return lax.ppermute(a, 'dp', [(j, i) for i, j in ring])  4.32 us
    ppermute x3, waiting for transfers between devices, to_x(): return lax.ppermute(a, 'dp', over_x)  3.97 us
    ppermute x3, starting transfers between devices, to_y(): return lax.ppermute(a, 'groups', over_y)  3.66 us
  transfers between devices with their start and end apart: 22, of which 14 were waited for; matrix products, arithmetic and copies ran while one was open for 0% of the time, Pallas kernels for 14%

profile of v6, /device:TPU:0, one launch (start us, length us, event | category | flops | bytes accessed | tf_op | source)
XLA Modules:
  0.0 71.8 jit_solution(11705143882214241799)
XLA Ops:
  0.0 1.1 %shard_map.46.refs_3_.refs_1_ = bf16[384,512]{1,0:T(8,128)(2,1)S(1)} custom-call(bf16[1,768,1024]{2,1,0:T(8,128)(2,1)} %rows_ref.2), custom_call_target="tpu_custom_call" | custom-call | flops 1 | bytes 1 | tf_op jit(solution)/shard_map/pallas_call | solution.py:187
  1.1 3.1 %collective-permute-start = (bf16[384,512]{1,0:T(8,128)(2,1)S(1)}, bf16[384,512]{1,0:T(8,128)(2,1)S(1)}, u32[]{:S(2)}, u32[]{:S(2)}) collective-permute-start(bf16[384,512]{1,0:T(8,128)(2,1)S(1)} %shard_map.46.refs_3_.refs_1_), channel_id=1, source_target_pairs={{0,4},{2,6},{4,8},{6,10},{8,12},{10,14},{12,0},{14,2},{1,5},{3,7},... | collective-permute-start | bytes 1179656 | tf_op jit(solution)/shard_map/ppermute | solution.py:445
  4.2 0.7 copy-done
  4.9 2.2 %shard_map.47 = (bf16[4,256,384]{2,1,0:T(8,128)(2,1)S(1)}, bf16[4,256,384]{2,1,0:T(8,128)(2,1)S(1)}, bf16[4,256,384]{2,1,0:T(8,128)(2,1)S(1)}, bf16[4,256,384]{2,1,0:T(8,128)(2,1)S(1)}, f32[256,128]{1,0:T(8,128)S(1)}) custom-call(bf16[256,6144]{1,0:T(8,128)(2,1)} %hidden_ref, bf16[6144]{0:T(1024)(128)(2,1)S(1)} %copy-done), custom_call_target="tpu_custom_call" | custom-call | flops 1 | bytes 1 | tf_op jit(solution)/shard_map/pallas_call | solution.py:228
  7.0 1.6 %collective-permute-start.4 = (bf16[4,256,384]{2,1,0:T(8,128)(2,1)S(1)}, bf16[4,256,384]{2,1,0:T(8,128)(2,1)S(1)}, u32[]{:S(2)}, u32[]{:S(2)}) collective-permute-start(bf16[4,256,384]{2,1,0:T(8,128)(2,1)S(1)} %get-tuple-element.114), channel_id=1, source_target_pairs={{0,16},{16,0},{1,17},{17,1},{2,18},{18,2},{3,19},{19,3},{4,20},{20... | collective-permute-start | bytes 2359304 | tf_op jit(solution)/shard_map/ppermute | solution.py:457
  8.6 1.5 %collective-permute-start.3 = (bf16[4,256,384]{2,1,0:T(8,128)(2,1)S(1)}, bf16[4,256,384]{2,1,0:T(8,128)(2,1)S(1)}, u32[]{:S(2)}, u32[]{:S(2)}) collective-permute-start(bf16[4,256,384]{2,1,0:T(8,128)(2,1)S(1)} %get-tuple-element.113), channel_id=1, source_target_pairs={{0,2},{2,0},{4,6},{6,4},{8,10},{10,8},{12,14},{14,12},{1,3},{3,1},... | collective-permute-start | bytes 2359304 | tf_op jit(solution)/shard_map/ppermute | solution.py:454
  10.1 1.1 %shard_map.48.refs_4_ = bf16[384,512]{1,0:T(8,128)(2,1)S(1)} custom-call(bf16[1,768,1024]{2,1,0:T(8,128)(2,1)} %rows_ref.2), custom_call_target="tpu_custom_call" | custom-call | flops 1 | bytes 1 | tf_op jit(solution)/shard_map/pallas_call | solution.py:187
  11.2 2.3 %collective-permute-start.5 = (bf16[384,512]{1,0:T(8,128)(2,1)S(1)}, bf16[384,512]{1,0:T(8,128)(2,1)S(1)}, u32[]{:S(2)}, u32[]{:S(2)}) collective-permute-start(bf16[384,512]{1,0:T(8,128)(2,1)S(1)} %shard_map.46.refs_3_.refs_1_), channel_id=1, source_target_pairs={{4,0},{6,2},{8,4},{10,6},{12,8},{14,10},{0,12},{2,14},{5,1},{7,3},... | collective-permute-start | bytes 1179656 | tf_op jit(solution)/shard_map/ppermute | solution.py:448
  13.5 1.1 %shard_map.49 = (f32[256,128]{1,0:T(8,128)S(1)}, f32[256,128]{1,0:T(8,128)S(1)}, f32[256,256]{1,0:T(8,128)S(1)}, f32[256,128]{1,0:T(8,128)S(1)}) custom-call(s32[1,2]{1,0:T(1,128)S(1)} %copy-done.1, f32[256,128]{1,0:T(8,128)S(1)} %get-tuple-element.103._.own_ref), custom_call_target="tpu_custom_call" | custom-call | flops 1 | bytes 1 | tf_op jit(solution)/shard_map/pallas_call | solution.py:326
  15.4 3.4 %collective-permute-start.2 = (bf16[4,256,384]{2,1,0:T(8,128)(2,1)S(1)}, bf16[4,256,384]{2,1,0:T(8,128)(2,1)S(1)}, u32[]{:S(2)}, u32[]{:S(2)}) collective-permute-start(bf16[4,256,384]{2,1,0:T(8,128)(2,1)S(1)} %get-tuple-element.111), channel_id=1, source_target_pairs={{0,18},{2,16},{4,22},{6,20},{8,26},{10,24},{12,30},{14,28},{16,2},... | collective-permute-start | bytes 2359304 | tf_op jit(solution)/shard_map/ppermute | solution.py:451
  18.8 4.9 %collective-permute-done.5.refs_5_.refs_4_ = bf16[384,512]{1,0:T(8,128)(2,1)S(1)} collective-permute-done((bf16[384,512]{1,0:T(8,128)(2,1)S(1)}, bf16[384,512]{1,0:T(8,128)(2,1)S(1)}, u32[]{:S(2)}, u32[]{:S(2)}) %collective-permute-start.5) | collective-permute-done | bytes 393248 | tf_op jit(solution)/shard_map/ppermute | solution.py:448
  23.7 3.0 %collective-permute-start.6 = (bf16[384,512]{1,0:T(8,128)(2,1)S(1)}, bf16[384,512]{1,0:T(8,128)(2,1)S(1)}, u32[]{:S(2)}, u32[]{:S(2)}) collective-permute-start(bf16[384,512]{1,0:T(8,128)(2,1)S(1)} %collective-permute-done.refs_4_.refs_2_), channel_id=1, source_target_pairs={{0,4},{2,6},{4,8},{6,10},{8,12},{10,14},{12,0},{14,2},{1,5},{3,7},... | collective-permute-start | bytes 1179656 | tf_op jit(solution)/shard_map/ppermute | solution.py:445
  26.7 2.2 %collective-permute-done.3.refs_0_.refs_2_ = bf16[4,256,384]{2,1,0:T(8,128)(2,1)S(1)} collective-permute-done((bf16[4,256,384]{2,1,0:T(8,128)(2,1)S(1)}, bf16[4,256,384]{2,1,0:T(8,128)(2,1)S(1)}, u32[]{:S(2)}, u32[]{:S(2)}) %collective-permute-start.3) | collective-permute-done | bytes 786464 | tf_op jit(solution)/shard_map/ppermute | solution.py:454
  29.0 8.4 %collective-permute-done.7.refs_5_ = bf16[384,512]{1,0:T(8,128)(2,1)S(1)} collective-permute-done((bf16[384,512]{1,0:T(8,128)(2,1)S(1)}, bf16[384,512]{1,0:T(8,128)(2,1)S(1)}, u32[]{:S(2)}, u32[]{:S(2)}) %collective-permute-start.7) | collective-permute-done | bytes 393248 | tf_op jit(solution)/shard_map/ppermute | solution.py:445
  37.3 1.4 %shard_map.51.refs_4_ = f32[3,256,512]{2,1,0:T(8,128)S(1)} custom-call(bf16[4,256,384]{2,1,0:T(8,128)(2,1)S(1)} %collective-permute-done.3.refs_0_.refs_2_, bf16[4,256,384]{2,1,0:T(8,128)(2,1)S(1)} %collective-permute-done.4.refs_1_.refs_3_, bf16[4,256,384]{2,1,0:T(8,128)(2,1)S(1)} %get-tuple-element.120.refs_2_.refs_1_, ...), custom_call_target="tpu_custom_call" | custom-call | flops 1 | bytes 1 | tf_op jit(solution)/shard_map/pallas_call | solution.py:279
  38.7 6.9 %collective-permute-done.6.refs_3_ = bf16[384,512]{1,0:T(8,128)(2,1)S(1)} collective-permute-done((bf16[384,512]{1,0:T(8,128)(2,1)S(1)}, bf16[384,512]{1,0:T(8,128)(2,1)S(1)}, u32[]{:S(2)}, u32[]{:S(2)}) %collective-permute-start.6) | collective-permute-done | bytes 393248 | tf_op jit(solution)/shard_map/ppermute | solution.py:445
  46.8 2.0 %collective-permute-start.8 = (bf16[384,512]{1,0:T(8,128)(2,1)S(1)}, bf16[384,512]{1,0:T(8,128)(2,1)S(1)}, u32[]{:S(2)}, u32[]{:S(2)}) collective-permute-start(bf16[384,512]{1,0:T(8,128)(2,1)S(1)} %shard_map.48.refs_4_), channel_id=1, source_target_pairs={{4,0},{6,2},{8,4},{10,6},{12,8},{14,10},{0,12},{2,14},{5,1},{7,3},... | collective-permute-start | bytes 1179656 | tf_op jit(solution)/shard_map/ppermute | solution.py:448
  48.8 0.7 shard_map.53
  50.1 1.5 %collective-permute-start.12 = (bf16[2,256,128]{2,1,0:T(8,128)(2,1)S(1)}, bf16[2,256,128]{2,1,0:T(8,128)(2,1)S(1)}, u32[]{:S(2)}, u32[]{:S(2)}) collective-permute-start(bf16[2,256,128]{2,1,0:T(8,128)(2,1)S(1)} %get-tuple-element.140), channel_id=1, source_target_pairs={{0,2},{2,0},{4,6},{6,4},{8,10},{10,8},{12,14},{14,12},{1,3},{3,1},... | collective-permute-start | bytes 393224 | tf_op jit(solution)/shard_map/ppermute | solution.py:454
  51.6 1.7 %collective-permute-start.15 = (bf16[2,256,128]{2,1,0:T(8,128)(2,1)S(1)}, bf16[2,256,128]{2,1,0:T(8,128)(2,1)S(1)}, u32[]{:S(2)}, u32[]{:S(2)}) collective-permute-start(bf16[2,256,128]{2,1,0:T(8,128)(2,1)S(1)} %shard_map.56), channel_id=1, source_target_pairs={{0,18},{2,16},{4,22},{6,20},{8,26},{10,24},{12,30},{14,28},{16,2},... | collective-permute-start | bytes 393224 | tf_op jit(solution)/shard_map/ppermute | solution.py:451
  53.3 1.8 %shard_map.55.refs_5_ = f32[4,256,512]{2,1,0:T(8,128)S(1)} custom-call(bf16[4,256,384]{2,1,0:T(8,128)(2,1)S(1)} %collective-permute-done.2.refs_0_, bf16[4,256,384]{2,1,0:T(8,128)(2,1)S(1)} %get-tuple-element.120.refs_2_.refs_1_, bf16[4,256,384]{2,1,0:T(8,128)(2,1)S(1)} %collective-permute-done.3.refs_0_.refs_2_, ...), custom_call_target="tpu_custom_call" | custom-call | flops 1 | bytes 1 | tf_op jit(solution)/shard_map/pallas_call | solution.py:279
  55.6 0.8 %collective-permute-done.12.r1.refs_2_ = bf16[2,256,128]{2,1,0:T(8,128)(2,1)S(1)} collective-permute-done((bf16[2,256,128]{2,1,0:T(8,128)(2,1)S(1)}, bf16[2,256,128]{2,1,0:T(8,128)(2,1)S(1)}, u32[]{:S(2)}, u32[]{:S(2)}) %collective-permute-start.12) | collective-permute-done | bytes 131104 | tf_op jit(solution)/shard_map/ppermute | solution.py:454
  56.4 1.9 %collective-permute-done.8.refs_4_ = bf16[384,512]{1,0:T(8,128)(2,1)S(1)} collective-permute-done((bf16[384,512]{1,0:T(8,128)(2,1)S(1)}, bf16[384,512]{1,0:T(8,128)(2,1)S(1)}, u32[]{:S(2)}, u32[]{:S(2)}) %collective-permute-start.8) | collective-permute-done | bytes 393248 | tf_op jit(solution)/shard_map/ppermute | solution.py:448
  58.3 0.7 shard_map.57
  60.2 0.9 %collective-permute-done.16.refs_0_ = bf16[4,256,128]{2,1,0:T(8,128)(2,1)S(1)} collective-permute-done((bf16[4,256,128]{2,1,0:T(8,128)(2,1)S(1)}, bf16[4,256,128]{2,1,0:T(8,128)(2,1)S(1)}, u32[]{:S(2)}, u32[]{:S(2)}) %collective-permute-start.16) | collective-permute-done | bytes 262176 | tf_op jit(solution)/shard_map/ppermute | solution.py:442
  61.1 1.4 %collective-permute-start.17 = (bf16[2,256,128]{2,1,0:T(8,128)(2,1)S(1)}, bf16[2,256,128]{2,1,0:T(8,128)(2,1)S(1)}, u32[]{:S(2)}, u32[]{:S(2)}) collective-permute-start(bf16[2,256,128]{2,1,0:T(8,128)(2,1)S(1)} %get-tuple-element.167), channel_id=1, source_target_pairs={{0,18},{2,16},{4,22},{6,20},{8,26},{10,24},{12,30},{14,28},{16,2},... | collective-permute-start | bytes 393224 | tf_op jit(solution)/shard_map/ppermute | solution.py:451
  63.1 1.7 %collective-permute-start.21 = (bf16[2,256,128]{2,1,0:T(8,128)(2,1)S(1)}, bf16[2,256,128]{2,1,0:T(8,128)(2,1)S(1)}, u32[]{:S(2)}, u32[]{:S(2)}) collective-permute-start(bf16[2,256,128]{2,1,0:T(8,128)(2,1)S(1)} %get-tuple-element.178), channel_id=1, source_target_pairs={{0,16},{16,0},{1,17},{17,1},{2,18},{18,2},{3,19},{19,3},{4,20},{20... | collective-permute-start | bytes 393224 | tf_op jit(solution)/shard_map/ppermute | solution.py:457
  64.8 1.3 %collective-permute-done.18.refs_10_ = bf16[256,128]{1,0:T(8,128)(2,1)S(1)} collective-permute-done((bf16[256,128]{1,0:T(8,128)(2,1)S(1)}, bf16[256,128]{1,0:T(8,128)(2,1)S(1)}, u32[]{:S(2)}, u32[]{:S(2)}) %collective-permute-start.18) | collective-permute-done | bytes 65568 | tf_op jit(solution)/shard_map/ppermute | solution.py:442
  66.7 1.8 %collective-permute-done.17.refs_1_ = bf16[2,256,128]{2,1,0:T(8,128)(2,1)S(1)} collective-permute-done((bf16[2,256,128]{2,1,0:T(8,128)(2,1)S(1)}, bf16[2,256,128]{2,1,0:T(8,128)(2,1)S(1)}, u32[]{:S(2)}, u32[]{:S(2)}) %collective-permute-start.17) | collective-permute-done | bytes 131104 | tf_op jit(solution)/shard_map/ppermute | solution.py:451
  68.5 0.9 %collective-permute-done.20.refs_2_ = bf16[2,256,128]{2,1,0:T(8,128)(2,1)S(1)} collective-permute-done((bf16[2,256,128]{2,1,0:T(8,128)(2,1)S(1)}, bf16[2,256,128]{2,1,0:T(8,128)(2,1)S(1)}, u32[]{:S(2)}, u32[]{:S(2)}) %collective-permute-start.20) | collective-permute-done | bytes 131104 | tf_op jit(solution)/shard_map/ppermute | solution.py:454
  69.3 1.1 %collective-permute-done.21.refs_3_ = bf16[2,256,128]{2,1,0:T(8,128)(2,1)S(1)} collective-permute-done((bf16[2,256,128]{2,1,0:T(8,128)(2,1)S(1)}, bf16[2,256,128]{2,1,0:T(8,128)(2,1)S(1)}, u32[]{:S(2)}, u32[]{:S(2)}) %collective-permute-start.21) | collective-permute-done | bytes 131104 | tf_op jit(solution)/shard_map/ppermute | solution.py:457
  70.5 1.4 %shard_map.62 = bf16[256,384]{1,0:T(8,128)(2,1)} custom-call(f32[2,256,128]{2,1,0:T(8,128)S(1)} %get-tuple-element.166.refs_0_, bf16[2,256,128]{2,1,0:T(8,128)(2,1)S(1)} %collective-permute-done.17.refs_1_, bf16[2,256,128]{2,1,0:T(8,128)(2,1)S(1)} %collective-permute-done.20.refs_2_, bf16[2,256,128]{2,1,0:T(8,128)(2,1)S(1)} %collective-permute-done.21.refs_3_, ...), custom_call_target="tpu_custom_call" | custom-call | flops 1 | bytes 1 | tf_op jit(solution)/shard_map/pallas_call | solution.py:416
  (33 shorter events, 5.5 us)
Async XLA Ops:
  1.1 14.3 %collective-permute-start = (bf16[384,512]{1,0:T(8,128)(2,1)S(1)}, bf16[384,512]{1,0:T(8,128)(2,1)S(1)}, u32[]{:S(2)}, u32[]{:S(2)}) collective-permute-start(bf16[384,512]{1,0:T(8,128)(2,1)S(1)} %shard_map.46.refs_3_.refs_1_), channel_id=1, source_target_pairs={{0,4},{2,6},{4,8},{6,10},{8,12},{10,14},{12,0},{14,2},{1,5},{3,7},... | collective-permute-start | bytes 1179656 | tf_op jit(solution)/shard_map/ppermute | solution.py:445
  4.2 0.7 copy-start
  4.9 8.6 %copy-start.1 = (s32[1,2]{1,0:T(1,128)S(1)}, s32[1,2]{1,0:T(1,128)}, u32[]{:S(2)}) copy-start(s32[1,2]{1,0:T(1,128)} %lengths_ref.1) | copy-start | bytes 28
  7.0 19.7 %collective-permute-start.4 = (bf16[4,256,384]{2,1,0:T(8,128)(2,1)S(1)}, bf16[4,256,384]{2,1,0:T(8,128)(2,1)S(1)}, u32[]{:S(2)}, u32[]{:S(2)}) collective-permute-start(bf16[4,256,384]{2,1,0:T(8,128)(2,1)S(1)} %get-tuple-element.114), channel_id=1, source_target_pairs={{0,16},{16,0},{1,17},{17,1},{2,18},{18,2},{3,19},{19,3},{4,20},{20... | collective-permute-start | bytes 2359304 | tf_op jit(solution)/shard_map/ppermute | solution.py:457
  8.6 6.0 %collective-permute-start.1 = (f32[256,128]{1,0:T(8,128)S(1)}, f32[256,128]{1,0:T(8,128)S(1)}, u32[]{:S(2)}, u32[]{:S(2)}) collective-permute-start(f32[256,128]{1,0:T(8,128)S(1)} %get-tuple-element.103._.own_ref), channel_id=1, source_target_pairs={{0,1},{1,0},{2,3},{3,2},{4,5},{5,4},{6,7},{7,6},{8,9},{9,8},{10,11... | collective-permute-start | bytes 393224 | tf_op jit(solution)/shard_map/ppermute | solution.py:442
  8.6 20.3 %collective-permute-start.3 = (bf16[4,256,384]{2,1,0:T(8,128)(2,1)S(1)}, bf16[4,256,384]{2,1,0:T(8,128)(2,1)S(1)}, u32[]{:S(2)}, u32[]{:S(2)}) collective-permute-start(bf16[4,256,384]{2,1,0:T(8,128)(2,1)S(1)} %get-tuple-element.113), channel_id=1, source_target_pairs={{0,2},{2,0},{4,6},{6,4},{8,10},{10,8},{12,14},{14,12},{1,3},{3,1},... | collective-permute-start | bytes 2359304 | tf_op jit(solution)/shard_map/ppermute | solution.py:454
  11.2 12.5 %collective-permute-start.5 = (bf16[384,512]{1,0:T(8,128)(2,1)S(1)}, bf16[384,512]{1,0:T(8,128)(2,1)S(1)}, u32[]{:S(2)}, u32[]{:S(2)}) collective-permute-start(bf16[384,512]{1,0:T(8,128)(2,1)S(1)} %shard_map.46.refs_3_.refs_1_), channel_id=1, source_target_pairs={{4,0},{6,2},{8,4},{10,6},{12,8},{14,10},{0,12},{2,14},{5,1},{7,3},... | collective-permute-start | bytes 1179656 | tf_op jit(solution)/shard_map/ppermute | solution.py:448
  15.4 31.4 %collective-permute-start.2 = (bf16[4,256,384]{2,1,0:T(8,128)(2,1)S(1)}, bf16[4,256,384]{2,1,0:T(8,128)(2,1)S(1)}, u32[]{:S(2)}, u32[]{:S(2)}) collective-permute-start(bf16[4,256,384]{2,1,0:T(8,128)(2,1)S(1)} %get-tuple-element.111), channel_id=1, source_target_pairs={{0,18},{2,16},{4,22},{6,20},{8,26},{10,24},{12,30},{14,28},{16,2},... | collective-permute-start | bytes 2359304 | tf_op jit(solution)/shard_map/ppermute | solution.py:451
  18.8 18.5 %collective-permute-start.7 = (bf16[384,512]{1,0:T(8,128)(2,1)S(1)}, bf16[384,512]{1,0:T(8,128)(2,1)S(1)}, u32[]{:S(2)}, u32[]{:S(2)}) collective-permute-start(bf16[384,512]{1,0:T(8,128)(2,1)S(1)} %shard_map.48.refs_4_), channel_id=1, source_target_pairs={{0,4},{2,6},{4,8},{6,10},{8,12},{10,14},{12,0},{14,2},{1,5},{3,7},... | collective-permute-start | bytes 1179656 | tf_op jit(solution)/shard_map/ppermute | solution.py:445
  23.7 21.9 %collective-permute-start.6 = (bf16[384,512]{1,0:T(8,128)(2,1)S(1)}, bf16[384,512]{1,0:T(8,128)(2,1)S(1)}, u32[]{:S(2)}, u32[]{:S(2)}) collective-permute-start(bf16[384,512]{1,0:T(8,128)(2,1)S(1)} %collective-permute-done.refs_4_.refs_2_), channel_id=1, source_target_pairs={{0,4},{2,6},{4,8},{6,10},{8,12},{10,14},{12,0},{14,2},{1,5},{3,7},... | collective-permute-start | bytes 1179656 | tf_op jit(solution)/shard_map/ppermute | solution.py:445
  37.3 14.2 %collective-permute-start.9 = (bf16[384,512]{1,0:T(8,128)(2,1)S(1)}, bf16[384,512]{1,0:T(8,128)(2,1)S(1)}, u32[]{:S(2)}, u32[]{:S(2)}) collective-permute-start(bf16[384,512]{1,0:T(8,128)(2,1)S(1)} %collective-permute-done.7.refs_5_), channel_id=1, source_target_pairs={{0,4},{2,6},{4,8},{6,10},{8,12},{10,14},{12,0},{14,2},{1,5},{3,7},... | collective-permute-start | bytes 1179656 | tf_op jit(solution)/shard_map/ppermute | solution.py:445
  46.2 3.3 %collective-permute-start.10 = (bf16[3,256,128]{2,1,0:T(8,128)(2,1)S(1)}, bf16[3,256,128]{2,1,0:T(8,128)(2,1)S(1)}, u32[]{:S(2)}, u32[]{:S(2)}) collective-permute-start(bf16[3,256,128]{2,1,0:T(8,128)(2,1)S(1)} %get-tuple-element.128), channel_id=1, source_target_pairs={{0,1},{1,0},{2,3},{3,2},{4,5},{5,4},{6,7},{7,6},{8,9},{9,8},{10,11... | collective-permute-start | bytes 589832 | tf_op jit(solution)/shard_map/ppermute | solution.py:442
  46.3 3.2 %collective-permute-start.11 = (bf16[3,256,128]{2,1,0:T(8,128)(2,1)S(1)}, bf16[3,256,128]{2,1,0:T(8,128)(2,1)S(1)}, u32[]{:S(2)}, u32[]{:S(2)}) collective-permute-start(bf16[3,256,128]{2,1,0:T(8,128)(2,1)S(1)} %get-tuple-element.134), channel_id=1, source_target_pairs={{0,1},{1,0},{2,3},{3,2},{4,5},{5,4},{6,7},{7,6},{8,9},{9,8},{10,11... | collective-permute-start | bytes 589832 | tf_op jit(solution)/shard_map/ppermute | solution.py:442
  46.8 11.5 %collective-permute-start.8 = (bf16[384,512]{1,0:T(8,128)(2,1)S(1)}, bf16[384,512]{1,0:T(8,128)(2,1)S(1)}, u32[]{:S(2)}, u32[]{:S(2)}) collective-permute-start(bf16[384,512]{1,0:T(8,128)(2,1)S(1)} %shard_map.48.refs_4_), channel_id=1, source_target_pairs={{4,0},{6,2},{8,4},{10,6},{12,8},{14,10},{0,12},{2,14},{5,1},{7,3},... | collective-permute-start | bytes 1179656 | tf_op jit(solution)/shard_map/ppermute | solution.py:448
  49.6 2.0 %collective-permute-start.14 = (bf16[2,256,128]{2,1,0:T(8,128)(2,1)S(1)}, bf16[2,256,128]{2,1,0:T(8,128)(2,1)S(1)}, u32[]{:S(2)}, u32[]{:S(2)}) collective-permute-start(bf16[2,256,128]{2,1,0:T(8,128)(2,1)S(1)} %get-tuple-element.141), channel_id=1, source_target_pairs={{0,1},{1,0},{2,3},{3,2},{4,5},{5,4},{6,7},{7,6},{8,9},{9,8},{10,11... | collective-permute-start | bytes 393224 | tf_op jit(solution)/shard_map/ppermute | solution.py:442
  49.7 5.9 %collective-permute-start.13 = (bf16[2,256,128]{2,1,0:T(8,128)(2,1)S(1)}, bf16[2,256,128]{2,1,0:T(8,128)(2,1)S(1)}, u32[]{:S(2)}, u32[]{:S(2)}) collective-permute-start(bf16[2,256,128]{2,1,0:T(8,128)(2,1)S(1)} %get-tuple-element.143), channel_id=1, source_target_pairs={{0,16},{16,0},{1,17},{17,1},{2,18},{18,2},{3,19},{19,3},{4,20},{20... | collective-permute-start | bytes 393224 | tf_op jit(solution)/shard_map/ppermute | solution.py:457
  50.1 6.3 %collective-permute-start.12 = (bf16[2,256,128]{2,1,0:T(8,128)(2,1)S(1)}, bf16[2,256,128]{2,1,0:T(8,128)(2,1)S(1)}, u32[]{:S(2)}, u32[]{:S(2)}) collective-permute-start(bf16[2,256,128]{2,1,0:T(8,128)(2,1)S(1)} %get-tuple-element.140), channel_id=1, source_target_pairs={{0,2},{2,0},{4,6},{6,4},{8,10},{10,8},{12,14},{14,12},{1,3},{3,1},... | collective-permute-start | bytes 393224 | tf_op jit(solution)/shard_map/ppermute | solution.py:454
  51.6 7.9 %collective-permute-start.15 = (bf16[2,256,128]{2,1,0:T(8,128)(2,1)S(1)}, bf16[2,256,128]{2,1,0:T(8,128)(2,1)S(1)}, u32[]{:S(2)}, u32[]{:S(2)}) collective-permute-start(bf16[2,256,128]{2,1,0:T(8,128)(2,1)S(1)} %shard_map.56), channel_id=1, source_target_pairs={{0,18},{2,16},{4,22},{6,20},{8,26},{10,24},{12,30},{14,28},{16,2},... | collective-permute-start | bytes 393224 | tf_op jit(solution)/shard_map/ppermute | solution.py:451
  59.6 1.5 %collective-permute-start.16 = (bf16[4,256,128]{2,1,0:T(8,128)(2,1)S(1)}, bf16[4,256,128]{2,1,0:T(8,128)(2,1)S(1)}, u32[]{:S(2)}, u32[]{:S(2)}) collective-permute-start(bf16[4,256,128]{2,1,0:T(8,128)(2,1)S(1)} %get-tuple-element.157), channel_id=1, source_target_pairs={{0,1},{1,0},{2,3},{3,2},{4,5},{5,4},{6,7},{7,6},{8,9},{9,8},{10,11... | collective-permute-start | bytes 786440 | tf_op jit(solution)/shard_map/ppermute | solution.py:442
  59.6 2.9 %collective-permute-start.19 = (bf16[4,256,128]{2,1,0:T(8,128)(2,1)S(1)}, bf16[4,256,128]{2,1,0:T(8,128)(2,1)S(1)}, u32[]{:S(2)}, u32[]{:S(2)}) collective-permute-start(bf16[4,256,128]{2,1,0:T(8,128)(2,1)S(1)} %get-tuple-element.170), channel_id=1, source_target_pairs={{0,1},{1,0},{2,3},{3,2},{4,5},{5,4},{6,7},{7,6},{8,9},{9,8},{10,11... | collective-permute-start | bytes 786440 | tf_op jit(solution)/shard_map/ppermute | solution.py:442
  61.1 7.3 %collective-permute-start.17 = (bf16[2,256,128]{2,1,0:T(8,128)(2,1)S(1)}, bf16[2,256,128]{2,1,0:T(8,128)(2,1)S(1)}, u32[]{:S(2)}, u32[]{:S(2)}) collective-permute-start(bf16[2,256,128]{2,1,0:T(8,128)(2,1)S(1)} %get-tuple-element.167), channel_id=1, source_target_pairs={{0,18},{2,16},{4,22},{6,20},{8,26},{10,24},{12,30},{14,28},{16,2},... | collective-permute-start | bytes 393224 | tf_op jit(solution)/shard_map/ppermute | solution.py:451
  62.6 6.8 %collective-permute-start.20 = (bf16[2,256,128]{2,1,0:T(8,128)(2,1)S(1)}, bf16[2,256,128]{2,1,0:T(8,128)(2,1)S(1)}, u32[]{:S(2)}, u32[]{:S(2)}) collective-permute-start(bf16[2,256,128]{2,1,0:T(8,128)(2,1)S(1)} %get-tuple-element.174), channel_id=1, source_target_pairs={{0,2},{2,0},{4,6},{6,4},{8,10},{10,8},{12,14},{14,12},{1,3},{3,1},... | collective-permute-start | bytes 393224 | tf_op jit(solution)/shard_map/ppermute | solution.py:454
  63.1 7.3 %collective-permute-start.21 = (bf16[2,256,128]{2,1,0:T(8,128)(2,1)S(1)}, bf16[2,256,128]{2,1,0:T(8,128)(2,1)S(1)}, u32[]{:S(2)}, u32[]{:S(2)}) collective-permute-start(bf16[2,256,128]{2,1,0:T(8,128)(2,1)S(1)} %get-tuple-element.178), channel_id=1, source_target_pairs={{0,16},{16,0},{1,17},{17,1},{2,18},{18,2},{3,19},{19,3},{4,20},{20... | collective-permute-start | bytes 393224 | tf_op jit(solution)/shard_map/ppermute | solution.py:457
  64.8 1.3 %collective-permute-start.18 = (bf16[256,128]{1,0:T(8,128)(2,1)S(1)}, bf16[256,128]{1,0:T(8,128)(2,1)S(1)}, u32[]{:S(2)}, u32[]{:S(2)}) collective-permute-start(bf16[256,128]{1,0:T(8,128)(2,1)S(1)} %shard_map.58.refs_9_), channel_id=1, source_target_pairs={{0,1},{1,0},{2,3},{3,2},{4,5},{5,4},{6,7},{7,6},{8,9},{9,8},{10,11... | collective-permute-start | bytes 196616 | tf_op jit(solution)/shard_map/ppermute | solution.py:442

commit v7 on v6

--- a/solution.py
+++ b/solution.py
@@ -194,15 +194,18 @@
 
 
 def gate_kernel(part, depth, hidden_ref, gain_ref, *refs):
-    piece_refs, (sq_ref, slab_ref, row_ref, sems) = refs[:4], refs[4:]
+    piece_refs, (sq_ref, slab_ref, flat_ref, row_ref, sems) = refs[:4], refs[4:]
     place = lax.axis_index("dp")
     x, z, y = place % 2, place // 2, lax.axis_index("groups")
     wide = 4 * part
     columns = [pl.ds(pl.multiple_of(lax.rem(z - k + depth, depth) * wide, HEAD), wide) for k in range(depth)]
     copies = [pltpu.make_async_copy(hidden_ref.at[:, c], slab_ref.at[k], sems.at[k]) for k, c in enumerate(columns)]
+    gain_copy = pltpu.make_async_copy(gain_ref, flat_ref, sems.at[depth])
+    gain_copy.start()
     for copy in copies:
         copy.start()
-    row_ref[0, :] = gain_ref[...].astype(jnp.float32)
+    gain_copy.wait()
+    row_ref[0, :] = flat_ref[...].astype(jnp.float32)
     tokens = hidden_ref.shape[0]
     height = 64
     for k, copy in enumerate(copies):
@@ -228,14 +231,15 @@
     return call(
         functools.partial(gate_kernel, part, depth),
         (piece,) * 4 + (jax.ShapeDtypeStruct((tokens, HEAD), jnp.float32),),
-        in_specs=[pl.BlockSpec(memory_space=pltpu.HBM), WHOLE],
+        in_specs=[pl.BlockSpec(memory_space=pltpu.HBM)] * 2,
         out_specs=[WHOLE] * 5,
         scratch_shapes=[
             pltpu.VMEM((depth, tokens, 4 * part), jnp.bfloat16),
+            pltpu.VMEM(norm_gain.shape, norm_gain.dtype),
             pltpu.VMEM((1, norm_gain.shape[0]), jnp.float32),
-            pltpu.SemaphoreType.DMA((depth,)),
+            pltpu.SemaphoreType.DMA((depth + 1,)),
         ],
-    )(pltpu.with_memory_space_constraint(hidden_in, pltpu.HBM), norm_gain)
+    )(*(pltpu.with_memory_space_constraint(a, pltpu.HBM) for a in (hidden_in, norm_gain)))
 
 
 def matmul_kernel(firsts, n_acts, n_more, sent, *refs):

time: 72 us -> 71.3 us (level)
  waiting for transfers between devices: 32.8 us -> 34 us
  starting transfers between devices: 25.3 us -> 24.1 us
    ppermute x3, waiting for transfers between devices: 3.97 us -> 5.29 us  [to_x(): return lax.ppermute(a, 'dp', over_x)]
    ppermute x4, waiting for transfers between devices: 16 us -> 17 us  [on_ring(): return lax.ppermute(a, 'dp', ring)]
    ppermute x4, starting transfers between devices: 6.08 us -> 5.12 us  [on_ring(): return lax.ppermute(a, 'dp', ring)]
    ppermute x3, waiting for transfers between devices: 1.59 us -> 0.69 us  [to_y(): return lax.ppermute(a, 'groups', over_y)]
  transfers between devices with their start and end apart: 22 -> 22, of which waited for: 14 -> 14; matrix products, arithmetic and copies ran while one was open for 0% -> 0% of each run, Pallas kernels for 14% -> 15%
where the time goes in v7:
time: 71.3 us; the launch traced here: 71.1 us
  waiting for transfers between devices  34 us (48%)
  starting transfers between devices  24.1 us (34%)
  Pallas kernels  12.8 us (18%)
    ppermute x4, waiting for transfers between devices, on_ring(): return lax.ppermute(a, 'dp', ring)  17 us
    ppermute x2, waiting for transfers between devices, back(): return lax.ppermute(a, 'dp', [(j, i) for i, j in ring])  7.04 us
    ppermute x3, starting transfers between devices, to_far(): return lax.ppermute(a, ('groups', 'dp'), across)  7.02 us
    ppermute x3, waiting for transfers between devices, to_x(): return lax.ppermute(a, 'dp', over_x)  5.29 us
    ppermute x4, starting transfers between devices, on_ring(): return lax.ppermute(a, 'dp', ring)  5.12 us
    pallas_call x5, Pallas kernels, matmul(): call(functools.partial(matmul_kernel, firsts, len(acts), len(so_far), sen...  5.11 us
    ppermute x2, starting transfers between devices, back(): return lax.ppermute(a, 'dp', [(j, i) for i, j in ring])  4.1 us
    ppermute x3, starting transfers between devices, to_y(): return lax.ppermute(a, 'groups', over_y)  3.53 us
  transfers between devices with their start and end apart: 22, of which 14 were waited for; matrix products, arithmetic and copies ran while one was open for 0% of the time, Pallas kernels for 15%

profile of v7, /device:TPU:0, one launch (start us, length us, event | category | flops | bytes accessed | tf_op | source)
XLA Modules:
  0.0 71.1 jit_solution(671227531509619025)
XLA Ops:
  0.0 1.1 %shard_map.46.refs_3_.refs_1_ = bf16[384,512]{1,0:T(8,128)(2,1)S(1)} custom-call(bf16[1,768,1024]{2,1,0:T(8,128)(2,1)} %rows_ref.2), custom_call_target="tpu_custom_call" | custom-call | flops 1 | bytes 1 | tf_op jit(solution)/shard_map/pallas_call | solution.py:187
  1.1 3.1 %collective-permute-start = (bf16[384,512]{1,0:T(8,128)(2,1)S(1)}, bf16[384,512]{1,0:T(8,128)(2,1)S(1)}, u32[]{:S(2)}, u32[]{:S(2)}) collective-permute-start(bf16[384,512]{1,0:T(8,128)(2,1)S(1)} %shard_map.46.refs_3_.refs_1_), channel_id=1, source_target_pairs={{0,4},{2,6},{4,8},{6,10},{8,12},{10,14},{12,0},{14,2},{1,5},{3,7},... | collective-permute-start | bytes 1179656 | tf_op jit(solution)/shard_map/ppermute | solution.py:449
  4.2 2.2 %shard_map.47 = (bf16[4,256,384]{2,1,0:T(8,128)(2,1)S(1)}, bf16[4,256,384]{2,1,0:T(8,128)(2,1)S(1)}, bf16[4,256,384]{2,1,0:T(8,128)(2,1)S(1)}, bf16[4,256,384]{2,1,0:T(8,128)(2,1)S(1)}, f32[256,128]{1,0:T(8,128)S(1)}) custom-call(bf16[256,6144]{1,0:T(8,128)(2,1)} %hidden_ref, bf16[6144]{0:T(1024)(128)(2,1)} %gain_ref.1), custom_call_target="tpu_custom_call" | custom-call | flops 1 | bytes 1 | tf_op jit(solution)/shard_map/pallas_call | solution.py:231
  6.3 1.6 %collective-permute-start.4 = (bf16[4,256,384]{2,1,0:T(8,128)(2,1)S(1)}, bf16[4,256,384]{2,1,0:T(8,128)(2,1)S(1)}, u32[]{:S(2)}, u32[]{:S(2)}) collective-permute-start(bf16[4,256,384]{2,1,0:T(8,128)(2,1)S(1)} %get-tuple-element.114), channel_id=1, source_target_pairs={{0,16},{16,0},{1,17},{17,1},{2,18},{18,2},{3,19},{19,3},{4,20},{20... | collective-permute-start | bytes 2359304 | tf_op jit(solution)/shard_map/ppermute | solution.py:461
  7.9 1.5 %collective-permute-start.3 = (bf16[4,256,384]{2,1,0:T(8,128)(2,1)S(1)}, bf16[4,256,384]{2,1,0:T(8,128)(2,1)S(1)}, u32[]{:S(2)}, u32[]{:S(2)}) collective-permute-start(bf16[4,256,384]{2,1,0:T(8,128)(2,1)S(1)} %get-tuple-element.113), channel_id=1, source_target_pairs={{0,2},{2,0},{4,6},{6,4},{8,10},{10,8},{12,14},{14,12},{1,3},{3,1},... | collective-permute-start | bytes 2359304 | tf_op jit(solution)/shard_map/ppermute | solution.py:458
  9.4 1.1 %shard_map.48.refs_4_ = bf16[384,512]{1,0:T(8,128)(2,1)S(1)} custom-call(bf16[1,768,1024]{2,1,0:T(8,128)(2,1)} %rows_ref.2), custom_call_target="tpu_custom_call" | custom-call | flops 1 | bytes 1 | tf_op jit(solution)/shard_map/pallas_call | solution.py:187
  10.5 2.3 %collective-permute-start.5 = (bf16[384,512]{1,0:T(8,128)(2,1)S(1)}, bf16[384,512]{1,0:T(8,128)(2,1)S(1)}, u32[]{:S(2)}, u32[]{:S(2)}) collective-permute-start(bf16[384,512]{1,0:T(8,128)(2,1)S(1)} %shard_map.46.refs_3_.refs_1_), channel_id=1, source_target_pairs={{4,0},{6,2},{8,4},{10,6},{12,8},{14,10},{0,12},{2,14},{5,1},{7,3},... | collective-permute-start | bytes 1179656 | tf_op jit(solution)/shard_map/ppermute | solution.py:452
  12.8 1.1 %shard_map.49 = (f32[256,128]{1,0:T(8,128)S(1)}, f32[256,128]{1,0:T(8,128)S(1)}, f32[256,256]{1,0:T(8,128)S(1)}, f32[256,128]{1,0:T(8,128)S(1)}) custom-call(s32[1,2]{1,0:T(1,128)S(1)} %copy-done, f32[256,128]{1,0:T(8,128)S(1)} %get-tuple-element.103._.own_ref), custom_call_target="tpu_custom_call" | custom-call | flops 1 | bytes 1 | tf_op jit(solution)/shard_map/pallas_call | solution.py:330
  14.0 1.5 %collective-permute-done.refs_4_.refs_2_ = bf16[384,512]{1,0:T(8,128)(2,1)S(1)} collective-permute-done((bf16[384,512]{1,0:T(8,128)(2,1)S(1)}, bf16[384,512]{1,0:T(8,128)(2,1)S(1)}, u32[]{:S(2)}, u32[]{:S(2)}) %collective-permute-start) | collective-permute-done | bytes 393248 | tf_op jit(solution)/shard_map/ppermute | solution.py:449
  15.5 3.4 %collective-permute-start.2 = (bf16[4,256,384]{2,1,0:T(8,128)(2,1)S(1)}, bf16[4,256,384]{2,1,0:T(8,128)(2,1)S(1)}, u32[]{:S(2)}, u32[]{:S(2)}) collective-permute-start(bf16[4,256,384]{2,1,0:T(8,128)(2,1)S(1)} %get-tuple-element.111), channel_id=1, source_target_pairs={{0,18},{2,16},{4,22},{6,20},{8,26},{10,24},{12,30},{14,28},{16,2},... | collective-permute-start | bytes 2359304 | tf_op jit(solution)/shard_map/ppermute | solution.py:455
  18.9 5.5 %collective-permute-done.5.refs_5_.refs_4_ = bf16[384,512]{1,0:T(8,128)(2,1)S(1)} collective-permute-done((bf16[384,512]{1,0:T(8,128)(2,1)S(1)}, bf16[384,512]{1,0:T(8,128)(2,1)S(1)}, u32[]{:S(2)}, u32[]{:S(2)}) %collective-permute-start.5) | collective-permute-done | bytes 393248 | tf_op jit(solution)/shard_map/ppermute | solution.py:452
  24.3 2.0 %collective-permute-start.6 = (bf16[384,512]{1,0:T(8,128)(2,1)S(1)}, bf16[384,512]{1,0:T(8,128)(2,1)S(1)}, u32[]{:S(2)}, u32[]{:S(2)}) collective-permute-start(bf16[384,512]{1,0:T(8,128)(2,1)S(1)} %collective-permute-done.refs_4_.refs_2_), channel_id=1, source_target_pairs={{0,4},{2,6},{4,8},{6,10},{8,12},{10,14},{12,0},{14,2},{1,5},{3,7},... | collective-permute-start | bytes 1179656 | tf_op jit(solution)/shard_map/ppermute | solution.py:449
  26.4 1.9 %collective-permute-done.3.refs_0_.refs_2_ = bf16[4,256,384]{2,1,0:T(8,128)(2,1)S(1)} collective-permute-done((bf16[4,256,384]{2,1,0:T(8,128)(2,1)S(1)}, bf16[4,256,384]{2,1,0:T(8,128)(2,1)S(1)}, u32[]{:S(2)}, u32[]{:S(2)}) %collective-permute-start.3) | collective-permute-done | bytes 786464 | tf_op jit(solution)/shard_map/ppermute | solution.py:458
  28.3 8.5 %collective-permute-done.7.refs_5_ = bf16[384,512]{1,0:T(8,128)(2,1)S(1)} collective-permute-done((bf16[384,512]{1,0:T(8,128)(2,1)S(1)}, bf16[384,512]{1,0:T(8,128)(2,1)S(1)}, u32[]{:S(2)}, u32[]{:S(2)}) %collective-permute-start.7) | collective-permute-done | bytes 393248 | tf_op jit(solution)/shard_map/ppermute | solution.py:449
  36.7 1.4 %shard_map.51.refs_4_ = f32[3,256,512]{2,1,0:T(8,128)S(1)} custom-call(bf16[4,256,384]{2,1,0:T(8,128)(2,1)S(1)} %collective-permute-done.3.refs_0_.refs_2_, bf16[4,256,384]{2,1,0:T(8,128)(2,1)S(1)} %collective-permute-done.4.refs_1_.refs_3_, bf16[4,256,384]{2,1,0:T(8,128)(2,1)S(1)} %get-tuple-element.120.refs_2_.refs_1_, ...), custom_call_target="tpu_custom_call" | custom-call | flops 1 | bytes 1 | tf_op jit(solution)/shard_map/pallas_call | solution.py:283
  38.1 7.0 %collective-permute-done.6.refs_3_ = bf16[384,512]{1,0:T(8,128)(2,1)S(1)} collective-permute-done((bf16[384,512]{1,0:T(8,128)(2,1)S(1)}, bf16[384,512]{1,0:T(8,128)(2,1)S(1)}, u32[]{:S(2)}, u32[]{:S(2)}) %collective-permute-start.6) | collective-permute-done | bytes 393248 | tf_op jit(solution)/shard_map/ppermute | solution.py:449
  46.3 1.8 %collective-permute-start.8 = (bf16[384,512]{1,0:T(8,128)(2,1)S(1)}, bf16[384,512]{1,0:T(8,128)(2,1)S(1)}, u32[]{:S(2)}, u32[]{:S(2)}) collective-permute-start(bf16[384,512]{1,0:T(8,128)(2,1)S(1)} %shard_map.48.refs_4_), channel_id=1, source_target_pairs={{4,0},{6,2},{8,4},{10,6},{12,8},{14,10},{0,12},{2,14},{5,1},{7,3},... | collective-permute-start | bytes 1179656 | tf_op jit(solution)/shard_map/ppermute | solution.py:452
  49.0 1.2 %collective-permute-start.13 = (bf16[2,256,128]{2,1,0:T(8,128)(2,1)S(1)}, bf16[2,256,128]{2,1,0:T(8,128)(2,1)S(1)}, u32[]{:S(2)}, u32[]{:S(2)}) collective-permute-start(bf16[2,256,128]{2,1,0:T(8,128)(2,1)S(1)} %get-tuple-element.143), channel_id=1, source_target_pairs={{0,16},{16,0},{1,17},{17,1},{2,18},{18,2},{3,19},{19,3},{4,20},{20... | collective-permute-start | bytes 393224 | tf_op jit(solution)/shard_map/ppermute | solution.py:461
  50.2 0.7 %collective-permute-start.12 = (bf16[2,256,128]{2,1,0:T(8,128)(2,1)S(1)}, bf16[2,256,128]{2,1,0:T(8,128)(2,1)S(1)}, u32[]{:S(2)}, u32[]{:S(2)}) collective-permute-start(bf16[2,256,128]{2,1,0:T(8,128)(2,1)S(1)} %get-tuple-element.140), channel_id=1, source_target_pairs={{0,2},{2,0},{4,6},{6,4},{8,10},{10,8},{12,14},{14,12},{1,3},{3,1},... | collective-permute-start | bytes 393224 | tf_op jit(solution)/shard_map/ppermute | solution.py:458
  50.9 1.7 %collective-permute-start.15 = (bf16[2,256,128]{2,1,0:T(8,128)(2,1)S(1)}, bf16[2,256,128]{2,1,0:T(8,128)(2,1)S(1)}, u32[]{:S(2)}, u32[]{:S(2)}) collective-permute-start(bf16[2,256,128]{2,1,0:T(8,128)(2,1)S(1)} %shard_map.56), channel_id=1, source_target_pairs={{0,18},{2,16},{4,22},{6,20},{8,26},{10,24},{12,30},{14,28},{16,2},... | collective-permute-start | bytes 393224 | tf_op jit(solution)/shard_map/ppermute | solution.py:455
  52.6 1.8 %shard_map.55.refs_5_ = f32[4,256,512]{2,1,0:T(8,128)S(1)} custom-call(bf16[4,256,384]{2,1,0:T(8,128)(2,1)S(1)} %collective-permute-done.2.refs_0_, bf16[4,256,384]{2,1,0:T(8,128)(2,1)S(1)} %get-tuple-element.120.refs_2_.refs_1_, bf16[4,256,384]{2,1,0:T(8,128)(2,1)S(1)} %collective-permute-done.3.refs_0_.refs_2_, ...), custom_call_target="tpu_custom_call" | custom-call | flops 1 | bytes 1 | tf_op jit(solution)/shard_map/pallas_call | solution.py:283
  54.9 1.6 %collective-permute-done.12.r1.refs_2_ = bf16[2,256,128]{2,1,0:T(8,128)(2,1)S(1)} collective-permute-done((bf16[2,256,128]{2,1,0:T(8,128)(2,1)S(1)}, bf16[2,256,128]{2,1,0:T(8,128)(2,1)S(1)}, u32[]{:S(2)}, u32[]{:S(2)}) %collective-permute-start.12) | collective-permute-done | bytes 131104 | tf_op jit(solution)/shard_map/ppermute | solution.py:458
  56.5 1.6 %collective-permute-done.8.refs_4_ = bf16[384,512]{1,0:T(8,128)(2,1)S(1)} collective-permute-done((bf16[384,512]{1,0:T(8,128)(2,1)S(1)}, bf16[384,512]{1,0:T(8,128)(2,1)S(1)}, u32[]{:S(2)}, u32[]{:S(2)}) %collective-permute-start.8) | collective-permute-done | bytes 393248 | tf_op jit(solution)/shard_map/ppermute | solution.py:452
  58.1 0.7 shard_map.57
  59.5 0.9 %collective-permute-done.16.refs_0_ = bf16[4,256,128]{2,1,0:T(8,128)(2,1)S(1)} collective-permute-done((bf16[4,256,128]{2,1,0:T(8,128)(2,1)S(1)}, bf16[4,256,128]{2,1,0:T(8,128)(2,1)S(1)}, u32[]{:S(2)}, u32[]{:S(2)}) %collective-permute-start.16) | collective-permute-done | bytes 262176 | tf_op jit(solution)/shard_map/ppermute | solution.py:446
  60.5 1.9 %collective-permute-start.17 = (bf16[2,256,128]{2,1,0:T(8,128)(2,1)S(1)}, bf16[2,256,128]{2,1,0:T(8,128)(2,1)S(1)}, u32[]{:S(2)}, u32[]{:S(2)}) collective-permute-start(bf16[2,256,128]{2,1,0:T(8,128)(2,1)S(1)} %get-tuple-element.167), channel_id=1, source_target_pairs={{0,18},{2,16},{4,22},{6,20},{8,26},{10,24},{12,30},{14,28},{16,2},... | collective-permute-start | bytes 393224 | tf_op jit(solution)/shard_map/ppermute | solution.py:455
  62.4 0.9 %collective-permute-start.20 = (bf16[2,256,128]{2,1,0:T(8,128)(2,1)S(1)}, bf16[2,256,128]{2,1,0:T(8,128)(2,1)S(1)}, u32[]{:S(2)}, u32[]{:S(2)}) collective-permute-start(bf16[2,256,128]{2,1,0:T(8,128)(2,1)S(1)} %get-tuple-element.174), channel_id=1, source_target_pairs={{0,2},{2,0},{4,6},{6,4},{8,10},{10,8},{12,14},{14,12},{1,3},{3,1},... | collective-permute-start | bytes 393224 | tf_op jit(solution)/shard_map/ppermute | solution.py:458
  63.4 0.8 %collective-permute-start.21 = (bf16[2,256,128]{2,1,0:T(8,128)(2,1)S(1)}, bf16[2,256,128]{2,1,0:T(8,128)(2,1)S(1)}, u32[]{:S(2)}, u32[]{:S(2)}) collective-permute-start(bf16[2,256,128]{2,1,0:T(8,128)(2,1)S(1)} %get-tuple-element.178), channel_id=1, source_target_pairs={{0,16},{16,0},{1,17},{17,1},{2,18},{18,2},{3,19},{19,3},{4,20},{20... | collective-permute-start | bytes 393224 | tf_op jit(solution)/shard_map/ppermute | solution.py:461
  64.1 1.3 %collective-permute-done.18.refs_10_ = bf16[256,128]{1,0:T(8,128)(2,1)S(1)} collective-permute-done((bf16[256,128]{1,0:T(8,128)(2,1)S(1)}, bf16[256,128]{1,0:T(8,128)(2,1)S(1)}, u32[]{:S(2)}, u32[]{:S(2)}) %collective-permute-start.18) | collective-permute-done | bytes 65568 | tf_op jit(solution)/shard_map/ppermute | solution.py:446
  66.0 1.8 %collective-permute-done.17.refs_1_ = bf16[2,256,128]{2,1,0:T(8,128)(2,1)S(1)} collective-permute-done((bf16[2,256,128]{2,1,0:T(8,128)(2,1)S(1)}, bf16[2,256,128]{2,1,0:T(8,128)(2,1)S(1)}, u32[]{:S(2)}, u32[]{:S(2)}) %collective-permute-start.17) | collective-permute-done | bytes 131104 | tf_op jit(solution)/shard_map/ppermute | solution.py:455
  67.8 1.8 %collective-permute-done.20.refs_2_ = bf16[2,256,128]{2,1,0:T(8,128)(2,1)S(1)} collective-permute-done((bf16[2,256,128]{2,1,0:T(8,128)(2,1)S(1)}, bf16[2,256,128]{2,1,0:T(8,128)(2,1)S(1)}, u32[]{:S(2)}, u32[]{:S(2)}) %collective-permute-start.20) | collective-permute-done | bytes 131104 | tf_op jit(solution)/shard_map/ppermute | solution.py:458
  69.8 1.4 %shard_map.62 = bf16[256,384]{1,0:T(8,128)(2,1)} custom-call(f32[2,256,128]{2,1,0:T(8,128)S(1)} %get-tuple-element.166.refs_0_, bf16[2,256,128]{2,1,0:T(8,128)(2,1)S(1)} %collective-permute-done.17.refs_1_, bf16[2,256,128]{2,1,0:T(8,128)(2,1)S(1)} %collective-permute-done.20.refs_2_, bf16[2,256,128]{2,1,0:T(8,128)(2,1)S(1)} %collective-permute-done.21.refs_3_, ...), custom_call_target="tpu_custom_call" | custom-call | flops 1 | bytes 1 | tf_op jit(solution)/shard_map/pallas_call | solution.py:420
  (31 shorter events, 4.2 us)
Async XLA Ops:
  1.1 11.7 %copy-start = (s32[1,2]{1,0:T(1,128)S(1)}, s32[1,2]{1,0:T(1,128)}, u32[]{:S(2)}) copy-start(s32[1,2]{1,0:T(1,128)} %lengths_ref.1) | copy-start | bytes 28
  1.1 14.4 %collective-permute-start = (bf16[384,512]{1,0:T(8,128)(2,1)S(1)}, bf16[384,512]{1,0:T(8,128)(2,1)S(1)}, u32[]{:S(2)}, u32[]{:S(2)}) collective-permute-start(bf16[384,512]{1,0:T(8,128)(2,1)S(1)} %shard_map.46.refs_3_.refs_1_), channel_id=1, source_target_pairs={{0,4},{2,6},{4,8},{6,10},{8,12},{10,14},{12,0},{14,2},{1,5},{3,7},... | collective-permute-start | bytes 1179656 | tf_op jit(solution)/shard_map/ppermute | solution.py:449
  6.3 20.0 %collective-permute-start.4 = (bf16[4,256,384]{2,1,0:T(8,128)(2,1)S(1)}, bf16[4,256,384]{2,1,0:T(8,128)(2,1)S(1)}, u32[]{:S(2)}, u32[]{:S(2)}) collective-permute-start(bf16[4,256,384]{2,1,0:T(8,128)(2,1)S(1)} %get-tuple-element.114), channel_id=1, source_target_pairs={{0,16},{16,0},{1,17},{17,1},{2,18},{18,2},{3,19},{19,3},{4,20},{20... | collective-permute-start | bytes 2359304 | tf_op jit(solution)/shard_map/ppermute | solution.py:461
  7.9 6.0 %collective-permute-start.1 = (f32[256,128]{1,0:T(8,128)S(1)}, f32[256,128]{1,0:T(8,128)S(1)}, u32[]{:S(2)}, u32[]{:S(2)}) collective-permute-start(f32[256,128]{1,0:T(8,128)S(1)} %get-tuple-element.103._.own_ref), channel_id=1, source_target_pairs={{0,1},{1,0},{2,3},{3,2},{4,5},{5,4},{6,7},{7,6},{8,9},{9,8},{10,11... | collective-permute-start | bytes 393224 | tf_op jit(solution)/shard_map/ppermute | solution.py:446
  7.9 20.3 %collective-permute-start.3 = (bf16[4,256,384]{2,1,0:T(8,128)(2,1)S(1)}, bf16[4,256,384]{2,1,0:T(8,128)(2,1)S(1)}, u32[]{:S(2)}, u32[]{:S(2)}) collective-permute-start(bf16[4,256,384]{2,1,0:T(8,128)(2,1)S(1)} %get-tuple-element.113), channel_id=1, source_target_pairs={{0,2},{2,0},{4,6},{6,4},{8,10},{10,8},{12,14},{14,12},{1,3},{3,1},... | collective-permute-start | bytes 2359304 | tf_op jit(solution)/shard_map/ppermute | solution.py:458
  10.5 13.8 %collective-permute-start.5 = (bf16[384,512]{1,0:T(8,128)(2,1)S(1)}, bf16[384,512]{1,0:T(8,128)(2,1)S(1)}, u32[]{:S(2)}, u32[]{:S(2)}) collective-permute-start(bf16[384,512]{1,0:T(8,128)(2,1)S(1)} %shard_map.46.refs_3_.refs_1_), channel_id=1, source_target_pairs={{4,0},{6,2},{8,4},{10,6},{12,8},{14,10},{0,12},{2,14},{5,1},{7,3},... | collective-permute-start | bytes 1179656 | tf_op jit(solution)/shard_map/ppermute | solution.py:452
  15.5 30.8 %collective-permute-start.2 = (bf16[4,256,384]{2,1,0:T(8,128)(2,1)S(1)}, bf16[4,256,384]{2,1,0:T(8,128)(2,1)S(1)}, u32[]{:S(2)}, u32[]{:S(2)}) collective-permute-start(bf16[4,256,384]{2,1,0:T(8,128)(2,1)S(1)} %get-tuple-element.111), channel_id=1, source_target_pairs={{0,18},{2,16},{4,22},{6,20},{8,26},{10,24},{12,30},{14,28},{16,2},... | collective-permute-start | bytes 2359304 | tf_op jit(solution)/shard_map/ppermute | solution.py:455
  18.9 17.8 %collective-permute-start.7 = (bf16[384,512]{1,0:T(8,128)(2,1)S(1)}, bf16[384,512]{1,0:T(8,128)(2,1)S(1)}, u32[]{:S(2)}, u32[]{:S(2)}) collective-permute-start(bf16[384,512]{1,0:T(8,128)(2,1)S(1)} %shard_map.48.refs_4_), channel_id=1, source_target_pairs={{0,4},{2,6},{4,8},{6,10},{8,12},{10,14},{12,0},{14,2},{1,5},{3,7},... | collective-permute-start | bytes 1179656 | tf_op jit(solution)/shard_map/ppermute | solution.py:449
  24.3 20.8 %collective-permute-start.6 = (bf16[384,512]{1,0:T(8,128)(2,1)S(1)}, bf16[384,512]{1,0:T(8,128)(2,1)S(1)}, u32[]{:S(2)}, u32[]{:S(2)}) collective-permute-start(bf16[384,512]{1,0:T(8,128)(2,1)S(1)} %collective-permute-done.refs_4_.refs_2_), channel_id=1, source_target_pairs={{0,4},{2,6},{4,8},{6,10},{8,12},{10,14},{12,0},{14,2},{1,5},{3,7},... | collective-permute-start | bytes 1179656 | tf_op jit(solution)/shard_map/ppermute | solution.py:449
  36.7 14.2 %collective-permute-start.9 = (bf16[384,512]{1,0:T(8,128)(2,1)S(1)}, bf16[384,512]{1,0:T(8,128)(2,1)S(1)}, u32[]{:S(2)}, u32[]{:S(2)}) collective-permute-start(bf16[384,512]{1,0:T(8,128)(2,1)S(1)} %collective-permute-done.7.refs_5_), channel_id=1, source_target_pairs={{0,4},{2,6},{4,8},{6,10},{8,12},{10,14},{12,0},{14,2},{1,5},{3,7},... | collective-permute-start | bytes 1179656 | tf_op jit(solution)/shard_map/ppermute | solution.py:449
  45.7 3.1 %collective-permute-start.10 = (bf16[3,256,128]{2,1,0:T(8,128)(2,1)S(1)}, bf16[3,256,128]{2,1,0:T(8,128)(2,1)S(1)}, u32[]{:S(2)}, u32[]{:S(2)}) collective-permute-start(bf16[3,256,128]{2,1,0:T(8,128)(2,1)S(1)} %get-tuple-element.128), channel_id=1, source_target_pairs={{0,1},{1,0},{2,3},{3,2},{4,5},{5,4},{6,7},{7,6},{8,9},{9,8},{10,11... | collective-permute-start | bytes 589832 | tf_op jit(solution)/shard_map/ppermute | solution.py:446
  45.8 3.0 %collective-permute-start.11 = (bf16[3,256,128]{2,1,0:T(8,128)(2,1)S(1)}, bf16[3,256,128]{2,1,0:T(8,128)(2,1)S(1)}, u32[]{:S(2)}, u32[]{:S(2)}) collective-permute-start(bf16[3,256,128]{2,1,0:T(8,128)(2,1)S(1)} %get-tuple-element.134), channel_id=1, source_target_pairs={{0,1},{1,0},{2,3},{3,2},{4,5},{5,4},{6,7},{7,6},{8,9},{9,8},{10,11... | collective-permute-start | bytes 589832 | tf_op jit(solution)/shard_map/ppermute | solution.py:446
  46.3 11.8 %collective-permute-start.8 = (bf16[384,512]{1,0:T(8,128)(2,1)S(1)}, bf16[384,512]{1,0:T(8,128)(2,1)S(1)}, u32[]{:S(2)}, u32[]{:S(2)}) collective-permute-start(bf16[384,512]{1,0:T(8,128)(2,1)S(1)} %shard_map.48.refs_4_), channel_id=1, source_target_pairs={{4,0},{6,2},{8,4},{10,6},{12,8},{14,10},{0,12},{2,14},{5,1},{7,3},... | collective-permute-start | bytes 1179656 | tf_op jit(solution)/shard_map/ppermute | solution.py:452
  48.9 2.0 %collective-permute-start.14 = (bf16[2,256,128]{2,1,0:T(8,128)(2,1)S(1)}, bf16[2,256,128]{2,1,0:T(8,128)(2,1)S(1)}, u32[]{:S(2)}, u32[]{:S(2)}) collective-permute-start(bf16[2,256,128]{2,1,0:T(8,128)(2,1)S(1)} %get-tuple-element.141), channel_id=1, source_target_pairs={{0,1},{1,0},{2,3},{3,2},{4,5},{5,4},{6,7},{7,6},{8,9},{9,8},{10,11... | collective-permute-start | bytes 393224 | tf_op jit(solution)/shard_map/ppermute | solution.py:446
  49.0 5.9 %collective-permute-start.13 = (bf16[2,256,128]{2,1,0:T(8,128)(2,1)S(1)}, bf16[2,256,128]{2,1,0:T(8,128)(2,1)S(1)}, u32[]{:S(2)}, u32[]{:S(2)}) collective-permute-start(bf16[2,256,128]{2,1,0:T(8,128)(2,1)S(1)} %get-tuple-element.143), channel_id=1, source_target_pairs={{0,16},{16,0},{1,17},{17,1},{2,18},{18,2},{3,19},{19,3},{4,20},{20... | collective-permute-start | bytes 393224 | tf_op jit(solution)/shard_map/ppermute | solution.py:461
  50.2 6.3 %collective-permute-start.12 = (bf16[2,256,128]{2,1,0:T(8,128)(2,1)S(1)}, bf16[2,256,128]{2,1,0:T(8,128)(2,1)S(1)}, u32[]{:S(2)}, u32[]{:S(2)}) collective-permute-start(bf16[2,256,128]{2,1,0:T(8,128)(2,1)S(1)} %get-tuple-element.140), channel_id=1, source_target_pairs={{0,2},{2,0},{4,6},{6,4},{8,10},{10,8},{12,14},{14,12},{1,3},{3,1},... | collective-permute-start | bytes 393224 | tf_op jit(solution)/shard_map/ppermute | solution.py:458
  50.9 8.0 %collective-permute-start.15 = (bf16[2,256,128]{2,1,0:T(8,128)(2,1)S(1)}, bf16[2,256,128]{2,1,0:T(8,128)(2,1)S(1)}, u32[]{:S(2)}, u32[]{:S(2)}) collective-permute-start(bf16[2,256,128]{2,1,0:T(8,128)(2,1)S(1)} %shard_map.56), channel_id=1, source_target_pairs={{0,18},{2,16},{4,22},{6,20},{8,26},{10,24},{12,30},{14,28},{16,2},... | collective-permute-start | bytes 393224 | tf_op jit(solution)/shard_map/ppermute | solution.py:455
  58.9 1.5 %collective-permute-start.16 = (bf16[4,256,128]{2,1,0:T(8,128)(2,1)S(1)}, bf16[4,256,128]{2,1,0:T(8,128)(2,1)S(1)}, u32[]{:S(2)}, u32[]{:S(2)}) collective-permute-start(bf16[4,256,128]{2,1,0:T(8,128)(2,1)S(1)} %get-tuple-element.157), channel_id=1, source_target_pairs={{0,1},{1,0},{2,3},{3,2},{4,5},{5,4},{6,7},{7,6},{8,9},{9,8},{10,11... | collective-permute-start | bytes 786440 | tf_op jit(solution)/shard_map/ppermute | solution.py:446
  58.9 3.5 %collective-permute-start.19 = (bf16[4,256,128]{2,1,0:T(8,128)(2,1)S(1)}, bf16[4,256,128]{2,1,0:T(8,128)(2,1)S(1)}, u32[]{:S(2)}, u32[]{:S(2)}) collective-permute-start(bf16[4,256,128]{2,1,0:T(8,128)(2,1)S(1)} %get-tuple-element.170), channel_id=1, source_target_pairs={{0,1},{1,0},{2,3},{3,2},{4,5},{5,4},{6,7},{7,6},{8,9},{9,8},{10,11... | collective-permute-start | bytes 786440 | tf_op jit(solution)/shard_map/ppermute | solution.py:446
  60.5 7.3 %collective-permute-start.17 = (bf16[2,256,128]{2,1,0:T(8,128)(2,1)S(1)}, bf16[2,256,128]{2,1,0:T(8,128)(2,1)S(1)}, u32[]{:S(2)}, u32[]{:S(2)}) collective-permute-start(bf16[2,256,128]{2,1,0:T(8,128)(2,1)S(1)} %get-tuple-element.167), channel_id=1, source_target_pairs={{0,18},{2,16},{4,22},{6,20},{8,26},{10,24},{12,30},{14,28},{16,2},... | collective-permute-start | bytes 393224 | tf_op jit(solution)/shard_map/ppermute | solution.py:455
  62.4 7.1 %collective-permute-start.20 = (bf16[2,256,128]{2,1,0:T(8,128)(2,1)S(1)}, bf16[2,256,128]{2,1,0:T(8,128)(2,1)S(1)}, u32[]{:S(2)}, u32[]{:S(2)}) collective-permute-start(bf16[2,256,128]{2,1,0:T(8,128)(2,1)S(1)} %get-tuple-element.174), channel_id=1, source_target_pairs={{0,2},{2,0},{4,6},{6,4},{8,10},{10,8},{12,14},{14,12},{1,3},{3,1},... | collective-permute-start | bytes 393224 | tf_op jit(solution)/shard_map/ppermute | solution.py:458
  63.4 6.4 %collective-permute-start.21 = (bf16[2,256,128]{2,1,0:T(8,128)(2,1)S(1)}, bf16[2,256,128]{2,1,0:T(8,128)(2,1)S(1)}, u32[]{:S(2)}, u32[]{:S(2)}) collective-permute-start(bf16[2,256,128]{2,1,0:T(8,128)(2,1)S(1)} %get-tuple-element.178), channel_id=1, source_target_pairs={{0,16},{16,0},{1,17},{17,1},{2,18},{18,2},{3,19},{19,3},{4,20},{20... | collective-permute-start | bytes 393224 | tf_op jit(solution)/shard_map/ppermute | solution.py:461
  64.1 1.3 %collective-permute-start.18 = (bf16[256,128]{1,0:T(8,128)(2,1)S(1)}, bf16[256,128]{1,0:T(8,128)(2,1)S(1)}, u32[]{:S(2)}, u32[]{:S(2)}) collective-permute-start(bf16[256,128]{1,0:T(8,128)(2,1)S(1)} %shard_map.58.refs_9_), channel_id=1, source_target_pairs={{0,1},{1,0},{2,3},{3,2},{4,5},{5,4},{6,7},{7,6},{8,9},{9,8},{10,11... | collective-permute-start | bytes 196616 | tf_op jit(solution)/shard_map/ppermute | solution.py:446

commit v8 on v7

--- a/solution.py
+++ b/solution.py
@@ -159,38 +159,19 @@
     )
 
 
-def select_kernel(columns, part, rows_ref, *refs):
-    out_refs, sems = refs[:len(columns)], refs[-1]
-    rows = pl.ds(pl.multiple_of(lax.axis_index("groups") * part, HEAD), part)
-    copies = []
+def split_kernel(columns, rows_ref, *out_refs):
     for starts, out_ref in zip(columns, out_refs):
-        at = 0
-        while at < len(starts):
-            more = 1
-            while at + more < len(starts) and starts[at + more] == starts[at] + more * HEAD:
-                more += 1
-            copies.append(pltpu.make_async_copy(
-                rows_ref.at[0, rows, pl.ds(starts[at], more * HEAD)],
-                out_ref.at[:, pl.ds(at * HEAD, more * HEAD)],
-                sems.at[len(copies)],
-            ))
-            at += more
-    for copy in copies:
-        copy.start()
-    for copy in copies:
-        copy.wait()
-
-
-def select(projection, part, columns):
-    chunk = jax.ShapeDtypeStruct((part, len(columns[0]) * HEAD), projection.dtype)
-    out_shape = (chunk,) * len(columns)
+        for i, start in enumerate(starts):
+            out_ref[:, i * HEAD:(i + 1) * HEAD] = rows_ref[:, start:start + HEAD]
+
+
+def split(rows, columns):
     return call(
-        functools.partial(select_kernel, columns, part),
-        out_shape,
-        in_specs=[pl.BlockSpec(memory_space=pltpu.HBM)],
-        out_specs=[WHOLE] * len(out_shape),
-        scratch_shapes=[pltpu.SemaphoreType.DMA((len(columns) * len(columns[0]),))],
-    )(pltpu.with_memory_space_constraint(projection, pltpu.HBM))
+        functools.partial(split_kernel, columns),
+        tuple(jax.ShapeDtypeStruct((rows.shape[0], len(c) * HEAD), rows.dtype) for c in columns),
+        in_specs=[WHOLE],
+        out_specs=[WHOLE] * len(columns),
+    )(rows)
 
 
 def gate_kernel(part, depth, hidden_ref, gain_ref, *refs):
@@ -242,7 +223,7 @@
     )(*(pltpu.with_memory_space_constraint(a, pltpu.HBM) for a in (hidden_in, norm_gain)))
 
 
-def matmul_kernel(firsts, n_acts, n_more, sent, *refs):
+def matmul_kernel(firsts, n_acts, n_more, sent, paired, *refs):
     is_first = lax.axis_index("tensor") == 0
     acts, refs = refs[:n_acts], refs[n_acts:]
     slots, refs = refs[:len(firsts)], refs[len(firsts):]
@@ -264,14 +245,15 @@
         n_blocks = mine_ref.shape[1]
         per = n_acts * n_blocks // sent
         for g in range(n_blocks):
-            low = total[:, g * wide:g * wide + HEAD]
-            high = total[:, g * wide + HEAD:(g + 1) * wide]
+            at, apart = (g * wide, HEAD) if paired else (g * HEAD, n_blocks * HEAD)
+            low = total[:, at:at + HEAD]
+            high = total[:, at + apart:at + apart + HEAD]
             spot = p * n_blocks + g
             theirs_refs[spot // per][spot % per] = jnp.where(is_first, high, low).astype(jnp.bfloat16)
             mine_ref[p, g] = jnp.where(is_first, low, high)
 
 
-def matmul(acts, slots, firsts, so_far=(), sent=0):
+def matmul(acts, slots, firsts, so_far=(), sent=0, paired=True):
     n_blocks = slots[0].shape[1] // (2 * HEAD)
     tokens = acts[0].shape[1]
     args = [*acts, *slots, *so_far]
@@ -281,7 +263,7 @@
     else:
         out_shape = (jax.ShapeDtypeStruct((len(acts), tokens, n_blocks * 2 * HEAD), jnp.float32),)
     outs = call(
-        functools.partial(matmul_kernel, firsts, len(acts), len(so_far), sent),
+        functools.partial(matmul_kernel, firsts, len(acts), len(so_far), sent, paired),
         out_shape,
         in_specs=[WHOLE] * len(args),
         out_specs=[WHOLE] * len(out_shape),
@@ -378,19 +360,19 @@
     copies = []
 
     def put(source, at):
-        copies.append(pltpu.make_async_copy(source, out_ref.at[:, pl.ds(at, source.shape[1])], sems.at[len(copies)]))
+        where = pl.ds(pl.multiple_of(at, HEAD), HEAD)
+        copies.append(pltpu.make_async_copy(source, out_ref.at[:, where], sems.at[len(copies)]))
         copies[-1].start()
 
     is_key = lax.axis_index("tensor") == 0
     mine, other = mine_ref[...], other_ref[...]
     keys = jnp.where(is_key, mine, other)
     values = jnp.where(is_key, other, mine)
-    before = 0
+    count = parts[0].shape[0] - first
+    before = jnp.where(is_key, HEAD, 0)
     for earlier_ref in earlier_refs:
-        put(earlier_ref, before)
-        before += earlier_ref.shape[1]
+        put(earlier_ref, jnp.where(is_key, 0, count * HEAD))
     tokens = mine.shape[0]
-    count = parts[0].shape[0] - first
     query = [turned(summed(parts, first + i, scale_ref), cosine_ref, sine_ref).astype(jnp.bfloat16) for i in range(count)]
     scores = lax.dot_general(
         jnp.concatenate(query, axis=0), keys, (((1,), (1,)), ((), ())), preferred_element_type=jnp.float32
@@ -470,30 +452,30 @@
         last[:] = held[:1]
         return held[0] if len(values) == 1 else held
 
-    blocks = [[(QHEADS + c) * HEAD for c in range(tensor)]]
-    blocks += [[(c * heads_local + i) * HEAD for c in range(tensor)] for i in range(heads_local)]
-    columns = [blocks[0] + blocks[1], blocks[2] + blocks[3]]
-    a0, = select(projection, part, columns[:1])
+    columns_a = [(QHEADS + c) * HEAD for c in range(tensor)] + [0, (QHEADS - 1) * HEAD]
+    columns_b = [i * HEAD for i in range(1, QHEADS - 1)]
+    start = (0, lax.axis_index("groups") * part, 0)
+    rows = lax.dynamic_slice(projection, start, (1, part, projection.shape[2]))[0]
+    b0, a0 = split(rows, (columns_b, columns_a))
+    b1 = on_ring(b0)
+    far, near_x, near_y, own, squares = after(*gate(hidden_in, norm_gain, part, depth))
+    near_x = to_x(near_x)
+    near_y = to_y(near_y)
     a0 = after(a0)
     a1 = on_ring(a0)
-    far, near_x, near_y, own, squares = after(*gate(after(hidden_in), norm_gain, part, depth))
-    near_x = to_x(near_x)
-    near_y = to_y(near_y)
-    b0, = select(after(projection), part, columns[1:])
-    b0, a0 = after(b0, a0)
-    a3 = back(a0)
     other_squares = to_core(squares)
     tabled = after(*tables(tokens, lengths, after(squares)))
     scale = after(inv_rms(squares, after(other_squares)))
 
-    a1, b0, far = after(a1, b0, far)
-    b1 = on_ring(b0)
+    b1, a0, far = after(b1, a0, far)
+    a3 = back(a0)
     far = to_far(far)
-    a3, a1 = after(a3, a1)
+    a1 = after(a1)
     a2 = on_ring(a1)
+    b0 = after(b0)
     near_y = after(near_y)
     near_x = after(near_x)
-    b1 = after(b1)
+    a3, b1 = after(a3, b1)
     b2 = on_ring(b1)
     early = (near_x, near_y, own)
     front = after(matmul(early, (a0, a1, a3), (0, 1, 3)))
@@ -520,7 +502,7 @@
 
     b3 = after(b3)
     parts_a = after(sums, sums_far, sums_x, sums_y)
-    *theirs, mine = after(*matmul(acts, (b3,), (3,), (front,), sent=2))
+    *theirs, mine = after(*matmul(acts, (b3,), (3,), (front,), sent=2, paired=False))
     swapped = [to_core(t) for t in theirs]
     kv = after(call(
         kv_kernel,

time: 71.3 us -> 71.2 us (level)
  Pallas kernels: 12.8 us -> 10.8 us
  local copies, waits for them, and re-layouts: 0.01 us -> 1.47 us
  waiting for transfers between devices: 34 us -> 35 us
    pallas_call x2 -> x1, Pallas kernels: 2.15 us -> 0.08 us  [split(): call(functools.partial(split_kernel, columns), tuple((jax.ShapeDtypeStruc...]
    ppermute x3, waiting for transfers between devices: 5.29 us -> 7.04 us  [to_x(): return lax.ppermute(a, 'dp', over_x)]
    unnamed x2 -> x4, local copies, waits for them, and re-layouts: 0.01 us -> 1.41 us
    ppermute x3, starting transfers between devices: 7.02 us -> 6.12 us  [to_far(): return lax.ppermute(a, ('groups', 'dp'), across)]
    ppermute x4, waiting for transfers between devices: 17 us -> 16.1 us  [on_ring(): return lax.ppermute(a, 'dp', ring)]
  transfers between devices with their start and end apart: 22 -> 22, of which waited for: 14 -> 13; matrix products, arithmetic and copies ran while one was open for 0% -> 0% of each run, Pallas kernels for 15% -> 13%
where the time goes in v8:
time: 71.2 us; the launch traced here: 71.1 us
  waiting for transfers between devices  35 us (49%)
  starting transfers between devices  23.7 us (33%)
  Pallas kernels  10.8 us (15%)
  local copies, waits for them, and re-layouts  1.47 us (2%)
    ppermute x4, waiting for transfers between devices, on_ring(): return lax.ppermute(a, 'dp', ring)  16.1 us
    ppermute x3, waiting for transfers between devices, to_x(): return lax.ppermute(a, 'dp', over_x)  7.04 us
    ppermute x2, waiting for transfers between devices, back(): return lax.ppermute(a, 'dp', [(j, i) for i, j in ring])  6.64 us
    ppermute x3, starting transfers between devices, to_far(): return lax.ppermute(a, ('groups', 'dp'), across)  6.12 us
    pallas_call x5, Pallas kernels, matmul(): call(functools.partial(matmul_kernel, firsts, len(acts), len(so_far), sen...  5.11 us
    ppermute x4, starting transfers between devices, on_ring(): return lax.ppermute(a, 'dp', ring)  5.05 us
    ppermute x3, starting transfers between devices, to_y(): return lax.ppermute(a, 'groups', over_y)  3.84 us
    ppermute x2, starting transfers between devices, back(): return lax.ppermute(a, 'dp', [(j, i) for i, j in ring])  3.84 us
  transfers between devices with their start and end apart: 22, of which 13 were waited for; matrix products, arithmetic and copies ran while one was open for 0% of the time, Pallas kernels for 13%

profile of v8, /device:TPU:0, one launch (start us, length us, event | category | flops | bytes accessed | tf_op | source)
XLA Modules:
  0.0 71.1 jit_solution(13290197550069573403)
XLA Ops:
  0.0 1.4 %copy-done = bf16[1,768,1024]{2,1,0:T(8,128)(2,1)S(1)} copy-done((bf16[1,768,1024]{2,1,0:T(8,128)(2,1)S(1)}, bf16[1,768,1024]{2,1,0:T(8,128)(2,1)}, u32[]{:S(2)}) %copy-start) | copy-done | bytes 1572888
  1.6 3.1 %collective-permute-start = (bf16[384,512]{1,0:T(8,128)(2,1)S(1)}, bf16[384,512]{1,0:T(8,128)(2,1)S(1)}, u32[]{:S(2)}, u32[]{:S(2)}) collective-permute-start(bf16[384,512]{1,0:T(8,128)(2,1)S(1)} %get-tuple-element.119.refs_4_), channel_id=1, source_target_pairs={{0,4},{2,6},{4,8},{6,10},{8,12},{10,14},{12,0},{14,2},{1,5},{3,7},... | collective-permute-start | bytes 1179656 | tf_op jit(solution)/shard_map/ppermute | solution.py:431
  4.6 2.2 %shard_map.47 = (bf16[4,256,384]{2,1,0:T(8,128)(2,1)S(1)}, bf16[4,256,384]{2,1,0:T(8,128)(2,1)S(1)}, bf16[4,256,384]{2,1,0:T(8,128)(2,1)S(1)}, bf16[4,256,384]{2,1,0:T(8,128)(2,1)S(1)}, f32[256,128]{1,0:T(8,128)S(1)}) custom-call(bf16[256,6144]{1,0:T(8,128)(2,1)} %hidden_ref.1, bf16[6144]{0:T(1024)(128)(2,1)} %gain_ref.1), custom_call_target="tpu_custom_call" | custom-call | flops 1 | bytes 1 | tf_op jit(solution)/shard_map/pallas_call | solution.py:212
  6.8 1.6 %collective-permute-start.5 = (bf16[4,256,384]{2,1,0:T(8,128)(2,1)S(1)}, bf16[4,256,384]{2,1,0:T(8,128)(2,1)S(1)}, u32[]{:S(2)}, u32[]{:S(2)}) collective-permute-start(bf16[4,256,384]{2,1,0:T(8,128)(2,1)S(1)} %get-tuple-element.106), channel_id=1, source_target_pairs={{0,16},{16,0},{1,17},{17,1},{2,18},{18,2},{3,19},{19,3},{4,20},{20... | collective-permute-start | bytes 2359304 | tf_op jit(solution)/shard_map/ppermute | solution.py:443
  8.4 1.5 %collective-permute-start.4 = (bf16[4,256,384]{2,1,0:T(8,128)(2,1)S(1)}, bf16[4,256,384]{2,1,0:T(8,128)(2,1)S(1)}, u32[]{:S(2)}, u32[]{:S(2)}) collective-permute-start(bf16[4,256,384]{2,1,0:T(8,128)(2,1)S(1)} %get-tuple-element.105), channel_id=1, source_target_pairs={{0,2},{2,0},{4,6},{6,4},{8,10},{10,8},{12,14},{14,12},{1,3},{3,1},... | collective-permute-start | bytes 2359304 | tf_op jit(solution)/shard_map/ppermute | solution.py:440
  9.9 1.6 %collective-permute-start.3 = (bf16[384,512]{1,0:T(8,128)(2,1)S(1)}, bf16[384,512]{1,0:T(8,128)(2,1)S(1)}, u32[]{:S(2)}, u32[]{:S(2)}) collective-permute-start(bf16[384,512]{1,0:T(8,128)(2,1)S(1)} %get-tuple-element.110.refs_3_.refs_1_), channel_id=1, source_target_pairs={{0,4},{2,6},{4,8},{6,10},{8,12},{10,14},{12,0},{14,2},{1,5},{3,7},... | collective-permute-start | bytes 1179656 | tf_op jit(solution)/shard_map/ppermute | solution.py:431
  11.5 1.1 %shard_map.48 = (f32[256,128]{1,0:T(8,128)S(1)}, f32[256,128]{1,0:T(8,128)S(1)}, f32[256,256]{1,0:T(8,128)S(1)}, f32[256,128]{1,0:T(8,128)S(1)}) custom-call(s32[1,2]{1,0:T(1,128)S(1)} %copy-done.1, f32[256,128]{1,0:T(8,128)S(1)} %get-tuple-element.93._.own_ref), custom_call_target="tpu_custom_call" | custom-call | flops 1 | bytes 1 | tf_op jit(solution)/shard_map/pallas_call | solution.py:312
  12.7 3.9 %collective-permute-done.refs_5_ = bf16[384,512]{1,0:T(8,128)(2,1)S(1)} collective-permute-done((bf16[384,512]{1,0:T(8,128)(2,1)S(1)}, bf16[384,512]{1,0:T(8,128)(2,1)S(1)}, u32[]{:S(2)}, u32[]{:S(2)}) %collective-permute-start) | collective-permute-done | bytes 393248 | tf_op jit(solution)/shard_map/ppermute | solution.py:431
  16.6 2.7 %collective-permute-start.2 = (bf16[4,256,384]{2,1,0:T(8,128)(2,1)S(1)}, bf16[4,256,384]{2,1,0:T(8,128)(2,1)S(1)}, u32[]{:S(2)}, u32[]{:S(2)}) collective-permute-start(bf16[4,256,384]{2,1,0:T(8,128)(2,1)S(1)} %get-tuple-element.101), channel_id=1, source_target_pairs={{0,18},{2,16},{4,22},{6,20},{8,26},{10,24},{12,30},{14,28},{16,2},... | collective-permute-start | bytes 2359304 | tf_op jit(solution)/shard_map/ppermute | solution.py:437
  19.3 1.8 %collective-permute-start.7 = (bf16[384,512]{1,0:T(8,128)(2,1)S(1)}, bf16[384,512]{1,0:T(8,128)(2,1)S(1)}, u32[]{:S(2)}, u32[]{:S(2)}) collective-permute-start(bf16[384,512]{1,0:T(8,128)(2,1)S(1)} %get-tuple-element.110.refs_3_.refs_1_), channel_id=1, source_target_pairs={{4,0},{6,2},{8,4},{10,6},{12,8},{14,10},{0,12},{2,14},{5,1},{7,3},... | collective-permute-start | bytes 1179656 | tf_op jit(solution)/shard_map/ppermute | solution.py:434
  21.1 4.0 %collective-permute-done.3.refs_4_.refs_2_ = bf16[384,512]{1,0:T(8,128)(2,1)S(1)} collective-permute-done((bf16[384,512]{1,0:T(8,128)(2,1)S(1)}, bf16[384,512]{1,0:T(8,128)(2,1)S(1)}, u32[]{:S(2)}, u32[]{:S(2)}) %collective-permute-start.3) | collective-permute-done | bytes 393248 | tf_op jit(solution)/shard_map/ppermute | solution.py:431
  25.1 0.8 %collective-permute-done.5.refs_1_.refs_3_ = bf16[4,256,384]{2,1,0:T(8,128)(2,1)S(1)} collective-permute-done((bf16[4,256,384]{2,1,0:T(8,128)(2,1)S(1)}, bf16[4,256,384]{2,1,0:T(8,128)(2,1)S(1)}, u32[]{:S(2)}, u32[]{:S(2)}) %collective-permute-start.5) | collective-permute-done | bytes 786464 | tf_op jit(solution)/shard_map/ppermute | solution.py:443
  25.9 2.8 %collective-permute-done.4.refs_0_.refs_2_ = bf16[4,256,384]{2,1,0:T(8,128)(2,1)S(1)} collective-permute-done((bf16[4,256,384]{2,1,0:T(8,128)(2,1)S(1)}, bf16[4,256,384]{2,1,0:T(8,128)(2,1)S(1)}, u32[]{:S(2)}, u32[]{:S(2)}) %collective-permute-start.4) | collective-permute-done | bytes 786464 | tf_op jit(solution)/shard_map/ppermute | solution.py:440
  28.7 4.8 %collective-permute-done.7.refs_5_.refs_4_ = bf16[384,512]{1,0:T(8,128)(2,1)S(1)} collective-permute-done((bf16[384,512]{1,0:T(8,128)(2,1)S(1)}, bf16[384,512]{1,0:T(8,128)(2,1)S(1)}, u32[]{:S(2)}, u32[]{:S(2)}) %collective-permute-start.7) | collective-permute-done | bytes 393248 | tf_op jit(solution)/shard_map/ppermute | solution.py:434
  33.9 1.4 %shard_map.50.refs_4_ = f32[3,256,512]{2,1,0:T(8,128)S(1)} custom-call(bf16[4,256,384]{2,1,0:T(8,128)(2,1)S(1)} %collective-permute-done.4.refs_0_.refs_2_, bf16[4,256,384]{2,1,0:T(8,128)(2,1)S(1)} %collective-permute-done.5.refs_1_.refs_3_, bf16[4,256,384]{2,1,0:T(8,128)(2,1)S(1)} %get-tuple-element.109.refs_2_.refs_1_, ...), custom_call_target="tpu_custom_call" | custom-call | flops 1 | bytes 1 | tf_op jit(solution)/shard_map/pallas_call | solution.py:265
  35.3 8.1 %collective-permute-done.6.refs_3_ = bf16[384,512]{1,0:T(8,128)(2,1)S(1)} collective-permute-done((bf16[384,512]{1,0:T(8,128)(2,1)S(1)}, bf16[384,512]{1,0:T(8,128)(2,1)S(1)}, u32[]{:S(2)}, u32[]{:S(2)}) %collective-permute-start.6) | collective-permute-done | bytes 393248 | tf_op jit(solution)/shard_map/ppermute | solution.py:431
  45.2 2.0 %collective-permute-start.8 = (bf16[384,512]{1,0:T(8,128)(2,1)S(1)}, bf16[384,512]{1,0:T(8,128)(2,1)S(1)}, u32[]{:S(2)}, u32[]{:S(2)}) collective-permute-start(bf16[384,512]{1,0:T(8,128)(2,1)S(1)} %get-tuple-element.119.refs_4_), channel_id=1, source_target_pairs={{4,0},{6,2},{8,4},{10,6},{12,8},{14,10},{0,12},{2,14},{5,1},{7,3},... | collective-permute-start | bytes 1179656 | tf_op jit(solution)/shard_map/ppermute | solution.py:434
  47.2 0.7 shard_map.52
  48.1 1.8 %collective-permute-start.13 = (bf16[2,256,128]{2,1,0:T(8,128)(2,1)S(1)}, bf16[2,256,128]{2,1,0:T(8,128)(2,1)S(1)}, u32[]{:S(2)}, u32[]{:S(2)}) collective-permute-start(bf16[2,256,128]{2,1,0:T(8,128)(2,1)S(1)} %get-tuple-element.133), channel_id=1, source_target_pairs={{0,16},{16,0},{1,17},{17,1},{2,18},{18,2},{3,19},{19,3},{4,20},{20... | collective-permute-start | bytes 393224 | tf_op jit(solution)/shard_map/ppermute | solution.py:443
  49.8 1.5 %collective-permute-start.12 = (bf16[2,256,128]{2,1,0:T(8,128)(2,1)S(1)}, bf16[2,256,128]{2,1,0:T(8,128)(2,1)S(1)}, u32[]{:S(2)}, u32[]{:S(2)}) collective-permute-start(bf16[2,256,128]{2,1,0:T(8,128)(2,1)S(1)} %get-tuple-element.130), channel_id=1, source_target_pairs={{0,2},{2,0},{4,6},{6,4},{8,10},{10,8},{12,14},{14,12},{1,3},{3,1},... | collective-permute-start | bytes 393224 | tf_op jit(solution)/shard_map/ppermute | solution.py:440
  51.4 0.9 %collective-permute-start.15 = (bf16[2,256,128]{2,1,0:T(8,128)(2,1)S(1)}, bf16[2,256,128]{2,1,0:T(8,128)(2,1)S(1)}, u32[]{:S(2)}, u32[]{:S(2)}) collective-permute-start(bf16[2,256,128]{2,1,0:T(8,128)(2,1)S(1)} %shard_map.55), channel_id=1, source_target_pairs={{0,18},{2,16},{4,22},{6,20},{8,26},{10,24},{12,30},{14,28},{16,2},... | collective-permute-start | bytes 393224 | tf_op jit(solution)/shard_map/ppermute | solution.py:437
  52.3 1.8 %shard_map.54.refs_5_ = f32[4,256,512]{2,1,0:T(8,128)S(1)} custom-call(bf16[4,256,384]{2,1,0:T(8,128)(2,1)S(1)} %collective-permute-done.2.refs_0_, bf16[4,256,384]{2,1,0:T(8,128)(2,1)S(1)} %get-tuple-element.109.refs_2_.refs_1_, bf16[4,256,384]{2,1,0:T(8,128)(2,1)S(1)} %collective-permute-done.4.refs_0_.refs_2_, ...), custom_call_target="tpu_custom_call" | custom-call | flops 1 | bytes 1 | tf_op jit(solution)/shard_map/pallas_call | solution.py:265
  54.1 2.1 %collective-permute-done.12.r1.refs_2_ = bf16[2,256,128]{2,1,0:T(8,128)(2,1)S(1)} collective-permute-done((bf16[2,256,128]{2,1,0:T(8,128)(2,1)S(1)}, bf16[2,256,128]{2,1,0:T(8,128)(2,1)S(1)}, u32[]{:S(2)}, u32[]{:S(2)}) %collective-permute-start.12) | collective-permute-done | bytes 131104 | tf_op jit(solution)/shard_map/ppermute | solution.py:440
  56.2 1.8 %collective-permute-done.8.refs_4_ = bf16[384,512]{1,0:T(8,128)(2,1)S(1)} collective-permute-done((bf16[384,512]{1,0:T(8,128)(2,1)S(1)}, bf16[384,512]{1,0:T(8,128)(2,1)S(1)}, u32[]{:S(2)}, u32[]{:S(2)}) %collective-permute-start.8) | collective-permute-done | bytes 393248 | tf_op jit(solution)/shard_map/ppermute | solution.py:434
  58.0 0.7 shard_map.56
  59.4 0.9 %collective-permute-done.16.refs_0_ = bf16[4,256,128]{2,1,0:T(8,128)(2,1)S(1)} collective-permute-done((bf16[4,256,128]{2,1,0:T(8,128)(2,1)S(1)}, bf16[4,256,128]{2,1,0:T(8,128)(2,1)S(1)}, u32[]{:S(2)}, u32[]{:S(2)}) %collective-permute-start.16) | collective-permute-done | bytes 262176 | tf_op jit(solution)/shard_map/ppermute | solution.py:428
  60.4 2.5 %collective-permute-start.17 = (bf16[2,256,128]{2,1,0:T(8,128)(2,1)S(1)}, bf16[2,256,128]{2,1,0:T(8,128)(2,1)S(1)}, u32[]{:S(2)}, u32[]{:S(2)}) collective-permute-start(bf16[2,256,128]{2,1,0:T(8,128)(2,1)S(1)} %get-tuple-element.157), channel_id=1, source_target_pairs={{0,18},{2,16},{4,22},{6,20},{8,26},{10,24},{12,30},{14,28},{16,2},... | collective-permute-start | bytes 393224 | tf_op jit(solution)/shard_map/ppermute | solution.py:437
  62.9 0.6 collective-permute-start.20
  64.0 1.3 %collective-permute-done.18.refs_10_ = bf16[256,128]{1,0:T(8,128)(2,1)S(1)} collective-permute-done((bf16[256,128]{1,0:T(8,128)(2,1)S(1)}, bf16[256,128]{1,0:T(8,128)(2,1)S(1)}, u32[]{:S(2)}, u32[]{:S(2)}) %collective-permute-start.18) | collective-permute-done | bytes 65568 | tf_op jit(solution)/shard_map/ppermute | solution.py:428
  65.9 1.8 %collective-permute-done.17.refs_1_ = bf16[2,256,128]{2,1,0:T(8,128)(2,1)S(1)} collective-permute-done((bf16[2,256,128]{2,1,0:T(8,128)(2,1)S(1)}, bf16[2,256,128]{2,1,0:T(8,128)(2,1)S(1)}, u32[]{:S(2)}, u32[]{:S(2)}) %collective-permute-start.17) | collective-permute-done | bytes 131104 | tf_op jit(solution)/shard_map/ppermute | solution.py:437
  67.7 2.1 %collective-permute-done.20.refs_2_ = bf16[2,256,128]{2,1,0:T(8,128)(2,1)S(1)} collective-permute-done((bf16[2,256,128]{2,1,0:T(8,128)(2,1)S(1)}, bf16[2,256,128]{2,1,0:T(8,128)(2,1)S(1)}, u32[]{:S(2)}, u32[]{:S(2)}) %collective-permute-start.20) | collective-permute-done | bytes 131104 | tf_op jit(solution)/shard_map/ppermute | solution.py:440
  69.7 1.4 %shard_map.61 = bf16[256,384]{1,0:T(8,128)(2,1)} custom-call(f32[2,256,128]{2,1,0:T(8,128)S(1)} %get-tuple-element.156.refs_0_, bf16[2,256,128]{2,1,0:T(8,128)(2,1)S(1)} %collective-permute-done.17.refs_1_, bf16[2,256,128]{2,1,0:T(8,128)(2,1)S(1)} %collective-permute-done.20.refs_2_, bf16[2,256,128]{2,1,0:T(8,128)(2,1)S(1)} %collective-permute-done.21.refs_3_, ...), custom_call_target="tpu_custom_call" | custom-call | flops 1 | bytes 1 | tf_op jit(solution)/shard_map/pallas_call | solution.py:402
  (33 shorter events, 4.4 us)
Async XLA Ops:
  0.0 1.4 %copy-start = (bf16[1,768,1024]{2,1,0:T(8,128)(2,1)S(1)}, bf16[1,768,1024]{2,1,0:T(8,128)(2,1)}, u32[]{:S(2)}) copy-start(bf16[1,768,1024]{2,1,0:T(8,128)(2,1)} %param.6) | copy-start | bytes 4718596
  1.6 9.9 %copy-start.1 = (s32[1,2]{1,0:T(1,128)S(1)}, s32[1,2]{1,0:T(1,128)}, u32[]{:S(2)}) copy-start(s32[1,2]{1,0:T(1,128)} %lengths_ref.1) | copy-start | bytes 28
  1.6 15.0 %collective-permute-start = (bf16[384,512]{1,0:T(8,128)(2,1)S(1)}, bf16[384,512]{1,0:T(8,128)(2,1)S(1)}, u32[]{:S(2)}, u32[]{:S(2)}) collective-permute-start(bf16[384,512]{1,0:T(8,128)(2,1)S(1)} %get-tuple-element.119.refs_4_), channel_id=1, source_target_pairs={{0,4},{2,6},{4,8},{6,10},{8,12},{10,14},{12,0},{14,2},{1,5},{3,7},... | collective-permute-start | bytes 1179656 | tf_op jit(solution)/shard_map/ppermute | solution.py:431
  6.8 19.1 %collective-permute-start.5 = (bf16[4,256,384]{2,1,0:T(8,128)(2,1)S(1)}, bf16[4,256,384]{2,1,0:T(8,128)(2,1)S(1)}, u32[]{:S(2)}, u32[]{:S(2)}) collective-permute-start(bf16[4,256,384]{2,1,0:T(8,128)(2,1)S(1)} %get-tuple-element.106), channel_id=1, source_target_pairs={{0,16},{16,0},{1,17},{17,1},{2,18},{18,2},{3,19},{19,3},{4,20},{20... | collective-permute-start | bytes 2359304 | tf_op jit(solution)/shard_map/ppermute | solution.py:443
  8.4 4.2 %collective-permute-start.1 = (f32[256,128]{1,0:T(8,128)S(1)}, f32[256,128]{1,0:T(8,128)S(1)}, u32[]{:S(2)}, u32[]{:S(2)}) collective-permute-start(f32[256,128]{1,0:T(8,128)S(1)} %get-tuple-element.93._.own_ref), channel_id=1, source_target_pairs={{0,1},{1,0},{2,3},{3,2},{4,5},{5,4},{6,7},{7,6},{8,9},{9,8},{10,11... | collective-permute-start | bytes 393224 | tf_op jit(solution)/shard_map/ppermute | solution.py:428
  8.4 20.3 %collective-permute-start.4 = (bf16[4,256,384]{2,1,0:T(8,128)(2,1)S(1)}, bf16[4,256,384]{2,1,0:T(8,128)(2,1)S(1)}, u32[]{:S(2)}, u32[]{:S(2)}) collective-permute-start(bf16[4,256,384]{2,1,0:T(8,128)(2,1)S(1)} %get-tuple-element.105), channel_id=1, source_target_pairs={{0,2},{2,0},{4,6},{6,4},{8,10},{10,8},{12,14},{14,12},{1,3},{3,1},... | collective-permute-start | bytes 2359304 | tf_op jit(solution)/shard_map/ppermute | solution.py:440
  9.9 15.2 %collective-permute-start.3 = (bf16[384,512]{1,0:T(8,128)(2,1)S(1)}, bf16[384,512]{1,0:T(8,128)(2,1)S(1)}, u32[]{:S(2)}, u32[]{:S(2)}) collective-permute-start(bf16[384,512]{1,0:T(8,128)(2,1)S(1)} %get-tuple-element.110.refs_3_.refs_1_), channel_id=1, source_target_pairs={{0,4},{2,6},{4,8},{6,10},{8,12},{10,14},{12,0},{14,2},{1,5},{3,7},... | collective-permute-start | bytes 1179656 | tf_op jit(solution)/shard_map/ppermute | solution.py:431
  16.6 28.5 %collective-permute-start.2 = (bf16[4,256,384]{2,1,0:T(8,128)(2,1)S(1)}, bf16[4,256,384]{2,1,0:T(8,128)(2,1)S(1)}, u32[]{:S(2)}, u32[]{:S(2)}) collective-permute-start(bf16[4,256,384]{2,1,0:T(8,128)(2,1)S(1)} %get-tuple-element.101), channel_id=1, source_target_pairs={{0,18},{2,16},{4,22},{6,20},{8,26},{10,24},{12,30},{14,28},{16,2},... | collective-permute-start | bytes 2359304 | tf_op jit(solution)/shard_map/ppermute | solution.py:437
  19.3 14.2 %collective-permute-start.7 = (bf16[384,512]{1,0:T(8,128)(2,1)S(1)}, bf16[384,512]{1,0:T(8,128)(2,1)S(1)}, u32[]{:S(2)}, u32[]{:S(2)}) collective-permute-start(bf16[384,512]{1,0:T(8,128)(2,1)S(1)} %get-tuple-element.110.refs_3_.refs_1_), channel_id=1, source_target_pairs={{4,0},{6,2},{8,4},{10,6},{12,8},{14,10},{0,12},{2,14},{5,1},{7,3},... | collective-permute-start | bytes 1179656 | tf_op jit(solution)/shard_map/ppermute | solution.py:434
  25.1 18.3 %collective-permute-start.6 = (bf16[384,512]{1,0:T(8,128)(2,1)S(1)}, bf16[384,512]{1,0:T(8,128)(2,1)S(1)}, u32[]{:S(2)}, u32[]{:S(2)}) collective-permute-start(bf16[384,512]{1,0:T(8,128)(2,1)S(1)} %collective-permute-done.3.refs_4_.refs_2_), channel_id=1, source_target_pairs={{0,4},{2,6},{4,8},{6,10},{8,12},{10,14},{12,0},{14,2},{1,5},{3,7},... | collective-permute-start | bytes 1179656 | tf_op jit(solution)/shard_map/ppermute | solution.py:431
  33.6 17.8 %collective-permute-start.9 = (bf16[384,512]{1,0:T(8,128)(2,1)S(1)}, bf16[384,512]{1,0:T(8,128)(2,1)S(1)}, u32[]{:S(2)}, u32[]{:S(2)}) collective-permute-start(bf16[384,512]{1,0:T(8,128)(2,1)S(1)} %collective-permute-done.refs_5_), channel_id=1, source_target_pairs={{0,4},{2,6},{4,8},{6,10},{8,12},{10,14},{12,0},{14,2},{1,5},{3,7},... | collective-permute-start | bytes 1179656 | tf_op jit(solution)/shard_map/ppermute | solution.py:431
  44.0 3.9 %collective-permute-start.10 = (bf16[3,256,128]{2,1,0:T(8,128)(2,1)S(1)}, bf16[3,256,128]{2,1,0:T(8,128)(2,1)S(1)}, u32[]{:S(2)}, u32[]{:S(2)}) collective-permute-start(bf16[3,256,128]{2,1,0:T(8,128)(2,1)S(1)} %get-tuple-element.117), channel_id=1, source_target_pairs={{0,1},{1,0},{2,3},{3,2},{4,5},{5,4},{6,7},{7,6},{8,9},{9,8},{10,11... | collective-permute-start | bytes 589832 | tf_op jit(solution)/shard_map/ppermute | solution.py:428
  44.1 3.8 %collective-permute-start.11 = (bf16[3,256,128]{2,1,0:T(8,128)(2,1)S(1)}, bf16[3,256,128]{2,1,0:T(8,128)(2,1)S(1)}, u32[]{:S(2)}, u32[]{:S(2)}) collective-permute-start(bf16[3,256,128]{2,1,0:T(8,128)(2,1)S(1)} %get-tuple-element.124), channel_id=1, source_target_pairs={{0,1},{1,0},{2,3},{3,2},{4,5},{5,4},{6,7},{7,6},{8,9},{9,8},{10,11... | collective-permute-start | bytes 589832 | tf_op jit(solution)/shard_map/ppermute | solution.py:428
  45.2 12.8 %collective-permute-start.8 = (bf16[384,512]{1,0:T(8,128)(2,1)S(1)}, bf16[384,512]{1,0:T(8,128)(2,1)S(1)}, u32[]{:S(2)}, u32[]{:S(2)}) collective-permute-start(bf16[384,512]{1,0:T(8,128)(2,1)S(1)} %get-tuple-element.119.refs_4_), channel_id=1, source_target_pairs={{4,0},{6,2},{8,4},{10,6},{12,8},{14,10},{0,12},{2,14},{5,1},{7,3},... | collective-permute-start | bytes 1179656 | tf_op jit(solution)/shard_map/ppermute | solution.py:434
  48.0 3.4 %collective-permute-start.14 = (bf16[2,256,128]{2,1,0:T(8,128)(2,1)S(1)}, bf16[2,256,128]{2,1,0:T(8,128)(2,1)S(1)}, u32[]{:S(2)}, u32[]{:S(2)}) collective-permute-start(bf16[2,256,128]{2,1,0:T(8,128)(2,1)S(1)} %get-tuple-element.131), channel_id=1, source_target_pairs={{0,1},{1,0},{2,3},{3,2},{4,5},{5,4},{6,7},{7,6},{8,9},{9,8},{10,11... | collective-permute-start | bytes 393224 | tf_op jit(solution)/shard_map/ppermute | solution.py:428
  48.1 6.0 %collective-permute-start.13 = (bf16[2,256,128]{2,1,0:T(8,128)(2,1)S(1)}, bf16[2,256,128]{2,1,0:T(8,128)(2,1)S(1)}, u32[]{:S(2)}, u32[]{:S(2)}) collective-permute-start(bf16[2,256,128]{2,1,0:T(8,128)(2,1)S(1)} %get-tuple-element.133), channel_id=1, source_target_pairs={{0,16},{16,0},{1,17},{17,1},{2,18},{18,2},{3,19},{19,3},{4,20},{20... | collective-permute-start | bytes 393224 | tf_op jit(solution)/shard_map/ppermute | solution.py:443
  49.8 6.3 %collective-permute-start.12 = (bf16[2,256,128]{2,1,0:T(8,128)(2,1)S(1)}, bf16[2,256,128]{2,1,0:T(8,128)(2,1)S(1)}, u32[]{:S(2)}, u32[]{:S(2)}) collective-permute-start(bf16[2,256,128]{2,1,0:T(8,128)(2,1)S(1)} %get-tuple-element.130), channel_id=1, source_target_pairs={{0,2},{2,0},{4,6},{6,4},{8,10},{10,8},{12,14},{14,12},{1,3},{3,1},... | collective-permute-start | bytes 393224 | tf_op jit(solution)/shard_map/ppermute | solution.py:440
  51.4 7.3 %collective-permute-start.15 = (bf16[2,256,128]{2,1,0:T(8,128)(2,1)S(1)}, bf16[2,256,128]{2,1,0:T(8,128)(2,1)S(1)}, u32[]{:S(2)}, u32[]{:S(2)}) collective-permute-start(bf16[2,256,128]{2,1,0:T(8,128)(2,1)S(1)} %shard_map.55), channel_id=1, source_target_pairs={{0,18},{2,16},{4,22},{6,20},{8,26},{10,24},{12,30},{14,28},{16,2},... | collective-permute-start | bytes 393224 | tf_op jit(solution)/shard_map/ppermute | solution.py:437
  58.7 1.6 %collective-permute-start.16 = (bf16[4,256,128]{2,1,0:T(8,128)(2,1)S(1)}, bf16[4,256,128]{2,1,0:T(8,128)(2,1)S(1)}, u32[]{:S(2)}, u32[]{:S(2)}) collective-permute-start(bf16[4,256,128]{2,1,0:T(8,128)(2,1)S(1)} %get-tuple-element.147), channel_id=1, source_target_pairs={{0,1},{1,0},{2,3},{3,2},{4,5},{5,4},{6,7},{7,6},{8,9},{9,8},{10,11... | collective-permute-start | bytes 786440 | tf_op jit(solution)/shard_map/ppermute | solution.py:428
  58.8 4.1 %collective-permute-start.19 = (bf16[4,256,128]{2,1,0:T(8,128)(2,1)S(1)}, bf16[4,256,128]{2,1,0:T(8,128)(2,1)S(1)}, u32[]{:S(2)}, u32[]{:S(2)}) collective-permute-start(bf16[4,256,128]{2,1,0:T(8,128)(2,1)S(1)} %get-tuple-element.160), channel_id=1, source_target_pairs={{0,1},{1,0},{2,3},{3,2},{4,5},{5,4},{6,7},{7,6},{8,9},{9,8},{10,11... | collective-permute-start | bytes 786440 | tf_op jit(solution)/shard_map/ppermute | solution.py:428
  60.4 7.3 %collective-permute-start.17 = (bf16[2,256,128]{2,1,0:T(8,128)(2,1)S(1)}, bf16[2,256,128]{2,1,0:T(8,128)(2,1)S(1)}, u32[]{:S(2)}, u32[]{:S(2)}) collective-permute-start(bf16[2,256,128]{2,1,0:T(8,128)(2,1)S(1)} %get-tuple-element.157), channel_id=1, source_target_pairs={{0,18},{2,16},{4,22},{6,20},{8,26},{10,24},{12,30},{14,28},{16,2},... | collective-permute-start | bytes 393224 | tf_op jit(solution)/shard_map/ppermute | solution.py:437
  62.9 6.8 %collective-permute-start.20 = (bf16[2,256,128]{2,1,0:T(8,128)(2,1)S(1)}, bf16[2,256,128]{2,1,0:T(8,128)(2,1)S(1)}, u32[]{:S(2)}, u32[]{:S(2)}) collective-permute-start(bf16[2,256,128]{2,1,0:T(8,128)(2,1)S(1)} %get-tuple-element.164), channel_id=1, source_target_pairs={{0,2},{2,0},{4,6},{6,4},{8,10},{10,8},{12,14},{14,12},{1,3},{3,1},... | collective-permute-start | bytes 393224 | tf_op jit(solution)/shard_map/ppermute | solution.py:440
  63.5 6.2 %collective-permute-start.21 = (bf16[2,256,128]{2,1,0:T(8,128)(2,1)S(1)}, bf16[2,256,128]{2,1,0:T(8,128)(2,1)S(1)}, u32[]{:S(2)}, u32[]{:S(2)}) collective-permute-start(bf16[2,256,128]{2,1,0:T(8,128)(2,1)S(1)} %get-tuple-element.168), channel_id=1, source_target_pairs={{0,16},{16,0},{1,17},{17,1},{2,18},{18,2},{3,19},{19,3},{4,20},{20... | collective-permute-start | bytes 393224 | tf_op jit(solution)/shard_map/ppermute | solution.py:443
  64.0 1.3 %collective-permute-start.18 = (bf16[256,128]{1,0:T(8,128)(2,1)S(1)}, bf16[256,128]{1,0:T(8,128)(2,1)S(1)}, u32[]{:S(2)}, u32[]{:S(2)}) collective-permute-start(bf16[256,128]{1,0:T(8,128)(2,1)S(1)} %shard_map.57.refs_9_), channel_id=1, source_target_pairs={{0,1},{1,0},{2,3},{3,2},{4,5},{5,4},{6,7},{7,6},{8,9},{9,8},{10,11... | collective-permute-start | bytes 196616 | tf_op jit(solution)/shard_map/ppermute | solution.py:428

commit v9 on v8

--- a/solution.py
+++ b/solution.py
@@ -159,19 +159,38 @@
     )
 
 
-def split_kernel(columns, rows_ref, *out_refs):
+def select_kernel(columns, part, rows_ref, *refs):
+    out_refs, sems = refs[:len(columns)], refs[-1]
+    rows = pl.ds(pl.multiple_of(lax.axis_index("groups") * part, HEAD), part)
+    copies = []
     for starts, out_ref in zip(columns, out_refs):
-        for i, start in enumerate(starts):
-            out_ref[:, i * HEAD:(i + 1) * HEAD] = rows_ref[:, start:start + HEAD]
-
-
-def split(rows, columns):
+        at = 0
+        while at < len(starts):
+            more = 1
+            while at + more < len(starts) and starts[at + more] == starts[at] + more * HEAD:
+                more += 1
+            copies.append(pltpu.make_async_copy(
+                rows_ref.at[0, rows, pl.ds(starts[at], more * HEAD)],
+                out_ref.at[:, pl.ds(at * HEAD, more * HEAD)],
+                sems.at[len(copies)],
+            ))
+            at += more
+    for copy in copies:
+        copy.start()
+    for copy in copies:
+        copy.wait()
+
+
+def select(projection, part, columns):
+    chunk = jax.ShapeDtypeStruct((part, len(columns[0]) * HEAD), projection.dtype)
+    out_shape = (chunk,) * len(columns)
     return call(
-        functools.partial(split_kernel, columns),
-        tuple(jax.ShapeDtypeStruct((rows.shape[0], len(c) * HEAD), rows.dtype) for c in columns),
-        in_specs=[WHOLE],
-        out_specs=[WHOLE] * len(columns),
-    )(rows)
+        functools.partial(select_kernel, columns, part),
+        out_shape,
+        in_specs=[pl.BlockSpec(memory_space=pltpu.HBM)],
+        out_specs=[WHOLE] * len(out_shape),
+        scratch_shapes=[pltpu.SemaphoreType.DMA((len(columns) * len(columns[0]),))],
+    )(projection)
 
 
 def gate_kernel(part, depth, hidden_ref, gain_ref, *refs):
@@ -452,15 +471,18 @@
         last[:] = held[:1]
         return held[0] if len(values) == 1 else held
 
-    columns_a = [(QHEADS + c) * HEAD for c in range(tensor)] + [0, (QHEADS - 1) * HEAD]
-    columns_b = [i * HEAD for i in range(1, QHEADS - 1)]
-    start = (0, lax.axis_index("groups") * part, 0)
-    rows = lax.dynamic_slice(projection, start, (1, part, projection.shape[2]))[0]
-    b0, a0 = split(rows, (columns_b, columns_a))
-    b1 = on_ring(b0)
+    columns = [(QHEADS + c) * HEAD for c in range(tensor)] + [0, (QHEADS - 1) * HEAD]
+
+    def rows_b(projection):
+        flat = projection.reshape(projection.shape[1:])
+        start = (lax.axis_index("groups") * part, HEAD)
+        return lax.dynamic_slice(flat, start, (part, 2 * (heads_local - 1) * HEAD))
+
+    b1 = on_ring(rows_b(projection))
     far, near_x, near_y, own, squares = after(*gate(hidden_in, norm_gain, part, depth))
     near_x = to_x(near_x)
     near_y = to_y(near_y)
+    a0, = select(after(projection), part, [columns])
     a0 = after(a0)
     a1 = on_ring(a0)
     other_squares = to_core(squares)
@@ -472,7 +494,7 @@
     far = to_far(far)
     a1 = after(a1)
     a2 = on_ring(a1)
-    b0 = after(b0)
+    b0 = after(rows_b(after(projection)))
     near_y = after(near_y)
     near_x = after(near_x)
     a3, b1 = after(a3, b1)

time: 71.2 us -> 70.7 us (level)
    unnamed x4, local copies, waits for them, and re-layouts: 1.41 us -> 0.01 us
    dynamic_slice x0 -> x2, local copies, waits for them, and re-layouts: none -> 1.05 us  [rows_b(): return lax.dynamic_slice(flat, start, (part, 2 * (heads_local - 1) * HEAD))]
where the time goes in v9:
time: 70.7 us; the launch traced here: 70.6 us
  waiting for transfers between devices  34.8 us (49%)
  starting transfers between devices  23.7 us (34%)
  Pallas kernels  10.8 us (15%)
  local copies, waits for them, and re-layouts  1.06 us (1%)
    ppermute x4, waiting for transfers between devices, on_ring(): return lax.ppermute(a, 'dp', ring)  16.1 us
    ppermute x3, waiting for transfers between devices, to_x(): return lax.ppermute(a, 'dp', over_x)  7.14 us
    ppermute x2, waiting for transfers between devices, back(): return lax.ppermute(a, 'dp', [(j, i) for i, j in ring])  6.47 us
    ppermute x3, starting transfers between devices, to_far(): return lax.ppermute(a, ('groups', 'dp'), across)  5.99 us
    pallas_call x5, Pallas kernels, matmul(): call(functools.partial(matmul_kernel, firsts, len(acts), len(so_far), sen...  5.12 us
    ppermute x4, starting transfers between devices, on_ring(): return lax.ppermute(a, 'dp', ring)  5.1 us
    ppermute x2, starting transfers between devices, back(): return lax.ppermute(a, 'dp', [(j, i) for i, j in ring])  3.94 us
    ppermute x3, starting transfers between devices, to_y(): return lax.ppermute(a, 'groups', over_y)  3.88 us
  transfers between devices with their start and end apart: 22, of which 13 were waited for; matrix products, arithmetic and copies ran while one was open for 0% of the time, Pallas kernels for 13%

profile of v9, /device:TPU:0, one launch (start us, length us, event | category | flops | bytes accessed | tf_op | source)
XLA Modules:
  0.0 70.6 jit_solution(16604328083551268234)
XLA Ops:
  0.0 1.0 %dynamic-slice_bitcast_fusion.1 = bf16[384,512]{1,0:T(8,128)(2,1)S(1)} fusion(bf16[1,768,1024]{2,1,0:T(8,128)(2,1)} %rows_ref, s32[]{:T(128)S(6)} %select_n.4), kind=kLoop, calls=%fused_computation.1 | loop fusion | bytes 786436 | tf_op jit(solution)/shard_map/dynamic_slice | solution.py:479
  1.0 3.1 %collective-permute-start = (bf16[384,512]{1,0:T(8,128)(2,1)S(1)}, bf16[384,512]{1,0:T(8,128)(2,1)S(1)}, u32[]{:S(2)}, u32[]{:S(2)}) collective-permute-start(bf16[384,512]{1,0:T(8,128)(2,1)S(1)} %dynamic-slice_bitcast_fusion.1), channel_id=1, source_target_pairs={{0,4},{2,6},{4,8},{6,10},{8,12},{10,14},{12,0},{14,2},{1,5},{3,7},... | collective-permute-start | bytes 1179656 | tf_op jit(solution)/shard_map/ppermute | solution.py:450
  4.1 2.2 %shard_map.46 = (bf16[4,256,384]{2,1,0:T(8,128)(2,1)S(1)}, bf16[4,256,384]{2,1,0:T(8,128)(2,1)S(1)}, bf16[4,256,384]{2,1,0:T(8,128)(2,1)S(1)}, bf16[4,256,384]{2,1,0:T(8,128)(2,1)S(1)}, f32[256,128]{1,0:T(8,128)S(1)}) custom-call(bf16[256,6144]{1,0:T(8,128)(2,1)} %hidden_ref.1, bf16[6144]{0:T(1024)(128)(2,1)} %gain_ref.1), custom_call_target="tpu_custom_call" | custom-call | flops 1 | bytes 1 | tf_op jit(solution)/shard_map/pallas_call | solution.py:231
  6.3 1.6 %collective-permute-start.5 = (bf16[4,256,384]{2,1,0:T(8,128)(2,1)S(1)}, bf16[4,256,384]{2,1,0:T(8,128)(2,1)S(1)}, u32[]{:S(2)}, u32[]{:S(2)}) collective-permute-start(bf16[4,256,384]{2,1,0:T(8,128)(2,1)S(1)} %get-tuple-element.106), channel_id=1, source_target_pairs={{0,16},{16,0},{1,17},{17,1},{2,18},{18,2},{3,19},{19,3},{4,20},{20... | collective-permute-start | bytes 2359304 | tf_op jit(solution)/shard_map/ppermute | solution.py:462
  7.9 1.5 %collective-permute-start.4 = (bf16[4,256,384]{2,1,0:T(8,128)(2,1)S(1)}, bf16[4,256,384]{2,1,0:T(8,128)(2,1)S(1)}, u32[]{:S(2)}, u32[]{:S(2)}) collective-permute-start(bf16[4,256,384]{2,1,0:T(8,128)(2,1)S(1)} %get-tuple-element.105), channel_id=1, source_target_pairs={{0,2},{2,0},{4,6},{6,4},{8,10},{10,8},{12,14},{14,12},{1,3},{3,1},... | collective-permute-start | bytes 2359304 | tf_op jit(solution)/shard_map/ppermute | solution.py:459
  9.5 1.6 %collective-permute-start.3 = (bf16[384,512]{1,0:T(8,128)(2,1)S(1)}, bf16[384,512]{1,0:T(8,128)(2,1)S(1)}, u32[]{:S(2)}, u32[]{:S(2)}) collective-permute-start(bf16[384,512]{1,0:T(8,128)(2,1)S(1)} %shard_map.47.refs_3_.refs_1_), channel_id=1, source_target_pairs={{0,4},{2,6},{4,8},{6,10},{8,12},{10,14},{12,0},{14,2},{1,5},{3,7},... | collective-permute-start | bytes 1179656 | tf_op jit(solution)/shard_map/ppermute | solution.py:450
  11.1 1.1 %shard_map.48 = (f32[256,128]{1,0:T(8,128)S(1)}, f32[256,128]{1,0:T(8,128)S(1)}, f32[256,256]{1,0:T(8,128)S(1)}, f32[256,128]{1,0:T(8,128)S(1)}) custom-call(s32[1,2]{1,0:T(1,128)S(1)} %copy-done.1, f32[256,128]{1,0:T(8,128)S(1)} %get-tuple-element.92._.own_ref), custom_call_target="tpu_custom_call" | custom-call | flops 1 | bytes 1 | tf_op jit(solution)/shard_map/pallas_call | solution.py:331
  12.3 3.7 %collective-permute-done.refs_5_ = bf16[384,512]{1,0:T(8,128)(2,1)S(1)} collective-permute-done((bf16[384,512]{1,0:T(8,128)(2,1)S(1)}, bf16[384,512]{1,0:T(8,128)(2,1)S(1)}, u32[]{:S(2)}, u32[]{:S(2)}) %collective-permute-start) | collective-permute-done | bytes 393248 | tf_op jit(solution)/shard_map/ppermute | solution.py:450
  16.1 2.7 %collective-permute-start.2 = (bf16[4,256,384]{2,1,0:T(8,128)(2,1)S(1)}, bf16[4,256,384]{2,1,0:T(8,128)(2,1)S(1)}, u32[]{:S(2)}, u32[]{:S(2)}) collective-permute-start(bf16[4,256,384]{2,1,0:T(8,128)(2,1)S(1)} %get-tuple-element.100), channel_id=1, source_target_pairs={{0,18},{2,16},{4,22},{6,20},{8,26},{10,24},{12,30},{14,28},{16,2},... | collective-permute-start | bytes 2359304 | tf_op jit(solution)/shard_map/ppermute | solution.py:456
  18.8 1.8 %collective-permute-start.7 = (bf16[384,512]{1,0:T(8,128)(2,1)S(1)}, bf16[384,512]{1,0:T(8,128)(2,1)S(1)}, u32[]{:S(2)}, u32[]{:S(2)}) collective-permute-start(bf16[384,512]{1,0:T(8,128)(2,1)S(1)} %shard_map.47.refs_3_.refs_1_), channel_id=1, source_target_pairs={{4,0},{6,2},{8,4},{10,6},{12,8},{14,10},{0,12},{2,14},{5,1},{7,3},... | collective-permute-start | bytes 1179656 | tf_op jit(solution)/shard_map/ppermute | solution.py:453
  20.6 4.0 %collective-permute-done.3.refs_4_.refs_2_ = bf16[384,512]{1,0:T(8,128)(2,1)S(1)} collective-permute-done((bf16[384,512]{1,0:T(8,128)(2,1)S(1)}, bf16[384,512]{1,0:T(8,128)(2,1)S(1)}, u32[]{:S(2)}, u32[]{:S(2)}) %collective-permute-start.3) | collective-permute-done | bytes 393248 | tf_op jit(solution)/shard_map/ppermute | solution.py:450
  24.6 0.7 %collective-permute-done.5.refs_1_.refs_3_ = bf16[4,256,384]{2,1,0:T(8,128)(2,1)S(1)} collective-permute-done((bf16[4,256,384]{2,1,0:T(8,128)(2,1)S(1)}, bf16[4,256,384]{2,1,0:T(8,128)(2,1)S(1)}, u32[]{:S(2)}, u32[]{:S(2)}) %collective-permute-start.5) | collective-permute-done | bytes 786464 | tf_op jit(solution)/shard_map/ppermute | solution.py:462
  25.4 2.8 %collective-permute-done.4.refs_0_.refs_2_ = bf16[4,256,384]{2,1,0:T(8,128)(2,1)S(1)} collective-permute-done((bf16[4,256,384]{2,1,0:T(8,128)(2,1)S(1)}, bf16[4,256,384]{2,1,0:T(8,128)(2,1)S(1)}, u32[]{:S(2)}, u32[]{:S(2)}) %collective-permute-start.4) | collective-permute-done | bytes 786464 | tf_op jit(solution)/shard_map/ppermute | solution.py:459
  28.2 4.8 %collective-permute-done.7.refs_5_.refs_4_ = bf16[384,512]{1,0:T(8,128)(2,1)S(1)} collective-permute-done((bf16[384,512]{1,0:T(8,128)(2,1)S(1)}, bf16[384,512]{1,0:T(8,128)(2,1)S(1)}, u32[]{:S(2)}, u32[]{:S(2)}) %collective-permute-start.7) | collective-permute-done | bytes 393248 | tf_op jit(solution)/shard_map/ppermute | solution.py:453
  33.4 1.4 %shard_map.50.refs_4_ = f32[3,256,512]{2,1,0:T(8,128)S(1)} custom-call(bf16[4,256,384]{2,1,0:T(8,128)(2,1)S(1)} %collective-permute-done.4.refs_0_.refs_2_, bf16[4,256,384]{2,1,0:T(8,128)(2,1)S(1)} %collective-permute-done.5.refs_1_.refs_3_, bf16[4,256,384]{2,1,0:T(8,128)(2,1)S(1)} %get-tuple-element.109.refs_2_.refs_1_, ...), custom_call_target="tpu_custom_call" | custom-call | flops 1 | bytes 1 | tf_op jit(solution)/shard_map/pallas_call | solution.py:284
  34.8 8.3 %collective-permute-done.6.refs_3_ = bf16[384,512]{1,0:T(8,128)(2,1)S(1)} collective-permute-done((bf16[384,512]{1,0:T(8,128)(2,1)S(1)}, bf16[384,512]{1,0:T(8,128)(2,1)S(1)}, u32[]{:S(2)}, u32[]{:S(2)}) %collective-permute-start.6) | collective-permute-done | bytes 393248 | tf_op jit(solution)/shard_map/ppermute | solution.py:450
  44.6 2.1 %collective-permute-start.8 = (bf16[384,512]{1,0:T(8,128)(2,1)S(1)}, bf16[384,512]{1,0:T(8,128)(2,1)S(1)}, u32[]{:S(2)}, u32[]{:S(2)}) collective-permute-start(bf16[384,512]{1,0:T(8,128)(2,1)S(1)} %dynamic-slice_bitcast_fusion.refs_4_), channel_id=1, source_target_pairs={{4,0},{6,2},{8,4},{10,6},{12,8},{14,10},{0,12},{2,14},{5,1},{7,3},... | collective-permute-start | bytes 1179656 | tf_op jit(solution)/shard_map/ppermute | solution.py:453
  46.8 0.7 shard_map.52
  47.7 1.8 %collective-permute-start.13 = (bf16[2,256,128]{2,1,0:T(8,128)(2,1)S(1)}, bf16[2,256,128]{2,1,0:T(8,128)(2,1)S(1)}, u32[]{:S(2)}, u32[]{:S(2)}) collective-permute-start(bf16[2,256,128]{2,1,0:T(8,128)(2,1)S(1)} %get-tuple-element.133), channel_id=1, source_target_pairs={{0,16},{16,0},{1,17},{17,1},{2,18},{18,2},{3,19},{19,3},{4,20},{20... | collective-permute-start | bytes 393224 | tf_op jit(solution)/shard_map/ppermute | solution.py:462
  49.5 1.5 %collective-permute-start.12 = (bf16[2,256,128]{2,1,0:T(8,128)(2,1)S(1)}, bf16[2,256,128]{2,1,0:T(8,128)(2,1)S(1)}, u32[]{:S(2)}, u32[]{:S(2)}) collective-permute-start(bf16[2,256,128]{2,1,0:T(8,128)(2,1)S(1)} %get-tuple-element.130), channel_id=1, source_target_pairs={{0,2},{2,0},{4,6},{6,4},{8,10},{10,8},{12,14},{14,12},{1,3},{3,1},... | collective-permute-start | bytes 393224 | tf_op jit(solution)/shard_map/ppermute | solution.py:459
  51.0 0.8 %collective-permute-start.15 = (bf16[2,256,128]{2,1,0:T(8,128)(2,1)S(1)}, bf16[2,256,128]{2,1,0:T(8,128)(2,1)S(1)}, u32[]{:S(2)}, u32[]{:S(2)}) collective-permute-start(bf16[2,256,128]{2,1,0:T(8,128)(2,1)S(1)} %shard_map.55), channel_id=1, source_target_pairs={{0,18},{2,16},{4,22},{6,20},{8,26},{10,24},{12,30},{14,28},{16,2},... | collective-permute-start | bytes 393224 | tf_op jit(solution)/shard_map/ppermute | solution.py:456
  51.8 1.8 %shard_map.54.refs_5_ = f32[4,256,512]{2,1,0:T(8,128)S(1)} custom-call(bf16[4,256,384]{2,1,0:T(8,128)(2,1)S(1)} %collective-permute-done.2.refs_0_, bf16[4,256,384]{2,1,0:T(8,128)(2,1)S(1)} %get-tuple-element.109.refs_2_.refs_1_, bf16[4,256,384]{2,1,0:T(8,128)(2,1)S(1)} %collective-permute-done.4.refs_0_.refs_2_, ...), custom_call_target="tpu_custom_call" | custom-call | flops 1 | bytes 1 | tf_op jit(solution)/shard_map/pallas_call | solution.py:284
  53.6 2.2 %collective-permute-done.12.r1.refs_2_ = bf16[2,256,128]{2,1,0:T(8,128)(2,1)S(1)} collective-permute-done((bf16[2,256,128]{2,1,0:T(8,128)(2,1)S(1)}, bf16[2,256,128]{2,1,0:T(8,128)(2,1)S(1)}, u32[]{:S(2)}, u32[]{:S(2)}) %collective-permute-start.12) | collective-permute-done | bytes 131104 | tf_op jit(solution)/shard_map/ppermute | solution.py:459
  55.8 1.7 %collective-permute-done.8.refs_4_ = bf16[384,512]{1,0:T(8,128)(2,1)S(1)} collective-permute-done((bf16[384,512]{1,0:T(8,128)(2,1)S(1)}, bf16[384,512]{1,0:T(8,128)(2,1)S(1)}, u32[]{:S(2)}, u32[]{:S(2)}) %collective-permute-start.8) | collective-permute-done | bytes 393248 | tf_op jit(solution)/shard_map/ppermute | solution.py:453
  57.5 0.7 %shard_map.56 = (bf16[4,256,128]{2,1,0:T(8,128)(2,1)S(1)}, bf16[4,256,128]{2,1,0:T(8,128)(2,1)S(1)}, f32[4,2,256,128]{3,2,1,0:T(8,128)S(1)}) custom-call(bf16[4,256,384]{2,1,0:T(8,128)(2,1)S(1)} %collective-permute-done.2.refs_0_, bf16[4,256,384]{2,1,0:T(8,128)(2,1)S(1)} %get-tuple-element.109.refs_2_.refs_1_, ...), custom_call_target="tpu_custom_call" | custom-call | flops 1 | bytes 1 | tf_op jit(solution)/shard_map/pallas_call | solution.py:284
  58.9 0.9 %collective-permute-done.16.refs_0_ = bf16[4,256,128]{2,1,0:T(8,128)(2,1)S(1)} collective-permute-done((bf16[4,256,128]{2,1,0:T(8,128)(2,1)S(1)}, bf16[4,256,128]{2,1,0:T(8,128)(2,1)S(1)}, u32[]{:S(2)}, u32[]{:S(2)}) %collective-permute-start.16) | collective-permute-done | bytes 262176 | tf_op jit(solution)/shard_map/ppermute | solution.py:447
  59.8 2.5 %collective-permute-start.17 = (bf16[2,256,128]{2,1,0:T(8,128)(2,1)S(1)}, bf16[2,256,128]{2,1,0:T(8,128)(2,1)S(1)}, u32[]{:S(2)}, u32[]{:S(2)}) collective-permute-start(bf16[2,256,128]{2,1,0:T(8,128)(2,1)S(1)} %get-tuple-element.157), channel_id=1, source_target_pairs={{0,18},{2,16},{4,22},{6,20},{8,26},{10,24},{12,30},{14,28},{16,2},... | collective-permute-start | bytes 393224 | tf_op jit(solution)/shard_map/ppermute | solution.py:456
  62.4 0.6 collective-permute-start.20
  63.5 1.3 %collective-permute-done.18.refs_10_ = bf16[256,128]{1,0:T(8,128)(2,1)S(1)} collective-permute-done((bf16[256,128]{1,0:T(8,128)(2,1)S(1)}, bf16[256,128]{1,0:T(8,128)(2,1)S(1)}, u32[]{:S(2)}, u32[]{:S(2)}) %collective-permute-start.18) | collective-permute-done | bytes 65568 | tf_op jit(solution)/shard_map/ppermute | solution.py:447
  65.4 1.8 %collective-permute-done.17.refs_1_ = bf16[2,256,128]{2,1,0:T(8,128)(2,1)S(1)} collective-permute-done((bf16[2,256,128]{2,1,0:T(8,128)(2,1)S(1)}, bf16[2,256,128]{2,1,0:T(8,128)(2,1)S(1)}, u32[]{:S(2)}, u32[]{:S(2)}) %collective-permute-start.17) | collective-permute-done | bytes 131104 | tf_op jit(solution)/shard_map/ppermute | solution.py:456
  67.2 2.1 %collective-permute-done.20.refs_2_ = bf16[2,256,128]{2,1,0:T(8,128)(2,1)S(1)} collective-permute-done((bf16[2,256,128]{2,1,0:T(8,128)(2,1)S(1)}, bf16[2,256,128]{2,1,0:T(8,128)(2,1)S(1)}, u32[]{:S(2)}, u32[]{:S(2)}) %collective-permute-start.20) | collective-permute-done | bytes 131104 | tf_op jit(solution)/shard_map/ppermute | solution.py:459
  69.2 1.4 %shard_map.61 = bf16[256,384]{1,0:T(8,128)(2,1)} custom-call(f32[2,256,128]{2,1,0:T(8,128)S(1)} %get-tuple-element.156.refs_0_, bf16[2,256,128]{2,1,0:T(8,128)(2,1)S(1)} %collective-permute-done.17.refs_1_, bf16[2,256,128]{2,1,0:T(8,128)(2,1)S(1)} %collective-permute-done.20.refs_2_, bf16[2,256,128]{2,1,0:T(8,128)(2,1)S(1)} %collective-permute-done.21.refs_3_, ...), custom_call_target="tpu_custom_call" | custom-call | flops 1 | bytes 1 | tf_op jit(solution)/shard_map/pallas_call | solution.py:421
  (34 shorter events, 4.2 us)
Async XLA Ops:
  1.0 8.4 %copy-start = (bf16[1,768,1024]{2,1,0:T(8,128)(2,1)S(1)}, bf16[1,768,1024]{2,1,0:T(8,128)(2,1)}, u32[]{:S(2)}) copy-start(bf16[1,768,1024]{2,1,0:T(8,128)(2,1)} %rows_ref) | copy-start | bytes 4718596
  1.0 15.0 %collective-permute-start = (bf16[384,512]{1,0:T(8,128)(2,1)S(1)}, bf16[384,512]{1,0:T(8,128)(2,1)S(1)}, u32[]{:S(2)}, u32[]{:S(2)}) collective-permute-start(bf16[384,512]{1,0:T(8,128)(2,1)S(1)} %dynamic-slice_bitcast_fusion.1), channel_id=1, source_target_pairs={{0,4},{2,6},{4,8},{6,10},{8,12},{10,14},{12,0},{14,2},{1,5},{3,7},... | collective-permute-start | bytes 1179656 | tf_op jit(solution)/shard_map/ppermute | solution.py:450
  6.3 4.8 %copy-start.1 = (s32[1,2]{1,0:T(1,128)S(1)}, s32[1,2]{1,0:T(1,128)}, u32[]{:S(2)}) copy-start(s32[1,2]{1,0:T(1,128)} %lengths_ref.1) | copy-start | bytes 28
  6.3 19.1 %collective-permute-start.5 = (bf16[4,256,384]{2,1,0:T(8,128)(2,1)S(1)}, bf16[4,256,384]{2,1,0:T(8,128)(2,1)S(1)}, u32[]{:S(2)}, u32[]{:S(2)}) collective-permute-start(bf16[4,256,384]{2,1,0:T(8,128)(2,1)S(1)} %get-tuple-element.106), channel_id=1, source_target_pairs={{0,16},{16,0},{1,17},{17,1},{2,18},{18,2},{3,19},{19,3},{4,20},{20... | collective-permute-start | bytes 2359304 | tf_op jit(solution)/shard_map/ppermute | solution.py:462
  7.9 4.3 %collective-permute-start.1 = (f32[256,128]{1,0:T(8,128)S(1)}, f32[256,128]{1,0:T(8,128)S(1)}, u32[]{:S(2)}, u32[]{:S(2)}) collective-permute-start(f32[256,128]{1,0:T(8,128)S(1)} %get-tuple-element.92._.own_ref), channel_id=1, source_target_pairs={{0,1},{1,0},{2,3},{3,2},{4,5},{5,4},{6,7},{7,6},{8,9},{9,8},{10,11... | collective-permute-start | bytes 393224 | tf_op jit(solution)/shard_map/ppermute | solution.py:447
  7.9 20.3 %collective-permute-start.4 = (bf16[4,256,384]{2,1,0:T(8,128)(2,1)S(1)}, bf16[4,256,384]{2,1,0:T(8,128)(2,1)S(1)}, u32[]{:S(2)}, u32[]{:S(2)}) collective-permute-start(bf16[4,256,384]{2,1,0:T(8,128)(2,1)S(1)} %get-tuple-element.105), channel_id=1, source_target_pairs={{0,2},{2,0},{4,6},{6,4},{8,10},{10,8},{12,14},{14,12},{1,3},{3,1},... | collective-permute-start | bytes 2359304 | tf_op jit(solution)/shard_map/ppermute | solution.py:459
  9.5 15.1 %collective-permute-start.3 = (bf16[384,512]{1,0:T(8,128)(2,1)S(1)}, bf16[384,512]{1,0:T(8,128)(2,1)S(1)}, u32[]{:S(2)}, u32[]{:S(2)}) collective-permute-start(bf16[384,512]{1,0:T(8,128)(2,1)S(1)} %shard_map.47.refs_3_.refs_1_), channel_id=1, source_target_pairs={{0,4},{2,6},{4,8},{6,10},{8,12},{10,14},{12,0},{14,2},{1,5},{3,7},... | collective-permute-start | bytes 1179656 | tf_op jit(solution)/shard_map/ppermute | solution.py:450
  16.1 28.6 %collective-permute-start.2 = (bf16[4,256,384]{2,1,0:T(8,128)(2,1)S(1)}, bf16[4,256,384]{2,1,0:T(8,128)(2,1)S(1)}, u32[]{:S(2)}, u32[]{:S(2)}) collective-permute-start(bf16[4,256,384]{2,1,0:T(8,128)(2,1)S(1)} %get-tuple-element.100), channel_id=1, source_target_pairs={{0,18},{2,16},{4,22},{6,20},{8,26},{10,24},{12,30},{14,28},{16,2},... | collective-permute-start | bytes 2359304 | tf_op jit(solution)/shard_map/ppermute | solution.py:456
  18.8 14.2 %collective-permute-start.7 = (bf16[384,512]{1,0:T(8,128)(2,1)S(1)}, bf16[384,512]{1,0:T(8,128)(2,1)S(1)}, u32[]{:S(2)}, u32[]{:S(2)}) collective-permute-start(bf16[384,512]{1,0:T(8,128)(2,1)S(1)} %shard_map.47.refs_3_.refs_1_), channel_id=1, source_target_pairs={{4,0},{6,2},{8,4},{10,6},{12,8},{14,10},{0,12},{2,14},{5,1},{7,3},... | collective-permute-start | bytes 1179656 | tf_op jit(solution)/shard_map/ppermute | solution.py:453
  24.6 18.5 %collective-permute-start.6 = (bf16[384,512]{1,0:T(8,128)(2,1)S(1)}, bf16[384,512]{1,0:T(8,128)(2,1)S(1)}, u32[]{:S(2)}, u32[]{:S(2)}) collective-permute-start(bf16[384,512]{1,0:T(8,128)(2,1)S(1)} %collective-permute-done.3.refs_4_.refs_2_), channel_id=1, source_target_pairs={{0,4},{2,6},{4,8},{6,10},{8,12},{10,14},{12,0},{14,2},{1,5},{3,7},... | collective-permute-start | bytes 1179656 | tf_op jit(solution)/shard_map/ppermute | solution.py:450
  33.0 17.9 %collective-permute-start.9 = (bf16[384,512]{1,0:T(8,128)(2,1)S(1)}, bf16[384,512]{1,0:T(8,128)(2,1)S(1)}, u32[]{:S(2)}, u32[]{:S(2)}) collective-permute-start(bf16[384,512]{1,0:T(8,128)(2,1)S(1)} %collective-permute-done.refs_5_), channel_id=1, source_target_pairs={{0,4},{2,6},{4,8},{6,10},{8,12},{10,14},{12,0},{14,2},{1,5},{3,7},... | collective-permute-start | bytes 1179656 | tf_op jit(solution)/shard_map/ppermute | solution.py:450
  43.7 3.8 %collective-permute-start.10 = (bf16[3,256,128]{2,1,0:T(8,128)(2,1)S(1)}, bf16[3,256,128]{2,1,0:T(8,128)(2,1)S(1)}, u32[]{:S(2)}, u32[]{:S(2)}) collective-permute-start(bf16[3,256,128]{2,1,0:T(8,128)(2,1)S(1)} %get-tuple-element.117), channel_id=1, source_target_pairs={{0,1},{1,0},{2,3},{3,2},{4,5},{5,4},{6,7},{7,6},{8,9},{9,8},{10,11... | collective-permute-start | bytes 589832 | tf_op jit(solution)/shard_map/ppermute | solution.py:447
  43.8 3.7 %collective-permute-start.11 = (bf16[3,256,128]{2,1,0:T(8,128)(2,1)S(1)}, bf16[3,256,128]{2,1,0:T(8,128)(2,1)S(1)}, u32[]{:S(2)}, u32[]{:S(2)}) collective-permute-start(bf16[3,256,128]{2,1,0:T(8,128)(2,1)S(1)} %get-tuple-element.124), channel_id=1, source_target_pairs={{0,1},{1,0},{2,3},{3,2},{4,5},{5,4},{6,7},{7,6},{8,9},{9,8},{10,11... | collective-permute-start | bytes 589832 | tf_op jit(solution)/shard_map/ppermute | solution.py:447
  44.6 12.8 %collective-permute-start.8 = (bf16[384,512]{1,0:T(8,128)(2,1)S(1)}, bf16[384,512]{1,0:T(8,128)(2,1)S(1)}, u32[]{:S(2)}, u32[]{:S(2)}) collective-permute-start(bf16[384,512]{1,0:T(8,128)(2,1)S(1)} %dynamic-slice_bitcast_fusion.refs_4_), channel_id=1, source_target_pairs={{4,0},{6,2},{8,4},{10,6},{12,8},{14,10},{0,12},{2,14},{5,1},{7,3},... | collective-permute-start | bytes 1179656 | tf_op jit(solution)/shard_map/ppermute | solution.py:453
  47.6 3.4 %collective-permute-start.14 = (bf16[2,256,128]{2,1,0:T(8,128)(2,1)S(1)}, bf16[2,256,128]{2,1,0:T(8,128)(2,1)S(1)}, u32[]{:S(2)}, u32[]{:S(2)}) collective-permute-start(bf16[2,256,128]{2,1,0:T(8,128)(2,1)S(1)} %get-tuple-element.131), channel_id=1, source_target_pairs={{0,1},{1,0},{2,3},{3,2},{4,5},{5,4},{6,7},{7,6},{8,9},{9,8},{10,11... | collective-permute-start | bytes 393224 | tf_op jit(solution)/shard_map/ppermute | solution.py:447
  47.7 5.9 %collective-permute-start.13 = (bf16[2,256,128]{2,1,0:T(8,128)(2,1)S(1)}, bf16[2,256,128]{2,1,0:T(8,128)(2,1)S(1)}, u32[]{:S(2)}, u32[]{:S(2)}) collective-permute-start(bf16[2,256,128]{2,1,0:T(8,128)(2,1)S(1)} %get-tuple-element.133), channel_id=1, source_target_pairs={{0,16},{16,0},{1,17},{17,1},{2,18},{18,2},{3,19},{19,3},{4,20},{20... | collective-permute-start | bytes 393224 | tf_op jit(solution)/shard_map/ppermute | solution.py:462
  49.5 6.3 %collective-permute-start.12 = (bf16[2,256,128]{2,1,0:T(8,128)(2,1)S(1)}, bf16[2,256,128]{2,1,0:T(8,128)(2,1)S(1)}, u32[]{:S(2)}, u32[]{:S(2)}) collective-permute-start(bf16[2,256,128]{2,1,0:T(8,128)(2,1)S(1)} %get-tuple-element.130), channel_id=1, source_target_pairs={{0,2},{2,0},{4,6},{6,4},{8,10},{10,8},{12,14},{14,12},{1,3},{3,1},... | collective-permute-start | bytes 393224 | tf_op jit(solution)/shard_map/ppermute | solution.py:459
  51.0 7.2 %collective-permute-start.15 = (bf16[2,256,128]{2,1,0:T(8,128)(2,1)S(1)}, bf16[2,256,128]{2,1,0:T(8,128)(2,1)S(1)}, u32[]{:S(2)}, u32[]{:S(2)}) collective-permute-start(bf16[2,256,128]{2,1,0:T(8,128)(2,1)S(1)} %shard_map.55), channel_id=1, source_target_pairs={{0,18},{2,16},{4,22},{6,20},{8,26},{10,24},{12,30},{14,28},{16,2},... | collective-permute-start | bytes 393224 | tf_op jit(solution)/shard_map/ppermute | solution.py:456
  58.2 1.6 %collective-permute-start.16 = (bf16[4,256,128]{2,1,0:T(8,128)(2,1)S(1)}, bf16[4,256,128]{2,1,0:T(8,128)(2,1)S(1)}, u32[]{:S(2)}, u32[]{:S(2)}) collective-permute-start(bf16[4,256,128]{2,1,0:T(8,128)(2,1)S(1)} %get-tuple-element.147), channel_id=1, source_target_pairs={{0,1},{1,0},{2,3},{3,2},{4,5},{5,4},{6,7},{7,6},{8,9},{9,8},{10,11... | collective-permute-start | bytes 786440 | tf_op jit(solution)/shard_map/ppermute | solution.py:447
  58.3 4.1 %collective-permute-start.19 = (bf16[4,256,128]{2,1,0:T(8,128)(2,1)S(1)}, bf16[4,256,128]{2,1,0:T(8,128)(2,1)S(1)}, u32[]{:S(2)}, u32[]{:S(2)}) collective-permute-start(bf16[4,256,128]{2,1,0:T(8,128)(2,1)S(1)} %get-tuple-element.160), channel_id=1, source_target_pairs={{0,1},{1,0},{2,3},{3,2},{4,5},{5,4},{6,7},{7,6},{8,9},{9,8},{10,11... | collective-permute-start | bytes 786440 | tf_op jit(solution)/shard_map/ppermute | solution.py:447
  59.8 7.3 %collective-permute-start.17 = (bf16[2,256,128]{2,1,0:T(8,128)(2,1)S(1)}, bf16[2,256,128]{2,1,0:T(8,128)(2,1)S(1)}, u32[]{:S(2)}, u32[]{:S(2)}) collective-permute-start(bf16[2,256,128]{2,1,0:T(8,128)(2,1)S(1)} %get-tuple-element.157), channel_id=1, source_target_pairs={{0,18},{2,16},{4,22},{6,20},{8,26},{10,24},{12,30},{14,28},{16,2},... | collective-permute-start | bytes 393224 | tf_op jit(solution)/shard_map/ppermute | solution.py:456
  62.4 6.8 %collective-permute-start.20 = (bf16[2,256,128]{2,1,0:T(8,128)(2,1)S(1)}, bf16[2,256,128]{2,1,0:T(8,128)(2,1)S(1)}, u32[]{:S(2)}, u32[]{:S(2)}) collective-permute-start(bf16[2,256,128]{2,1,0:T(8,128)(2,1)S(1)} %get-tuple-element.164), channel_id=1, source_target_pairs={{0,2},{2,0},{4,6},{6,4},{8,10},{10,8},{12,14},{14,12},{1,3},{3,1},... | collective-permute-start | bytes 393224 | tf_op jit(solution)/shard_map/ppermute | solution.py:459
  63.0 6.2 %collective-permute-start.21 = (bf16[2,256,128]{2,1,0:T(8,128)(2,1)S(1)}, bf16[2,256,128]{2,1,0:T(8,128)(2,1)S(1)}, u32[]{:S(2)}, u32[]{:S(2)}) collective-permute-start(bf16[2,256,128]{2,1,0:T(8,128)(2,1)S(1)} %get-tuple-element.168), channel_id=1, source_target_pairs={{0,16},{16,0},{1,17},{17,1},{2,18},{18,2},{3,19},{19,3},{4,20},{20... | collective-permute-start | bytes 393224 | tf_op jit(solution)/shard_map/ppermute | solution.py:462
  63.5 1.3 %collective-permute-start.18 = (bf16[256,128]{1,0:T(8,128)(2,1)S(1)}, bf16[256,128]{1,0:T(8,128)(2,1)S(1)}, u32[]{:S(2)}, u32[]{:S(2)}) collective-permute-start(bf16[256,128]{1,0:T(8,128)(2,1)S(1)} %shard_map.57.refs_9_), channel_id=1, source_target_pairs={{0,1},{1,0},{2,3},{3,2},{4,5},{5,4},{6,7},{7,6},{8,9},{9,8},{10,11... | collective-permute-start | bytes 196616 | tf_op jit(solution)/shard_map/ppermute | solution.py:447

commit v10 on v9

--- a/solution.py
+++ b/solution.py
@@ -290,6 +290,34 @@
     return outs if sent else outs[0]
 
 
+def half_kernel(first, swapped, n_acts, *refs):
+    acts, (slot_ref, more_ref), out_refs = refs[:n_acts], refs[n_acts:n_acts + 2], refs[n_acts + 2:]
+    core = lax.axis_index("tensor")
+    width = slot_ref.shape[1] // 2
+    where = pl.ds(pl.multiple_of((1 - core if swapped else core) * width, HEAD), width)
+    right = slot_ref[:, where]
+    n_blocks = width // HEAD
+    per = n_acts * n_blocks // len(out_refs)
+    for p in range(n_acts):
+        total = jnp.dot(acts[p][first], right, preferred_element_type=jnp.float32) + more_ref[p, :, where]
+        for g in range(n_blocks):
+            spot = p * n_blocks + g
+            out_ref = out_refs[spot // per]
+            out_ref[spot % per] = total[:, g * HEAD:(g + 1) * HEAD].astype(out_ref.dtype)
+
+
+def half_matmul(acts, slot, first, so_far, swapped, pieces, dtype):
+    tokens, width = acts[0].shape[1], slot.shape[1] // 2
+    args = [*acts, slot, so_far]
+    rows = len(acts) * width // HEAD // pieces
+    return call(
+        functools.partial(half_kernel, first, swapped, len(acts)),
+        (jax.ShapeDtypeStruct((rows, tokens, HEAD), dtype),) * pieces,
+        in_specs=[WHOLE] * len(args),
+        out_specs=[WHOLE] * pieces,
+    )(*args)
+
+
 def join_kernel(n_came, first, mine_ref, *refs):
     came_refs, out_refs = refs[:n_came], refs[n_came:]
     n_blocks = mine_ref.shape[1]
@@ -524,8 +552,10 @@
 
     b3 = after(b3)
     parts_a = after(sums, sums_far, sums_x, sums_y)
-    *theirs, mine = after(*matmul(acts, (b3,), (3,), (front,), sent=2, paired=False))
+    theirs = after(*half_matmul(acts, b3, 3, front, True, 2, jnp.bfloat16))
     swapped = [to_core(t) for t in theirs]
+    mine, = half_matmul(acts, after(b3), 3, front, False, 1, jnp.float32)
+    mine = mine.reshape(len(acts), -1, *mine.shape[1:])
     kv = after(call(
         kv_kernel,
         jax.ShapeDtypeStruct((tokens, HEAD), jnp.bfloat16),

time: 70.7 us -> 70.5 us (level)
    pallas_call x0 -> x2, Pallas kernels: none -> 0.87 us  [half_matmul(): call(functools.partial(half_kernel, first, swapped, len(acts)), (jax.Shap...]
    pallas_call x5 -> x4, Pallas kernels: 5.12 us -> 4.41 us  [matmul(): call(functools.partial(matmul_kernel, firsts, len(acts), len(so_far), sen...]
  transfers between devices with their start and end apart: 22 -> 22, of which waited for: 13 -> 13; matrix products, arithmetic and copies ran while one was open for 0% -> 0% of each run, Pallas kernels for 13% -> 14%
where the time goes in v10:
time: 70.5 us; the launch traced here: 70.3 us
  waiting for transfers between devices  34.4 us (49%)
  starting transfers between devices  23.7 us (34%)
  Pallas kernels  11 us (16%)
  local copies, waits for them, and re-layouts  1.06 us (2%)
    ppermute x4, waiting for transfers between devices, on_ring(): return lax.ppermute(a, 'dp', ring)  16.1 us
    ppermute x3, waiting for transfers between devices, to_x(): return lax.ppermute(a, 'dp', over_x)  7.14 us
    ppermute x2, waiting for transfers between devices, back(): return lax.ppermute(a, 'dp', [(j, i) for i, j in ring])  6.47 us
    ppermute x3, starting transfers between devices, to_far(): return lax.ppermute(a, ('groups', 'dp'), across)  6 us
    ppermute x4, starting transfers between devices, on_ring(): return lax.ppermute(a, 'dp', ring)  5.1 us
    pallas_call x4, Pallas kernels, matmul(): call(functools.partial(matmul_kernel, firsts, len(acts), len(so_far), sen...  4.41 us
    ppermute x2, starting transfers between devices, back(): return lax.ppermute(a, 'dp', [(j, i) for i, j in ring])  3.94 us
    ppermute x3, starting transfers between devices, to_y(): return lax.ppermute(a, 'groups', over_y)  3.88 us
  transfers between devices with their start and end apart: 22, of which 13 were waited for; matrix products, arithmetic and copies ran while one was open for 0% of the time, Pallas kernels for 14%

profile of v10, /device:TPU:0, one launch (start us, length us, event | category | flops | bytes accessed | tf_op | source)
XLA Modules:
  0.0 70.3 jit_solution(7338339508607054234)
XLA Ops:
  0.0 1.0 %dynamic-slice_bitcast_fusion.1 = bf16[384,512]{1,0:T(8,128)(2,1)S(1)} fusion(bf16[1,768,1024]{2,1,0:T(8,128)(2,1)} %rows_ref, s32[]{:T(128)S(6)} %select_n.4), kind=kLoop, calls=%fused_computation.1 | loop fusion | bytes 786436 | tf_op jit(solution)/shard_map/dynamic_slice | solution.py:507
  1.0 3.1 %collective-permute-start = (bf16[384,512]{1,0:T(8,128)(2,1)S(1)}, bf16[384,512]{1,0:T(8,128)(2,1)S(1)}, u32[]{:S(2)}, u32[]{:S(2)}) collective-permute-start(bf16[384,512]{1,0:T(8,128)(2,1)S(1)} %dynamic-slice_bitcast_fusion.1), channel_id=1, source_target_pairs={{0,4},{2,6},{4,8},{6,10},{8,12},{10,14},{12,0},{14,2},{1,5},{3,7},... | collective-permute-start | bytes 1179656 | tf_op jit(solution)/shard_map/ppermute | solution.py:478
  4.1 2.2 %shard_map.46 = (bf16[4,256,384]{2,1,0:T(8,128)(2,1)S(1)}, bf16[4,256,384]{2,1,0:T(8,128)(2,1)S(1)}, bf16[4,256,384]{2,1,0:T(8,128)(2,1)S(1)}, bf16[4,256,384]{2,1,0:T(8,128)(2,1)S(1)}, f32[256,128]{1,0:T(8,128)S(1)}) custom-call(bf16[256,6144]{1,0:T(8,128)(2,1)} %hidden_ref.1, bf16[6144]{0:T(1024)(128)(2,1)} %gain_ref.1), custom_call_target="tpu_custom_call" | custom-call | flops 1 | bytes 1 | tf_op jit(solution)/shard_map/pallas_call | solution.py:231
  6.3 1.6 %collective-permute-start.5 = (bf16[4,256,384]{2,1,0:T(8,128)(2,1)S(1)}, bf16[4,256,384]{2,1,0:T(8,128)(2,1)S(1)}, u32[]{:S(2)}, u32[]{:S(2)}) collective-permute-start(bf16[4,256,384]{2,1,0:T(8,128)(2,1)S(1)} %get-tuple-element.105), channel_id=1, source_target_pairs={{0,16},{16,0},{1,17},{17,1},{2,18},{18,2},{3,19},{19,3},{4,20},{20... | collective-permute-start | bytes 2359304 | tf_op jit(solution)/shard_map/ppermute | solution.py:490
  7.9 1.5 %collective-permute-start.4 = (bf16[4,256,384]{2,1,0:T(8,128)(2,1)S(1)}, bf16[4,256,384]{2,1,0:T(8,128)(2,1)S(1)}, u32[]{:S(2)}, u32[]{:S(2)}) collective-permute-start(bf16[4,256,384]{2,1,0:T(8,128)(2,1)S(1)} %get-tuple-element.104), channel_id=1, source_target_pairs={{0,2},{2,0},{4,6},{6,4},{8,10},{10,8},{12,14},{14,12},{1,3},{3,1},... | collective-permute-start | bytes 2359304 | tf_op jit(solution)/shard_map/ppermute | solution.py:487
  9.5 1.6 %collective-permute-start.3 = (bf16[384,512]{1,0:T(8,128)(2,1)S(1)}, bf16[384,512]{1,0:T(8,128)(2,1)S(1)}, u32[]{:S(2)}, u32[]{:S(2)}) collective-permute-start(bf16[384,512]{1,0:T(8,128)(2,1)S(1)} %shard_map.47.refs_3_.refs_1_), channel_id=1, source_target_pairs={{0,4},{2,6},{4,8},{6,10},{8,12},{10,14},{12,0},{14,2},{1,5},{3,7},... | collective-permute-start | bytes 1179656 | tf_op jit(solution)/shard_map/ppermute | solution.py:478
  11.1 1.1 %shard_map.48 = (f32[256,128]{1,0:T(8,128)S(1)}, f32[256,128]{1,0:T(8,128)S(1)}, f32[256,256]{1,0:T(8,128)S(1)}, f32[256,128]{1,0:T(8,128)S(1)}) custom-call(s32[1,2]{1,0:T(1,128)S(1)} %copy-done.1, f32[256,128]{1,0:T(8,128)S(1)} %get-tuple-element.91._.own_ref), custom_call_target="tpu_custom_call" | custom-call | flops 1 | bytes 1 | tf_op jit(solution)/shard_map/pallas_call | solution.py:359
  12.3 3.7 %collective-permute-done.refs_5_ = bf16[384,512]{1,0:T(8,128)(2,1)S(1)} collective-permute-done((bf16[384,512]{1,0:T(8,128)(2,1)S(1)}, bf16[384,512]{1,0:T(8,128)(2,1)S(1)}, u32[]{:S(2)}, u32[]{:S(2)}) %collective-permute-start) | collective-permute-done | bytes 393248 | tf_op jit(solution)/shard_map/ppermute | solution.py:478
  16.1 2.7 %collective-permute-start.2 = (bf16[4,256,384]{2,1,0:T(8,128)(2,1)S(1)}, bf16[4,256,384]{2,1,0:T(8,128)(2,1)S(1)}, u32[]{:S(2)}, u32[]{:S(2)}) collective-permute-start(bf16[4,256,384]{2,1,0:T(8,128)(2,1)S(1)} %get-tuple-element.99), channel_id=1, source_target_pairs={{0,18},{2,16},{4,22},{6,20},{8,26},{10,24},{12,30},{14,28},{16,2},... | collective-permute-start | bytes 2359304 | tf_op jit(solution)/shard_map/ppermute | solution.py:484
  18.8 1.8 %collective-permute-start.7 = (bf16[384,512]{1,0:T(8,128)(2,1)S(1)}, bf16[384,512]{1,0:T(8,128)(2,1)S(1)}, u32[]{:S(2)}, u32[]{:S(2)}) collective-permute-start(bf16[384,512]{1,0:T(8,128)(2,1)S(1)} %shard_map.47.refs_3_.refs_1_), channel_id=1, source_target_pairs={{4,0},{6,2},{8,4},{10,6},{12,8},{14,10},{0,12},{2,14},{5,1},{7,3},... | collective-permute-start | bytes 1179656 | tf_op jit(solution)/shard_map/ppermute | solution.py:481
  20.6 4.0 %collective-permute-done.3.refs_4_.refs_2_ = bf16[384,512]{1,0:T(8,128)(2,1)S(1)} collective-permute-done((bf16[384,512]{1,0:T(8,128)(2,1)S(1)}, bf16[384,512]{1,0:T(8,128)(2,1)S(1)}, u32[]{:S(2)}, u32[]{:S(2)}) %collective-permute-start.3) | collective-permute-done | bytes 393248 | tf_op jit(solution)/shard_map/ppermute | solution.py:478
  24.6 0.7 %collective-permute-done.5.refs_1_.refs_3_ = bf16[4,256,384]{2,1,0:T(8,128)(2,1)S(1)} collective-permute-done((bf16[4,256,384]{2,1,0:T(8,128)(2,1)S(1)}, bf16[4,256,384]{2,1,0:T(8,128)(2,1)S(1)}, u32[]{:S(2)}, u32[]{:S(2)}) %collective-permute-start.5) | collective-permute-done | bytes 786464 | tf_op jit(solution)/shard_map/ppermute | solution.py:490
  25.4 2.8 %collective-permute-done.4.refs_0_.refs_2_ = bf16[4,256,384]{2,1,0:T(8,128)(2,1)S(1)} collective-permute-done((bf16[4,256,384]{2,1,0:T(8,128)(2,1)S(1)}, bf16[4,256,384]{2,1,0:T(8,128)(2,1)S(1)}, u32[]{:S(2)}, u32[]{:S(2)}) %collective-permute-start.4) | collective-permute-done | bytes 786464 | tf_op jit(solution)/shard_map/ppermute | solution.py:487
  28.2 4.8 %collective-permute-done.7.refs_5_.refs_4_ = bf16[384,512]{1,0:T(8,128)(2,1)S(1)} collective-permute-done((bf16[384,512]{1,0:T(8,128)(2,1)S(1)}, bf16[384,512]{1,0:T(8,128)(2,1)S(1)}, u32[]{:S(2)}, u32[]{:S(2)}) %collective-permute-start.7) | collective-permute-done | bytes 393248 | tf_op jit(solution)/shard_map/ppermute | solution.py:481
  33.4 1.4 %shard_map.50.refs_4_ = f32[3,256,512]{2,1,0:T(8,128)S(1)} custom-call(bf16[4,256,384]{2,1,0:T(8,128)(2,1)S(1)} %collective-permute-done.4.refs_0_.refs_2_, bf16[4,256,384]{2,1,0:T(8,128)(2,1)S(1)} %collective-permute-done.5.refs_1_.refs_3_, bf16[4,256,384]{2,1,0:T(8,128)(2,1)S(1)} %get-tuple-element.108.refs_2_.refs_1_, ...), custom_call_target="tpu_custom_call" | custom-call | flops 1 | bytes 1 | tf_op jit(solution)/shard_map/pallas_call | solution.py:284
  34.8 8.3 %collective-permute-done.6.refs_3_ = bf16[384,512]{1,0:T(8,128)(2,1)S(1)} collective-permute-done((bf16[384,512]{1,0:T(8,128)(2,1)S(1)}, bf16[384,512]{1,0:T(8,128)(2,1)S(1)}, u32[]{:S(2)}, u32[]{:S(2)}) %collective-permute-start.6) | collective-permute-done | bytes 393248 | tf_op jit(solution)/shard_map/ppermute | solution.py:478
  43.1 0.6 shard_map.51
  44.6 2.1 %collective-permute-start.8 = (bf16[384,512]{1,0:T(8,128)(2,1)S(1)}, bf16[384,512]{1,0:T(8,128)(2,1)S(1)}, u32[]{:S(2)}, u32[]{:S(2)}) collective-permute-start(bf16[384,512]{1,0:T(8,128)(2,1)S(1)} %dynamic-slice_bitcast_fusion.refs_4_), channel_id=1, source_target_pairs={{4,0},{6,2},{8,4},{10,6},{12,8},{14,10},{0,12},{2,14},{5,1},{7,3},... | collective-permute-start | bytes 1179656 | tf_op jit(solution)/shard_map/ppermute | solution.py:481
  46.8 0.7 shard_map.52
  47.7 1.8 %collective-permute-start.13 = (bf16[2,256,128]{2,1,0:T(8,128)(2,1)S(1)}, bf16[2,256,128]{2,1,0:T(8,128)(2,1)S(1)}, u32[]{:S(2)}, u32[]{:S(2)}) collective-permute-start(bf16[2,256,128]{2,1,0:T(8,128)(2,1)S(1)} %get-tuple-element.132), channel_id=1, source_target_pairs={{0,16},{16,0},{1,17},{17,1},{2,18},{18,2},{3,19},{19,3},{4,20},{20... | collective-permute-start | bytes 393224 | tf_op jit(solution)/shard_map/ppermute | solution.py:490
  49.5 1.5 %collective-permute-start.12 = (bf16[2,256,128]{2,1,0:T(8,128)(2,1)S(1)}, bf16[2,256,128]{2,1,0:T(8,128)(2,1)S(1)}, u32[]{:S(2)}, u32[]{:S(2)}) collective-permute-start(bf16[2,256,128]{2,1,0:T(8,128)(2,1)S(1)} %get-tuple-element.129), channel_id=1, source_target_pairs={{0,2},{2,0},{4,6},{6,4},{8,10},{10,8},{12,14},{14,12},{1,3},{3,1},... | collective-permute-start | bytes 393224 | tf_op jit(solution)/shard_map/ppermute | solution.py:487
  51.0 0.8 %collective-permute-start.15 = (bf16[2,256,128]{2,1,0:T(8,128)(2,1)S(1)}, bf16[2,256,128]{2,1,0:T(8,128)(2,1)S(1)}, u32[]{:S(2)}, u32[]{:S(2)}) collective-permute-start(bf16[2,256,128]{2,1,0:T(8,128)(2,1)S(1)} %shard_map.55), channel_id=1, source_target_pairs={{0,18},{2,16},{4,22},{6,20},{8,26},{10,24},{12,30},{14,28},{16,2},... | collective-permute-start | bytes 393224 | tf_op jit(solution)/shard_map/ppermute | solution.py:484
  51.8 1.8 %shard_map.54.refs_5_ = f32[4,256,512]{2,1,0:T(8,128)S(1)} custom-call(bf16[4,256,384]{2,1,0:T(8,128)(2,1)S(1)} %collective-permute-done.2.refs_0_, bf16[4,256,384]{2,1,0:T(8,128)(2,1)S(1)} %get-tuple-element.108.refs_2_.refs_1_, bf16[4,256,384]{2,1,0:T(8,128)(2,1)S(1)} %collective-permute-done.4.refs_0_.refs_2_, ...), custom_call_target="tpu_custom_call" | custom-call | flops 1 | bytes 1 | tf_op jit(solution)/shard_map/pallas_call | solution.py:284
  53.6 2.2 %collective-permute-done.12.r1.refs_2_ = bf16[2,256,128]{2,1,0:T(8,128)(2,1)S(1)} collective-permute-done((bf16[2,256,128]{2,1,0:T(8,128)(2,1)S(1)}, bf16[2,256,128]{2,1,0:T(8,128)(2,1)S(1)}, u32[]{:S(2)}, u32[]{:S(2)}) %collective-permute-start.12) | collective-permute-done | bytes 131104 | tf_op jit(solution)/shard_map/ppermute | solution.py:487
  55.8 1.7 %collective-permute-done.8.refs_4_ = bf16[384,512]{1,0:T(8,128)(2,1)S(1)} collective-permute-done((bf16[384,512]{1,0:T(8,128)(2,1)S(1)}, bf16[384,512]{1,0:T(8,128)(2,1)S(1)}, u32[]{:S(2)}, u32[]{:S(2)}) %collective-permute-start.8) | collective-permute-done | bytes 393248 | tf_op jit(solution)/shard_map/ppermute | solution.py:481
  59.6 2.5 %collective-permute-start.17 = (bf16[2,256,128]{2,1,0:T(8,128)(2,1)S(1)}, bf16[2,256,128]{2,1,0:T(8,128)(2,1)S(1)}, u32[]{:S(2)}, u32[]{:S(2)}) collective-permute-start(bf16[2,256,128]{2,1,0:T(8,128)(2,1)S(1)} %get-tuple-element.155), channel_id=1, source_target_pairs={{0,18},{2,16},{4,22},{6,20},{8,26},{10,24},{12,30},{14,28},{16,2},... | collective-permute-start | bytes 393224 | tf_op jit(solution)/shard_map/ppermute | solution.py:484
  62.2 0.6 collective-permute-start.20
  63.3 1.3 %collective-permute-done.18.refs_10_ = bf16[256,128]{1,0:T(8,128)(2,1)S(1)} collective-permute-done((bf16[256,128]{1,0:T(8,128)(2,1)S(1)}, bf16[256,128]{1,0:T(8,128)(2,1)S(1)}, u32[]{:S(2)}, u32[]{:S(2)}) %collective-permute-start.18) | collective-permute-done | bytes 65568 | tf_op jit(solution)/shard_map/ppermute | solution.py:475
  64.5 0.6 shard_map.61.refs_11_
  65.1 1.8 %collective-permute-done.17.refs_1_ = bf16[2,256,128]{2,1,0:T(8,128)(2,1)S(1)} collective-permute-done((bf16[2,256,128]{2,1,0:T(8,128)(2,1)S(1)}, bf16[2,256,128]{2,1,0:T(8,128)(2,1)S(1)}, u32[]{:S(2)}, u32[]{:S(2)}) %collective-permute-start.17) | collective-permute-done | bytes 131104 | tf_op jit(solution)/shard_map/ppermute | solution.py:484
  66.9 2.1 %collective-permute-done.20.refs_2_ = bf16[2,256,128]{2,1,0:T(8,128)(2,1)S(1)} collective-permute-done((bf16[2,256,128]{2,1,0:T(8,128)(2,1)S(1)}, bf16[2,256,128]{2,1,0:T(8,128)(2,1)S(1)}, u32[]{:S(2)}, u32[]{:S(2)}) %collective-permute-start.20) | collective-permute-done | bytes 131104 | tf_op jit(solution)/shard_map/ppermute | solution.py:487
  69.0 1.4 %shard_map.62 = bf16[256,384]{1,0:T(8,128)(2,1)} custom-call(f32[2,256,128]{2,1,0:T(8,128)S(1)} %get-tuple-element.154.refs_0_, bf16[2,256,128]{2,1,0:T(8,128)(2,1)S(1)} %collective-permute-done.17.refs_1_, bf16[2,256,128]{2,1,0:T(8,128)(2,1)S(1)} %collective-permute-done.20.refs_2_, bf16[2,256,128]{2,1,0:T(8,128)(2,1)S(1)} %collective-permute-done.21.refs_3_, ...), custom_call_target="tpu_custom_call" | custom-call | flops 1 | bytes 1 | tf_op jit(solution)/shard_map/pallas_call | solution.py:449
  (35 shorter events, 4.4 us)
Async XLA Ops:
  1.0 8.4 %copy-start = (bf16[1,768,1024]{2,1,0:T(8,128)(2,1)S(1)}, bf16[1,768,1024]{2,1,0:T(8,128)(2,1)}, u32[]{:S(2)}) copy-start(bf16[1,768,1024]{2,1,0:T(8,128)(2,1)} %rows_ref) | copy-start | bytes 4718596
  1.0 15.0 %collective-permute-start = (bf16[384,512]{1,0:T(8,128)(2,1)S(1)}, bf16[384,512]{1,0:T(8,128)(2,1)S(1)}, u32[]{:S(2)}, u32[]{:S(2)}) collective-permute-start(bf16[384,512]{1,0:T(8,128)(2,1)S(1)} %dynamic-slice_bitcast_fusion.1), channel_id=1, source_target_pairs={{0,4},{2,6},{4,8},{6,10},{8,12},{10,14},{12,0},{14,2},{1,5},{3,7},... | collective-permute-start | bytes 1179656 | tf_op jit(solution)/shard_map/ppermute | solution.py:478
  6.3 4.8 %copy-start.1 = (s32[1,2]{1,0:T(1,128)S(1)}, s32[1,2]{1,0:T(1,128)}, u32[]{:S(2)}) copy-start(s32[1,2]{1,0:T(1,128)} %lengths_ref.1) | copy-start | bytes 28
  6.3 19.1 %collective-permute-start.5 = (bf16[4,256,384]{2,1,0:T(8,128)(2,1)S(1)}, bf16[4,256,384]{2,1,0:T(8,128)(2,1)S(1)}, u32[]{:S(2)}, u32[]{:S(2)}) collective-permute-start(bf16[4,256,384]{2,1,0:T(8,128)(2,1)S(1)} %get-tuple-element.105), channel_id=1, source_target_pairs={{0,16},{16,0},{1,17},{17,1},{2,18},{18,2},{3,19},{19,3},{4,20},{20... | collective-permute-start | bytes 2359304 | tf_op jit(solution)/shard_map/ppermute | solution.py:490
  7.9 4.3 %collective-permute-start.1 = (f32[256,128]{1,0:T(8,128)S(1)}, f32[256,128]{1,0:T(8,128)S(1)}, u32[]{:S(2)}, u32[]{:S(2)}) collective-permute-start(f32[256,128]{1,0:T(8,128)S(1)} %get-tuple-element.91._.own_ref), channel_id=1, source_target_pairs={{0,1},{1,0},{2,3},{3,2},{4,5},{5,4},{6,7},{7,6},{8,9},{9,8},{10,11... | collective-permute-start | bytes 393224 | tf_op jit(solution)/shard_map/ppermute | solution.py:475
  7.9 20.3 %collective-permute-start.4 = (bf16[4,256,384]{2,1,0:T(8,128)(2,1)S(1)}, bf16[4,256,384]{2,1,0:T(8,128)(2,1)S(1)}, u32[]{:S(2)}, u32[]{:S(2)}) collective-permute-start(bf16[4,256,384]{2,1,0:T(8,128)(2,1)S(1)} %get-tuple-element.104), channel_id=1, source_target_pairs={{0,2},{2,0},{4,6},{6,4},{8,10},{10,8},{12,14},{14,12},{1,3},{3,1},... | collective-permute-start | bytes 2359304 | tf_op jit(solution)/shard_map/ppermute | solution.py:487
  9.5 15.1 %collective-permute-start.3 = (bf16[384,512]{1,0:T(8,128)(2,1)S(1)}, bf16[384,512]{1,0:T(8,128)(2,1)S(1)}, u32[]{:S(2)}, u32[]{:S(2)}) collective-permute-start(bf16[384,512]{1,0:T(8,128)(2,1)S(1)} %shard_map.47.refs_3_.refs_1_), channel_id=1, source_target_pairs={{0,4},{2,6},{4,8},{6,10},{8,12},{10,14},{12,0},{14,2},{1,5},{3,7},... | collective-permute-start | bytes 1179656 | tf_op jit(solution)/shard_map/ppermute | solution.py:478
  16.1 28.6 %collective-permute-start.2 = (bf16[4,256,384]{2,1,0:T(8,128)(2,1)S(1)}, bf16[4,256,384]{2,1,0:T(8,128)(2,1)S(1)}, u32[]{:S(2)}, u32[]{:S(2)}) collective-permute-start(bf16[4,256,384]{2,1,0:T(8,128)(2,1)S(1)} %get-tuple-element.99), channel_id=1, source_target_pairs={{0,18},{2,16},{4,22},{6,20},{8,26},{10,24},{12,30},{14,28},{16,2},... | collective-permute-start | bytes 2359304 | tf_op jit(solution)/shard_map/ppermute | solution.py:484
  18.8 14.2 %collective-permute-start.7 = (bf16[384,512]{1,0:T(8,128)(2,1)S(1)}, bf16[384,512]{1,0:T(8,128)(2,1)S(1)}, u32[]{:S(2)}, u32[]{:S(2)}) collective-permute-start(bf16[384,512]{1,0:T(8,128)(2,1)S(1)} %shard_map.47.refs_3_.refs_1_), channel_id=1, source_target_pairs={{4,0},{6,2},{8,4},{10,6},{12,8},{14,10},{0,12},{2,14},{5,1},{7,3},... | collective-permute-start | bytes 1179656 | tf_op jit(solution)/shard_map/ppermute | solution.py:481
  24.6 18.5 %collective-permute-start.6 = (bf16[384,512]{1,0:T(8,128)(2,1)S(1)}, bf16[384,512]{1,0:T(8,128)(2,1)S(1)}, u32[]{:S(2)}, u32[]{:S(2)}) collective-permute-start(bf16[384,512]{1,0:T(8,128)(2,1)S(1)} %collective-permute-done.3.refs_4_.refs_2_), channel_id=1, source_target_pairs={{0,4},{2,6},{4,8},{6,10},{8,12},{10,14},{12,0},{14,2},{1,5},{3,7},... | collective-permute-start | bytes 1179656 | tf_op jit(solution)/shard_map/ppermute | solution.py:478
  33.0 17.9 %collective-permute-start.9 = (bf16[384,512]{1,0:T(8,128)(2,1)S(1)}, bf16[384,512]{1,0:T(8,128)(2,1)S(1)}, u32[]{:S(2)}, u32[]{:S(2)}) collective-permute-start(bf16[384,512]{1,0:T(8,128)(2,1)S(1)} %collective-permute-done.refs_5_), channel_id=1, source_target_pairs={{0,4},{2,6},{4,8},{6,10},{8,12},{10,14},{12,0},{14,2},{1,5},{3,7},... | collective-permute-start | bytes 1179656 | tf_op jit(solution)/shard_map/ppermute | solution.py:478
  43.7 3.8 %collective-permute-start.10 = (bf16[3,256,128]{2,1,0:T(8,128)(2,1)S(1)}, bf16[3,256,128]{2,1,0:T(8,128)(2,1)S(1)}, u32[]{:S(2)}, u32[]{:S(2)}) collective-permute-start(bf16[3,256,128]{2,1,0:T(8,128)(2,1)S(1)} %get-tuple-element.116), channel_id=1, source_target_pairs={{0,1},{1,0},{2,3},{3,2},{4,5},{5,4},{6,7},{7,6},{8,9},{9,8},{10,11... | collective-permute-start | bytes 589832 | tf_op jit(solution)/shard_map/ppermute | solution.py:475
  43.8 3.7 %collective-permute-start.11 = (bf16[3,256,128]{2,1,0:T(8,128)(2,1)S(1)}, bf16[3,256,128]{2,1,0:T(8,128)(2,1)S(1)}, u32[]{:S(2)}, u32[]{:S(2)}) collective-permute-start(bf16[3,256,128]{2,1,0:T(8,128)(2,1)S(1)} %get-tuple-element.123), channel_id=1, source_target_pairs={{0,1},{1,0},{2,3},{3,2},{4,5},{5,4},{6,7},{7,6},{8,9},{9,8},{10,11... | collective-permute-start | bytes 589832 | tf_op jit(solution)/shard_map/ppermute | solution.py:475
  44.6 12.8 %collective-permute-start.8 = (bf16[384,512]{1,0:T(8,128)(2,1)S(1)}, bf16[384,512]{1,0:T(8,128)(2,1)S(1)}, u32[]{:S(2)}, u32[]{:S(2)}) collective-permute-start(bf16[384,512]{1,0:T(8,128)(2,1)S(1)} %dynamic-slice_bitcast_fusion.refs_4_), channel_id=1, source_target_pairs={{4,0},{6,2},{8,4},{10,6},{12,8},{14,10},{0,12},{2,14},{5,1},{7,3},... | collective-permute-start | bytes 1179656 | tf_op jit(solution)/shard_map/ppermute | solution.py:481
  47.6 3.4 %collective-permute-start.14 = (bf16[2,256,128]{2,1,0:T(8,128)(2,1)S(1)}, bf16[2,256,128]{2,1,0:T(8,128)(2,1)S(1)}, u32[]{:S(2)}, u32[]{:S(2)}) collective-permute-start(bf16[2,256,128]{2,1,0:T(8,128)(2,1)S(1)} %get-tuple-element.130), channel_id=1, source_target_pairs={{0,1},{1,0},{2,3},{3,2},{4,5},{5,4},{6,7},{7,6},{8,9},{9,8},{10,11... | collective-permute-start | bytes 393224 | tf_op jit(solution)/shard_map/ppermute | solution.py:475
  47.7 5.9 %collective-permute-start.13 = (bf16[2,256,128]{2,1,0:T(8,128)(2,1)S(1)}, bf16[2,256,128]{2,1,0:T(8,128)(2,1)S(1)}, u32[]{:S(2)}, u32[]{:S(2)}) collective-permute-start(bf16[2,256,128]{2,1,0:T(8,128)(2,1)S(1)} %get-tuple-element.132), channel_id=1, source_target_pairs={{0,16},{16,0},{1,17},{17,1},{2,18},{18,2},{3,19},{19,3},{4,20},{20... | collective-permute-start | bytes 393224 | tf_op jit(solution)/shard_map/ppermute | solution.py:490
  49.5 6.3 %collective-permute-start.12 = (bf16[2,256,128]{2,1,0:T(8,128)(2,1)S(1)}, bf16[2,256,128]{2,1,0:T(8,128)(2,1)S(1)}, u32[]{:S(2)}, u32[]{:S(2)}) collective-permute-start(bf16[2,256,128]{2,1,0:T(8,128)(2,1)S(1)} %get-tuple-element.129), channel_id=1, source_target_pairs={{0,2},{2,0},{4,6},{6,4},{8,10},{10,8},{12,14},{14,12},{1,3},{3,1},... | collective-permute-start | bytes 393224 | tf_op jit(solution)/shard_map/ppermute | solution.py:487
  51.0 6.9 %collective-permute-start.15 = (bf16[2,256,128]{2,1,0:T(8,128)(2,1)S(1)}, bf16[2,256,128]{2,1,0:T(8,128)(2,1)S(1)}, u32[]{:S(2)}, u32[]{:S(2)}) collective-permute-start(bf16[2,256,128]{2,1,0:T(8,128)(2,1)S(1)} %shard_map.55), channel_id=1, source_target_pairs={{0,18},{2,16},{4,22},{6,20},{8,26},{10,24},{12,30},{14,28},{16,2},... | collective-permute-start | bytes 393224 | tf_op jit(solution)/shard_map/ppermute | solution.py:484
  57.9 1.6 %collective-permute-start.16 = (bf16[4,256,128]{2,1,0:T(8,128)(2,1)S(1)}, bf16[4,256,128]{2,1,0:T(8,128)(2,1)S(1)}, u32[]{:S(2)}, u32[]{:S(2)}) collective-permute-start(bf16[4,256,128]{2,1,0:T(8,128)(2,1)S(1)} %get-tuple-element.144), channel_id=1, source_target_pairs={{0,1},{1,0},{2,3},{3,2},{4,5},{5,4},{6,7},{7,6},{8,9},{9,8},{10,11... | collective-permute-start | bytes 786440 | tf_op jit(solution)/shard_map/ppermute | solution.py:475
  58.0 4.1 %collective-permute-start.19 = (bf16[4,256,128]{2,1,0:T(8,128)(2,1)S(1)}, bf16[4,256,128]{2,1,0:T(8,128)(2,1)S(1)}, u32[]{:S(2)}, u32[]{:S(2)}) collective-permute-start(bf16[4,256,128]{2,1,0:T(8,128)(2,1)S(1)} %get-tuple-element.158), channel_id=1, source_target_pairs={{0,1},{1,0},{2,3},{3,2},{4,5},{5,4},{6,7},{7,6},{8,9},{9,8},{10,11... | collective-permute-start | bytes 786440 | tf_op jit(solution)/shard_map/ppermute | solution.py:475
  59.6 7.3 %collective-permute-start.17 = (bf16[2,256,128]{2,1,0:T(8,128)(2,1)S(1)}, bf16[2,256,128]{2,1,0:T(8,128)(2,1)S(1)}, u32[]{:S(2)}, u32[]{:S(2)}) collective-permute-start(bf16[2,256,128]{2,1,0:T(8,128)(2,1)S(1)} %get-tuple-element.155), channel_id=1, source_target_pairs={{0,18},{2,16},{4,22},{6,20},{8,26},{10,24},{12,30},{14,28},{16,2},... | collective-permute-start | bytes 393224 | tf_op jit(solution)/shard_map/ppermute | solution.py:484
  62.2 6.8 %collective-permute-start.20 = (bf16[2,256,128]{2,1,0:T(8,128)(2,1)S(1)}, bf16[2,256,128]{2,1,0:T(8,128)(2,1)S(1)}, u32[]{:S(2)}, u32[]{:S(2)}) collective-permute-start(bf16[2,256,128]{2,1,0:T(8,128)(2,1)S(1)} %get-tuple-element.162), channel_id=1, source_target_pairs={{0,2},{2,0},{4,6},{6,4},{8,10},{10,8},{12,14},{14,12},{1,3},{3,1},... | collective-permute-start | bytes 393224 | tf_op jit(solution)/shard_map/ppermute | solution.py:487
  62.7 6.2 %collective-permute-start.21 = (bf16[2,256,128]{2,1,0:T(8,128)(2,1)S(1)}, bf16[2,256,128]{2,1,0:T(8,128)(2,1)S(1)}, u32[]{:S(2)}, u32[]{:S(2)}) collective-permute-start(bf16[2,256,128]{2,1,0:T(8,128)(2,1)S(1)} %get-tuple-element.166), channel_id=1, source_target_pairs={{0,16},{16,0},{1,17},{17,1},{2,18},{18,2},{3,19},{19,3},{4,20},{20... | collective-permute-start | bytes 393224 | tf_op jit(solution)/shard_map/ppermute | solution.py:490
  63.3 1.3 %collective-permute-start.18 = (bf16[256,128]{1,0:T(8,128)(2,1)S(1)}, bf16[256,128]{1,0:T(8,128)(2,1)S(1)}, u32[]{:S(2)}, u32[]{:S(2)}) collective-permute-start(bf16[256,128]{1,0:T(8,128)(2,1)S(1)} %shard_map.58.refs_9_), channel_id=1, source_target_pairs={{0,1},{1,0},{2,3},{3,2},{4,5},{5,4},{6,7},{7,6},{8,9},{9,8},{10,11... | collective-permute-start | bytes 196616 | tf_op jit(solution)/shard_map/ppermute | solution.py:475

commit v11 on v10

--- a/solution.py
+++ b/solution.py
@@ -290,7 +290,7 @@
     return outs if sent else outs[0]
 
 
-def half_kernel(first, swapped, n_acts, *refs):
+def half_kernel(first, swapped, n_acts, skip, *refs):
     acts, (slot_ref, more_ref), out_refs = refs[:n_acts], refs[n_acts:n_acts + 2], refs[n_acts + 2:]
     core = lax.axis_index("tensor")
     width = slot_ref.shape[1] // 2
@@ -299,19 +299,19 @@
     n_blocks = width // HEAD
     per = n_acts * n_blocks // len(out_refs)
     for p in range(n_acts):
-        total = jnp.dot(acts[p][first], right, preferred_element_type=jnp.float32) + more_ref[p, :, where]
+        total = jnp.dot(acts[p][first], right, preferred_element_type=jnp.float32) + more_ref[skip + p, :, where]
         for g in range(n_blocks):
             spot = p * n_blocks + g
             out_ref = out_refs[spot // per]
             out_ref[spot % per] = total[:, g * HEAD:(g + 1) * HEAD].astype(out_ref.dtype)
 
 
-def half_matmul(acts, slot, first, so_far, swapped, pieces, dtype):
+def half_matmul(acts, slot, first, so_far, swapped, pieces, dtype, skip=0):
     tokens, width = acts[0].shape[1], slot.shape[1] // 2
     args = [*acts, slot, so_far]
     rows = len(acts) * width // HEAD // pieces
     return call(
-        functools.partial(half_kernel, first, swapped, len(acts)),
+        functools.partial(half_kernel, first, swapped, len(acts), skip),
         (jax.ShapeDtypeStruct((rows, tokens, HEAD), dtype),) * pieces,
         in_specs=[WHOLE] * len(args),
         out_specs=[WHOLE] * pieces,
@@ -552,10 +552,16 @@
 
     b3 = after(b3)
     parts_a = after(sums, sums_far, sums_x, sums_y)
-    theirs = after(*half_matmul(acts, b3, 3, front, True, 2, jnp.bfloat16))
-    swapped = [to_core(t) for t in theirs]
-    mine, = half_matmul(acts, after(b3), 3, front, False, 1, jnp.float32)
-    mine = mine.reshape(len(acts), -1, *mine.shape[1:])
+    theirs, = half_matmul(acts[:2], b3, 3, front, True, 1, jnp.bfloat16)
+    theirs = after(theirs)
+    swapped = [to_core(theirs)]
+    theirs, = half_matmul(acts[2:], after(b3), 3, front, True, 1, jnp.bfloat16, 2)
+    theirs = after(theirs)
+    swapped.append(to_core(theirs))
+    mine = []
+    for skip in (0, 2):
+        total, = half_matmul(acts[skip:skip + 2], after(b3), 3, front, False, 1, jnp.float32, skip)
+        mine.append(total.reshape(2, -1, *total.shape[1:]))
     kv = after(call(
         kv_kernel,
         jax.ShapeDtypeStruct((tokens, HEAD), jnp.bfloat16),
@@ -563,9 +569,9 @@
         out_specs=WHOLE,
     )(*parts_a, scale, *tabled[:2]))
     vk = to_core(kv)
-    sums_far, sums = after(*join(mine, (after(swapped[0]),), (jnp.bfloat16, jnp.float32)))
+    sums_far, sums = after(*join(mine[0], (after(swapped[0]),), (jnp.bfloat16, jnp.float32)))
     sums_far = to_far(sums_far)
-    sums_x, sums_y = after(*join(mine, (after(swapped[1]),), (jnp.bfloat16, jnp.bfloat16), first=2))
+    sums_x, sums_y = after(*join(mine[1], (after(swapped[1]),), (jnp.bfloat16, jnp.bfloat16)))
     sums_x = to_x(sums_x)
     sums_y = to_y(sums_y)
     vk = after(vk)

time: 70.5 us -> 70.3 us (level)
  transfers between devices with their start and end apart: 22 -> 22, of which waited for: 13 -> 12; matrix products, arithmetic and copies ran while one was open for 0% -> 0% of each run, Pallas kernels for 14% -> 14%
where the time goes in v11:
time: 70.3 us; the launch traced here: 70.2 us
  waiting for transfers between devices  33.8 us (48%)
  starting transfers between devices  23.8 us (34%)
  Pallas kernels  11.3 us (16%)
  local copies, waits for them, and re-layouts  1.06 us (2%)
    ppermute x4, waiting for transfers between devices, on_ring(): return lax.ppermute(a, 'dp', ring)  16.1 us
    ppermute x3, waiting for transfers between devices, to_x(): return lax.ppermute(a, 'dp', over_x)  7.03 us
    ppermute x2, waiting for transfers between devices, back(): return lax.ppermute(a, 'dp', [(j, i) for i, j in ring])  6.47 us
    ppermute x3, starting transfers between devices, to_far(): return lax.ppermute(a, ('groups', 'dp'), across)  5.99 us
    ppermute x4, starting transfers between devices, on_ring(): return lax.ppermute(a, 'dp', ring)  5.1 us
    pallas_call x4, Pallas kernels, matmul(): call(functools.partial(matmul_kernel, firsts, len(acts), len(so_far), sen...  4.41 us
    ppermute x2, starting transfers between devices, back(): return lax.ppermute(a, 'dp', [(j, i) for i, j in ring])  3.94 us
    ppermute x3, starting transfers between devices, to_y(): return lax.ppermute(a, 'groups', over_y)  3.88 us
  transfers between devices with their start and end apart: 22, of which 12 were waited for; matrix products, arithmetic and copies ran while one was open for 0% of the time, Pallas kernels for 14%

profile of v11, /device:TPU:0, one launch (start us, length us, event | category | flops | bytes accessed | tf_op | source)
XLA Modules:
  0.0 70.2 jit_solution(2128892597270542803)
XLA Ops:
  0.0 1.0 %dynamic-slice_bitcast_fusion.1 = bf16[384,512]{1,0:T(8,128)(2,1)S(1)} fusion(bf16[1,768,1024]{2,1,0:T(8,128)(2,1)} %rows_ref, s32[]{:T(128)S(6)} %select_n.4), kind=kLoop, calls=%fused_computation.1 | loop fusion | bytes 786436 | tf_op jit(solution)/shard_map/dynamic_slice | solution.py:507
  1.0 3.1 %collective-permute-start = (bf16[384,512]{1,0:T(8,128)(2,1)S(1)}, bf16[384,512]{1,0:T(8,128)(2,1)S(1)}, u32[]{:S(2)}, u32[]{:S(2)}) collective-permute-start(bf16[384,512]{1,0:T(8,128)(2,1)S(1)} %dynamic-slice_bitcast_fusion.1), channel_id=1, source_target_pairs={{0,4},{2,6},{4,8},{6,10},{8,12},{10,14},{12,0},{14,2},{1,5},{3,7},... | collective-permute-start | bytes 1179656 | tf_op jit(solution)/shard_map/ppermute | solution.py:478
  4.1 2.2 %shard_map.46 = (bf16[4,256,384]{2,1,0:T(8,128)(2,1)S(1)}, bf16[4,256,384]{2,1,0:T(8,128)(2,1)S(1)}, bf16[4,256,384]{2,1,0:T(8,128)(2,1)S(1)}, bf16[4,256,384]{2,1,0:T(8,128)(2,1)S(1)}, f32[256,128]{1,0:T(8,128)S(1)}) custom-call(bf16[256,6144]{1,0:T(8,128)(2,1)} %hidden_ref.1, bf16[6144]{0:T(1024)(128)(2,1)} %gain_ref.1), custom_call_target="tpu_custom_call" | custom-call | flops 1 | bytes 1 | tf_op jit(solution)/shard_map/pallas_call | solution.py:231
  6.3 1.6 %collective-permute-start.5 = (bf16[4,256,384]{2,1,0:T(8,128)(2,1)S(1)}, bf16[4,256,384]{2,1,0:T(8,128)(2,1)S(1)}, u32[]{:S(2)}, u32[]{:S(2)}) collective-permute-start(bf16[4,256,384]{2,1,0:T(8,128)(2,1)S(1)} %get-tuple-element.105), channel_id=1, source_target_pairs={{0,16},{16,0},{1,17},{17,1},{2,18},{18,2},{3,19},{19,3},{4,20},{20... | collective-permute-start | bytes 2359304 | tf_op jit(solution)/shard_map/ppermute | solution.py:490
  7.9 1.5 %collective-permute-start.4 = (bf16[4,256,384]{2,1,0:T(8,128)(2,1)S(1)}, bf16[4,256,384]{2,1,0:T(8,128)(2,1)S(1)}, u32[]{:S(2)}, u32[]{:S(2)}) collective-permute-start(bf16[4,256,384]{2,1,0:T(8,128)(2,1)S(1)} %get-tuple-element.104), channel_id=1, source_target_pairs={{0,2},{2,0},{4,6},{6,4},{8,10},{10,8},{12,14},{14,12},{1,3},{3,1},... | collective-permute-start | bytes 2359304 | tf_op jit(solution)/shard_map/ppermute | solution.py:487
  9.5 1.6 %collective-permute-start.3 = (bf16[384,512]{1,0:T(8,128)(2,1)S(1)}, bf16[384,512]{1,0:T(8,128)(2,1)S(1)}, u32[]{:S(2)}, u32[]{:S(2)}) collective-permute-start(bf16[384,512]{1,0:T(8,128)(2,1)S(1)} %shard_map.47.refs_3_.refs_1_), channel_id=1, source_target_pairs={{0,4},{2,6},{4,8},{6,10},{8,12},{10,14},{12,0},{14,2},{1,5},{3,7},... | collective-permute-start | bytes 1179656 | tf_op jit(solution)/shard_map/ppermute | solution.py:478
  11.1 1.1 %shard_map.48 = (f32[256,128]{1,0:T(8,128)S(1)}, f32[256,128]{1,0:T(8,128)S(1)}, f32[256,256]{1,0:T(8,128)S(1)}, f32[256,128]{1,0:T(8,128)S(1)}) custom-call(s32[1,2]{1,0:T(1,128)S(1)} %copy-done.1, f32[256,128]{1,0:T(8,128)S(1)} %get-tuple-element.91._.own_ref), custom_call_target="tpu_custom_call" | custom-call | flops 1 | bytes 1 | tf_op jit(solution)/shard_map/pallas_call | solution.py:359
  12.3 3.7 %collective-permute-done.refs_5_ = bf16[384,512]{1,0:T(8,128)(2,1)S(1)} collective-permute-done((bf16[384,512]{1,0:T(8,128)(2,1)S(1)}, bf16[384,512]{1,0:T(8,128)(2,1)S(1)}, u32[]{:S(2)}, u32[]{:S(2)}) %collective-permute-start) | collective-permute-done | bytes 393248 | tf_op jit(solution)/shard_map/ppermute | solution.py:478
  16.1 2.7 %collective-permute-start.2 = (bf16[4,256,384]{2,1,0:T(8,128)(2,1)S(1)}, bf16[4,256,384]{2,1,0:T(8,128)(2,1)S(1)}, u32[]{:S(2)}, u32[]{:S(2)}) collective-permute-start(bf16[4,256,384]{2,1,0:T(8,128)(2,1)S(1)} %get-tuple-element.99), channel_id=1, source_target_pairs={{0,18},{2,16},{4,22},{6,20},{8,26},{10,24},{12,30},{14,28},{16,2},... | collective-permute-start | bytes 2359304 | tf_op jit(solution)/shard_map/ppermute | solution.py:484
  18.8 1.8 %collective-permute-start.7 = (bf16[384,512]{1,0:T(8,128)(2,1)S(1)}, bf16[384,512]{1,0:T(8,128)(2,1)S(1)}, u32[]{:S(2)}, u32[]{:S(2)}) collective-permute-start(bf16[384,512]{1,0:T(8,128)(2,1)S(1)} %shard_map.47.refs_3_.refs_1_), channel_id=1, source_target_pairs={{4,0},{6,2},{8,4},{10,6},{12,8},{14,10},{0,12},{2,14},{5,1},{7,3},... | collective-permute-start | bytes 1179656 | tf_op jit(solution)/shard_map/ppermute | solution.py:481
  20.6 4.0 %collective-permute-done.3.refs_4_.refs_2_ = bf16[384,512]{1,0:T(8,128)(2,1)S(1)} collective-permute-done((bf16[384,512]{1,0:T(8,128)(2,1)S(1)}, bf16[384,512]{1,0:T(8,128)(2,1)S(1)}, u32[]{:S(2)}, u32[]{:S(2)}) %collective-permute-start.3) | collective-permute-done | bytes 393248 | tf_op jit(solution)/shard_map/ppermute | solution.py:478
  24.6 0.7 %collective-permute-done.5.refs_1_.refs_3_ = bf16[4,256,384]{2,1,0:T(8,128)(2,1)S(1)} collective-permute-done((bf16[4,256,384]{2,1,0:T(8,128)(2,1)S(1)}, bf16[4,256,384]{2,1,0:T(8,128)(2,1)S(1)}, u32[]{:S(2)}, u32[]{:S(2)}) %collective-permute-start.5) | collective-permute-done | bytes 786464 | tf_op jit(solution)/shard_map/ppermute | solution.py:490
  25.4 2.8 %collective-permute-done.4.refs_0_.refs_2_ = bf16[4,256,384]{2,1,0:T(8,128)(2,1)S(1)} collective-permute-done((bf16[4,256,384]{2,1,0:T(8,128)(2,1)S(1)}, bf16[4,256,384]{2,1,0:T(8,128)(2,1)S(1)}, u32[]{:S(2)}, u32[]{:S(2)}) %collective-permute-start.4) | collective-permute-done | bytes 786464 | tf_op jit(solution)/shard_map/ppermute | solution.py:487
  28.2 4.8 %collective-permute-done.7.refs_5_.refs_4_ = bf16[384,512]{1,0:T(8,128)(2,1)S(1)} collective-permute-done((bf16[384,512]{1,0:T(8,128)(2,1)S(1)}, bf16[384,512]{1,0:T(8,128)(2,1)S(1)}, u32[]{:S(2)}, u32[]{:S(2)}) %collective-permute-start.7) | collective-permute-done | bytes 393248 | tf_op jit(solution)/shard_map/ppermute | solution.py:481
  33.4 1.4 %shard_map.50.refs_4_ = f32[3,256,512]{2,1,0:T(8,128)S(1)} custom-call(bf16[4,256,384]{2,1,0:T(8,128)(2,1)S(1)} %collective-permute-done.4.refs_0_.refs_2_, bf16[4,256,384]{2,1,0:T(8,128)(2,1)S(1)} %collective-permute-done.5.refs_1_.refs_3_, bf16[4,256,384]{2,1,0:T(8,128)(2,1)S(1)} %get-tuple-element.108.refs_2_.refs_1_, ...), custom_call_target="tpu_custom_call" | custom-call | flops 1 | bytes 1 | tf_op jit(solution)/shard_map/pallas_call | solution.py:284
  34.8 8.3 %collective-permute-done.6.refs_3_ = bf16[384,512]{1,0:T(8,128)(2,1)S(1)} collective-permute-done((bf16[384,512]{1,0:T(8,128)(2,1)S(1)}, bf16[384,512]{1,0:T(8,128)(2,1)S(1)}, u32[]{:S(2)}, u32[]{:S(2)}) %collective-permute-start.6) | collective-permute-done | bytes 393248 | tf_op jit(solution)/shard_map/ppermute | solution.py:478
  43.1 0.6 shard_map.51
  44.6 2.1 %collective-permute-start.8 = (bf16[384,512]{1,0:T(8,128)(2,1)S(1)}, bf16[384,512]{1,0:T(8,128)(2,1)S(1)}, u32[]{:S(2)}, u32[]{:S(2)}) collective-permute-start(bf16[384,512]{1,0:T(8,128)(2,1)S(1)} %dynamic-slice_bitcast_fusion.refs_4_), channel_id=1, source_target_pairs={{4,0},{6,2},{8,4},{10,6},{12,8},{14,10},{0,12},{2,14},{5,1},{7,3},... | collective-permute-start | bytes 1179656 | tf_op jit(solution)/shard_map/ppermute | solution.py:481
  46.8 0.7 shard_map.52
  47.7 1.8 %collective-permute-start.13 = (bf16[2,256,128]{2,1,0:T(8,128)(2,1)S(1)}, bf16[2,256,128]{2,1,0:T(8,128)(2,1)S(1)}, u32[]{:S(2)}, u32[]{:S(2)}) collective-permute-start(bf16[2,256,128]{2,1,0:T(8,128)(2,1)S(1)} %get-tuple-element.132), channel_id=1, source_target_pairs={{0,16},{16,0},{1,17},{17,1},{2,18},{18,2},{3,19},{19,3},{4,20},{20... | collective-permute-start | bytes 393224 | tf_op jit(solution)/shard_map/ppermute | solution.py:490
  49.5 1.5 %collective-permute-start.12 = (bf16[2,256,128]{2,1,0:T(8,128)(2,1)S(1)}, bf16[2,256,128]{2,1,0:T(8,128)(2,1)S(1)}, u32[]{:S(2)}, u32[]{:S(2)}) collective-permute-start(bf16[2,256,128]{2,1,0:T(8,128)(2,1)S(1)} %get-tuple-element.129), channel_id=1, source_target_pairs={{0,2},{2,0},{4,6},{6,4},{8,10},{10,8},{12,14},{14,12},{1,3},{3,1},... | collective-permute-start | bytes 393224 | tf_op jit(solution)/shard_map/ppermute | solution.py:487
  51.0 0.8 %collective-permute-start.15 = (bf16[2,256,128]{2,1,0:T(8,128)(2,1)S(1)}, bf16[2,256,128]{2,1,0:T(8,128)(2,1)S(1)}, u32[]{:S(2)}, u32[]{:S(2)}) collective-permute-start(bf16[2,256,128]{2,1,0:T(8,128)(2,1)S(1)} %shard_map.55), channel_id=1, source_target_pairs={{0,18},{2,16},{4,22},{6,20},{8,26},{10,24},{12,30},{14,28},{16,2},... | collective-permute-start | bytes 393224 | tf_op jit(solution)/shard_map/ppermute | solution.py:484
  51.8 1.8 %shard_map.54.refs_3_ = f32[4,256,512]{2,1,0:T(8,128)S(1)} custom-call(bf16[4,256,384]{2,1,0:T(8,128)(2,1)S(1)} %collective-permute-done.2.refs_0_, bf16[4,256,384]{2,1,0:T(8,128)(2,1)S(1)} %get-tuple-element.108.refs_2_.refs_1_, bf16[4,256,384]{2,1,0:T(8,128)(2,1)S(1)} %collective-permute-done.4.refs_0_.refs_2_, ...), custom_call_target="tpu_custom_call" | custom-call | flops 1 | bytes 1 | tf_op jit(solution)/shard_map/pallas_call | solution.py:284
  53.6 2.2 %collective-permute-done.12.r1.refs_2_ = bf16[2,256,128]{2,1,0:T(8,128)(2,1)S(1)} collective-permute-done((bf16[2,256,128]{2,1,0:T(8,128)(2,1)S(1)}, bf16[2,256,128]{2,1,0:T(8,128)(2,1)S(1)}, u32[]{:S(2)}, u32[]{:S(2)}) %collective-permute-start.12) | collective-permute-done | bytes 131104 | tf_op jit(solution)/shard_map/ppermute | solution.py:487
  55.8 1.7 %collective-permute-done.8.refs_2_ = bf16[384,512]{1,0:T(8,128)(2,1)S(1)} collective-permute-done((bf16[384,512]{1,0:T(8,128)(2,1)S(1)}, bf16[384,512]{1,0:T(8,128)(2,1)S(1)}, u32[]{:S(2)}, u32[]{:S(2)}) %collective-permute-start.8) | collective-permute-done | bytes 393248 | tf_op jit(solution)/shard_map/ppermute | solution.py:481
  59.5 2.5 %collective-permute-start.17 = (bf16[2,256,128]{2,1,0:T(8,128)(2,1)S(1)}, bf16[2,256,128]{2,1,0:T(8,128)(2,1)S(1)}, u32[]{:S(2)}, u32[]{:S(2)}) collective-permute-start(bf16[2,256,128]{2,1,0:T(8,128)(2,1)S(1)} %get-tuple-element.156), channel_id=1, source_target_pairs={{0,18},{2,16},{4,22},{6,20},{8,26},{10,24},{12,30},{14,28},{16,2},... | collective-permute-start | bytes 393224 | tf_op jit(solution)/shard_map/ppermute | solution.py:484
  62.1 0.6 collective-permute-start.20
  63.2 1.3 %collective-permute-done.18.refs_10_ = bf16[256,128]{1,0:T(8,128)(2,1)S(1)} collective-permute-done((bf16[256,128]{1,0:T(8,128)(2,1)S(1)}, bf16[256,128]{1,0:T(8,128)(2,1)S(1)}, u32[]{:S(2)}, u32[]{:S(2)}) %collective-permute-start.18) | collective-permute-done | bytes 65568 | tf_op jit(solution)/shard_map/ppermute | solution.py:475
  64.5 0.6 shard_map.63.refs_11_
  65.1 1.8 %collective-permute-done.17.refs_1_ = bf16[2,256,128]{2,1,0:T(8,128)(2,1)S(1)} collective-permute-done((bf16[2,256,128]{2,1,0:T(8,128)(2,1)S(1)}, bf16[2,256,128]{2,1,0:T(8,128)(2,1)S(1)}, u32[]{:S(2)}, u32[]{:S(2)}) %collective-permute-start.17) | collective-permute-done | bytes 131104 | tf_op jit(solution)/shard_map/ppermute | solution.py:484
  66.9 2.0 %collective-permute-done.20.refs_2_ = bf16[2,256,128]{2,1,0:T(8,128)(2,1)S(1)} collective-permute-done((bf16[2,256,128]{2,1,0:T(8,128)(2,1)S(1)}, bf16[2,256,128]{2,1,0:T(8,128)(2,1)S(1)}, u32[]{:S(2)}, u32[]{:S(2)}) %collective-permute-start.20) | collective-permute-done | bytes 131104 | tf_op jit(solution)/shard_map/ppermute | solution.py:487
  68.8 1.4 %shard_map.64 = bf16[256,384]{1,0:T(8,128)(2,1)} custom-call(f32[2,256,128]{2,1,0:T(8,128)S(1)} %get-tuple-element.155.refs_0_, bf16[2,256,128]{2,1,0:T(8,128)(2,1)S(1)} %collective-permute-done.17.refs_1_, bf16[2,256,128]{2,1,0:T(8,128)(2,1)S(1)} %collective-permute-done.20.refs_2_, bf16[2,256,128]{2,1,0:T(8,128)(2,1)S(1)} %collective-permute-done.21.refs_3_, ...), custom_call_target="tpu_custom_call" | custom-call | flops 1 | bytes 1 | tf_op jit(solution)/shard_map/pallas_call | solution.py:449
  (37 shorter events, 4.4 us)
Async XLA Ops:
  1.0 8.4 %copy-start = (bf16[1,768,1024]{2,1,0:T(8,128)(2,1)S(1)}, bf16[1,768,1024]{2,1,0:T(8,128)(2,1)}, u32[]{:S(2)}) copy-start(bf16[1,768,1024]{2,1,0:T(8,128)(2,1)} %rows_ref) | copy-start | bytes 4718596
  1.0 15.0 %collective-permute-start = (bf16[384,512]{1,0:T(8,128)(2,1)S(1)}, bf16[384,512]{1,0:T(8,128)(2,1)S(1)}, u32[]{:S(2)}, u32[]{:S(2)}) collective-permute-start(bf16[384,512]{1,0:T(8,128)(2,1)S(1)} %dynamic-slice_bitcast_fusion.1), channel_id=1, source_target_pairs={{0,4},{2,6},{4,8},{6,10},{8,12},{10,14},{12,0},{14,2},{1,5},{3,7},... | collective-permute-start | bytes 1179656 | tf_op jit(solution)/shard_map/ppermute | solution.py:478
  6.3 4.8 %copy-start.1 = (s32[1,2]{1,0:T(1,128)S(1)}, s32[1,2]{1,0:T(1,128)}, u32[]{:S(2)}) copy-start(s32[1,2]{1,0:T(1,128)} %lengths_ref.1) | copy-start | bytes 28
  6.3 19.1 %collective-permute-start.5 = (bf16[4,256,384]{2,1,0:T(8,128)(2,1)S(1)}, bf16[4,256,384]{2,1,0:T(8,128)(2,1)S(1)}, u32[]{:S(2)}, u32[]{:S(2)}) collective-permute-start(bf16[4,256,384]{2,1,0:T(8,128)(2,1)S(1)} %get-tuple-element.105), channel_id=1, source_target_pairs={{0,16},{16,0},{1,17},{17,1},{2,18},{18,2},{3,19},{19,3},{4,20},{20... | collective-permute-start | bytes 2359304 | tf_op jit(solution)/shard_map/ppermute | solution.py:490
  7.9 4.3 %collective-permute-start.1 = (f32[256,128]{1,0:T(8,128)S(1)}, f32[256,128]{1,0:T(8,128)S(1)}, u32[]{:S(2)}, u32[]{:S(2)}) collective-permute-start(f32[256,128]{1,0:T(8,128)S(1)} %get-tuple-element.91._.own_ref), channel_id=1, source_target_pairs={{0,1},{1,0},{2,3},{3,2},{4,5},{5,4},{6,7},{7,6},{8,9},{9,8},{10,11... | collective-permute-start | bytes 393224 | tf_op jit(solution)/shard_map/ppermute | solution.py:475
  7.9 20.3 %collective-permute-start.4 = (bf16[4,256,384]{2,1,0:T(8,128)(2,1)S(1)}, bf16[4,256,384]{2,1,0:T(8,128)(2,1)S(1)}, u32[]{:S(2)}, u32[]{:S(2)}) collective-permute-start(bf16[4,256,384]{2,1,0:T(8,128)(2,1)S(1)} %get-tuple-element.104), channel_id=1, source_target_pairs={{0,2},{2,0},{4,6},{6,4},{8,10},{10,8},{12,14},{14,12},{1,3},{3,1},... | collective-permute-start | bytes 2359304 | tf_op jit(solution)/shard_map/ppermute | solution.py:487
  9.5 15.1 %collective-permute-start.3 = (bf16[384,512]{1,0:T(8,128)(2,1)S(1)}, bf16[384,512]{1,0:T(8,128)(2,1)S(1)}, u32[]{:S(2)}, u32[]{:S(2)}) collective-permute-start(bf16[384,512]{1,0:T(8,128)(2,1)S(1)} %shard_map.47.refs_3_.refs_1_), channel_id=1, source_target_pairs={{0,4},{2,6},{4,8},{6,10},{8,12},{10,14},{12,0},{14,2},{1,5},{3,7},... | collective-permute-start | bytes 1179656 | tf_op jit(solution)/shard_map/ppermute | solution.py:478
  16.1 28.6 %collective-permute-start.2 = (bf16[4,256,384]{2,1,0:T(8,128)(2,1)S(1)}, bf16[4,256,384]{2,1,0:T(8,128)(2,1)S(1)}, u32[]{:S(2)}, u32[]{:S(2)}) collective-permute-start(bf16[4,256,384]{2,1,0:T(8,128)(2,1)S(1)} %get-tuple-element.99), channel_id=1, source_target_pairs={{0,18},{2,16},{4,22},{6,20},{8,26},{10,24},{12,30},{14,28},{16,2},... | collective-permute-start | bytes 2359304 | tf_op jit(solution)/shard_map/ppermute | solution.py:484
  18.8 14.2 %collective-permute-start.7 = (bf16[384,512]{1,0:T(8,128)(2,1)S(1)}, bf16[384,512]{1,0:T(8,128)(2,1)S(1)}, u32[]{:S(2)}, u32[]{:S(2)}) collective-permute-start(bf16[384,512]{1,0:T(8,128)(2,1)S(1)} %shard_map.47.refs_3_.refs_1_), channel_id=1, source_target_pairs={{4,0},{6,2},{8,4},{10,6},{12,8},{14,10},{0,12},{2,14},{5,1},{7,3},... | collective-permute-start | bytes 1179656 | tf_op jit(solution)/shard_map/ppermute | solution.py:481
  24.6 18.5 %collective-permute-start.6 = (bf16[384,512]{1,0:T(8,128)(2,1)S(1)}, bf16[384,512]{1,0:T(8,128)(2,1)S(1)}, u32[]{:S(2)}, u32[]{:S(2)}) collective-permute-start(bf16[384,512]{1,0:T(8,128)(2,1)S(1)} %collective-permute-done.3.refs_4_.refs_2_), channel_id=1, source_target_pairs={{0,4},{2,6},{4,8},{6,10},{8,12},{10,14},{12,0},{14,2},{1,5},{3,7},... | collective-permute-start | bytes 1179656 | tf_op jit(solution)/shard_map/ppermute | solution.py:478
  33.0 17.9 %collective-permute-start.9 = (bf16[384,512]{1,0:T(8,128)(2,1)S(1)}, bf16[384,512]{1,0:T(8,128)(2,1)S(1)}, u32[]{:S(2)}, u32[]{:S(2)}) collective-permute-start(bf16[384,512]{1,0:T(8,128)(2,1)S(1)} %collective-permute-done.refs_5_), channel_id=1, source_target_pairs={{0,4},{2,6},{4,8},{6,10},{8,12},{10,14},{12,0},{14,2},{1,5},{3,7},... | collective-permute-start | bytes 1179656 | tf_op jit(solution)/shard_map/ppermute | solution.py:478
  43.7 3.8 %collective-permute-start.10 = (bf16[3,256,128]{2,1,0:T(8,128)(2,1)S(1)}, bf16[3,256,128]{2,1,0:T(8,128)(2,1)S(1)}, u32[]{:S(2)}, u32[]{:S(2)}) collective-permute-start(bf16[3,256,128]{2,1,0:T(8,128)(2,1)S(1)} %get-tuple-element.116), channel_id=1, source_target_pairs={{0,1},{1,0},{2,3},{3,2},{4,5},{5,4},{6,7},{7,6},{8,9},{9,8},{10,11... | collective-permute-start | bytes 589832 | tf_op jit(solution)/shard_map/ppermute | solution.py:475
  43.8 3.7 %collective-permute-start.11 = (bf16[3,256,128]{2,1,0:T(8,128)(2,1)S(1)}, bf16[3,256,128]{2,1,0:T(8,128)(2,1)S(1)}, u32[]{:S(2)}, u32[]{:S(2)}) collective-permute-start(bf16[3,256,128]{2,1,0:T(8,128)(2,1)S(1)} %get-tuple-element.123), channel_id=1, source_target_pairs={{0,1},{1,0},{2,3},{3,2},{4,5},{5,4},{6,7},{7,6},{8,9},{9,8},{10,11... | collective-permute-start | bytes 589832 | tf_op jit(solution)/shard_map/ppermute | solution.py:475
  44.6 12.8 %collective-permute-start.8 = (bf16[384,512]{1,0:T(8,128)(2,1)S(1)}, bf16[384,512]{1,0:T(8,128)(2,1)S(1)}, u32[]{:S(2)}, u32[]{:S(2)}) collective-permute-start(bf16[384,512]{1,0:T(8,128)(2,1)S(1)} %dynamic-slice_bitcast_fusion.refs_4_), channel_id=1, source_target_pairs={{4,0},{6,2},{8,4},{10,6},{12,8},{14,10},{0,12},{2,14},{5,1},{7,3},... | collective-permute-start | bytes 1179656 | tf_op jit(solution)/shard_map/ppermute | solution.py:481
  47.6 3.4 %collective-permute-start.14 = (bf16[2,256,128]{2,1,0:T(8,128)(2,1)S(1)}, bf16[2,256,128]{2,1,0:T(8,128)(2,1)S(1)}, u32[]{:S(2)}, u32[]{:S(2)}) collective-permute-start(bf16[2,256,128]{2,1,0:T(8,128)(2,1)S(1)} %get-tuple-element.130), channel_id=1, source_target_pairs={{0,1},{1,0},{2,3},{3,2},{4,5},{5,4},{6,7},{7,6},{8,9},{9,8},{10,11... | collective-permute-start | bytes 393224 | tf_op jit(solution)/shard_map/ppermute | solution.py:475
  47.7 5.9 %collective-permute-start.13 = (bf16[2,256,128]{2,1,0:T(8,128)(2,1)S(1)}, bf16[2,256,128]{2,1,0:T(8,128)(2,1)S(1)}, u32[]{:S(2)}, u32[]{:S(2)}) collective-permute-start(bf16[2,256,128]{2,1,0:T(8,128)(2,1)S(1)} %get-tuple-element.132), channel_id=1, source_target_pairs={{0,16},{16,0},{1,17},{17,1},{2,18},{18,2},{3,19},{19,3},{4,20},{20... | collective-permute-start | bytes 393224 | tf_op jit(solution)/shard_map/ppermute | solution.py:490
  49.5 6.3 %collective-permute-start.12 = (bf16[2,256,128]{2,1,0:T(8,128)(2,1)S(1)}, bf16[2,256,128]{2,1,0:T(8,128)(2,1)S(1)}, u32[]{:S(2)}, u32[]{:S(2)}) collective-permute-start(bf16[2,256,128]{2,1,0:T(8,128)(2,1)S(1)} %get-tuple-element.129), channel_id=1, source_target_pairs={{0,2},{2,0},{4,6},{6,4},{8,10},{10,8},{12,14},{14,12},{1,3},{3,1},... | collective-permute-start | bytes 393224 | tf_op jit(solution)/shard_map/ppermute | solution.py:487
  51.0 6.8 %collective-permute-start.15 = (bf16[2,256,128]{2,1,0:T(8,128)(2,1)S(1)}, bf16[2,256,128]{2,1,0:T(8,128)(2,1)S(1)}, u32[]{:S(2)}, u32[]{:S(2)}) collective-permute-start(bf16[2,256,128]{2,1,0:T(8,128)(2,1)S(1)} %shard_map.55), channel_id=1, source_target_pairs={{0,18},{2,16},{4,22},{6,20},{8,26},{10,24},{12,30},{14,28},{16,2},... | collective-permute-start | bytes 393224 | tf_op jit(solution)/shard_map/ppermute | solution.py:484
  57.8 1.7 %collective-permute-start.16 = (bf16[4,256,128]{2,1,0:T(8,128)(2,1)S(1)}, bf16[4,256,128]{2,1,0:T(8,128)(2,1)S(1)}, u32[]{:S(2)}, u32[]{:S(2)}) collective-permute-start(bf16[4,256,128]{2,1,0:T(8,128)(2,1)S(1)} %shard_map.56), channel_id=1, source_target_pairs={{0,1},{1,0},{2,3},{3,2},{4,5},{5,4},{6,7},{7,6},{8,9},{9,8},{10,11... | collective-permute-start | bytes 786440 | tf_op jit(solution)/shard_map/ppermute | solution.py:475
  58.2 3.9 %collective-permute-start.19 = (bf16[4,256,128]{2,1,0:T(8,128)(2,1)S(1)}, bf16[4,256,128]{2,1,0:T(8,128)(2,1)S(1)}, u32[]{:S(2)}, u32[]{:S(2)}) collective-permute-start(bf16[4,256,128]{2,1,0:T(8,128)(2,1)S(1)} %shard_map.57), channel_id=1, source_target_pairs={{0,1},{1,0},{2,3},{3,2},{4,5},{5,4},{6,7},{7,6},{8,9},{9,8},{10,11... | collective-permute-start | bytes 786440 | tf_op jit(solution)/shard_map/ppermute | solution.py:475
  59.5 7.3 %collective-permute-start.17 = (bf16[2,256,128]{2,1,0:T(8,128)(2,1)S(1)}, bf16[2,256,128]{2,1,0:T(8,128)(2,1)S(1)}, u32[]{:S(2)}, u32[]{:S(2)}) collective-permute-start(bf16[2,256,128]{2,1,0:T(8,128)(2,1)S(1)} %get-tuple-element.156), channel_id=1, source_target_pairs={{0,18},{2,16},{4,22},{6,20},{8,26},{10,24},{12,30},{14,28},{16,2},... | collective-permute-start | bytes 393224 | tf_op jit(solution)/shard_map/ppermute | solution.py:484
  62.1 6.7 %collective-permute-start.20 = (bf16[2,256,128]{2,1,0:T(8,128)(2,1)S(1)}, bf16[2,256,128]{2,1,0:T(8,128)(2,1)S(1)}, u32[]{:S(2)}, u32[]{:S(2)}) collective-permute-start(bf16[2,256,128]{2,1,0:T(8,128)(2,1)S(1)} %get-tuple-element.162), channel_id=1, source_target_pairs={{0,2},{2,0},{4,6},{6,4},{8,10},{10,8},{12,14},{14,12},{1,3},{3,1},... | collective-permute-start | bytes 393224 | tf_op jit(solution)/shard_map/ppermute | solution.py:487
  62.7 6.1 %collective-permute-start.21 = (bf16[2,256,128]{2,1,0:T(8,128)(2,1)S(1)}, bf16[2,256,128]{2,1,0:T(8,128)(2,1)S(1)}, u32[]{:S(2)}, u32[]{:S(2)}) collective-permute-start(bf16[2,256,128]{2,1,0:T(8,128)(2,1)S(1)} %get-tuple-element.166), channel_id=1, source_target_pairs={{0,16},{16,0},{1,17},{17,1},{2,18},{18,2},{3,19},{19,3},{4,20},{20... | collective-permute-start | bytes 393224 | tf_op jit(solution)/shard_map/ppermute | solution.py:490
  63.2 1.3 %collective-permute-start.18 = (bf16[256,128]{1,0:T(8,128)(2,1)S(1)}, bf16[256,128]{1,0:T(8,128)(2,1)S(1)}, u32[]{:S(2)}, u32[]{:S(2)}) collective-permute-start(bf16[256,128]{1,0:T(8,128)(2,1)S(1)} %shard_map.59.refs_9_), channel_id=1, source_target_pairs={{0,1},{1,0},{2,3},{3,2},{4,5},{5,4},{6,7},{7,6},{8,9},{9,8},{10,11... | collective-permute-start | bytes 196616 | tf_op jit(solution)/shard_map/ppermute | solution.py:475

commit v12 on v11

--- a/solution.py
+++ b/solution.py
@@ -562,6 +562,8 @@
     for skip in (0, 2):
         total, = half_matmul(acts[skip:skip + 2], after(b3), 3, front, False, 1, jnp.float32, skip)
         mine.append(total.reshape(2, -1, *total.shape[1:]))
+    sums_far, sums = after(*join(mine[0], (after(swapped[0]),), (jnp.bfloat16, jnp.float32)))
+    sums_far = to_far(sums_far)
     kv = after(call(
         kv_kernel,
         jax.ShapeDtypeStruct((tokens, HEAD), jnp.bfloat16),
@@ -569,8 +571,6 @@
         out_specs=WHOLE,
     )(*parts_a, scale, *tabled[:2]))
     vk = to_core(kv)
-    sums_far, sums = after(*join(mine[0], (after(swapped[0]),), (jnp.bfloat16, jnp.float32)))
-    sums_far = to_far(sums_far)
     sums_x, sums_y = after(*join(mine[1], (after(swapped[1]),), (jnp.bfloat16, jnp.bfloat16)))
     sums_x = to_x(sums_x)
     sums_y = to_y(sums_y)

time: 70.3 us -> 70.3 us (level)
  no operation moved by 1% of the time
where the time goes in v12:
time: 70.3 us; the launch traced here: 70.2 us
  waiting for transfers between devices  33.8 us (48%)
  starting transfers between devices  23.8 us (34%)
  Pallas kernels  11.3 us (16%)
  local copies, waits for them, and re-layouts  1.06 us (2%)
    ppermute x4, waiting for transfers between devices, on_ring(): return lax.ppermute(a, 'dp', ring)  16.1 us
    ppermute x3, waiting for transfers between devices, to_x(): return lax.ppermute(a, 'dp', over_x)  7.03 us
    ppermute x2, waiting for transfers between devices, back(): return lax.ppermute(a, 'dp', [(j, i) for i, j in ring])  6.47 us
    ppermute x3, starting transfers between devices, to_far(): return lax.ppermute(a, ('groups', 'dp'), across)  5.99 us
    ppermute x4, starting transfers between devices, on_ring(): return lax.ppermute(a, 'dp', ring)  5.1 us
    pallas_call x4, Pallas kernels, matmul(): call(functools.partial(matmul_kernel, firsts, len(acts), len(so_far), sen...  4.41 us
    ppermute x2, starting transfers between devices, back(): return lax.ppermute(a, 'dp', [(j, i) for i, j in ring])  3.94 us
    ppermute x3, starting transfers between devices, to_y(): return lax.ppermute(a, 'groups', over_y)  3.88 us
  transfers between devices with their start and end apart: 22, of which 12 were waited for; matrix products, arithmetic and copies ran while one was open for 0% of the time, Pallas kernels for 14%

profile of v12, /device:TPU:0, one launch (start us, length us, event | category | flops | bytes accessed | tf_op | source)
XLA Modules:
  0.0 70.2 jit_solution(2128892597270542803)
XLA Ops:
  0.0 1.0 %dynamic-slice_bitcast_fusion.1 = bf16[384,512]{1,0:T(8,128)(2,1)S(1)} fusion(bf16[1,768,1024]{2,1,0:T(8,128)(2,1)} %rows_ref, s32[]{:T(128)S(6)} %select_n.4), kind=kLoop, calls=%fused_computation.1 | loop fusion | bytes 786436 | tf_op jit(solution)/shard_map/dynamic_slice | solution.py:507
  1.0 3.1 %collective-permute-start = (bf16[384,512]{1,0:T(8,128)(2,1)S(1)}, bf16[384,512]{1,0:T(8,128)(2,1)S(1)}, u32[]{:S(2)}, u32[]{:S(2)}) collective-permute-start(bf16[384,512]{1,0:T(8,128)(2,1)S(1)} %dynamic-slice_bitcast_fusion.1), channel_id=1, source_target_pairs={{0,4},{2,6},{4,8},{6,10},{8,12},{10,14},{12,0},{14,2},{1,5},{3,7},... | collective-permute-start | bytes 1179656 | tf_op jit(solution)/shard_map/ppermute | solution.py:478
  4.1 2.2 %shard_map.46 = (bf16[4,256,384]{2,1,0:T(8,128)(2,1)S(1)}, bf16[4,256,384]{2,1,0:T(8,128)(2,1)S(1)}, bf16[4,256,384]{2,1,0:T(8,128)(2,1)S(1)}, bf16[4,256,384]{2,1,0:T(8,128)(2,1)S(1)}, f32[256,128]{1,0:T(8,128)S(1)}) custom-call(bf16[256,6144]{1,0:T(8,128)(2,1)} %hidden_ref.1, bf16[6144]{0:T(1024)(128)(2,1)} %gain_ref.1), custom_call_target="tpu_custom_call" | custom-call | flops 1 | bytes 1 | tf_op jit(solution)/shard_map/pallas_call | solution.py:231
  6.3 1.6 %collective-permute-start.5 = (bf16[4,256,384]{2,1,0:T(8,128)(2,1)S(1)}, bf16[4,256,384]{2,1,0:T(8,128)(2,1)S(1)}, u32[]{:S(2)}, u32[]{:S(2)}) collective-permute-start(bf16[4,256,384]{2,1,0:T(8,128)(2,1)S(1)} %get-tuple-element.105), channel_id=1, source_target_pairs={{0,16},{16,0},{1,17},{17,1},{2,18},{18,2},{3,19},{19,3},{4,20},{20... | collective-permute-start | bytes 2359304 | tf_op jit(solution)/shard_map/ppermute | solution.py:490
  7.9 1.5 %collective-permute-start.4 = (bf16[4,256,384]{2,1,0:T(8,128)(2,1)S(1)}, bf16[4,256,384]{2,1,0:T(8,128)(2,1)S(1)}, u32[]{:S(2)}, u32[]{:S(2)}) collective-permute-start(bf16[4,256,384]{2,1,0:T(8,128)(2,1)S(1)} %get-tuple-element.104), channel_id=1, source_target_pairs={{0,2},{2,0},{4,6},{6,4},{8,10},{10,8},{12,14},{14,12},{1,3},{3,1},... | collective-permute-start | bytes 2359304 | tf_op jit(solution)/shard_map/ppermute | solution.py:487
  9.5 1.6 %collective-permute-start.3 = (bf16[384,512]{1,0:T(8,128)(2,1)S(1)}, bf16[384,512]{1,0:T(8,128)(2,1)S(1)}, u32[]{:S(2)}, u32[]{:S(2)}) collective-permute-start(bf16[384,512]{1,0:T(8,128)(2,1)S(1)} %shard_map.47.refs_3_.refs_1_), channel_id=1, source_target_pairs={{0,4},{2,6},{4,8},{6,10},{8,12},{10,14},{12,0},{14,2},{1,5},{3,7},... | collective-permute-start | bytes 1179656 | tf_op jit(solution)/shard_map/ppermute | solution.py:478
  11.1 1.1 %shard_map.48 = (f32[256,128]{1,0:T(8,128)S(1)}, f32[256,128]{1,0:T(8,128)S(1)}, f32[256,256]{1,0:T(8,128)S(1)}, f32[256,128]{1,0:T(8,128)S(1)}) custom-call(s32[1,2]{1,0:T(1,128)S(1)} %copy-done.1, f32[256,128]{1,0:T(8,128)S(1)} %get-tuple-element.91._.own_ref), custom_call_target="tpu_custom_call" | custom-call | flops 1 | bytes 1 | tf_op jit(solution)/shard_map/pallas_call | solution.py:359
  12.3 3.7 %collective-permute-done.refs_5_ = bf16[384,512]{1,0:T(8,128)(2,1)S(1)} collective-permute-done((bf16[384,512]{1,0:T(8,128)(2,1)S(1)}, bf16[384,512]{1,0:T(8,128)(2,1)S(1)}, u32[]{:S(2)}, u32[]{:S(2)}) %collective-permute-start) | collective-permute-done | bytes 393248 | tf_op jit(solution)/shard_map/ppermute | solution.py:478
  16.1 2.7 %collective-permute-start.2 = (bf16[4,256,384]{2,1,0:T(8,128)(2,1)S(1)}, bf16[4,256,384]{2,1,0:T(8,128)(2,1)S(1)}, u32[]{:S(2)}, u32[]{:S(2)}) collective-permute-start(bf16[4,256,384]{2,1,0:T(8,128)(2,1)S(1)} %get-tuple-element.99), channel_id=1, source_target_pairs={{0,18},{2,16},{4,22},{6,20},{8,26},{10,24},{12,30},{14,28},{16,2},... | collective-permute-start | bytes 2359304 | tf_op jit(solution)/shard_map/ppermute | solution.py:484
  18.8 1.8 %collective-permute-start.7 = (bf16[384,512]{1,0:T(8,128)(2,1)S(1)}, bf16[384,512]{1,0:T(8,128)(2,1)S(1)}, u32[]{:S(2)}, u32[]{:S(2)}) collective-permute-start(bf16[384,512]{1,0:T(8,128)(2,1)S(1)} %shard_map.47.refs_3_.refs_1_), channel_id=1, source_target_pairs={{4,0},{6,2},{8,4},{10,6},{12,8},{14,10},{0,12},{2,14},{5,1},{7,3},... | collective-permute-start | bytes 1179656 | tf_op jit(solution)/shard_map/ppermute | solution.py:481
  20.6 4.0 %collective-permute-done.3.refs_4_.refs_2_ = bf16[384,512]{1,0:T(8,128)(2,1)S(1)} collective-permute-done((bf16[384,512]{1,0:T(8,128)(2,1)S(1)}, bf16[384,512]{1,0:T(8,128)(2,1)S(1)}, u32[]{:S(2)}, u32[]{:S(2)}) %collective-permute-start.3) | collective-permute-done | bytes 393248 | tf_op jit(solution)/shard_map/ppermute | solution.py:478
  24.6 0.7 %collective-permute-done.5.refs_1_.refs_3_ = bf16[4,256,384]{2,1,0:T(8,128)(2,1)S(1)} collective-permute-done((bf16[4,256,384]{2,1,0:T(8,128)(2,1)S(1)}, bf16[4,256,384]{2,1,0:T(8,128)(2,1)S(1)}, u32[]{:S(2)}, u32[]{:S(2)}) %collective-permute-start.5) | collective-permute-done | bytes 786464 | tf_op jit(solution)/shard_map/ppermute | solution.py:490
  25.4 2.8 %collective-permute-done.4.refs_0_.refs_2_ = bf16[4,256,384]{2,1,0:T(8,128)(2,1)S(1)} collective-permute-done((bf16[4,256,384]{2,1,0:T(8,128)(2,1)S(1)}, bf16[4,256,384]{2,1,0:T(8,128)(2,1)S(1)}, u32[]{:S(2)}, u32[]{:S(2)}) %collective-permute-start.4) | collective-permute-done | bytes 786464 | tf_op jit(solution)/shard_map/ppermute | solution.py:487
  28.2 4.8 %collective-permute-done.7.refs_5_.refs_4_ = bf16[384,512]{1,0:T(8,128)(2,1)S(1)} collective-permute-done((bf16[384,512]{1,0:T(8,128)(2,1)S(1)}, bf16[384,512]{1,0:T(8,128)(2,1)S(1)}, u32[]{:S(2)}, u32[]{:S(2)}) %collective-permute-start.7) | collective-permute-done | bytes 393248 | tf_op jit(solution)/shard_map/ppermute | solution.py:481
  33.4 1.4 %shard_map.50.refs_4_ = f32[3,256,512]{2,1,0:T(8,128)S(1)} custom-call(bf16[4,256,384]{2,1,0:T(8,128)(2,1)S(1)} %collective-permute-done.4.refs_0_.refs_2_, bf16[4,256,384]{2,1,0:T(8,128)(2,1)S(1)} %collective-permute-done.5.refs_1_.refs_3_, bf16[4,256,384]{2,1,0:T(8,128)(2,1)S(1)} %get-tuple-element.108.refs_2_.refs_1_, ...), custom_call_target="tpu_custom_call" | custom-call | flops 1 | bytes 1 | tf_op jit(solution)/shard_map/pallas_call | solution.py:284
  34.8 8.3 %collective-permute-done.6.refs_3_ = bf16[384,512]{1,0:T(8,128)(2,1)S(1)} collective-permute-done((bf16[384,512]{1,0:T(8,128)(2,1)S(1)}, bf16[384,512]{1,0:T(8,128)(2,1)S(1)}, u32[]{:S(2)}, u32[]{:S(2)}) %collective-permute-start.6) | collective-permute-done | bytes 393248 | tf_op jit(solution)/shard_map/ppermute | solution.py:478
  43.1 0.6 shard_map.51
  44.6 2.1 %collective-permute-start.8 = (bf16[384,512]{1,0:T(8,128)(2,1)S(1)}, bf16[384,512]{1,0:T(8,128)(2,1)S(1)}, u32[]{:S(2)}, u32[]{:S(2)}) collective-permute-start(bf16[384,512]{1,0:T(8,128)(2,1)S(1)} %dynamic-slice_bitcast_fusion.refs_4_), channel_id=1, source_target_pairs={{4,0},{6,2},{8,4},{10,6},{12,8},{14,10},{0,12},{2,14},{5,1},{7,3},... | collective-permute-start | bytes 1179656 | tf_op jit(solution)/shard_map/ppermute | solution.py:481
  46.8 0.7 shard_map.52
  47.7 1.8 %collective-permute-start.13 = (bf16[2,256,128]{2,1,0:T(8,128)(2,1)S(1)}, bf16[2,256,128]{2,1,0:T(8,128)(2,1)S(1)}, u32[]{:S(2)}, u32[]{:S(2)}) collective-permute-start(bf16[2,256,128]{2,1,0:T(8,128)(2,1)S(1)} %get-tuple-element.132), channel_id=1, source_target_pairs={{0,16},{16,0},{1,17},{17,1},{2,18},{18,2},{3,19},{19,3},{4,20},{20... | collective-permute-start | bytes 393224 | tf_op jit(solution)/shard_map/ppermute | solution.py:490
  49.5 1.5 %collective-permute-start.12 = (bf16[2,256,128]{2,1,0:T(8,128)(2,1)S(1)}, bf16[2,256,128]{2,1,0:T(8,128)(2,1)S(1)}, u32[]{:S(2)}, u32[]{:S(2)}) collective-permute-start(bf16[2,256,128]{2,1,0:T(8,128)(2,1)S(1)} %get-tuple-element.129), channel_id=1, source_target_pairs={{0,2},{2,0},{4,6},{6,4},{8,10},{10,8},{12,14},{14,12},{1,3},{3,1},... | collective-permute-start | bytes 393224 | tf_op jit(solution)/shard_map/ppermute | solution.py:487
  51.0 0.8 %collective-permute-start.15 = (bf16[2,256,128]{2,1,0:T(8,128)(2,1)S(1)}, bf16[2,256,128]{2,1,0:T(8,128)(2,1)S(1)}, u32[]{:S(2)}, u32[]{:S(2)}) collective-permute-start(bf16[2,256,128]{2,1,0:T(8,128)(2,1)S(1)} %shard_map.55), channel_id=1, source_target_pairs={{0,18},{2,16},{4,22},{6,20},{8,26},{10,24},{12,30},{14,28},{16,2},... | collective-permute-start | bytes 393224 | tf_op jit(solution)/shard_map/ppermute | solution.py:484
  51.8 1.8 %shard_map.54.refs_3_ = f32[4,256,512]{2,1,0:T(8,128)S(1)} custom-call(bf16[4,256,384]{2,1,0:T(8,128)(2,1)S(1)} %collective-permute-done.2.refs_0_, bf16[4,256,384]{2,1,0:T(8,128)(2,1)S(1)} %get-tuple-element.108.refs_2_.refs_1_, bf16[4,256,384]{2,1,0:T(8,128)(2,1)S(1)} %collective-permute-done.4.refs_0_.refs_2_, ...), custom_call_target="tpu_custom_call" | custom-call | flops 1 | bytes 1 | tf_op jit(solution)/shard_map/pallas_call | solution.py:284
  53.6 2.2 %collective-permute-done.12.r1.refs_2_ = bf16[2,256,128]{2,1,0:T(8,128)(2,1)S(1)} collective-permute-done((bf16[2,256,128]{2,1,0:T(8,128)(2,1)S(1)}, bf16[2,256,128]{2,1,0:T(8,128)(2,1)S(1)}, u32[]{:S(2)}, u32[]{:S(2)}) %collective-permute-start.12) | collective-permute-done | bytes 131104 | tf_op jit(solution)/shard_map/ppermute | solution.py:487
  55.8 1.7 %collective-permute-done.8.refs_2_ = bf16[384,512]{1,0:T(8,128)(2,1)S(1)} collective-permute-done((bf16[384,512]{1,0:T(8,128)(2,1)S(1)}, bf16[384,512]{1,0:T(8,128)(2,1)S(1)}, u32[]{:S(2)}, u32[]{:S(2)}) %collective-permute-start.8) | collective-permute-done | bytes 393248 | tf_op jit(solution)/shard_map/ppermute | solution.py:481
  59.5 2.5 %collective-permute-start.17 = (bf16[2,256,128]{2,1,0:T(8,128)(2,1)S(1)}, bf16[2,256,128]{2,1,0:T(8,128)(2,1)S(1)}, u32[]{:S(2)}, u32[]{:S(2)}) collective-permute-start(bf16[2,256,128]{2,1,0:T(8,128)(2,1)S(1)} %get-tuple-element.151), channel_id=1, source_target_pairs={{0,18},{2,16},{4,22},{6,20},{8,26},{10,24},{12,30},{14,28},{16,2},... | collective-permute-start | bytes 393224 | tf_op jit(solution)/shard_map/ppermute | solution.py:484
  62.1 0.6 collective-permute-start.20
  63.2 1.3 %collective-permute-done.18.refs_10_ = bf16[256,128]{1,0:T(8,128)(2,1)S(1)} collective-permute-done((bf16[256,128]{1,0:T(8,128)(2,1)S(1)}, bf16[256,128]{1,0:T(8,128)(2,1)S(1)}, u32[]{:S(2)}, u32[]{:S(2)}) %collective-permute-start.18) | collective-permute-done | bytes 65568 | tf_op jit(solution)/shard_map/ppermute | solution.py:475
  64.5 0.6 shard_map.63.refs_11_
  65.1 1.8 %collective-permute-done.17.refs_1_ = bf16[2,256,128]{2,1,0:T(8,128)(2,1)S(1)} collective-permute-done((bf16[2,256,128]{2,1,0:T(8,128)(2,1)S(1)}, bf16[2,256,128]{2,1,0:T(8,128)(2,1)S(1)}, u32[]{:S(2)}, u32[]{:S(2)}) %collective-permute-start.17) | collective-permute-done | bytes 131104 | tf_op jit(solution)/shard_map/ppermute | solution.py:484
  66.9 2.0 %collective-permute-done.20.refs_2_ = bf16[2,256,128]{2,1,0:T(8,128)(2,1)S(1)} collective-permute-done((bf16[2,256,128]{2,1,0:T(8,128)(2,1)S(1)}, bf16[2,256,128]{2,1,0:T(8,128)(2,1)S(1)}, u32[]{:S(2)}, u32[]{:S(2)}) %collective-permute-start.20) | collective-permute-done | bytes 131104 | tf_op jit(solution)/shard_map/ppermute | solution.py:487
  68.8 1.4 %shard_map.64 = bf16[256,384]{1,0:T(8,128)(2,1)} custom-call(f32[2,256,128]{2,1,0:T(8,128)S(1)} %get-tuple-element.150.refs_0_, bf16[2,256,128]{2,1,0:T(8,128)(2,1)S(1)} %collective-permute-done.17.refs_1_, bf16[2,256,128]{2,1,0:T(8,128)(2,1)S(1)} %collective-permute-done.20.refs_2_, bf16[2,256,128]{2,1,0:T(8,128)(2,1)S(1)} %collective-permute-done.21.refs_3_, ...), custom_call_target="tpu_custom_call" | custom-call | flops 1 | bytes 1 | tf_op jit(solution)/shard_map/pallas_call | solution.py:449
  (37 shorter events, 4.4 us)
Async XLA Ops:
  1.0 8.4 %copy-start = (bf16[1,768,1024]{2,1,0:T(8,128)(2,1)S(1)}, bf16[1,768,1024]{2,1,0:T(8,128)(2,1)}, u32[]{:S(2)}) copy-start(bf16[1,768,1024]{2,1,0:T(8,128)(2,1)} %rows_ref) | copy-start | bytes 4718596
  1.0 15.0 %collective-permute-start = (bf16[384,512]{1,0:T(8,128)(2,1)S(1)}, bf16[384,512]{1,0:T(8,128)(2,1)S(1)}, u32[]{:S(2)}, u32[]{:S(2)}) collective-permute-start(bf16[384,512]{1,0:T(8,128)(2,1)S(1)} %dynamic-slice_bitcast_fusion.1), channel_id=1, source_target_pairs={{0,4},{2,6},{4,8},{6,10},{8,12},{10,14},{12,0},{14,2},{1,5},{3,7},... | collective-permute-start | bytes 1179656 | tf_op jit(solution)/shard_map/ppermute | solution.py:478
  6.3 4.8 %copy-start.1 = (s32[1,2]{1,0:T(1,128)S(1)}, s32[1,2]{1,0:T(1,128)}, u32[]{:S(2)}) copy-start(s32[1,2]{1,0:T(1,128)} %lengths_ref.1) | copy-start | bytes 28
  6.3 19.1 %collective-permute-start.5 = (bf16[4,256,384]{2,1,0:T(8,128)(2,1)S(1)}, bf16[4,256,384]{2,1,0:T(8,128)(2,1)S(1)}, u32[]{:S(2)}, u32[]{:S(2)}) collective-permute-start(bf16[4,256,384]{2,1,0:T(8,128)(2,1)S(1)} %get-tuple-element.105), channel_id=1, source_target_pairs={{0,16},{16,0},{1,17},{17,1},{2,18},{18,2},{3,19},{19,3},{4,20},{20... | collective-permute-start | bytes 2359304 | tf_op jit(solution)/shard_map/ppermute | solution.py:490
  7.9 4.3 %collective-permute-start.1 = (f32[256,128]{1,0:T(8,128)S(1)}, f32[256,128]{1,0:T(8,128)S(1)}, u32[]{:S(2)}, u32[]{:S(2)}) collective-permute-start(f32[256,128]{1,0:T(8,128)S(1)} %get-tuple-element.91._.own_ref), channel_id=1, source_target_pairs={{0,1},{1,0},{2,3},{3,2},{4,5},{5,4},{6,7},{7,6},{8,9},{9,8},{10,11... | collective-permute-start | bytes 393224 | tf_op jit(solution)/shard_map/ppermute | solution.py:475
  7.9 20.3 %collective-permute-start.4 = (bf16[4,256,384]{2,1,0:T(8,128)(2,1)S(1)}, bf16[4,256,384]{2,1,0:T(8,128)(2,1)S(1)}, u32[]{:S(2)}, u32[]{:S(2)}) collective-permute-start(bf16[4,256,384]{2,1,0:T(8,128)(2,1)S(1)} %get-tuple-element.104), channel_id=1, source_target_pairs={{0,2},{2,0},{4,6},{6,4},{8,10},{10,8},{12,14},{14,12},{1,3},{3,1},... | collective-permute-start | bytes 2359304 | tf_op jit(solution)/shard_map/ppermute | solution.py:487
  9.5 15.1 %collective-permute-start.3 = (bf16[384,512]{1,0:T(8,128)(2,1)S(1)}, bf16[384,512]{1,0:T(8,128)(2,1)S(1)}, u32[]{:S(2)}, u32[]{:S(2)}) collective-permute-start(bf16[384,512]{1,0:T(8,128)(2,1)S(1)} %shard_map.47.refs_3_.refs_1_), channel_id=1, source_target_pairs={{0,4},{2,6},{4,8},{6,10},{8,12},{10,14},{12,0},{14,2},{1,5},{3,7},... | collective-permute-start | bytes 1179656 | tf_op jit(solution)/shard_map/ppermute | solution.py:478
  16.1 28.6 %collective-permute-start.2 = (bf16[4,256,384]{2,1,0:T(8,128)(2,1)S(1)}, bf16[4,256,384]{2,1,0:T(8,128)(2,1)S(1)}, u32[]{:S(2)}, u32[]{:S(2)}) collective-permute-start(bf16[4,256,384]{2,1,0:T(8,128)(2,1)S(1)} %get-tuple-element.99), channel_id=1, source_target_pairs={{0,18},{2,16},{4,22},{6,20},{8,26},{10,24},{12,30},{14,28},{16,2},... | collective-permute-start | bytes 2359304 | tf_op jit(solution)/shard_map/ppermute | solution.py:484
  18.8 14.2 %collective-permute-start.7 = (bf16[384,512]{1,0:T(8,128)(2,1)S(1)}, bf16[384,512]{1,0:T(8,128)(2,1)S(1)}, u32[]{:S(2)}, u32[]{:S(2)}) collective-permute-start(bf16[384,512]{1,0:T(8,128)(2,1)S(1)} %shard_map.47.refs_3_.refs_1_), channel_id=1, source_target_pairs={{4,0},{6,2},{8,4},{10,6},{12,8},{14,10},{0,12},{2,14},{5,1},{7,3},... | collective-permute-start | bytes 1179656 | tf_op jit(solution)/shard_map/ppermute | solution.py:481
  24.6 18.5 %collective-permute-start.6 = (bf16[384,512]{1,0:T(8,128)(2,1)S(1)}, bf16[384,512]{1,0:T(8,128)(2,1)S(1)}, u32[]{:S(2)}, u32[]{:S(2)}) collective-permute-start(bf16[384,512]{1,0:T(8,128)(2,1)S(1)} %collective-permute-done.3.refs_4_.refs_2_), channel_id=1, source_target_pairs={{0,4},{2,6},{4,8},{6,10},{8,12},{10,14},{12,0},{14,2},{1,5},{3,7},... | collective-permute-start | bytes 1179656 | tf_op jit(solution)/shard_map/ppermute | solution.py:478
  33.0 17.9 %collective-permute-start.9 = (bf16[384,512]{1,0:T(8,128)(2,1)S(1)}, bf16[384,512]{1,0:T(8,128)(2,1)S(1)}, u32[]{:S(2)}, u32[]{:S(2)}) collective-permute-start(bf16[384,512]{1,0:T(8,128)(2,1)S(1)} %collective-permute-done.refs_5_), channel_id=1, source_target_pairs={{0,4},{2,6},{4,8},{6,10},{8,12},{10,14},{12,0},{14,2},{1,5},{3,7},... | collective-permute-start | bytes 1179656 | tf_op jit(solution)/shard_map/ppermute | solution.py:478
  43.7 3.8 %collective-permute-start.10 = (bf16[3,256,128]{2,1,0:T(8,128)(2,1)S(1)}, bf16[3,256,128]{2,1,0:T(8,128)(2,1)S(1)}, u32[]{:S(2)}, u32[]{:S(2)}) collective-permute-start(bf16[3,256,128]{2,1,0:T(8,128)(2,1)S(1)} %get-tuple-element.116), channel_id=1, source_target_pairs={{0,1},{1,0},{2,3},{3,2},{4,5},{5,4},{6,7},{7,6},{8,9},{9,8},{10,11... | collective-permute-start | bytes 589832 | tf_op jit(solution)/shard_map/ppermute | solution.py:475
  43.8 3.7 %collective-permute-start.11 = (bf16[3,256,128]{2,1,0:T(8,128)(2,1)S(1)}, bf16[3,256,128]{2,1,0:T(8,128)(2,1)S(1)}, u32[]{:S(2)}, u32[]{:S(2)}) collective-permute-start(bf16[3,256,128]{2,1,0:T(8,128)(2,1)S(1)} %get-tuple-element.123), channel_id=1, source_target_pairs={{0,1},{1,0},{2,3},{3,2},{4,5},{5,4},{6,7},{7,6},{8,9},{9,8},{10,11... | collective-permute-start | bytes 589832 | tf_op jit(solution)/shard_map/ppermute | solution.py:475
  44.6 12.8 %collective-permute-start.8 = (bf16[384,512]{1,0:T(8,128)(2,1)S(1)}, bf16[384,512]{1,0:T(8,128)(2,1)S(1)}, u32[]{:S(2)}, u32[]{:S(2)}) collective-permute-start(bf16[384,512]{1,0:T(8,128)(2,1)S(1)} %dynamic-slice_bitcast_fusion.refs_4_), channel_id=1, source_target_pairs={{4,0},{6,2},{8,4},{10,6},{12,8},{14,10},{0,12},{2,14},{5,1},{7,3},... | collective-permute-start | bytes 1179656 | tf_op jit(solution)/shard_map/ppermute | solution.py:481
  47.6 3.4 %collective-permute-start.14 = (bf16[2,256,128]{2,1,0:T(8,128)(2,1)S(1)}, bf16[2,256,128]{2,1,0:T(8,128)(2,1)S(1)}, u32[]{:S(2)}, u32[]{:S(2)}) collective-permute-start(bf16[2,256,128]{2,1,0:T(8,128)(2,1)S(1)} %get-tuple-element.130), channel_id=1, source_target_pairs={{0,1},{1,0},{2,3},{3,2},{4,5},{5,4},{6,7},{7,6},{8,9},{9,8},{10,11... | collective-permute-start | bytes 393224 | tf_op jit(solution)/shard_map/ppermute | solution.py:475
  47.7 5.9 %collective-permute-start.13 = (bf16[2,256,128]{2,1,0:T(8,128)(2,1)S(1)}, bf16[2,256,128]{2,1,0:T(8,128)(2,1)S(1)}, u32[]{:S(2)}, u32[]{:S(2)}) collective-permute-start(bf16[2,256,128]{2,1,0:T(8,128)(2,1)S(1)} %get-tuple-element.132), channel_id=1, source_target_pairs={{0,16},{16,0},{1,17},{17,1},{2,18},{18,2},{3,19},{19,3},{4,20},{20... | collective-permute-start | bytes 393224 | tf_op jit(solution)/shard_map/ppermute | solution.py:490
  49.5 6.3 %collective-permute-start.12 = (bf16[2,256,128]{2,1,0:T(8,128)(2,1)S(1)}, bf16[2,256,128]{2,1,0:T(8,128)(2,1)S(1)}, u32[]{:S(2)}, u32[]{:S(2)}) collective-permute-start(bf16[2,256,128]{2,1,0:T(8,128)(2,1)S(1)} %get-tuple-element.129), channel_id=1, source_target_pairs={{0,2},{2,0},{4,6},{6,4},{8,10},{10,8},{12,14},{14,12},{1,3},{3,1},... | collective-permute-start | bytes 393224 | tf_op jit(solution)/shard_map/ppermute | solution.py:487
  51.0 6.8 %collective-permute-start.15 = (bf16[2,256,128]{2,1,0:T(8,128)(2,1)S(1)}, bf16[2,256,128]{2,1,0:T(8,128)(2,1)S(1)}, u32[]{:S(2)}, u32[]{:S(2)}) collective-permute-start(bf16[2,256,128]{2,1,0:T(8,128)(2,1)S(1)} %shard_map.55), channel_id=1, source_target_pairs={{0,18},{2,16},{4,22},{6,20},{8,26},{10,24},{12,30},{14,28},{16,2},... | collective-permute-start | bytes 393224 | tf_op jit(solution)/shard_map/ppermute | solution.py:484
  57.8 1.7 %collective-permute-start.16 = (bf16[4,256,128]{2,1,0:T(8,128)(2,1)S(1)}, bf16[4,256,128]{2,1,0:T(8,128)(2,1)S(1)}, u32[]{:S(2)}, u32[]{:S(2)}) collective-permute-start(bf16[4,256,128]{2,1,0:T(8,128)(2,1)S(1)} %shard_map.56), channel_id=1, source_target_pairs={{0,1},{1,0},{2,3},{3,2},{4,5},{5,4},{6,7},{7,6},{8,9},{9,8},{10,11... | collective-permute-start | bytes 786440 | tf_op jit(solution)/shard_map/ppermute | solution.py:475
  58.2 3.9 %collective-permute-start.19 = (bf16[4,256,128]{2,1,0:T(8,128)(2,1)S(1)}, bf16[4,256,128]{2,1,0:T(8,128)(2,1)S(1)}, u32[]{:S(2)}, u32[]{:S(2)}) collective-permute-start(bf16[4,256,128]{2,1,0:T(8,128)(2,1)S(1)} %shard_map.57), channel_id=1, source_target_pairs={{0,1},{1,0},{2,3},{3,2},{4,5},{5,4},{6,7},{7,6},{8,9},{9,8},{10,11... | collective-permute-start | bytes 786440 | tf_op jit(solution)/shard_map/ppermute | solution.py:475
  59.5 7.3 %collective-permute-start.17 = (bf16[2,256,128]{2,1,0:T(8,128)(2,1)S(1)}, bf16[2,256,128]{2,1,0:T(8,128)(2,1)S(1)}, u32[]{:S(2)}, u32[]{:S(2)}) collective-permute-start(bf16[2,256,128]{2,1,0:T(8,128)(2,1)S(1)} %get-tuple-element.151), channel_id=1, source_target_pairs={{0,18},{2,16},{4,22},{6,20},{8,26},{10,24},{12,30},{14,28},{16,2},... | collective-permute-start | bytes 393224 | tf_op jit(solution)/shard_map/ppermute | solution.py:484
  62.1 6.7 %collective-permute-start.20 = (bf16[2,256,128]{2,1,0:T(8,128)(2,1)S(1)}, bf16[2,256,128]{2,1,0:T(8,128)(2,1)S(1)}, u32[]{:S(2)}, u32[]{:S(2)}) collective-permute-start(bf16[2,256,128]{2,1,0:T(8,128)(2,1)S(1)} %get-tuple-element.162), channel_id=1, source_target_pairs={{0,2},{2,0},{4,6},{6,4},{8,10},{10,8},{12,14},{14,12},{1,3},{3,1},... | collective-permute-start | bytes 393224 | tf_op jit(solution)/shard_map/ppermute | solution.py:487
  62.7 6.1 %collective-permute-start.21 = (bf16[2,256,128]{2,1,0:T(8,128)(2,1)S(1)}, bf16[2,256,128]{2,1,0:T(8,128)(2,1)S(1)}, u32[]{:S(2)}, u32[]{:S(2)}) collective-permute-start(bf16[2,256,128]{2,1,0:T(8,128)(2,1)S(1)} %get-tuple-element.166), channel_id=1, source_target_pairs={{0,16},{16,0},{1,17},{17,1},{2,18},{18,2},{3,19},{19,3},{4,20},{20... | collective-permute-start | bytes 393224 | tf_op jit(solution)/shard_map/ppermute | solution.py:490
  63.2 1.3 %collective-permute-start.18 = (bf16[256,128]{1,0:T(8,128)(2,1)S(1)}, bf16[256,128]{1,0:T(8,128)(2,1)S(1)}, u32[]{:S(2)}, u32[]{:S(2)}) collective-permute-start(bf16[256,128]{1,0:T(8,128)(2,1)S(1)} %shard_map.60.refs_9_), channel_id=1, source_target_pairs={{0,1},{1,0},{2,3},{3,2},{4,5},{5,4},{6,7},{7,6},{8,9},{9,8},{10,11... | collective-permute-start | bytes 196616 | tf_op jit(solution)/shard_map/ppermute | solution.py:475
